TPU v7x, 256 devices: a whole 4x4x8 slice. The times are simulated.
256 devices in a mesh: wide: 16 (over y, z_hi, core), narrow: 16 (over z_lo, x).
Axes of the slice: x: 4, y: 4, z: 8 (z_hi: 2, z_lo: 4; z = z_hi * 4 + z_lo), core: 2. Of those that a mesh axis runs over, the one named last changes fastest.
Arguments:
- embeds: bfloat16 [32768, 512], P(('wide', 'narrow')), may hold values from -6 to 6
- weight: bfloat16 [512, 256], replicated, may hold values from -0.016479492 to 0.016479492
- solve: float32 [32768], P(('wide', 'narrow')), may hold values from -6 to 6
- probes: float32 [32768, 15], P(('wide', 'narrow')), may hold values from -6 to 6
- probe_solves: float32 [32768, 15], P(('wide', 'narrow')), may hold values from -6 to 6
Outputs:
- grad_rows: float32 [32768, 256], P(('wide', 'narrow'))
- grad_weight: float32 [512, 256], replicated
All inputs are finite; a program needn't handle non-finite values.
Results may differ from a plain program's by a relative error of at most 0.0042.
Values may be sent and summed in bfloat16 or wider, within the bound.
No kernel may reach another device: no remote copies, remote signals or barrier semaphores. Data moves between devices by JAX's collectives and lax.ppermute only.
A program may use at most 64 MiB of HBM per device.

v0:
```python
import math

import jax
import jax.numpy as jnp
from jax import lax
from jax.sharding import PartitionSpec as P


def side_rows(solve, probes, probe_solves):
    scale = (2.0 * probes.shape[1]) ** (-0.5)
    zero = jnp.zeros((solve.shape[0], 1), jnp.float32)
    left = jnp.concatenate([solve[:, None], probe_solves * scale, probes * scale, zero], axis=1)
    right = jnp.concatenate([solve[:, None], -probes * scale, -probe_solves * scale, zero], axis=1)
    return (left, right)


def pair_coupling(u_rows, left_rows, u_cols, right_cols):
    gram = jnp.einsum("rd,cd->rc", u_rows, u_cols, preferred_element_type=jnp.float32)
    row_sq = jnp.sum(jnp.square(u_rows.astype(jnp.float32)), axis=1)
    col_sq = jnp.sum(jnp.square(u_cols.astype(jnp.float32)), axis=1)
    dist = jnp.sqrt(jnp.maximum(row_sq[:, None] + col_sq[None, :] - 2.0 * gram, 0.0))
    root_five = math.sqrt(5.0)
    shape_term = 5.0 / 3.0 * (1.0 + root_five * dist) * jnp.exp(-root_five * dist)
    pair_weight = jnp.einsum(
        "rk,ck->rc",
        left_rows,
        right_cols,
        precision=lax.Precision.HIGHEST,
        preferred_element_type=jnp.float32,
    )
    return pair_weight * shape_term


def tile_terms(u_rows, left_rows, u_cols, right_cols):
    coupling = pair_coupling(u_rows, left_rows, u_cols, right_cols)
    mixed = jnp.dot(coupling.astype(jnp.bfloat16), u_cols, preferred_element_type=jnp.float32)
    return (mixed, jnp.sum(coupling, axis=1))


def make_sweep(u_rows, left_rows, carry, piece):
    u_cols, right_cols = piece
    width = u_cols.shape[0]
    step_cols = 512

    def one_step(index, state):
        cols = lax.dynamic_slice_in_dim(u_cols, index * step_cols, step_cols, 0)
        rights = lax.dynamic_slice_in_dim(right_cols, index * step_cols, step_cols, 0)
        mixed, row_total = tile_terms(u_rows, left_rows, cols, rights)
        return (state[0] + mixed, state[1] + row_total)

    return lax.fori_loop(0, width // step_cols, one_step, carry)


def empty_carry(rows, width):
    return (jnp.zeros((rows, width), jnp.float32), jnp.zeros((rows,), jnp.float32))


def shards(embeds, weight, solve, probes, probe_solves):
    feats = jnp.dot(embeds, weight, preferred_element_type=jnp.float32).astype(jnp.bfloat16)
    left, right = side_rows(solve, probes, probe_solves)
    rows, width = feats.shape
    bundle = (
        lax.all_gather(feats.astype(jnp.float32), "wide", axis=0, tiled=True).astype(feats.dtype),
        lax.all_gather(right, "wide", axis=0, tiled=True),
    )
    mixed, row_total = make_sweep(
        feats,
        left,
        empty_carry(rows, width),
        (
            lax.all_gather(bundle[0].astype(jnp.float32), "narrow", axis=0, tiled=True).astype(
                jnp.bfloat16
            ),
            lax.all_gather(bundle[1], "narrow", axis=0, tiled=True),
        ),
    )
    grad_rows = mixed - row_total[:, None] * feats.astype(jnp.float32)
    local_weight = jnp.dot(
        embeds.astype(jnp.float32).T,
        grad_rows,
        precision=lax.Precision.HIGHEST,
        preferred_element_type=jnp.float32,
    )
    grad_weight = lax.psum(local_weight, ("wide", "narrow"))
    total_points = rows * lax.axis_size("wide") * lax.axis_size("narrow")
    return (grad_rows, grad_weight / math.sqrt(total_points))


def solution(mesh):
    return jax.shard_map(
        shards,
        mesh=mesh,
        in_specs=(
            P(("wide", "narrow"), None),
            P(),
            P(("wide", "narrow")),
            P(("wide", "narrow"), None),
            P(("wide", "narrow"), None),
        ),
        out_specs=(P(("wide", "narrow"), None), P()),
        check_vma=False,
    )
```

profile of v0, /device:TPU:1, one launch (start us, length us, event | category | flops | bytes accessed | tf_op | source)
XLA Modules:
  0.0 986.7 jit_solution(12984123709124672464)
XLA Ops:
  8.1 1.7 convolution_convert_fusion
  11.4 37.2 %all_gather.12 = f32[2048,32]{0,1:T(8,128)} all-gather(f32[128,32]{0,1:T(8,128)S(1)} %get-tuple-element.185), channel_id=1, replica_groups=mesh['wide'=16,'narrow'=16] {'wide'}, dimensions={0}, use_global_device_ids=true | all-gather | bytes 278528 | tf_op jit(solution)/shard_map/all_gather | solution.py:64
  48.7 22.6 %all-gather.6.cloned.1.call-done = bf16[2048,256]{1,0:T(8,128)(2,1)} async-done(((bf16[128,256]{1,0:T(8,128)(2,1)}), bf16[2048,256]{1,0:T(8,128)(2,1)}) %all-gather.6.cloned.1.call-update) | async-done | bytes 1048592 | tf_op jit(solution)/shard_map/all_gather | solution.py:63
  71.5 75.9 %all-gather.4.cloned.1.call-done = f32[32768,32]{0,1:T(8,128)} async-done(((f32[2048,32]{0,1:T(8,128)}), f32[32768,32]{0,1:T(8,128)}) %all-gather.4.cloned.1.call-update) | async-done | bytes 4194320 | tf_op jit(solution)/shard_map/all_gather | solution.py:74
  147.4 195.9 %all-gather.8.cloned.1.call-done = bf16[32768,256]{1,0:T(8,128)(2,1)} async-done(((bf16[2048,256]{1,0:T(8,128)(2,1)}), bf16[32768,256]{1,0:T(8,128)(2,1)}) %all-gather.8.cloned.1.call-update) | async-done | bytes 16777232 | tf_op jit(solution)/shard_map/all_gather | solution.py:71
  343.4 384.0 %while.16 = (s32[]{:T(128)}, f32[128,256]{1,0:T(8,128)S(1)}, f32[128]{0:T(128)S(1)}, f32[32768,32]{0,1:T(8,128)}, f32[128,32]{1,0:T(8,128)S(1)}, /*index=5*/bf16...) while((s32[]{:T(128)}, f32[128,256]{1,0:T(8,128)S(1)}, ...), condition=%wide.region_4.0_spmd.clone, body=%wide.region_0.0_spmd.clone.sunk | while | flops 93617664 | bytes 2055358 | solution.py:51
  346.7 1.5 fusion.39
  352.7 1.5 fusion.39
  358.7 1.5 fusion.39
  364.7 1.5 fusion.39
  370.7 1.5 fusion.39
  376.7 1.5 fusion.39
  382.7 1.5 fusion.39
  388.7 1.5 fusion.39
  394.7 1.5 fusion.39
  400.7 1.5 fusion.39
  406.7 1.5 fusion.39
  412.7 1.5 fusion.39
  418.7 1.5 fusion.39
  424.7 1.5 fusion.39
  430.7 1.5 fusion.39
  436.7 1.5 fusion.39
  448.7 1.5 fusion.39
  460.7 1.5 fusion.39
  472.7 1.5 fusion.39
  484.7 1.5 fusion.39
  496.7 1.5 fusion.39
  508.7 1.5 fusion.39
  520.7 1.5 fusion.39
  532.7 1.5 fusion.39
  544.7 1.5 fusion.39
  556.7 1.5 fusion.39
  568.7 1.5 fusion.39
  580.7 1.5 fusion.39
  592.7 1.5 fusion.39
  604.7 1.5 fusion.39
  616.7 1.5 fusion.39
  628.7 1.5 fusion.39
  640.7 1.5 fusion.39
  652.7 1.5 fusion.39
  664.7 1.5 fusion.39
  676.7 1.5 fusion.39
  688.7 1.5 fusion.39
  700.7 1.5 fusion.39
  712.7 1.5 fusion.39
  724.7 1.5 fusion.39
  728.3 2.2 convolution_bitcast_fusion.1
  730.5 247.5 %all-reduce.2.cloned.1.call-done = f32[512,256]{0,1:T(8,128)} async-done(((f32[512,256]{0,1:T(8,128)}), f32[512,256]{0,1:T(8,128)}) %all-reduce.2.cloned.1.call-update) | async-done | bytes 524304 | tf_op jit(solution)/shard_map/psum | solution.py:84
  (365 shorter events, 328.2 us)
Async XLA Ops:
  7.2 1.0 copy-start
  7.2 64.2 %all-gather.6.cloned.1.call-start = ((), (), s32[]{:S(2)}) async-start(), calls=%async_computation.1 | async-start | bytes 1114112 | tf_op jit(solution)/shard_map/all_gather | solution.py:63
  9.9 137.6 %all-gather.4.cloned.1.call-start = ((), (), s32[]{:S(2)}) async-start(), calls=%async_computation | async-start | bytes 4456448 | tf_op jit(solution)/shard_map/all_gather | solution.py:74
  48.7 294.7 %all-gather.8.cloned.1.call-start = ((), (), s32[]{:S(2)}) async-start(), calls=%async_computation.2 | async-start | bytes 17825792 | tf_op jit(solution)/shard_map/all_gather | solution.py:71
  71.4 906.7 %all-reduce.2.cloned.1.call-start = ((), (), s32[]{:S(2)}) async-start(), calls=%async_computation.3 | async-start | bytes 1048576 | tf_op jit(solution)/shard_map/psum | solution.py:84
  728.3 251.8 %copy-start.1 = (f32[128,256]{1,0:T(8,128)}, f32[128,256]{1,0:T(8,128)S(1)}, u32[]{:S(2)}) copy-start(f32[128,256]{1,0:T(8,128)S(1)} %multiply_subtract_fusion) | copy-start | bytes 393220
Sparse Core Ops, SparseCore 0:
  11.3 60.0 all-gather.5
  73.1 74.2 all-gather.3
  149.2 194.1 all-gather.7
  730.6 247.3 all-reduce.1
where the time goes:
time: 999 us; the launch traced here: 987 us
  waiting for transfers between devices  542 us (54%)
  matrix products  253 us (25%)
  other arithmetic  135 us (14%)
  blocking collectives  37.2 us (4%)
  between operations  13.8 us (1%)
    psum x1, waiting for transfers between devices, shards(): grad_weight = lax.psum(local_weight, ('wide', 'narrow'))  248 us
    all_gather x1, waiting for transfers between devices, shards(): lax.all_gather(bundle[0].astype(jnp.float32), 'narrow', axis=0, tiled=True)  196 us
    dot_general x64, matrix products, pair_coupling(): jnp.einsum('rk,ck->rc', left_rows, right_cols, precision=lax.Precision.HI...  93.4 us
    dot_general x64, matrix products, pair_coupling(): jnp.einsum('rd,cd->rc', u_rows, u_cols, preferred_element_type=jnp.float32)  78.2 us
    dot_general x64, matrix products, tile_terms(): jnp.dot(coupling.astype(jnp.bfloat16), u_cols, preferred_element_type=jnp...  77.4 us
    all_gather x1, waiting for transfers between devices, shards(): lax.all_gather(bundle[1], 'narrow', axis=0, tiled=True)  75.9 us
    reduce_sum x64, other arithmetic, pair_coupling(): col_sq = jnp.sum(jnp.square(u_cols.astype(jnp.float32)), axis=1)  70.7 us
    reduce_sum x64, other arithmetic, pair_coupling(): row_sq = jnp.sum(jnp.square(u_rows.astype(jnp.float32)), axis=1)  60.4 us
  transfers between devices with their start and end apart: 4, of which 4 were waited for; matrix products, arithmetic and copies ran while one was open for 0% of the time, Pallas kernels for 0%

commit v1 on v0

v1 whole, which is shorter than its diff:
```python
import functools
import math

import jax
import jax.numpy as jnp
import numpy as np
from jax import lax
from jax.experimental import pallas as pl
from jax.experimental.pallas import tpu as pltpu
from jax.sharding import Mesh, PartitionSpec as P

LOG2E = math.log2(math.e)
ROOT5 = math.sqrt(5.0)
ALL = ("y", "zh", "core", "zl", "x")
PLANE = ("y", "core", "x")
DEPTH = ("zh", "zl")
F32 = jnp.float32
BF16 = jnp.bfloat16
VMEM = pl.BlockSpec(memory_space=pltpu.VMEM)


def params(mib):
    return pltpu.CompilerParams(vmem_limit_bytes=mib << 20)


def dot_nt(a, b):
    return lax.dot_general(a, b, (((1,), (1,)), ((), ())), preferred_element_type=F32)


def dot_tn(a, b):
    return lax.dot_general(a, b, (((0,), (0,)), ((), ())), preferred_element_type=F32)


def pack_kernel(embeds, weight, solve, probes, probe_solves, out):
    rows, width = embeds.shape[0], weight.shape[1]
    count = probes.shape[1]
    feats = jnp.dot(embeds[...], weight[...], preferred_element_type=F32).astype(BF16)
    out[:, :width] = feats
    wide = feats.astype(F32)
    sq = jnp.sum(wide * wide, axis=1, keepdims=True)
    sq_hi = sq.astype(BF16).astype(F32)
    sq_mid = (sq - sq_hi).astype(BF16).astype(F32)
    sq_lo = sq - sq_hi - sq_mid
    fold = math.sqrt(5.0 / 3.0 * ROOT5)
    scale = (2.0 * count) ** (-0.5) * fold
    factors = jnp.concatenate(
        [
            solve[...] * fold,
            probes[...] * -scale,
            probe_solves[...] * -scale,
            jnp.zeros((rows, 1), F32),
        ],
        axis=1,
    )
    hi = factors.astype(BF16).astype(F32)
    lo = factors - hi
    lane = lax.broadcasted_iota(jnp.int32, (rows, 32), 1)
    tail = jnp.where(lane == 0, sq_hi, jnp.where(lane == 1, sq_mid, jnp.where(lane == 2, sq_lo, 0.0)))
    out[:, width:] = jnp.concatenate([hi, lo, hi, tail], axis=1).astype(BF16)


def left_map(count):
    source = np.zeros((32,), np.int32)
    sign = np.zeros((32,), np.float32)
    sign[0] = 1.0
    for k in range(count):
        source[1 + k], sign[1 + k] = 1 + count + k, -1.0
        source[1 + count + k], sign[1 + count + k] = 1 + k, -1.0
    table = np.zeros((128, 128), np.float32)
    for group, offset in ((0, 0), (1, 0), (2, 32)):
        for k in range(32):
            table[offset + source[k], 32 * group + k] = sign[k]
    return jnp.asarray(table, BF16)


def tile_kernel(sub, step, table, rows_ref, *refs):
    *columns, out = refs
    width = out.shape[1]
    rows = rows_ref.shape[0]
    u_rows = rows_ref[:, :width]
    fac = rows_ref[:, width:]
    twice = (u_rows.astype(F32) * -2.0).astype(BF16)
    left = jnp.dot(fac, table[...], preferred_element_type=F32).astype(BF16)
    lane = lax.broadcasted_iota(jnp.int32, (128, 128), 0)
    pick = jnp.where((lane >= 96) & (lane < 99), 1.0, 0.0).astype(BF16)
    sq_rows = jnp.dot(fac, pick, preferred_element_type=F32)[:, :1]
    lane = lax.broadcasted_iota(jnp.int32, (8, 128), 1)
    pick_cols = jnp.where((lane >= 96) & (lane < 99), 1.0, 0.0).astype(BF16)
    blocks = [slice(k, k + sub) for k in range(0, rows, sub)]
    acc = [jnp.zeros((sub, width), F32) for _ in blocks]
    total = [jnp.zeros((sub, 128), F32) for _ in blocks]
    work = [
        (ref, start, k)
        for ref in columns
        for start in range(0, ref.shape[0], step)
        for k in range(len(blocks))
    ]

    def products(ref, start, k):
        u_cols = ref[start : start + step, :width]
        right = ref[start : start + step, width:]
        sq_cols = dot_nt(pick_cols, right)[:1]
        return u_cols, sq_cols, dot_nt(twice[blocks[k]], u_cols), dot_nt(left[blocks[k]], right)

    ahead = products(*work[0])
    for index, (_, _, k) in enumerate(work):
        u_cols, sq_cols, cross, pair = ahead
        if index + 1 < len(work):
            ahead = products(*work[index + 1])
        d2 = jnp.maximum((sq_rows[blocks[k]] + sq_cols) + cross, 1e-30)
        dist = d2 * lax.rsqrt(d2)
        coupling = pair * ((dist + 1.0 / ROOT5) * jnp.exp2(dist * (-ROOT5 * LOG2E)))
        for j in range(0, step, 128):
            total[k] = total[k] + coupling[:, j : j + 128]
        acc[k] = acc[k] + jnp.dot(coupling.astype(BF16), u_cols, preferred_element_type=F32)
    for k, block in enumerate(blocks):
        row_total = jnp.sum(total[k], axis=1, keepdims=True)
        out[block, :] = (acc[k] - row_total * u_rows[block].astype(F32)).astype(out.dtype)


def sum_rows_kernel(place, a, b, c, d, embeds, partial, own, *others):
    rows = own.shape[0]
    count = 1 + len(others)
    total = (a[...] + b[...].astype(F32)) + (c[...].astype(F32) + d[...].astype(F32))
    hi = total.astype(BF16)
    lo = (total - hi.astype(F32)).astype(BF16)
    own[...] = total[:rows]
    for k, ref in enumerate(others):
        ref[...] = hi[(k + 1) * rows : (k + 2) * rows]
    weight = jnp.zeros(partial.shape, F32)
    for k in range(count):
        start = pl.multiple_of(lax.rem(place[0] + k, count) * rows, rows)
        line = embeds[pl.ds(start, rows), :]
        block = slice(k * rows, (k + 1) * rows)
        weight = weight + (dot_tn(line, hi[block]) + dot_tn(line, lo[block]))
    partial[...] = weight.astype(BF16)


def finish_rows_kernel(own, b, c, d, grad_rows):
    grad_rows[...] = (own[...] + b[...].astype(F32)) + (c[...].astype(F32) + d[...].astype(F32))


def sum_spread_kernel(parts, out):
    total = parts[0].astype(F32)
    for k in range(1, parts.shape[0]):
        total = total + parts[k].astype(F32)
    low = total.astype(out.dtype)
    for k in range(out.shape[0]):
        out[k] = low


def sum_spread(parts, copies, dtype):
    return pl.pallas_call(
        sum_spread_kernel,
        out_shape=jax.ShapeDtypeStruct((copies,) + parts.shape[1:], dtype),
        in_specs=[VMEM],
        out_specs=VMEM,
        compiler_params=params(16),
        name="sum_spread",
    )(parts)


def ring(array, axis, size, shift):
    return lax.ppermute(array, axis, [(i, (i + shift) % size) for i in range(size)])


def exchange(array, axes):
    return lax.all_to_all(array, axes, split_axis=0, concat_axis=0, tiled=True)


def shards(sizes, embeds, weight, solve, probes, probe_solves):
    rows, width = embeds.shape[0], weight.shape[1]
    n_x, n_y, n_z = sizes["x"], sizes["y"], sizes["zh"] * sizes["zl"]
    pack = pl.pallas_call(
        pack_kernel,
        out_shape=jax.ShapeDtypeStruct((rows, width + 128), BF16),
        in_specs=[VMEM] * 5,
        out_specs=VMEM,
        compiler_params=params(16),
        name="pack",
    )(embeds, weight, solve[:, None], probes, probe_solves)

    embeds_line = lax.all_gather(embeds, "y", axis=0, tiled=True)

    line = jnp.concatenate([pack] + [ring(pack, "y", n_y, -d) for d in range(1, n_y)], axis=0)
    pair = jnp.concatenate([pack, ring(pack, DEPTH, n_z, n_z // 2)], axis=0)
    pair, _ = lax.optimization_barrier((pair, line))
    columns = [pair] + [ring(pair, DEPTH, n_z, d) for d in (1, -1, 2)]
    columns += [ring(part, "core", 2, 1) for part in columns]
    lines = [line] + [ring(line, "x", n_x, -d) for d in range(1, n_x)]


    table = left_map(probes.shape[1])
    back = {}
    for d in (0, 3, 1, 2):
        if d == 3:
            lines[d], _, embeds_line = lax.optimization_barrier((lines[d], back[0], embeds_line))
        elif d != 0:
            lines[d], _ = lax.optimization_barrier((lines[d], back[0]))
        part = pl.pallas_call(
            functools.partial(tile_kernel, 256, 256),
            out_shape=jax.ShapeDtypeStruct((n_y * rows, width), F32 if d == 0 else BF16),
            in_specs=[VMEM] * (2 + len(columns)),
            out_specs=VMEM,
            compiler_params=params(40),
            name="tile",
        )(table, lines[d], *columns)
        back[d] = part if d == 0 else ring(part, "x", n_x, d)

    sums = pl.pallas_call(
        sum_rows_kernel,
        out_shape=[
            jax.ShapeDtypeStruct((embeds.shape[1], width), BF16),
            jax.ShapeDtypeStruct((rows, width), F32),
        ]
        + [jax.ShapeDtypeStruct((rows, width), BF16)] * (n_y - 1),
        in_specs=[pl.BlockSpec(memory_space=pltpu.SMEM)] + [VMEM] * (n_x + 1),
        out_specs=[VMEM] * (n_y + 1),
        compiler_params=params(16),
        name="sum_rows",
    )(lax.axis_index("y")[None], *(back[d] for d in range(n_x)), embeds_line)
    partial, own_rows, *other_rows = sums
    arrived = [ring(block, "y", n_y, d + 1) for d, block in enumerate(other_rows)]

    n_plane = n_x * n_y * 2
    pieces = exchange(partial.reshape(n_plane, -1, width), PLANE)
    pieces, arrived = lax.optimization_barrier((pieces, arrived))
    pieces = exchange(sum_spread(pieces, n_z, F32), DEPTH)
    pieces = exchange(sum_spread(pieces, n_plane, BF16), PLANE)
    total_points = rows * n_plane * n_z
    grad_weight = pieces.reshape(-1, width).astype(F32) * (1.0 / math.sqrt(total_points))

    grad_rows = pl.pallas_call(
        finish_rows_kernel,
        out_shape=jax.ShapeDtypeStruct((rows, width), F32),
        in_specs=[VMEM] * 4,
        out_specs=VMEM,
        compiler_params=params(16),
        name="finish_rows",
    )(own_rows, *arrived)
    return grad_rows, grad_weight


def solution(mesh):
    sizes = {"y": 4, "zh": 2, "core": 2, "zl": 4, "x": 4}
    fine = Mesh(mesh.devices.reshape(tuple(sizes[a] for a in ALL)), ALL)
    return jax.shard_map(
        functools.partial(shards, sizes),
        mesh=fine,
        in_specs=(P(ALL, None), P(), P(ALL), P(ALL, None), P(ALL, None)),
        out_specs=(P(ALL, None), P()),
        check_vma=False,
    )
```

time: 999 us -> 122 us (0.12); the launches traced: 987 us -> 122 us
  waiting for transfers between devices: 542 us -> 27.7 us
  matrix products: 253 us -> 0 us
  other arithmetic: 135 us -> 0.92 us
  starting transfers between devices: 0.16 us -> 54.7 us
  blocking collectives: 37.2 us -> 21.4 us
  Pallas kernels: 0 us -> 13.5 us
  between operations: 13.8 us -> 0.79 us
    all_gather x3 -> x0, waiting for transfers between devices: 294 us -> none  [the longest x1 196 us: shards(): lax.all_gather(bundle[0].astype(jnp.float32), 'narrow', axis=0, tiled=True)]
    dot_general x194 -> x0, matrix products: 253 us -> none  [the longest x64 93.4 us: pair_coupling(): jnp.einsum('rk,ck->rc', left_rows, right_cols, precision=lax.Precision.HI...]
    psum x1 -> x0, waiting for transfers between devices: 248 us -> none  [shards(): grad_weight = lax.psum(local_weight, ('wide', 'narrow'))]
    reduce_sum x128 -> x0, other arithmetic: 131 us -> none  [the longest x64 70.7 us: pair_coupling(): col_sq = jnp.sum(jnp.square(u_cols.astype(jnp.float32)), axis=1)]
    ppermute x0 -> x20, starting transfers between devices: none -> 39.7 us  [ring(): lax.ppermute(array, axis, [(i, (i + shift) % size) for i in range(size)])]
    all_gather x1, blocking collectives: 37.2 us -> 11.3 us  [shards(): embeds_line = lax.all_gather(embeds, 'y', axis=0, tiled=True)]
    ppermute x0 -> x20, waiting for transfers between devices: none -> 19.5 us  [ring(): lax.ppermute(array, axis, [(i, (i + shift) % size) for i in range(size)])]
    all_to_all x0 -> x2, starting transfers between devices: none -> 15 us  [exchange(): return lax.all_to_all(array, axes, split_axis=0, concat_axis=0, tiled=True)]
  transfers between devices with their start and end apart: 4 -> 22, of which waited for: 4 -> 9; matrix products, arithmetic and copies ran while one was open for 0% -> 0% of each run, Pallas kernels for 0% -> 9%
where the time goes in v1:
time: 122 us
  starting transfers between devices  54.7 us (45%)
  waiting for transfers between devices  27.7 us (23%)
  blocking collectives  21.4 us (18%)
  Pallas kernels  13.5 us (11%)
  local copies, waits for them, and re-layouts  2.63 us (2%)
    ppermute x20, starting transfers between devices, ring(): lax.ppermute(array, axis, [(i, (i + shift) % size) for i in range(size)])  39.7 us
    ppermute x20, waiting for transfers between devices, ring(): lax.ppermute(array, axis, [(i, (i + shift) % size) for i in range(size)])  19.5 us
    all_to_all x2, starting transfers between devices, exchange(): return lax.all_to_all(array, axes, split_axis=0, concat_axis=0, tiled=True)  15 us
    all_gather x1, blocking collectives, shards(): embeds_line = lax.all_gather(embeds, 'y', axis=0, tiled=True)  11.3 us
    pallas_call x4, Pallas kernels, shards(): pl.pallas_call(functools.partial(tile_kernel, 256, 256), out_shape=jax.Sh...  10.2 us
    all_to_all x1, blocking collectives, exchange(): return lax.all_to_all(array, axes, split_axis=0, concat_axis=0, tiled=True)  10.1 us
    all_to_all x2, waiting for transfers between devices, exchange(): return lax.all_to_all(array, axes, split_axis=0, concat_axis=0, tiled=True)  8.21 us
    unnamed x12, local copies, waits for them, and re-layouts  2.52 us
  transfers between devices with their start and end apart: 22, of which 9 were waited for; matrix products, arithmetic and copies ran while one was open for 0% of the time, Pallas kernels for 9%

profile of v1, /device:TPU:1, one launch (start us, length us, event | category | flops | bytes accessed | tf_op | source)
XLA Modules:
  0.0 121.7 jit_solution(1080589872298605656)
XLA Ops:
  0.6 0.6 copy-done.4
  1.3 0.1 copy.8.solve
  1.4 0.8 copy.9.probes
  2.2 0.1 copy.10.probe_solves
  2.3 0.0 copy-start.2
  2.3 0.9 copy-done.2
  3.3 0.4 pack.1
  3.7 7.8 %collective-permute-start.3 = (bf16[128,384]{1,0:T(8,128)(2,1)S(1)}, bf16[128,384]{1,0:T(8,128)(2,1)S(1)}, u32[]{:S(2)}, u32[]{:S(2)}) collective-permute-start(bf16[128,384]{1,0:T(8,128)(2,1)S(1)} %pack.1), channel_id=1, source_target_pairs={{0,32},{4,36},{8,40},{12,44},{32,0},{36,4},{40,8},{44,12},{1,33},{... | collective-permute-start | bytes 294920 | tf_op jit(solution)/shard_map/ppermute | solution.py:164
  11.5 1.3 %collective-permute-start.2 = (bf16[128,384]{1,0:T(8,128)(2,1)S(1)}, bf16[128,384]{1,0:T(8,128)(2,1)S(1)}, u32[]{:S(2)}, u32[]{:S(2)}) collective-permute-start(bf16[128,384]{1,0:T(8,128)(2,1)S(1)} %pack.1), channel_id=1, source_target_pairs={{0,64},{64,128},{128,192},{192,0},{1,65},{65,129},{129,193},{193,1... | collective-permute-start | bytes 294920 | tf_op jit(solution)/shard_map/ppermute | solution.py:164
  12.8 2.6 %collective-permute-start.1 = (bf16[128,384]{1,0:T(8,128)(2,1)S(1)}, bf16[128,384]{1,0:T(8,128)(2,1)S(1)}, u32[]{:S(2)}, u32[]{:S(2)}) collective-permute-start(bf16[128,384]{1,0:T(8,128)(2,1)S(1)} %pack.1), channel_id=1, source_target_pairs={{0,128},{64,192},{128,0},{192,64},{1,129},{65,193},{129,1},{193,65... | collective-permute-start | bytes 294920 | tf_op jit(solution)/shard_map/ppermute | solution.py:164
  15.4 1.1 collective-permute-start
  16.5 2.6 %collective-permute-done.1 = bf16[128,384]{1,0:T(8,128)(2,1)S(1)} collective-permute-done((bf16[128,384]{1,0:T(8,128)(2,1)S(1)}, bf16[128,384]{1,0:T(8,128)(2,1)S(1)}, u32[]{:S(2)}, u32[]{:S(2)}) %collective-permute-start.1) | collective-permute-done | bytes 98336 | tf_op jit(solution)/shard_map/ppermute | solution.py:164
  19.1 0.4 collective-permute-done
  19.5 0.0 copy-start
  19.5 1.3 %collective-permute-start.6 = (bf16[256,384]{1,0:T(8,128)(2,1)S(1)}, bf16[256,384]{1,0:T(8,128)(2,1)S(1)}, u32[]{:S(2)}, u32[]{:S(2)}) collective-permute-start(bf16[256,384]{1,0:T(8,128)(2,1)S(1)} %pad_maximum_fusion.1.refs_0_), channel_id=1, source_target_pairs={{0,8},{4,12},{8,32},{12,36},{32,40},{36,44},{40,0},{44,4},{1,9},{5... | collective-permute-start | bytes 589832 | tf_op jit(solution)/shard_map/ppermute | solution.py:164
  20.8 2.3 %collective-permute-start.7 = (bf16[256,384]{1,0:T(8,128)(2,1)S(1)}, bf16[256,384]{1,0:T(8,128)(2,1)S(1)}, u32[]{:S(2)}, u32[]{:S(2)}) collective-permute-start(bf16[256,384]{1,0:T(8,128)(2,1)S(1)} %pad_maximum_fusion.1.refs_0_), channel_id=1, source_target_pairs={{0,16},{16,0},{1,17},{17,1},{2,18},{18,2},{3,19},{19,3},{4,20},{20... | collective-permute-start | bytes 589832 | tf_op jit(solution)/shard_map/ppermute | solution.py:164
  23.1 1.9 %collective-permute-start.5 = (bf16[256,384]{1,0:T(8,128)(2,1)S(1)}, bf16[256,384]{1,0:T(8,128)(2,1)S(1)}, u32[]{:S(2)}, u32[]{:S(2)}) collective-permute-start(bf16[256,384]{1,0:T(8,128)(2,1)S(1)} %pad_maximum_fusion.1.refs_0_), channel_id=1, source_target_pairs={{0,44},{4,0},{8,4},{12,8},{32,12},{36,32},{40,36},{44,40},{1,45},{... | collective-permute-start | bytes 589832 | tf_op jit(solution)/shard_map/ppermute | solution.py:164
  25.1 2.2 %collective-permute-done.6.refs_3_ = bf16[256,384]{1,0:T(8,128)(2,1)S(1)} collective-permute-done((bf16[256,384]{1,0:T(8,128)(2,1)S(1)}, bf16[256,384]{1,0:T(8,128)(2,1)S(1)}, u32[]{:S(2)}, u32[]{:S(2)}) %collective-permute-start.6) | collective-permute-done | bytes 196640 | tf_op jit(solution)/shard_map/ppermute | solution.py:164
  27.3 6.8 %collective-permute-start.10 = (bf16[256,384]{1,0:T(8,128)(2,1)S(1)}, bf16[256,384]{1,0:T(8,128)(2,1)S(1)}, u32[]{:S(2)}, u32[]{:S(2)}) collective-permute-start(bf16[256,384]{1,0:T(8,128)(2,1)S(1)} %collective-permute-done.6.refs_3_), channel_id=1, source_target_pairs={{0,16},{16,0},{1,17},{17,1},{2,18},{18,2},{3,19},{19,3},{4,20},{20... | collective-permute-start | bytes 589832 | tf_op jit(solution)/shard_map/ppermute | solution.py:164
  34.1 2.8 %collective-permute-start.13 = (bf16[512,384]{1,0:T(8,128)(2,1)S(1)}, bf16[512,384]{1,0:T(8,128)(2,1)S(1)}, u32[]{:S(2)}, u32[]{:S(2)}) collective-permute-start(bf16[512,384]{1,0:T(8,128)(2,1)S(1)} %pad_maximum_fusion.rows_ref), channel_id=1, source_target_pairs={{0,2},{1,3},{2,0},{3,1},{4,6},{5,7},{6,4},{7,5},{8,10},{9,11},{10,... | collective-permute-start | bytes 1179656 | tf_op jit(solution)/shard_map/ppermute | solution.py:164
  36.8 0.9 collective-permute-start.11
  37.7 0.6 collective-permute-start.15
  38.3 0.8 collective-permute-start.9
  39.2 0.1 collective-permute-start.8
  39.3 11.3 %all_gather.3.embeds = bf16[512,512]{1,0:T(8,128)(2,1)S(1)} all-gather(bf16[128,512]{1,0:T(8,128)(2,1)S(1)} %copy-done.1), channel_id=1, replica_groups=mesh['y'=4,'zh'=2,'core'=2,'zl'=4,'x'=4] {'y'}, dimensions={0}, use_global_device_ids=true | all-gather | bytes 655360 | tf_op jit(solution)/shard_map/all_gather | solution.py:183
  50.6 2.6 %tile.4.a = f32[512,256]{1,0:T(8,128)S(1)} custom-call(bf16[128,128]{1,0:T(8,128)(2,1)S(1)} %copy-done, bf16[512,384]{1,0:T(8,128)(2,1)S(1)} %pad_maximum_fusion.rows_ref, bf16[256,384]{1,0:T(8,128)(2,1)S(1)} %pad_maximum_fusion.1.refs_0_, bf16[256,384]{1,0:T(8,128)(2,1)S(1)} %collective-permute-done.4.refs_1_, ...), custom_call_target="tpu_custom_call" | custom-call | tf_op jit(solution)/shard_map/tile/pallas_call | solution.py:200
  53.1 1.7 %collective-permute-done.11.rows_ref = bf16[512,384]{1,0:T(8,128)(2,1)S(1)} collective-permute-done((bf16[512,384]{1,0:T(8,128)(2,1)S(1)}, bf16[512,384]{1,0:T(8,128)(2,1)S(1)}, u32[]{:S(2)}, u32[]{:S(2)}) %collective-permute-start.11) | collective-permute-done | bytes 393248 | tf_op jit(solution)/shard_map/ppermute | solution.py:164
  54.9 2.6 %tile.5 = bf16[512,256]{1,0:T(8,128)(2,1)S(1)} custom-call(bf16[128,128]{1,0:T(8,128)(2,1)S(1)} %copy-done, bf16[512,384]{1,0:T(8,128)(2,1)S(1)} %collective-permute-done.11.rows_ref, bf16[256,384]{1,0:T(8,128)(2,1)S(1)} %pad_maximum_fusion.1.refs_0_, bf16[256,384]{1,0:T(8,128)(2,1)S(1)} %collective-permute-done.4.refs_1_, ...), custom_call_target="tpu_custom_call" | custom-call | tf_op jit(solution)/shard_map/tile/pallas_call | solution.py:200
  57.4 1.5 %collective-permute-start.12 = (bf16[512,256]{1,0:T(8,128)(2,1)S(1)}, bf16[512,256]{1,0:T(8,128)(2,1)S(1)}, u32[]{:S(2)}, u32[]{:S(2)}) collective-permute-start(bf16[512,256]{1,0:T(8,128)(2,1)S(1)} %tile.5), channel_id=1, source_target_pairs={{0,1},{1,2},{2,3},{3,0},{4,5},{5,6},{6,7},{7,4},{8,9},{9,10},{10,1... | collective-permute-start | bytes 786440 | tf_op jit(solution)/shard_map/ppermute | solution.py:164
  59.0 2.6 %tile.6 = bf16[512,256]{1,0:T(8,128)(2,1)S(1)} custom-call(bf16[128,128]{1,0:T(8,128)(2,1)S(1)} %copy-done, bf16[512,384]{1,0:T(8,128)(2,1)S(1)} %collective-permute-done.13.rows_ref, bf16[256,384]{1,0:T(8,128)(2,1)S(1)} %pad_maximum_fusion.1.refs_0_, bf16[256,384]{1,0:T(8,128)(2,1)S(1)} %collective-permute-done.4.refs_1_, ...), custom_call_target="tpu_custom_call" | custom-call | tf_op jit(solution)/shard_map/tile/pallas_call | solution.py:200
  61.5 2.5 %collective-permute-start.14 = (bf16[512,256]{1,0:T(8,128)(2,1)S(1)}, bf16[512,256]{1,0:T(8,128)(2,1)S(1)}, u32[]{:S(2)}, u32[]{:S(2)}) collective-permute-start(bf16[512,256]{1,0:T(8,128)(2,1)S(1)} %tile.6), channel_id=1, source_target_pairs={{0,2},{1,3},{2,0},{3,1},{4,6},{5,7},{6,4},{7,5},{8,10},{9,11},{10,... | collective-permute-start | bytes 786440 | tf_op jit(solution)/shard_map/ppermute | solution.py:164
  64.0 2.6 %tile.7 = bf16[512,256]{1,0:T(8,128)(2,1)S(1)} custom-call(bf16[128,128]{1,0:T(8,128)(2,1)S(1)} %copy-done, bf16[512,384]{1,0:T(8,128)(2,1)S(1)} %collective-permute-done.15.rows_ref, bf16[256,384]{1,0:T(8,128)(2,1)S(1)} %pad_maximum_fusion.1.refs_0_, bf16[256,384]{1,0:T(8,128)(2,1)S(1)} %collective-permute-done.4.refs_1_, ...), custom_call_target="tpu_custom_call" | custom-call | tf_op jit(solution)/shard_map/tile/pallas_call | solution.py:200
  66.6 0.3 collective-permute-start.16
  66.9 6.0 %collective-permute-done.14.c = bf16[512,256]{1,0:T(8,128)(2,1)S(1)} collective-permute-done((bf16[512,256]{1,0:T(8,128)(2,1)S(1)}, bf16[512,256]{1,0:T(8,128)(2,1)S(1)}, u32[]{:S(2)}, u32[]{:S(2)}) %collective-permute-start.14) | collective-permute-done | bytes 262176 | tf_op jit(solution)/shard_map/ppermute | solution.py:164
  72.9 2.1 %collective-permute-done.16.d = bf16[512,256]{1,0:T(8,128)(2,1)S(1)} collective-permute-done((bf16[512,256]{1,0:T(8,128)(2,1)S(1)}, bf16[512,256]{1,0:T(8,128)(2,1)S(1)}, u32[]{:S(2)}, u32[]{:S(2)}) %collective-permute-start.16) | collective-permute-done | bytes 262176 | tf_op jit(solution)/shard_map/ppermute | solution.py:164
  75.1 1.5 %sum_rows.1 = (bf16[512,256]{1,0:T(8,128)(2,1)}, f32[128,256]{1,0:T(8,128)S(1)}, bf16[128,256]{1,0:T(8,128)(2,1)S(1)}, bf16[128,256]{1,0:T(8,128)(2,1)S(1)}, bf16[128,256]{1,0:T(8,128)(2,1)S(1)}) custom-call(s32[1]{0:T(128)} %bitcast.place, f32[512,256]{1,0:T(8,128)S(1)} %tile.4.a, bf16[512,256]{1,0:T(8,128)(2,1)S(1)} %collective-permute-done.12.b, ...), custom_call_target="tpu_custom_call" | custom-call | tf_op jit(solution)/shard_map/sum_rows/pallas_call | solution.py:210
  76.5 7.6 %all-to-all-start = ((bf16[32,16,256]{2,1,0:T(8,128)(2,1)}), bf16[32,16,256]{2,1,0:T(8,128)(2,1)S(1)}, u32[]{:S(2)}, u32[]{:S(2)}) async-start(bf16[32,16,256]{2,1,0:T(8,128)(2,1)} %bitcast.2), calls=%async_computation | async-start | bytes 524288 | tf_op jit(solution)/shard_map/all_to_all | solution.py:168
  84.1 1.5 %collective-permute-start.17 = (bf16[128,256]{1,0:T(8,128)(2,1)S(1)}, bf16[128,256]{1,0:T(8,128)(2,1)S(1)}, u32[]{:S(2)}, u32[]{:S(2)}) collective-permute-start(bf16[128,256]{1,0:T(8,128)(2,1)S(1)} %get-tuple-element.23), channel_id=1, source_target_pairs={{0,64},{64,128},{128,192},{192,0},{1,65},{65,129},{129,193},{193,1... | collective-permute-start | bytes 196616 | tf_op jit(solution)/shard_map/ppermute | solution.py:164
  85.6 2.4 %collective-permute-start.18 = (bf16[128,256]{1,0:T(8,128)(2,1)S(1)}, bf16[128,256]{1,0:T(8,128)(2,1)S(1)}, u32[]{:S(2)}, u32[]{:S(2)}) collective-permute-start(bf16[128,256]{1,0:T(8,128)(2,1)S(1)} %get-tuple-element.24), channel_id=1, source_target_pairs={{0,128},{64,192},{128,0},{192,64},{1,129},{65,193},{129,1},{193,65... | collective-permute-start | bytes 196616 | tf_op jit(solution)/shard_map/ppermute | solution.py:164
  88.1 1.1 collective-permute-start.19
  89.2 1.0 collective-permute-done.17.b
  90.1 3.5 %collective-permute-done.18.c = bf16[128,256]{1,0:T(8,128)(2,1)S(1)} collective-permute-done((bf16[128,256]{1,0:T(8,128)(2,1)S(1)}, bf16[128,256]{1,0:T(8,128)(2,1)S(1)}, u32[]{:S(2)}, u32[]{:S(2)}) %collective-permute-start.18) | collective-permute-done | bytes 65568 | tf_op jit(solution)/shard_map/ppermute | solution.py:164
  93.7 10.1 %all_to_all.15.parts = f32[8,16,256]{2,1,0:T(8,128)S(1)} all-to-all(f32[8,16,256]{2,1,0:T(8,128)S(1)} %sum_spread.2), channel_id=1, replica_groups=mesh['y'=4,'zh'=2,'core'=2,'zl'=4,'x'=4] {'zh','zl'}, dimensions={0} | all-to-all | bytes 262144 | tf_op jit(solution)/shard_map/all_to_all | solution.py:168
  103.8 0.7 sum_spread.3
  104.5 7.4 %all-to-all-start.2 = ((bf16[32,16,256]{2,1,0:T(8,128)(2,1)}), bf16[32,16,256]{2,1,0:T(8,128)(2,1)S(1)}, u32[]{:S(2)}, u32[]{:S(2)}) async-start(bf16[32,16,256]{2,1,0:T(8,128)(2,1)} %sum_spread.3), calls=%async_computation.2 | async-start | bytes 524288 | tf_op jit(solution)/shard_map/all_to_all | solution.py:168
  112.0 0.7 finish_rows.1
  112.6 8.2 %all-to-all-done.2 = bf16[32,16,256]{2,1,0:T(8,128)(2,1)S(1)} async-done(((bf16[32,16,256]{2,1,0:T(8,128)(2,1)}), bf16[32,16,256]{2,1,0:T(8,128)(2,1)S(1)}, u32[]{:S(2)}, u32[]{:S(2)}) %all-to-all-start.2) | async-done | bytes 262176 | tf_op jit(solution)/shard_map/all_to_all | solution.py:168
  120.9 0.9 convert_multiply_fusion
  (23 shorter events, 0.2 us)
Async XLA Ops:
  0.6 0.7 copy-start.4
  0.6 1.7 %copy-start.1 = (bf16[128,512]{1,0:T(8,128)(2,1)S(1)}, bf16[128,512]{1,0:T(8,128)(2,1)}, u32[]{:S(2)}) copy-start(bf16[128,512]{1,0:T(8,128)(2,1)} %embeds.1) | copy-start | bytes 393220
  1.4 0.8 copy-start.3
  2.3 1.0 copy-start.2
  3.7 12.8 %collective-permute-start.3 = (bf16[128,384]{1,0:T(8,128)(2,1)S(1)}, bf16[128,384]{1,0:T(8,128)(2,1)S(1)}, u32[]{:S(2)}, u32[]{:S(2)}) collective-permute-start(bf16[128,384]{1,0:T(8,128)(2,1)S(1)} %pack.1), channel_id=1, source_target_pairs={{0,32},{4,36},{8,40},{12,44},{32,0},{36,4},{40,8},{44,12},{1,33},{... | collective-permute-start | bytes 294920 | tf_op jit(solution)/shard_map/ppermute | solution.py:164
  11.5 5.0 %collective-permute-start.2 = (bf16[128,384]{1,0:T(8,128)(2,1)S(1)}, bf16[128,384]{1,0:T(8,128)(2,1)S(1)}, u32[]{:S(2)}, u32[]{:S(2)}) collective-permute-start(bf16[128,384]{1,0:T(8,128)(2,1)S(1)} %pack.1), channel_id=1, source_target_pairs={{0,64},{64,128},{128,192},{192,0},{1,65},{65,129},{129,193},{193,1... | collective-permute-start | bytes 294920 | tf_op jit(solution)/shard_map/ppermute | solution.py:164
  12.8 6.3 %collective-permute-start.1 = (bf16[128,384]{1,0:T(8,128)(2,1)S(1)}, bf16[128,384]{1,0:T(8,128)(2,1)S(1)}, u32[]{:S(2)}, u32[]{:S(2)}) collective-permute-start(bf16[128,384]{1,0:T(8,128)(2,1)S(1)} %pack.1), channel_id=1, source_target_pairs={{0,128},{64,192},{128,0},{192,64},{1,129},{65,193},{129,1},{193,65... | collective-permute-start | bytes 294920 | tf_op jit(solution)/shard_map/ppermute | solution.py:164
  15.4 4.1 %collective-permute-start = (bf16[128,384]{1,0:T(8,128)(2,1)S(1)}, bf16[128,384]{1,0:T(8,128)(2,1)S(1)}, u32[]{:S(2)}, u32[]{:S(2)}) collective-permute-start(bf16[128,384]{1,0:T(8,128)(2,1)S(1)} %pack.1), channel_id=1, source_target_pairs={{0,192},{64,0},{128,64},{192,128},{1,193},{65,1},{129,65},{193,129... | collective-permute-start | bytes 294920 | tf_op jit(solution)/shard_map/ppermute | solution.py:164
  19.5 31.0 %copy-start = (bf16[128,128]{1,0:T(8,128)(2,1)S(1)}, bf16[128,128]{1,0:T(8,128)(2,1)}, u32[]{:S(2)}) copy-start(bf16[128,128]{1,0:T(8,128)(2,1)} %constant.10.clone.table) | copy-start | bytes 98308
  19.5 7.7 %collective-permute-start.6 = (bf16[256,384]{1,0:T(8,128)(2,1)S(1)}, bf16[256,384]{1,0:T(8,128)(2,1)S(1)}, u32[]{:S(2)}, u32[]{:S(2)}) collective-permute-start(bf16[256,384]{1,0:T(8,128)(2,1)S(1)} %pad_maximum_fusion.1.refs_0_), channel_id=1, source_target_pairs={{0,8},{4,12},{8,32},{12,36},{32,40},{36,44},{40,0},{44,4},{1,9},{5... | collective-permute-start | bytes 589832 | tf_op jit(solution)/shard_map/ppermute | solution.py:164
  20.8 16.0 %collective-permute-start.7 = (bf16[256,384]{1,0:T(8,128)(2,1)S(1)}, bf16[256,384]{1,0:T(8,128)(2,1)S(1)}, u32[]{:S(2)}, u32[]{:S(2)}) collective-permute-start(bf16[256,384]{1,0:T(8,128)(2,1)S(1)} %pad_maximum_fusion.1.refs_0_), channel_id=1, source_target_pairs={{0,16},{16,0},{1,17},{17,1},{2,18},{18,2},{3,19},{19,3},{4,20},{20... | collective-permute-start | bytes 589832 | tf_op jit(solution)/shard_map/ppermute | solution.py:164
  23.1 14.6 %collective-permute-start.5 = (bf16[256,384]{1,0:T(8,128)(2,1)S(1)}, bf16[256,384]{1,0:T(8,128)(2,1)S(1)}, u32[]{:S(2)}, u32[]{:S(2)}) collective-permute-start(bf16[256,384]{1,0:T(8,128)(2,1)S(1)} %pad_maximum_fusion.1.refs_0_), channel_id=1, source_target_pairs={{0,44},{4,0},{8,4},{12,8},{32,12},{36,32},{40,36},{44,40},{1,45},{... | collective-permute-start | bytes 589832 | tf_op jit(solution)/shard_map/ppermute | solution.py:164
  25.1 13.2 %collective-permute-start.4 = (bf16[256,384]{1,0:T(8,128)(2,1)S(1)}, bf16[256,384]{1,0:T(8,128)(2,1)S(1)}, u32[]{:S(2)}, u32[]{:S(2)}) collective-permute-start(bf16[256,384]{1,0:T(8,128)(2,1)S(1)} %pad_maximum_fusion.1.refs_0_), channel_id=1, source_target_pairs={{0,4},{4,8},{8,12},{12,32},{32,36},{36,40},{40,44},{44,0},{1,5},{5... | collective-permute-start | bytes 589832 | tf_op jit(solution)/shard_map/ppermute | solution.py:164
  27.3 11.9 %collective-permute-start.10 = (bf16[256,384]{1,0:T(8,128)(2,1)S(1)}, bf16[256,384]{1,0:T(8,128)(2,1)S(1)}, u32[]{:S(2)}, u32[]{:S(2)}) collective-permute-start(bf16[256,384]{1,0:T(8,128)(2,1)S(1)} %collective-permute-done.6.refs_3_), channel_id=1, source_target_pairs={{0,16},{16,0},{1,17},{17,1},{2,18},{18,2},{3,19},{19,3},{4,20},{20... | collective-permute-start | bytes 589832 | tf_op jit(solution)/shard_map/ppermute | solution.py:164
  34.1 19.1 %collective-permute-start.13 = (bf16[512,384]{1,0:T(8,128)(2,1)S(1)}, bf16[512,384]{1,0:T(8,128)(2,1)S(1)}, u32[]{:S(2)}, u32[]{:S(2)}) collective-permute-start(bf16[512,384]{1,0:T(8,128)(2,1)S(1)} %pad_maximum_fusion.rows_ref), channel_id=1, source_target_pairs={{0,2},{1,3},{2,0},{3,1},{4,6},{5,7},{6,4},{7,5},{8,10},{9,11},{10,... | collective-permute-start | bytes 1179656 | tf_op jit(solution)/shard_map/ppermute | solution.py:164
  36.8 18.0 %collective-permute-start.11 = (bf16[512,384]{1,0:T(8,128)(2,1)S(1)}, bf16[512,384]{1,0:T(8,128)(2,1)S(1)}, u32[]{:S(2)}, u32[]{:S(2)}) collective-permute-start(bf16[512,384]{1,0:T(8,128)(2,1)S(1)} %pad_maximum_fusion.rows_ref), channel_id=1, source_target_pairs={{0,3},{1,0},{2,1},{3,2},{4,7},{5,4},{6,5},{7,6},{8,11},{9,8},{10,9... | collective-permute-start | bytes 1179656 | tf_op jit(solution)/shard_map/ppermute | solution.py:164
  37.7 26.3 %collective-permute-start.15 = (bf16[512,384]{1,0:T(8,128)(2,1)S(1)}, bf16[512,384]{1,0:T(8,128)(2,1)S(1)}, u32[]{:S(2)}, u32[]{:S(2)}) collective-permute-start(bf16[512,384]{1,0:T(8,128)(2,1)S(1)} %pad_maximum_fusion.rows_ref), channel_id=1, source_target_pairs={{0,1},{1,2},{2,3},{3,0},{4,5},{5,6},{6,7},{7,4},{8,9},{9,10},{10,1... | collective-permute-start | bytes 1179656 | tf_op jit(solution)/shard_map/ppermute | solution.py:164
  38.3 12.2 %collective-permute-start.9 = (bf16[256,384]{1,0:T(8,128)(2,1)S(1)}, bf16[256,384]{1,0:T(8,128)(2,1)S(1)}, u32[]{:S(2)}, u32[]{:S(2)}) collective-permute-start(bf16[256,384]{1,0:T(8,128)(2,1)S(1)} %collective-permute-done.5.refs_2_), channel_id=1, source_target_pairs={{0,16},{16,0},{1,17},{17,1},{2,18},{18,2},{3,19},{19,3},{4,20},{20... | collective-permute-start | bytes 589832 | tf_op jit(solution)/shard_map/ppermute | solution.py:164
  39.2 11.4 %collective-permute-start.8 = (bf16[256,384]{1,0:T(8,128)(2,1)S(1)}, bf16[256,384]{1,0:T(8,128)(2,1)S(1)}, u32[]{:S(2)}, u32[]{:S(2)}) collective-permute-start(bf16[256,384]{1,0:T(8,128)(2,1)S(1)} %collective-permute-done.4.refs_1_), channel_id=1, source_target_pairs={{0,16},{16,0},{1,17},{17,1},{2,18},{18,2},{3,19},{19,3},{4,20},{20... | collective-permute-start | bytes 589832 | tf_op jit(solution)/shard_map/ppermute | solution.py:164
  57.4 9.5 %collective-permute-start.12 = (bf16[512,256]{1,0:T(8,128)(2,1)S(1)}, bf16[512,256]{1,0:T(8,128)(2,1)S(1)}, u32[]{:S(2)}, u32[]{:S(2)}) collective-permute-start(bf16[512,256]{1,0:T(8,128)(2,1)S(1)} %tile.5), channel_id=1, source_target_pairs={{0,1},{1,2},{2,3},{3,0},{4,5},{5,6},{6,7},{7,4},{8,9},{9,10},{10,1... | collective-permute-start | bytes 786440 | tf_op jit(solution)/shard_map/ppermute | solution.py:164
  61.5 11.4 %collective-permute-start.14 = (bf16[512,256]{1,0:T(8,128)(2,1)S(1)}, bf16[512,256]{1,0:T(8,128)(2,1)S(1)}, u32[]{:S(2)}, u32[]{:S(2)}) collective-permute-start(bf16[512,256]{1,0:T(8,128)(2,1)S(1)} %tile.6), channel_id=1, source_target_pairs={{0,2},{1,3},{2,0},{3,1},{4,6},{5,7},{6,4},{7,5},{8,10},{9,11},{10,... | collective-permute-start | bytes 786440 | tf_op jit(solution)/shard_map/ppermute | solution.py:164
  66.6 8.5 %collective-permute-start.16 = (bf16[512,256]{1,0:T(8,128)(2,1)S(1)}, bf16[512,256]{1,0:T(8,128)(2,1)S(1)}, u32[]{:S(2)}, u32[]{:S(2)}) collective-permute-start(bf16[512,256]{1,0:T(8,128)(2,1)S(1)} %tile.7), channel_id=1, source_target_pairs={{0,3},{1,0},{2,1},{3,2},{4,7},{5,4},{6,5},{7,6},{8,11},{9,8},{10,9... | collective-permute-start | bytes 786440 | tf_op jit(solution)/shard_map/ppermute | solution.py:164
  76.5 17.1 %all-to-all-start = ((bf16[32,16,256]{2,1,0:T(8,128)(2,1)}), bf16[32,16,256]{2,1,0:T(8,128)(2,1)S(1)}, u32[]{:S(2)}, u32[]{:S(2)}) async-start(bf16[32,16,256]{2,1,0:T(8,128)(2,1)} %bitcast.2), calls=%async_computation | async-start | bytes 524288 | tf_op jit(solution)/shard_map/all_to_all | solution.py:168
  84.1 6.0 %collective-permute-start.17 = (bf16[128,256]{1,0:T(8,128)(2,1)S(1)}, bf16[128,256]{1,0:T(8,128)(2,1)S(1)}, u32[]{:S(2)}, u32[]{:S(2)}) collective-permute-start(bf16[128,256]{1,0:T(8,128)(2,1)S(1)} %get-tuple-element.23), channel_id=1, source_target_pairs={{0,64},{64,128},{128,192},{192,0},{1,65},{65,129},{129,193},{193,1... | collective-permute-start | bytes 196616 | tf_op jit(solution)/shard_map/ppermute | solution.py:164
  85.6 8.0 %collective-permute-start.18 = (bf16[128,256]{1,0:T(8,128)(2,1)S(1)}, bf16[128,256]{1,0:T(8,128)(2,1)S(1)}, u32[]{:S(2)}, u32[]{:S(2)}) collective-permute-start(bf16[128,256]{1,0:T(8,128)(2,1)S(1)} %get-tuple-element.24), channel_id=1, source_target_pairs={{0,128},{64,192},{128,0},{192,64},{1,129},{65,193},{129,1},{193,65... | collective-permute-start | bytes 196616 | tf_op jit(solution)/shard_map/ppermute | solution.py:164
  88.1 5.6 %collective-permute-start.19 = (bf16[128,256]{1,0:T(8,128)(2,1)S(1)}, bf16[128,256]{1,0:T(8,128)(2,1)S(1)}, u32[]{:S(2)}, u32[]{:S(2)}) collective-permute-start(bf16[128,256]{1,0:T(8,128)(2,1)S(1)} %get-tuple-element.25), channel_id=1, source_target_pairs={{0,192},{64,0},{128,64},{192,128},{1,193},{65,1},{129,65},{193,129... | collective-permute-start | bytes 196616 | tf_op jit(solution)/shard_map/ppermute | solution.py:164
  104.5 16.3 %all-to-all-start.2 = ((bf16[32,16,256]{2,1,0:T(8,128)(2,1)}), bf16[32,16,256]{2,1,0:T(8,128)(2,1)S(1)}, u32[]{:S(2)}, u32[]{:S(2)}) async-start(bf16[32,16,256]{2,1,0:T(8,128)(2,1)} %sum_spread.3), calls=%async_computation.2 | async-start | bytes 524288 | tf_op jit(solution)/shard_map/all_to_all | solution.py:168

commit v2 on v1

--- a/solution.py
+++ b/solution.py
@@ -31,7 +31,7 @@
     return lax.dot_general(a, b, (((0,), (0,)), ((), ())), preferred_element_type=F32)
 
 
-def pack_kernel(embeds, weight, solve, probes, probe_solves, out):
+def pack_kernel(embeds, weight, solve, probes, probe_solves, out, extended):
     rows, width = embeds.shape[0], weight.shape[1]
     count = probes.shape[1]
     feats = jnp.dot(embeds[...], weight[...], preferred_element_type=F32).astype(BF16)
@@ -56,7 +56,11 @@
     lo = factors - hi
     lane = lax.broadcasted_iota(jnp.int32, (rows, 32), 1)
     tail = jnp.where(lane == 0, sq_hi, jnp.where(lane == 1, sq_mid, jnp.where(lane == 2, sq_lo, 0.0)))
-    out[:, width:] = jnp.concatenate([hi, lo, hi, tail], axis=1).astype(BF16)
+    tail = jnp.concatenate([hi, lo, hi, tail], axis=1).astype(BF16)
+    out[:, width:] = tail
+    extended[:, :width] = feats
+    extended[:, width : width + 128] = tail
+    extended[:, width + 128 :] = embeds[...]
 
 
 def left_map(count):
@@ -118,21 +122,22 @@
         out[block, :] = (acc[k] - row_total * u_rows[block].astype(F32)).astype(out.dtype)
 
 
-def sum_rows_kernel(place, a, b, c, d, embeds, partial, own, *others):
-    rows = own.shape[0]
-    count = 1 + len(others)
-    total = (a[...] + b[...].astype(F32)) + (c[...].astype(F32) + d[...].astype(F32))
+def sum_rows_kernel(count, *refs):
+    parts, lines, (partial, own, *others) = refs[:count], refs[count : 2 * count], refs[2 * count :]
+    rows, width = own.shape
+    total = parts[0][...]
+    for ref in parts[1:]:
+        total = total + ref[...].astype(F32)
     hi = total.astype(BF16)
     lo = (total - hi.astype(F32)).astype(BF16)
     own[...] = total[:rows]
     for k, ref in enumerate(others):
         ref[...] = hi[(k + 1) * rows : (k + 2) * rows]
     weight = jnp.zeros(partial.shape, F32)
-    for k in range(count):
-        start = pl.multiple_of(lax.rem(place[0] + k, count) * rows, rows)
-        line = embeds[pl.ds(start, rows), :]
+    for k, ref in enumerate(lines):
         block = slice(k * rows, (k + 1) * rows)
-        weight = weight + (dot_tn(line, hi[block]) + dot_tn(line, lo[block]))
+        embeds = ref[:, width + 128 :]
+        weight = weight + (dot_tn(embeds, hi[block]) + dot_tn(embeds, lo[block]))
     partial[...] = weight.astype(BF16)
 
 
@@ -164,72 +169,71 @@
     return lax.ppermute(array, axis, [(i, (i + shift) % size) for i in range(size)])
 
 
+def turn(array, sizes, stage, shift):
+    dims = [sizes[a] for a in ALL]
+    perm = []
+    for source in range(math.prod(dims)):
+        place = list(np.unravel_index(source, dims))
+        axis = ALL.index(PLANE[0] if (place[ALL.index("core")] + stage) % 2 == 0 else PLANE[-1])
+        place[axis] = (place[axis] + shift) % dims[axis]
+        perm.append((source, int(np.ravel_multi_index(place, dims))))
+    return lax.ppermute(array, ALL, perm)
+
+
 def exchange(array, axes):
     return lax.all_to_all(array, axes, split_axis=0, concat_axis=0, tiled=True)
 
 
 def shards(sizes, embeds, weight, solve, probes, probe_solves):
     rows, width = embeds.shape[0], weight.shape[1]
-    n_x, n_y, n_z = sizes["x"], sizes["y"], sizes["zh"] * sizes["zl"]
-    pack = pl.pallas_call(
+    n_side, n_z = sizes["x"], sizes["zh"] * sizes["zl"]
+    pack, extended = pl.pallas_call(
         pack_kernel,
-        out_shape=jax.ShapeDtypeStruct((rows, width + 128), BF16),
+        out_shape=[
+            jax.ShapeDtypeStruct((rows, width + 128), BF16),
+            jax.ShapeDtypeStruct((rows, width + 128 + embeds.shape[1]), BF16),
+        ],
         in_specs=[VMEM] * 5,
-        out_specs=VMEM,
+        out_specs=[VMEM] * 2,
         compiler_params=params(16),
         name="pack",
     )(embeds, weight, solve[:, None], probes, probe_solves)
 
-    embeds_line = lax.all_gather(embeds, "y", axis=0, tiled=True)
-
-    line = jnp.concatenate([pack] + [ring(pack, "y", n_y, -d) for d in range(1, n_y)], axis=0)
+    blocks = [extended] + [turn(extended, sizes, 0, -d) for d in range(1, n_side)]
+    line = jnp.concatenate([block[:, : width + 128] for block in blocks], axis=0)
     pair = jnp.concatenate([pack, ring(pack, DEPTH, n_z, n_z // 2)], axis=0)
     pair, _ = lax.optimization_barrier((pair, line))
     columns = [pair] + [ring(pair, DEPTH, n_z, d) for d in (1, -1, 2)]
+    lines = [line] + [turn(line, sizes, 1, -d) for d in range(1, n_side)]
+    columns, lines = lax.optimization_barrier((columns, lines))
     columns += [ring(part, "core", 2, 1) for part in columns]
-    lines = [line] + [ring(line, "x", n_x, -d) for d in range(1, n_x)]
-
 
     table = left_map(probes.shape[1])
     back = {}
     for d in (0, 3, 1, 2):
-        if d == 3:
-            lines[d], _, embeds_line = lax.optimization_barrier((lines[d], back[0], embeds_line))
-        elif d != 0:
-            lines[d], _ = lax.optimization_barrier((lines[d], back[0]))
         part = pl.pallas_call(
             functools.partial(tile_kernel, 256, 256),
-            out_shape=jax.ShapeDtypeStruct((n_y * rows, width), F32 if d == 0 else BF16),
+            out_shape=jax.ShapeDtypeStruct((n_side * rows, width), F32 if d == 0 else BF16),
             in_specs=[VMEM] * (2 + len(columns)),
             out_specs=VMEM,
             compiler_params=params(40),
             name="tile",
         )(table, lines[d], *columns)
-        back[d] = part if d == 0 else ring(part, "x", n_x, d)
-
-    sums = pl.pallas_call(
-        sum_rows_kernel,
+        back[d] = part if d == 0 else turn(part, sizes, 1, d)
+
+    partial, own_rows, *other_rows = pl.pallas_call(
+        functools.partial(sum_rows_kernel, n_side),
         out_shape=[
             jax.ShapeDtypeStruct((embeds.shape[1], width), BF16),
             jax.ShapeDtypeStruct((rows, width), F32),
         ]
-        + [jax.ShapeDtypeStruct((rows, width), BF16)] * (n_y - 1),
-        in_specs=[pl.BlockSpec(memory_space=pltpu.SMEM)] + [VMEM] * (n_x + 1),
-        out_specs=[VMEM] * (n_y + 1),
+        + [jax.ShapeDtypeStruct((rows, width), BF16)] * (n_side - 1),
+        in_specs=[VMEM] * (2 * n_side),
+        out_specs=[VMEM] * (n_side + 1),
         compiler_params=params(16),
         name="sum_rows",
-    )(lax.axis_index("y")[None], *(back[d] for d in range(n_x)), embeds_line)
-    partial, own_rows, *other_rows = sums
-    arrived = [ring(block, "y", n_y, d + 1) for d, block in enumerate(other_rows)]
-
-    n_plane = n_x * n_y * 2
-    pieces = exchange(partial.reshape(n_plane, -1, width), PLANE)
-    pieces, arrived = lax.optimization_barrier((pieces, arrived))
-    pieces = exchange(sum_spread(pieces, n_z, F32), DEPTH)
-    pieces = exchange(sum_spread(pieces, n_plane, BF16), PLANE)
-    total_points = rows * n_plane * n_z
-    grad_weight = pieces.reshape(-1, width).astype(F32) * (1.0 / math.sqrt(total_points))
-
+    )(*(back[d] for d in range(n_side)), *blocks)
+    arrived = [turn(block, sizes, 0, d + 1) for d, block in enumerate(other_rows)]
     grad_rows = pl.pallas_call(
         finish_rows_kernel,
         out_shape=jax.ShapeDtypeStruct((rows, width), F32),
@@ -238,6 +242,14 @@
         compiler_params=params(16),
         name="finish_rows",
     )(own_rows, *arrived)
+
+    n_plane = n_side * n_side * 2
+    pieces = exchange(partial.reshape(n_plane, -1, width), PLANE)
+    pieces, grad_rows = lax.optimization_barrier((pieces, grad_rows))
+    pieces = exchange(sum_spread(pieces, n_z, F32), DEPTH)
+    pieces = exchange(sum_spread(pieces, n_plane, BF16), PLANE)
+    total_points = rows * n_plane * n_z
+    grad_weight = pieces.reshape(-1, width).astype(F32) * (1.0 / math.sqrt(total_points))
     return grad_rows, grad_weight
 
 

time: 122 us -> 112 us (0.918)
  waiting for transfers between devices: 27.7 us -> 15.3 us
  blocking collectives: 21.4 us -> 29.2 us
  starting transfers between devices: 54.7 us -> 48 us
  local copies, waits for them, and re-layouts: 2.63 us -> 4.2 us
    ppermute x0 -> x12, starting transfers between devices: none -> 25.4 us  [turn(): return lax.ppermute(array, ALL, perm)]
    ppermute x20 -> x8, starting transfers between devices: 39.7 us -> 16.1 us  [ring(): lax.ppermute(array, axis, [(i, (i + shift) % size) for i in range(size)])]
    all_to_all x1 -> x2, blocking collectives: 10.1 us -> 29.2 us  [exchange(): return lax.all_to_all(array, axes, split_axis=0, concat_axis=0, tiled=True)]
    all_gather x1 -> x0, blocking collectives: 11.3 us -> none  [shards(): embeds_line = lax.all_gather(embeds, 'y', axis=0, tiled=True)]
    ppermute x20 -> x8, waiting for transfers between devices: 19.5 us -> 9.92 us  [ring(): lax.ppermute(array, axis, [(i, (i + shift) % size) for i in range(size)])]
    all_to_all x2 -> x1, starting transfers between devices: 15 us -> 6.57 us  [exchange(): return lax.all_to_all(array, axes, split_axis=0, concat_axis=0, tiled=True)]
    all_to_all x2 -> x1, waiting for transfers between devices: 8.21 us -> 0.01 us  [exchange(): return lax.all_to_all(array, axes, split_axis=0, concat_axis=0, tiled=True)]
    ppermute x0 -> x12, waiting for transfers between devices: none -> 5.4 us  [turn(): return lax.ppermute(array, ALL, perm)]
  transfers between devices with their start and end apart: 22 -> 21, of which waited for: 9 -> 12; matrix products, arithmetic and copies ran while one was open for 0% -> 0% of each run, Pallas kernels for 9% -> 8%
where the time goes in v2:
time: 112 us; the launch traced here: 111 us
  starting transfers between devices  48 us (43%)
  blocking collectives  29.2 us (26%)
  waiting for transfers between devices  15.3 us (14%)
  Pallas kernels  12.8 us (11%)
  local copies, waits for them, and re-layouts  4.2 us (4%)
    all_to_all x2, blocking collectives, exchange(): return lax.all_to_all(array, axes, split_axis=0, concat_axis=0, tiled=True)  29.2 us
    ppermute x12, starting transfers between devices, turn(): return lax.ppermute(array, ALL, perm)  25.4 us
    ppermute x8, starting transfers between devices, ring(): lax.ppermute(array, axis, [(i, (i + shift) % size) for i in range(size)])  16.1 us
    pallas_call x4, Pallas kernels, shards(): pl.pallas_call(functools.partial(tile_kernel, 256, 256), out_shape=jax.Sh...  10.2 us
    ppermute x8, waiting for transfers between devices, ring(): lax.ppermute(array, axis, [(i, (i + shift) % size) for i in range(size)])  9.92 us
    all_to_all x1, starting transfers between devices, exchange(): return lax.all_to_all(array, axes, split_axis=0, concat_axis=0, tiled=True)  6.57 us
    ppermute x12, waiting for transfers between devices, turn(): return lax.ppermute(array, ALL, perm)  5.4 us
    unnamed x16, local copies, waits for them, and re-layouts  3.18 us
  transfers between devices with their start and end apart: 21, of which 12 were waited for; matrix products, arithmetic and copies ran while one was open for 0% of the time, Pallas kernels for 8%

profile of v2, /device:TPU:1, one launch (start us, length us, event | category | flops | bytes accessed | tf_op | source)
XLA Modules:
  0.0 111.3 jit_solution(12068055532303352482)
XLA Ops:
  0.6 0.6 copy-done.6
  1.3 0.1 copy.8.solve
  1.4 0.8 copy.9.probes
  2.2 0.1 copy.10.probe_solves
  2.3 0.9 copy-done.3
  3.3 0.4 pack.1
  3.7 2.1 %collective-permute-start.3 = (bf16[128,896]{1,0:T(8,128)(2,1)S(1)}, bf16[128,896]{1,0:T(8,128)(2,1)S(1)}, u32[]{:S(2)}, u32[]{:S(2)}) collective-permute-start(bf16[128,896]{1,0:T(8,128)(2,1)S(1)} %get-tuple-element.21.refs_4_), channel_id=1, source_target_pairs={{0,64},{1,65},{2,66},{3,67},{4,68},{5,69},{6,70},{7,71},{8,72},{9,... | collective-permute-start | bytes 688136 | tf_op jit(solution)/shard_map/ppermute | solution.py:180
  5.8 2.4 %collective-permute-start.2 = (bf16[128,896]{1,0:T(8,128)(2,1)S(1)}, bf16[128,896]{1,0:T(8,128)(2,1)S(1)}, u32[]{:S(2)}, u32[]{:S(2)}) collective-permute-start(bf16[128,896]{1,0:T(8,128)(2,1)S(1)} %get-tuple-element.21.refs_4_), channel_id=1, source_target_pairs={{0,128},{1,129},{2,130},{3,131},{4,132},{5,133},{6,134},{7,135},{8... | collective-permute-start | bytes 688136 | tf_op jit(solution)/shard_map/ppermute | solution.py:180
  8.2 1.2 %collective-permute-start.1 = (bf16[128,896]{1,0:T(8,128)(2,1)S(1)}, bf16[128,896]{1,0:T(8,128)(2,1)S(1)}, u32[]{:S(2)}, u32[]{:S(2)}) collective-permute-start(bf16[128,896]{1,0:T(8,128)(2,1)S(1)} %get-tuple-element.21.refs_4_), channel_id=1, source_target_pairs={{0,192},{1,193},{2,194},{3,195},{4,196},{5,197},{6,198},{7,199},{8... | collective-permute-start | bytes 688136 | tf_op jit(solution)/shard_map/ppermute | solution.py:180
  9.4 6.9 %collective-permute-start = (bf16[128,384]{1,0:T(8,128)(2,1)S(1)}, bf16[128,384]{1,0:T(8,128)(2,1)S(1)}, u32[]{:S(2)}, u32[]{:S(2)}) collective-permute-start(bf16[128,384]{1,0:T(8,128)(2,1)S(1)} %get-tuple-element.20), channel_id=1, source_target_pairs={{0,32},{4,36},{8,40},{12,44},{32,0},{36,4},{40,8},{44,12},{1,33},{... | collective-permute-start | bytes 294920 | tf_op jit(solution)/shard_map/ppermute | solution.py:169
  16.3 2.1 %collective-permute-done = bf16[128,384]{1,0:T(8,128)(2,1)S(1)} collective-permute-done((bf16[128,384]{1,0:T(8,128)(2,1)S(1)}, bf16[128,384]{1,0:T(8,128)(2,1)S(1)}, u32[]{:S(2)}, u32[]{:S(2)}) %collective-permute-start) | collective-permute-done | bytes 98336 | tf_op jit(solution)/shard_map/ppermute | solution.py:169
  18.5 0.6 copy-done.1
  19.1 0.9 slice-done
  20.1 2.6 %collective-permute-start.6 = (bf16[256,384]{1,0:T(8,128)(2,1)S(1)}, bf16[256,384]{1,0:T(8,128)(2,1)S(1)}, u32[]{:S(2)}, u32[]{:S(2)}) collective-permute-start(bf16[256,384]{1,0:T(8,128)(2,1)S(1)} %pad_maximum_fusion.1.refs_0_), channel_id=1, source_target_pairs={{0,8},{4,12},{8,32},{12,36},{32,40},{36,44},{40,0},{44,4},{1,9},{5... | collective-permute-start | bytes 589832 | tf_op jit(solution)/shard_map/ppermute | solution.py:169
  22.7 2.8 %collective-permute-start.9 = (bf16[512,384]{1,0:T(8,128)(2,1)S(1)}, bf16[512,384]{1,0:T(8,128)(2,1)S(1)}, u32[]{:S(2)}, u32[]{:S(2)}) collective-permute-start(bf16[512,384]{1,0:T(8,128)(2,1)S(1)} %pad_maximum_fusion.rows_ref), channel_id=1, source_target_pairs={{0,1},{1,2},{2,3},{3,0},{4,5},{5,6},{6,7},{7,4},{8,9},{9,10},{10,1... | collective-permute-start | bytes 1179656 | tf_op jit(solution)/shard_map/ppermute | solution.py:180
  25.5 2.4 %collective-permute-start.8 = (bf16[512,384]{1,0:T(8,128)(2,1)S(1)}, bf16[512,384]{1,0:T(8,128)(2,1)S(1)}, u32[]{:S(2)}, u32[]{:S(2)}) collective-permute-start(bf16[512,384]{1,0:T(8,128)(2,1)S(1)} %pad_maximum_fusion.rows_ref), channel_id=1, source_target_pairs={{0,2},{1,3},{2,0},{3,1},{4,6},{5,7},{6,4},{7,5},{8,10},{9,11},{10,... | collective-permute-start | bytes 1179656 | tf_op jit(solution)/shard_map/ppermute | solution.py:180
  27.9 1.1 %collective-permute-start.7 = (bf16[512,384]{1,0:T(8,128)(2,1)S(1)}, bf16[512,384]{1,0:T(8,128)(2,1)S(1)}, u32[]{:S(2)}, u32[]{:S(2)}) collective-permute-start(bf16[512,384]{1,0:T(8,128)(2,1)S(1)} %pad_maximum_fusion.rows_ref), channel_id=1, source_target_pairs={{0,3},{1,0},{2,1},{3,2},{4,7},{5,4},{6,5},{7,6},{8,11},{9,8},{10,9... | collective-permute-start | bytes 1179656 | tf_op jit(solution)/shard_map/ppermute | solution.py:180
  29.0 1.4 %collective-permute-start.5 = (bf16[256,384]{1,0:T(8,128)(2,1)S(1)}, bf16[256,384]{1,0:T(8,128)(2,1)S(1)}, u32[]{:S(2)}, u32[]{:S(2)}) collective-permute-start(bf16[256,384]{1,0:T(8,128)(2,1)S(1)} %pad_maximum_fusion.1.refs_0_), channel_id=1, source_target_pairs={{0,44},{4,0},{8,4},{12,8},{32,12},{36,32},{40,36},{44,40},{1,45},{... | collective-permute-start | bytes 589832 | tf_op jit(solution)/shard_map/ppermute | solution.py:169
  30.4 0.1 collective-permute-done.6.refs_3_
  30.5 3.5 %collective-permute-done.5.refs_2_ = bf16[256,384]{1,0:T(8,128)(2,1)S(1)} collective-permute-done((bf16[256,384]{1,0:T(8,128)(2,1)S(1)}, bf16[256,384]{1,0:T(8,128)(2,1)S(1)}, u32[]{:S(2)}, u32[]{:S(2)}) %collective-permute-start.5) | collective-permute-done | bytes 196640 | tf_op jit(solution)/shard_map/ppermute | solution.py:169
  33.9 2.8 %collective-permute-done.4.refs_1_ = bf16[256,384]{1,0:T(8,128)(2,1)S(1)} collective-permute-done((bf16[256,384]{1,0:T(8,128)(2,1)S(1)}, bf16[256,384]{1,0:T(8,128)(2,1)S(1)}, u32[]{:S(2)}, u32[]{:S(2)}) %collective-permute-start.4) | collective-permute-done | bytes 196640 | tf_op jit(solution)/shard_map/ppermute | solution.py:169
  36.8 0.7 collective-permute-done.8.rows_ref
  37.5 4.6 %collective-permute-start.10 = (bf16[256,384]{1,0:T(8,128)(2,1)S(1)}, bf16[256,384]{1,0:T(8,128)(2,1)S(1)}, u32[]{:S(2)}, u32[]{:S(2)}) collective-permute-start(bf16[256,384]{1,0:T(8,128)(2,1)S(1)} %pad_maximum_fusion.1.refs_0_), channel_id=1, source_target_pairs={{0,16},{16,0},{1,17},{17,1},{2,18},{18,2},{3,19},{19,3},{4,20},{20... | collective-permute-start | bytes 589832 | tf_op jit(solution)/shard_map/ppermute | solution.py:169
  42.2 0.4 collective-permute-start.12
  42.6 0.1 collective-permute-start.13
  42.7 0.5 collective-permute-done.10.refs_4_
  43.2 0.4 collective-permute-done.11.refs_5_
  43.5 0.3 collective-permute-done.12.refs_6_
  43.8 0.3 collective-permute-done.13.refs_7_
  44.1 2.6 %tile.5 = bf16[512,256]{1,0:T(8,128)(2,1)S(1)} custom-call(bf16[128,128]{1,0:T(8,128)(2,1)S(1)} %copy-done, bf16[512,384]{1,0:T(8,128)(2,1)S(1)} %collective-permute-done.7.rows_ref, bf16[256,384]{1,0:T(8,128)(2,1)S(1)} %pad_maximum_fusion.1.refs_0_, bf16[256,384]{1,0:T(8,128)(2,1)S(1)} %collective-permute-done.4.refs_1_, ...), custom_call_target="tpu_custom_call" | custom-call | tf_op jit(solution)/shard_map/tile/pallas_call | solution.py:214
  46.7 1.9 %collective-permute-start.14 = (bf16[512,256]{1,0:T(8,128)(2,1)S(1)}, bf16[512,256]{1,0:T(8,128)(2,1)S(1)}, u32[]{:S(2)}, u32[]{:S(2)}) collective-permute-start(bf16[512,256]{1,0:T(8,128)(2,1)S(1)} %tile.5), channel_id=1, source_target_pairs={{0,1},{1,2},{2,3},{3,0},{4,5},{5,6},{6,7},{7,4},{8,9},{9,10},{10,1... | collective-permute-start | bytes 786440 | tf_op jit(solution)/shard_map/ppermute | solution.py:180
  48.6 2.6 %tile.6 = bf16[512,256]{1,0:T(8,128)(2,1)S(1)} custom-call(bf16[128,128]{1,0:T(8,128)(2,1)S(1)} %copy-done, bf16[512,384]{1,0:T(8,128)(2,1)S(1)} %collective-permute-done.8.rows_ref, bf16[256,384]{1,0:T(8,128)(2,1)S(1)} %pad_maximum_fusion.1.refs_0_, bf16[256,384]{1,0:T(8,128)(2,1)S(1)} %collective-permute-done.4.refs_1_, ...), custom_call_target="tpu_custom_call" | custom-call | tf_op jit(solution)/shard_map/tile/pallas_call | solution.py:214
  51.1 4.7 %collective-permute-start.15 = (bf16[512,256]{1,0:T(8,128)(2,1)S(1)}, bf16[512,256]{1,0:T(8,128)(2,1)S(1)}, u32[]{:S(2)}, u32[]{:S(2)}) collective-permute-start(bf16[512,256]{1,0:T(8,128)(2,1)S(1)} %tile.6), channel_id=1, source_target_pairs={{0,2},{1,3},{2,0},{3,1},{4,6},{5,7},{6,4},{7,5},{8,10},{9,11},{10,... | collective-permute-start | bytes 786440 | tf_op jit(solution)/shard_map/ppermute | solution.py:180
  55.9 2.6 %tile.7 = bf16[512,256]{1,0:T(8,128)(2,1)S(1)} custom-call(bf16[128,128]{1,0:T(8,128)(2,1)S(1)} %copy-done, bf16[512,384]{1,0:T(8,128)(2,1)S(1)} %collective-permute-done.9.rows_ref, bf16[256,384]{1,0:T(8,128)(2,1)S(1)} %pad_maximum_fusion.1.refs_0_, bf16[256,384]{1,0:T(8,128)(2,1)S(1)} %collective-permute-done.4.refs_1_, ...), custom_call_target="tpu_custom_call" | custom-call | tf_op jit(solution)/shard_map/tile/pallas_call | solution.py:214
  58.4 1.7 %collective-permute-start.16 = (bf16[512,256]{1,0:T(8,128)(2,1)S(1)}, bf16[512,256]{1,0:T(8,128)(2,1)S(1)}, u32[]{:S(2)}, u32[]{:S(2)}) collective-permute-start(bf16[512,256]{1,0:T(8,128)(2,1)S(1)} %tile.7), channel_id=1, source_target_pairs={{0,3},{1,0},{2,1},{3,2},{4,7},{5,4},{6,5},{7,6},{8,11},{9,8},{10,9... | collective-permute-start | bytes 786440 | tf_op jit(solution)/shard_map/ppermute | solution.py:180
  60.1 2.6 %tile.4.refs_0_ = f32[512,256]{1,0:T(8,128)S(1)} custom-call(bf16[128,128]{1,0:T(8,128)(2,1)S(1)} %copy-done, bf16[512,384]{1,0:T(8,128)(2,1)S(1)} %pad_maximum_fusion.rows_ref, bf16[256,384]{1,0:T(8,128)(2,1)S(1)} %pad_maximum_fusion.1.refs_0_, bf16[256,384]{1,0:T(8,128)(2,1)S(1)} %collective-permute-done.4.refs_1_, ...), custom_call_target="tpu_custom_call" | custom-call | tf_op jit(solution)/shard_map/tile/pallas_call | solution.py:214
  62.7 1.2 %collective-permute-done.16.refs_3_ = bf16[512,256]{1,0:T(8,128)(2,1)S(1)} collective-permute-done((bf16[512,256]{1,0:T(8,128)(2,1)S(1)}, bf16[512,256]{1,0:T(8,128)(2,1)S(1)}, u32[]{:S(2)}, u32[]{:S(2)}) %collective-permute-start.16) | collective-permute-done | bytes 262176 | tf_op jit(solution)/shard_map/ppermute | solution.py:180
  64.0 1.5 %sum_rows.1 = (bf16[512,256]{1,0:T(8,128)(2,1)}, f32[128,256]{1,0:T(8,128)S(1)}, bf16[128,256]{1,0:T(8,128)(2,1)S(1)}, bf16[128,256]{1,0:T(8,128)(2,1)S(1)}, bf16[128,256]{1,0:T(8,128)(2,1)S(1)}) custom-call(f32[512,256]{1,0:T(8,128)S(1)} %tile.4.refs_0_, bf16[512,256]{1,0:T(8,128)(2,1)S(1)} %collective-permute-done.14.refs_1_, ...), custom_call_target="tpu_custom_call" | custom-call | tf_op jit(solution)/shard_map/sum_rows/pallas_call | solution.py:224
  65.4 6.6 %all-to-all-start = ((bf16[32,16,256]{2,1,0:T(8,128)(2,1)}), bf16[32,16,256]{2,1,0:T(8,128)(2,1)S(1)}, u32[]{:S(2)}, u32[]{:S(2)}) async-start(bf16[32,16,256]{2,1,0:T(8,128)(2,1)} %bitcast.1), calls=%async_computation | async-start | bytes 524288 | tf_op jit(solution)/shard_map/all_to_all | solution.py:184
  72.0 1.5 %collective-permute-start.17 = (bf16[128,256]{1,0:T(8,128)(2,1)S(1)}, bf16[128,256]{1,0:T(8,128)(2,1)S(1)}, u32[]{:S(2)}, u32[]{:S(2)}) collective-permute-start(bf16[128,256]{1,0:T(8,128)(2,1)S(1)} %get-tuple-element.33), channel_id=1, source_target_pairs={{0,64},{1,65},{2,66},{3,67},{4,68},{5,69},{6,70},{7,71},{8,72},{9,... | collective-permute-start | bytes 196616 | tf_op jit(solution)/shard_map/ppermute | solution.py:180
  73.5 2.4 %collective-permute-start.18 = (bf16[128,256]{1,0:T(8,128)(2,1)S(1)}, bf16[128,256]{1,0:T(8,128)(2,1)S(1)}, u32[]{:S(2)}, u32[]{:S(2)}) collective-permute-start(bf16[128,256]{1,0:T(8,128)(2,1)S(1)} %get-tuple-element.34), channel_id=1, source_target_pairs={{0,128},{1,129},{2,130},{3,131},{4,132},{5,133},{6,134},{7,135},{8... | collective-permute-start | bytes 196616 | tf_op jit(solution)/shard_map/ppermute | solution.py:180
  75.9 1.2 %collective-permute-start.19 = (bf16[128,256]{1,0:T(8,128)(2,1)S(1)}, bf16[128,256]{1,0:T(8,128)(2,1)S(1)}, u32[]{:S(2)}, u32[]{:S(2)}) collective-permute-start(bf16[128,256]{1,0:T(8,128)(2,1)S(1)} %get-tuple-element.35), channel_id=1, source_target_pairs={{0,192},{1,193},{2,194},{3,195},{4,196},{5,197},{6,198},{7,199},{8... | collective-permute-start | bytes 196616 | tf_op jit(solution)/shard_map/ppermute | solution.py:180
  77.0 2.4 %collective-permute-done.17.b = bf16[128,256]{1,0:T(8,128)(2,1)S(1)} collective-permute-done((bf16[128,256]{1,0:T(8,128)(2,1)S(1)}, bf16[128,256]{1,0:T(8,128)(2,1)S(1)}, u32[]{:S(2)}, u32[]{:S(2)}) %collective-permute-start.17) | collective-permute-done | bytes 65568 | tf_op jit(solution)/shard_map/ppermute | solution.py:180
  79.5 1.0 collective-permute-done.18.c
  80.5 0.7 finish_rows.1
  81.2 12.0 %all_to_all.15.parts = f32[8,16,256]{2,1,0:T(8,128)S(1)} all-to-all(f32[8,16,256]{2,1,0:T(8,128)S(1)} %sum_spread.2), channel_id=1, replica_groups=mesh['y'=4,'zh'=2,'core'=2,'zl'=4,'x'=4] {'zh','zl'}, dimensions={0} | all-to-all | bytes 262144 | tf_op jit(solution)/shard_map/all_to_all | solution.py:184
  93.3 17.1 %all_to_all.16 = bf16[32,16,256]{2,1,0:T(8,128)(2,1)S(1)} all-to-all(bf16[32,16,256]{2,1,0:T(8,128)(2,1)S(1)} %sum_spread.3), channel_id=1, replica_groups=mesh['y'=4,'zh'=2,'core'=2,'zl'=4,'x'=4] {'y','core','x'}, dimensions={0} | all-to-all | bytes 524288 | tf_op jit(solution)/shard_map/all_to_all | solution.py:184
  110.4 0.9 convert_multiply_fusion
  (30 shorter events, 0.3 us)
Async XLA Ops:
  0.6 0.7 copy-start.6
  0.6 1.7 %copy-start.4 = (bf16[128,512]{1,0:T(8,128)(2,1)S(1)}, bf16[128,512]{1,0:T(8,128)(2,1)}, u32[]{:S(2)}) copy-start(bf16[128,512]{1,0:T(8,128)(2,1)} %embeds.1) | copy-start | bytes 393220
  1.4 0.8 copy-start.5
  2.3 1.0 copy-start.3
  3.7 14.8 %collective-permute-start.3 = (bf16[128,896]{1,0:T(8,128)(2,1)S(1)}, bf16[128,896]{1,0:T(8,128)(2,1)S(1)}, u32[]{:S(2)}, u32[]{:S(2)}) collective-permute-start(bf16[128,896]{1,0:T(8,128)(2,1)S(1)} %get-tuple-element.21.refs_4_), channel_id=1, source_target_pairs={{0,64},{1,65},{2,66},{3,67},{4,68},{5,69},{6,70},{7,71},{8,72},{9,... | collective-permute-start | bytes 688136 | tf_op jit(solution)/shard_map/ppermute | solution.py:180
  5.8 12.7 %collective-permute-start.2 = (bf16[128,896]{1,0:T(8,128)(2,1)S(1)}, bf16[128,896]{1,0:T(8,128)(2,1)S(1)}, u32[]{:S(2)}, u32[]{:S(2)}) collective-permute-start(bf16[128,896]{1,0:T(8,128)(2,1)S(1)} %get-tuple-element.21.refs_4_), channel_id=1, source_target_pairs={{0,128},{1,129},{2,130},{3,131},{4,132},{5,133},{6,134},{7,135},{8... | collective-permute-start | bytes 688136 | tf_op jit(solution)/shard_map/ppermute | solution.py:180
  8.2 10.9 %collective-permute-start.1 = (bf16[128,896]{1,0:T(8,128)(2,1)S(1)}, bf16[128,896]{1,0:T(8,128)(2,1)S(1)}, u32[]{:S(2)}, u32[]{:S(2)}) collective-permute-start(bf16[128,896]{1,0:T(8,128)(2,1)S(1)} %get-tuple-element.21.refs_4_), channel_id=1, source_target_pairs={{0,192},{1,193},{2,194},{3,195},{4,196},{5,197},{6,198},{7,199},{8... | collective-permute-start | bytes 688136 | tf_op jit(solution)/shard_map/ppermute | solution.py:180
  9.4 9.0 %collective-permute-start = (bf16[128,384]{1,0:T(8,128)(2,1)S(1)}, bf16[128,384]{1,0:T(8,128)(2,1)S(1)}, u32[]{:S(2)}, u32[]{:S(2)}) collective-permute-start(bf16[128,384]{1,0:T(8,128)(2,1)S(1)} %get-tuple-element.20), channel_id=1, source_target_pairs={{0,32},{4,36},{8,40},{12,44},{32,0},{36,4},{40,8},{44,12},{1,33},{... | collective-permute-start | bytes 294920 | tf_op jit(solution)/shard_map/ppermute | solution.py:169
  18.4 0.7 copy-start.1
  19.1 0.9 slice-start
  20.0 24.1 %copy-start = (bf16[128,128]{1,0:T(8,128)(2,1)S(1)}, bf16[128,128]{1,0:T(8,128)(2,1)}, u32[]{:S(2)}) copy-start(bf16[128,128]{1,0:T(8,128)(2,1)} %constant.4.clone.table) | copy-start | bytes 98308
  20.1 10.4 %collective-permute-start.6 = (bf16[256,384]{1,0:T(8,128)(2,1)S(1)}, bf16[256,384]{1,0:T(8,128)(2,1)S(1)}, u32[]{:S(2)}, u32[]{:S(2)}) collective-permute-start(bf16[256,384]{1,0:T(8,128)(2,1)S(1)} %pad_maximum_fusion.1.refs_0_), channel_id=1, source_target_pairs={{0,8},{4,12},{8,32},{12,36},{32,40},{36,44},{40,0},{44,4},{1,9},{5... | collective-permute-start | bytes 589832 | tf_op jit(solution)/shard_map/ppermute | solution.py:169
  22.7 14.1 %collective-permute-start.9 = (bf16[512,384]{1,0:T(8,128)(2,1)S(1)}, bf16[512,384]{1,0:T(8,128)(2,1)S(1)}, u32[]{:S(2)}, u32[]{:S(2)}) collective-permute-start(bf16[512,384]{1,0:T(8,128)(2,1)S(1)} %pad_maximum_fusion.rows_ref), channel_id=1, source_target_pairs={{0,1},{1,2},{2,3},{3,0},{4,5},{5,6},{6,7},{7,4},{8,9},{9,10},{10,1... | collective-permute-start | bytes 1179656 | tf_op jit(solution)/shard_map/ppermute | solution.py:180
  25.5 12.0 %collective-permute-start.8 = (bf16[512,384]{1,0:T(8,128)(2,1)S(1)}, bf16[512,384]{1,0:T(8,128)(2,1)S(1)}, u32[]{:S(2)}, u32[]{:S(2)}) collective-permute-start(bf16[512,384]{1,0:T(8,128)(2,1)S(1)} %pad_maximum_fusion.rows_ref), channel_id=1, source_target_pairs={{0,2},{1,3},{2,0},{3,1},{4,6},{5,7},{6,4},{7,5},{8,10},{9,11},{10,... | collective-permute-start | bytes 1179656 | tf_op jit(solution)/shard_map/ppermute | solution.py:180
  27.9 9.7 %collective-permute-start.7 = (bf16[512,384]{1,0:T(8,128)(2,1)S(1)}, bf16[512,384]{1,0:T(8,128)(2,1)S(1)}, u32[]{:S(2)}, u32[]{:S(2)}) collective-permute-start(bf16[512,384]{1,0:T(8,128)(2,1)S(1)} %pad_maximum_fusion.rows_ref), channel_id=1, source_target_pairs={{0,3},{1,0},{2,1},{3,2},{4,7},{5,4},{6,5},{7,6},{8,11},{9,8},{10,9... | collective-permute-start | bytes 1179656 | tf_op jit(solution)/shard_map/ppermute | solution.py:180
  29.0 5.0 %collective-permute-start.5 = (bf16[256,384]{1,0:T(8,128)(2,1)S(1)}, bf16[256,384]{1,0:T(8,128)(2,1)S(1)}, u32[]{:S(2)}, u32[]{:S(2)}) collective-permute-start(bf16[256,384]{1,0:T(8,128)(2,1)S(1)} %pad_maximum_fusion.1.refs_0_), channel_id=1, source_target_pairs={{0,44},{4,0},{8,4},{12,8},{32,12},{36,32},{40,36},{44,40},{1,45},{... | collective-permute-start | bytes 589832 | tf_op jit(solution)/shard_map/ppermute | solution.py:169
  30.5 6.3 %collective-permute-start.4 = (bf16[256,384]{1,0:T(8,128)(2,1)S(1)}, bf16[256,384]{1,0:T(8,128)(2,1)S(1)}, u32[]{:S(2)}, u32[]{:S(2)}) collective-permute-start(bf16[256,384]{1,0:T(8,128)(2,1)S(1)} %pad_maximum_fusion.1.refs_0_), channel_id=1, source_target_pairs={{0,4},{4,8},{8,12},{12,32},{32,36},{36,40},{40,44},{44,0},{1,5},{5... | collective-permute-start | bytes 589832 | tf_op jit(solution)/shard_map/ppermute | solution.py:169
  37.5 5.6 %collective-permute-start.10 = (bf16[256,384]{1,0:T(8,128)(2,1)S(1)}, bf16[256,384]{1,0:T(8,128)(2,1)S(1)}, u32[]{:S(2)}, u32[]{:S(2)}) collective-permute-start(bf16[256,384]{1,0:T(8,128)(2,1)S(1)} %pad_maximum_fusion.1.refs_0_), channel_id=1, source_target_pairs={{0,16},{16,0},{1,17},{17,1},{2,18},{18,2},{3,19},{19,3},{4,20},{20... | collective-permute-start | bytes 589832 | tf_op jit(solution)/shard_map/ppermute | solution.py:169
  42.1 1.4 %collective-permute-start.11 = (bf16[256,384]{1,0:T(8,128)(2,1)S(1)}, bf16[256,384]{1,0:T(8,128)(2,1)S(1)}, u32[]{:S(2)}, u32[]{:S(2)}) collective-permute-start(bf16[256,384]{1,0:T(8,128)(2,1)S(1)} %collective-permute-done.4.refs_1_), channel_id=1, source_target_pairs={{0,16},{16,0},{1,17},{17,1},{2,18},{18,2},{3,19},{19,3},{4,20},{20... | collective-permute-start | bytes 589832 | tf_op jit(solution)/shard_map/ppermute | solution.py:169
  42.2 1.6 %collective-permute-start.12 = (bf16[256,384]{1,0:T(8,128)(2,1)S(1)}, bf16[256,384]{1,0:T(8,128)(2,1)S(1)}, u32[]{:S(2)}, u32[]{:S(2)}) collective-permute-start(bf16[256,384]{1,0:T(8,128)(2,1)S(1)} %collective-permute-done.5.refs_2_), channel_id=1, source_target_pairs={{0,16},{16,0},{1,17},{17,1},{2,18},{18,2},{3,19},{19,3},{4,20},{20... | collective-permute-start | bytes 589832 | tf_op jit(solution)/shard_map/ppermute | solution.py:169
  42.6 1.5 %collective-permute-start.13 = (bf16[256,384]{1,0:T(8,128)(2,1)S(1)}, bf16[256,384]{1,0:T(8,128)(2,1)S(1)}, u32[]{:S(2)}, u32[]{:S(2)}) collective-permute-start(bf16[256,384]{1,0:T(8,128)(2,1)S(1)} %collective-permute-done.6.refs_3_), channel_id=1, source_target_pairs={{0,16},{16,0},{1,17},{17,1},{2,18},{18,2},{3,19},{19,3},{4,20},{20... | collective-permute-start | bytes 589832 | tf_op jit(solution)/shard_map/ppermute | solution.py:169
  46.7 16.0 %collective-permute-start.14 = (bf16[512,256]{1,0:T(8,128)(2,1)S(1)}, bf16[512,256]{1,0:T(8,128)(2,1)S(1)}, u32[]{:S(2)}, u32[]{:S(2)}) collective-permute-start(bf16[512,256]{1,0:T(8,128)(2,1)S(1)} %tile.5), channel_id=1, source_target_pairs={{0,1},{1,2},{2,3},{3,0},{4,5},{5,6},{6,7},{7,4},{8,9},{9,10},{10,1... | collective-permute-start | bytes 786440 | tf_op jit(solution)/shard_map/ppermute | solution.py:180
  51.1 11.5 %collective-permute-start.15 = (bf16[512,256]{1,0:T(8,128)(2,1)S(1)}, bf16[512,256]{1,0:T(8,128)(2,1)S(1)}, u32[]{:S(2)}, u32[]{:S(2)}) collective-permute-start(bf16[512,256]{1,0:T(8,128)(2,1)S(1)} %tile.6), channel_id=1, source_target_pairs={{0,2},{1,3},{2,0},{3,1},{4,6},{5,7},{6,4},{7,5},{8,10},{9,11},{10,... | collective-permute-start | bytes 786440 | tf_op jit(solution)/shard_map/ppermute | solution.py:180
  58.4 5.5 %copy-start.2 = (bf16[128,896]{1,0:T(8,128)(2,1)S(1)}, bf16[128,896]{1,0:T(8,128)(2,1)}, u32[]{:S(2)}) copy-start(bf16[128,896]{1,0:T(8,128)(2,1)} %copy-done.1) | copy-start | bytes 688132
  58.4 5.5 %collective-permute-start.16 = (bf16[512,256]{1,0:T(8,128)(2,1)S(1)}, bf16[512,256]{1,0:T(8,128)(2,1)S(1)}, u32[]{:S(2)}, u32[]{:S(2)}) collective-permute-start(bf16[512,256]{1,0:T(8,128)(2,1)S(1)} %tile.7), channel_id=1, source_target_pairs={{0,3},{1,0},{2,1},{3,2},{4,7},{5,4},{6,5},{7,6},{8,11},{9,8},{10,9... | collective-permute-start | bytes 786440 | tf_op jit(solution)/shard_map/ppermute | solution.py:180
  65.4 15.7 %all-to-all-start = ((bf16[32,16,256]{2,1,0:T(8,128)(2,1)}), bf16[32,16,256]{2,1,0:T(8,128)(2,1)S(1)}, u32[]{:S(2)}, u32[]{:S(2)}) async-start(bf16[32,16,256]{2,1,0:T(8,128)(2,1)} %bitcast.1), calls=%async_computation | async-start | bytes 524288 | tf_op jit(solution)/shard_map/all_to_all | solution.py:184
  72.0 7.4 %collective-permute-start.17 = (bf16[128,256]{1,0:T(8,128)(2,1)S(1)}, bf16[128,256]{1,0:T(8,128)(2,1)S(1)}, u32[]{:S(2)}, u32[]{:S(2)}) collective-permute-start(bf16[128,256]{1,0:T(8,128)(2,1)S(1)} %get-tuple-element.33), channel_id=1, source_target_pairs={{0,64},{1,65},{2,66},{3,67},{4,68},{5,69},{6,70},{7,71},{8,72},{9,... | collective-permute-start | bytes 196616 | tf_op jit(solution)/shard_map/ppermute | solution.py:180
  73.5 7.0 %collective-permute-start.18 = (bf16[128,256]{1,0:T(8,128)(2,1)S(1)}, bf16[128,256]{1,0:T(8,128)(2,1)S(1)}, u32[]{:S(2)}, u32[]{:S(2)}) collective-permute-start(bf16[128,256]{1,0:T(8,128)(2,1)S(1)} %get-tuple-element.34), channel_id=1, source_target_pairs={{0,128},{1,129},{2,130},{3,131},{4,132},{5,133},{6,134},{7,135},{8... | collective-permute-start | bytes 196616 | tf_op jit(solution)/shard_map/ppermute | solution.py:180
  75.9 4.6 %collective-permute-start.19 = (bf16[128,256]{1,0:T(8,128)(2,1)S(1)}, bf16[128,256]{1,0:T(8,128)(2,1)S(1)}, u32[]{:S(2)}, u32[]{:S(2)}) collective-permute-start(bf16[128,256]{1,0:T(8,128)(2,1)S(1)} %get-tuple-element.35), channel_id=1, source_target_pairs={{0,192},{1,193},{2,194},{3,195},{4,196},{5,197},{6,198},{7,199},{8... | collective-permute-start | bytes 196616 | tf_op jit(solution)/shard_map/ppermute | solution.py:180

commit v3 on v2

--- a/solution.py
+++ b/solution.py
@@ -33,7 +33,7 @@
 
 def pack_kernel(embeds, weight, solve, probes, probe_solves, out, extended):
     rows, width = embeds.shape[0], weight.shape[1]
-    count = probes.shape[1]
+    count = probes.shape[0]
     feats = jnp.dot(embeds[...], weight[...], preferred_element_type=F32).astype(BF16)
     out[:, :width] = feats
     wide = feats.astype(F32)
@@ -44,14 +44,9 @@
     fold = math.sqrt(5.0 / 3.0 * ROOT5)
     scale = (2.0 * count) ** (-0.5) * fold
     factors = jnp.concatenate(
-        [
-            solve[...] * fold,
-            probes[...] * -scale,
-            probe_solves[...] * -scale,
-            jnp.zeros((rows, 1), F32),
-        ],
-        axis=1,
-    )
+        [solve[...] * fold, probes[...] * -scale, probe_solves[...] * -scale, jnp.zeros((1, rows), F32)],
+        axis=0,
+    ).T
     hi = factors.astype(BF16).astype(F32)
     lo = factors - hi
     lane = lax.broadcasted_iota(jnp.int32, (rows, 32), 1)
@@ -61,6 +56,14 @@
     extended[:, :width] = feats
     extended[:, width : width + 128] = tail
     extended[:, width + 128 :] = embeds[...]
+
+
+def split_kernel(count, *refs):
+    line, embeds = refs[count:]
+    rows, width = refs[0].shape[0], line.shape[1]
+    for k, ref in enumerate(refs[:count]):
+        line[k * rows : (k + 1) * rows, :] = ref[:, :width]
+        embeds[k * rows : (k + 1) * rows, :] = ref[:, width:]
 
 
 def left_map(count):
@@ -123,8 +126,8 @@
 
 
 def sum_rows_kernel(count, *refs):
-    parts, lines, (partial, own, *others) = refs[:count], refs[count : 2 * count], refs[2 * count :]
-    rows, width = own.shape
+    parts, (embeds, partial, own, *others) = refs[:count], refs[count:]
+    rows = own.shape[0]
     total = parts[0][...]
     for ref in parts[1:]:
         total = total + ref[...].astype(F32)
@@ -133,12 +136,7 @@
     own[...] = total[:rows]
     for k, ref in enumerate(others):
         ref[...] = hi[(k + 1) * rows : (k + 2) * rows]
-    weight = jnp.zeros(partial.shape, F32)
-    for k, ref in enumerate(lines):
-        block = slice(k * rows, (k + 1) * rows)
-        embeds = ref[:, width + 128 :]
-        weight = weight + (dot_tn(embeds, hi[block]) + dot_tn(embeds, lo[block]))
-    partial[...] = weight.astype(BF16)
+    partial[...] = (dot_tn(embeds[...], hi) + dot_tn(embeds[...], lo)).astype(BF16)
 
 
 def finish_rows_kernel(own, b, c, d, grad_rows):
@@ -169,15 +167,23 @@
     return lax.ppermute(array, axis, [(i, (i + shift) % size) for i in range(size)])
 
 
-def turn(array, sizes, stage, shift):
+def move(array, sizes, where):
     dims = [sizes[a] for a in ALL]
     perm = []
     for source in range(math.prod(dims)):
-        place = list(np.unravel_index(source, dims))
-        axis = ALL.index(PLANE[0] if (place[ALL.index("core")] + stage) % 2 == 0 else PLANE[-1])
-        place[axis] = (place[axis] + shift) % dims[axis]
-        perm.append((source, int(np.ravel_multi_index(place, dims))))
+        place = dict(zip(ALL, (int(i) for i in np.unravel_index(source, dims))))
+        for axis, shift in where(place["core"]).items():
+            if axis == "z":
+                z = (place["zh"] * sizes["zl"] + place["zl"] + shift) % (sizes["zh"] * sizes["zl"])
+                place["zh"], place["zl"] = divmod(z, sizes["zl"])
+            else:
+                place[axis] = (place[axis] + shift) % sizes[axis]
+        perm.append((source, int(np.ravel_multi_index([place[a] for a in ALL], dims))))
     return lax.ppermute(array, ALL, perm)
+
+
+def turn(array, sizes, stage, shift):
+    return move(array, sizes, lambda core: {"y" if (core + stage) % 2 == 0 else "x": shift})
 
 
 def exchange(array, axes):
@@ -197,16 +203,28 @@
         out_specs=[VMEM] * 2,
         compiler_params=params(16),
         name="pack",
-    )(embeds, weight, solve[:, None], probes, probe_solves)
+    )(embeds, weight, solve[None, :], probes.T, probe_solves.T)
 
     blocks = [extended] + [turn(extended, sizes, 0, -d) for d in range(1, n_side)]
-    line = jnp.concatenate([block[:, : width + 128] for block in blocks], axis=0)
+    line, embeds_line = pl.pallas_call(
+        functools.partial(split_kernel, n_side),
+        out_shape=[
+            jax.ShapeDtypeStruct((n_side * rows, width + 128), BF16),
+            jax.ShapeDtypeStruct((n_side * rows, embeds.shape[1]), BF16),
+        ],
+        in_specs=[VMEM] * n_side,
+        out_specs=[VMEM] * 2,
+        compiler_params=params(8),
+        name="split",
+    )(*blocks)
     pair = jnp.concatenate([pack, ring(pack, DEPTH, n_z, n_z // 2)], axis=0)
-    pair, _ = lax.optimization_barrier((pair, line))
-    columns = [pair] + [ring(pair, DEPTH, n_z, d) for d in (1, -1, 2)]
+    pair, line = lax.optimization_barrier((pair, line))
+    four = jnp.concatenate([pair, ring(pair, "core", 2, 1)], axis=0)
+    near = move(four, sizes, lambda core: {"z": 1 - 2 * core})
+    far = ring(pair, DEPTH, n_z, 2)
     lines = [line] + [turn(line, sizes, 1, -d) for d in range(1, n_side)]
-    columns, lines = lax.optimization_barrier((columns, lines))
-    columns += [ring(part, "core", 2, 1) for part in columns]
+    near, far, lines = lax.optimization_barrier((near, far, lines))
+    columns = [four, near, far, ring(near, "core", 2, 1), ring(far, "core", 2, 1)]
 
     table = left_map(probes.shape[1])
     back = {}
@@ -216,7 +234,7 @@
             out_shape=jax.ShapeDtypeStruct((n_side * rows, width), F32 if d == 0 else BF16),
             in_specs=[VMEM] * (2 + len(columns)),
             out_specs=VMEM,
-            compiler_params=params(40),
+            compiler_params=params(16),
             name="tile",
         )(table, lines[d], *columns)
         back[d] = part if d == 0 else turn(part, sizes, 1, d)
@@ -228,12 +246,20 @@
             jax.ShapeDtypeStruct((rows, width), F32),
         ]
         + [jax.ShapeDtypeStruct((rows, width), BF16)] * (n_side - 1),
-        in_specs=[VMEM] * (2 * n_side),
+        in_specs=[VMEM] * (n_side + 1),
         out_specs=[VMEM] * (n_side + 1),
         compiler_params=params(16),
         name="sum_rows",
-    )(*(back[d] for d in range(n_side)), *blocks)
+    )(*(back[d] for d in range(n_side)), embeds_line)
     arrived = [turn(block, sizes, 0, d + 1) for d, block in enumerate(other_rows)]
+    n_plane = n_side * n_side * 2
+    pieces = exchange(partial.reshape(n_plane, -1, width), PLANE)
+    pieces, arrived[0], arrived[1] = lax.optimization_barrier((pieces, arrived[0], arrived[1]))
+    pieces = exchange(sum_spread(pieces, n_z, F32), DEPTH)
+    pieces, arrived[2] = lax.optimization_barrier((pieces, arrived[2]))
+    pieces = exchange(sum_spread(pieces, n_plane, BF16), PLANE)
+    total_points = rows * n_plane * n_z
+    grad_weight = pieces.reshape(-1, width).astype(F32) * (1.0 / math.sqrt(total_points))
     grad_rows = pl.pallas_call(
         finish_rows_kernel,
         out_shape=jax.ShapeDtypeStruct((rows, width), F32),
@@ -242,14 +268,6 @@
         compiler_params=params(16),
         name="finish_rows",
     )(own_rows, *arrived)
-
-    n_plane = n_side * n_side * 2
-    pieces = exchange(partial.reshape(n_plane, -1, width), PLANE)
-    pieces, grad_rows = lax.optimization_barrier((pieces, grad_rows))
-    pieces = exchange(sum_spread(pieces, n_z, F32), DEPTH)
-    pieces = exchange(sum_spread(pieces, n_plane, BF16), PLANE)
-    total_points = rows * n_plane * n_z
-    grad_weight = pieces.reshape(-1, width).astype(F32) * (1.0 / math.sqrt(total_points))
     return grad_rows, grad_weight
 
 

time: 112 us -> 113 us (level)
  blocking collectives: 29.2 us -> 0 us
  waiting for transfers between devices: 15.3 us -> 36.8 us
  starting transfers between devices: 48 us -> 56.2 us
  Pallas kernels: 12.8 us -> 14.1 us
    all_to_all x2 -> x0, blocking collectives: 29.2 us -> none  [exchange(): return lax.all_to_all(array, axes, split_axis=0, concat_axis=0, tiled=True)]
    all_to_all x1 -> x3, waiting for transfers between devices: 0.01 us -> 13.5 us  [exchange(): return lax.all_to_all(array, axes, split_axis=0, concat_axis=0, tiled=True)]
    all_to_all x1 -> x3, starting transfers between devices: 6.57 us -> 18.8 us  [exchange(): return lax.all_to_all(array, axes, split_axis=0, concat_axis=0, tiled=True)]
    ppermute x8 -> x5, waiting for transfers between devices: 9.92 us -> 14.4 us  [ring(): lax.ppermute(array, axis, [(i, (i + shift) % size) for i in range(size)])]
    ppermute x12 -> x13, starting transfers between devices: 25.4 us -> 21.8 us  [move(): return lax.ppermute(array, ALL, perm)]
    ppermute x12 -> x13, waiting for transfers between devices: 5.4 us -> 8.82 us  [move(): return lax.ppermute(array, ALL, perm)]
    pallas_call x2, Pallas kernels: 0.08 us -> 1.43 us  [sum_spread(): pl.pallas_call(sum_spread_kernel, out_shape=jax.ShapeDtypeStruct((copies,...]
    unnamed x16 -> x13, local copies, waits for them, and re-layouts: 3.18 us -> 3.92 us
  transfers between devices with their start and end apart: 21 -> 21, of which waited for: 12 -> 10; matrix products, arithmetic and copies ran while one was open for 0% -> 0% of each run, Pallas kernels for 8% -> 7%
where the time goes in v3:
time: 113 us
  starting transfers between devices  56.2 us (50%)
  waiting for transfers between devices  36.8 us (33%)
  Pallas kernels  14.1 us (12%)
  local copies, waits for them, and re-layouts  3.95 us (3%)
    ppermute x13, starting transfers between devices, move(): return lax.ppermute(array, ALL, perm)  21.8 us
    all_to_all x3, starting transfers between devices, exchange(): return lax.all_to_all(array, axes, split_axis=0, concat_axis=0, tiled=True)  18.8 us
    ppermute x5, starting transfers between devices, ring(): lax.ppermute(array, axis, [(i, (i + shift) % size) for i in range(size)])  15.6 us
    ppermute x5, waiting for transfers between devices, ring(): lax.ppermute(array, axis, [(i, (i + shift) % size) for i in range(size)])  14.4 us
    all_to_all x3, waiting for transfers between devices, exchange(): return lax.all_to_all(array, axes, split_axis=0, concat_axis=0, tiled=True)  13.5 us
    pallas_call x4, Pallas kernels, shards(): pl.pallas_call(functools.partial(tile_kernel, 256, 256), out_shape=jax.Sh...  10.2 us
    ppermute x13, waiting for transfers between devices, move(): return lax.ppermute(array, ALL, perm)  8.82 us
    unnamed x13, local copies, waits for them, and re-layouts  3.92 us
  transfers between devices with their start and end apart: 21, of which 10 were waited for; matrix products, arithmetic and copies ran while one was open for 0% of the time, Pallas kernels for 7%

profile of v3, /device:TPU:1, one launch (start us, length us, event | category | flops | bytes accessed | tf_op | source)
XLA Modules:
  0.0 112.7 jit_solution(10151723751407544811)
XLA Ops:
  0.6 0.6 copy-done.5
  1.3 0.9 copy-done.1
  2.2 0.9 copy-done.2
  3.1 0.7 copy-done.3
  3.8 0.7 copy-done.4
  4.5 0.5 pack.1
  5.0 2.1 %collective-permute-start.3 = (bf16[128,896]{1,0:T(8,128)(2,1)S(1)}, bf16[128,896]{1,0:T(8,128)(2,1)S(1)}, u32[]{:S(2)}, u32[]{:S(2)}) collective-permute-start(bf16[128,896]{1,0:T(8,128)(2,1)S(1)} %get-tuple-element.25.refs_0_), channel_id=1, source_target_pairs={{0,64},{1,65},{2,66},{3,67},{4,68},{5,69},{6,70},{7,71},{8,72},{9,... | collective-permute-start | bytes 688136 | tf_op jit(solution)/shard_map/ppermute | solution.py:182
  7.1 2.5 %collective-permute-start.2 = (bf16[128,896]{1,0:T(8,128)(2,1)S(1)}, bf16[128,896]{1,0:T(8,128)(2,1)S(1)}, u32[]{:S(2)}, u32[]{:S(2)}) collective-permute-start(bf16[128,896]{1,0:T(8,128)(2,1)S(1)} %get-tuple-element.25.refs_0_), channel_id=1, source_target_pairs={{0,128},{1,129},{2,130},{3,131},{4,132},{5,133},{6,134},{7,135},{8... | collective-permute-start | bytes 688136 | tf_op jit(solution)/shard_map/ppermute | solution.py:182
  9.6 1.2 %collective-permute-start.1 = (bf16[128,896]{1,0:T(8,128)(2,1)S(1)}, bf16[128,896]{1,0:T(8,128)(2,1)S(1)}, u32[]{:S(2)}, u32[]{:S(2)}) collective-permute-start(bf16[128,896]{1,0:T(8,128)(2,1)S(1)} %get-tuple-element.25.refs_0_), channel_id=1, source_target_pairs={{0,192},{1,193},{2,194},{3,195},{4,196},{5,197},{6,198},{7,199},{8... | collective-permute-start | bytes 688136 | tf_op jit(solution)/shard_map/ppermute | solution.py:182
  10.7 6.9 %collective-permute-start = (bf16[128,384]{1,0:T(8,128)(2,1)S(1)}, bf16[128,384]{1,0:T(8,128)(2,1)S(1)}, u32[]{:S(2)}, u32[]{:S(2)}) collective-permute-start(bf16[128,384]{1,0:T(8,128)(2,1)S(1)} %get-tuple-element.24), channel_id=1, source_target_pairs={{0,32},{4,36},{8,40},{12,44},{32,0},{36,4},{40,8},{44,12},{1,33},{... | collective-permute-start | bytes 294920 | tf_op jit(solution)/shard_map/ppermute | solution.py:167
  17.6 2.1 %collective-permute-done = bf16[128,384]{1,0:T(8,128)(2,1)S(1)} collective-permute-done((bf16[128,384]{1,0:T(8,128)(2,1)S(1)}, bf16[128,384]{1,0:T(8,128)(2,1)S(1)}, u32[]{:S(2)}, u32[]{:S(2)}) %collective-permute-start) | collective-permute-done | bytes 98336 | tf_op jit(solution)/shard_map/ppermute | solution.py:167
  19.8 0.0 collective-permute-done.3.refs_3_
  19.8 0.1 split.1
  19.9 2.7 %collective-permute-start.4 = (bf16[256,384]{1,0:T(8,128)(2,1)S(1)}, bf16[256,384]{1,0:T(8,128)(2,1)S(1)}, u32[]{:S(2)}, u32[]{:S(2)}) collective-permute-start(bf16[256,384]{1,0:T(8,128)(2,1)S(1)} %pad_maximum_fusion), channel_id=1, source_target_pairs={{0,16},{16,0},{1,17},{17,1},{2,18},{18,2},{3,19},{19,3},{4,20},{20... | collective-permute-start | bytes 589832 | tf_op jit(solution)/shard_map/ppermute | solution.py:167
  22.6 1.2 %collective-permute-start.9 = (bf16[512,384]{1,0:T(8,128)(2,1)S(1)}, bf16[512,384]{1,0:T(8,128)(2,1)S(1)}, u32[]{:S(2)}, u32[]{:S(2)}) collective-permute-start(bf16[512,384]{1,0:T(8,128)(2,1)S(1)} %get-tuple-element.29.rows_ref), channel_id=1, source_target_pairs={{0,1},{1,2},{2,3},{3,0},{4,5},{5,6},{6,7},{7,4},{8,9},{9,10},{10,1... | collective-permute-start | bytes 1179656 | tf_op jit(solution)/shard_map/ppermute | solution.py:182
  23.8 1.5 %collective-permute-start.8 = (bf16[512,384]{1,0:T(8,128)(2,1)S(1)}, bf16[512,384]{1,0:T(8,128)(2,1)S(1)}, u32[]{:S(2)}, u32[]{:S(2)}) collective-permute-start(bf16[512,384]{1,0:T(8,128)(2,1)S(1)} %get-tuple-element.29.rows_ref), channel_id=1, source_target_pairs={{0,2},{1,3},{2,0},{3,1},{4,6},{5,7},{6,4},{7,5},{8,10},{9,11},{10,... | collective-permute-start | bytes 1179656 | tf_op jit(solution)/shard_map/ppermute | solution.py:182
  25.3 0.9 collective-permute-start.7
  26.2 0.0 copy-start
  26.2 4.5 %collective-permute-start.5 = (bf16[512,384]{1,0:T(8,128)(2,1)S(1)}, bf16[512,384]{1,0:T(8,128)(2,1)S(1)}, u32[]{:S(2)}, u32[]{:S(2)}) collective-permute-start(bf16[512,384]{1,0:T(8,128)(2,1)S(1)} %constant_dynamic-update-slice_fusion.refs_0_), channel_id=1, source_target_pairs={{0,4},{1,5},{2,6},{3,7},{4,8},{5,9},{6,10},{7,11},{8,12},{9,13},{1... | collective-permute-start | bytes 1179656 | tf_op jit(solution)/shard_map/ppermute | solution.py:182
  30.7 10.8 %collective-permute-done.6.refs_2_ = bf16[256,384]{1,0:T(8,128)(2,1)S(1)} collective-permute-done((bf16[256,384]{1,0:T(8,128)(2,1)S(1)}, bf16[256,384]{1,0:T(8,128)(2,1)S(1)}, u32[]{:S(2)}, u32[]{:S(2)}) %collective-permute-start.6) | collective-permute-done | bytes 196640 | tf_op jit(solution)/shard_map/ppermute | solution.py:167
  41.5 5.8 %collective-permute-start.10 = (bf16[512,384]{1,0:T(8,128)(2,1)S(1)}, bf16[512,384]{1,0:T(8,128)(2,1)S(1)}, u32[]{:S(2)}, u32[]{:S(2)}) collective-permute-start(bf16[512,384]{1,0:T(8,128)(2,1)S(1)} %collective-permute-done.5.refs_1_), channel_id=1, source_target_pairs={{0,16},{16,0},{1,17},{17,1},{2,18},{18,2},{3,19},{19,3},{4,20},{20... | collective-permute-start | bytes 1179656 | tf_op jit(solution)/shard_map/ppermute | solution.py:167
  47.4 0.1 collective-permute-start.11
  47.5 1.5 %collective-permute-done.11.refs_4_ = bf16[256,384]{1,0:T(8,128)(2,1)S(1)} collective-permute-done((bf16[256,384]{1,0:T(8,128)(2,1)S(1)}, bf16[256,384]{1,0:T(8,128)(2,1)S(1)}, u32[]{:S(2)}, u32[]{:S(2)}) %collective-permute-start.11) | collective-permute-done | bytes 196640 | tf_op jit(solution)/shard_map/ppermute | solution.py:167
  49.0 2.6 %tile.5 = bf16[512,256]{1,0:T(8,128)(2,1)S(1)} custom-call(bf16[128,128]{1,0:T(8,128)(2,1)S(1)} %copy-done, bf16[512,384]{1,0:T(8,128)(2,1)S(1)} %collective-permute-done.7.rows_ref, bf16[512,384]{1,0:T(8,128)(2,1)S(1)} %constant_dynamic-update-slice_fusion.refs_0_, bf16[512,384]{1,0:T(8,128)(2,1)S(1)} %collective-permute-done.5.refs_1_, ...), custom_call_target="tpu_custom_call" | custom-call | tf_op jit(solution)/shard_map/tile/pallas_call | solution.py:232
  51.6 0.4 collective-permute-start.12
  52.0 2.6 %tile.6 = bf16[512,256]{1,0:T(8,128)(2,1)S(1)} custom-call(bf16[128,128]{1,0:T(8,128)(2,1)S(1)} %copy-done, bf16[512,384]{1,0:T(8,128)(2,1)S(1)} %collective-permute-done.8.rows_ref, bf16[512,384]{1,0:T(8,128)(2,1)S(1)} %constant_dynamic-update-slice_fusion.refs_0_, bf16[512,384]{1,0:T(8,128)(2,1)S(1)} %collective-permute-done.5.refs_1_, ...), custom_call_target="tpu_custom_call" | custom-call | tf_op jit(solution)/shard_map/tile/pallas_call | solution.py:232
  54.5 1.5 %collective-permute-start.13 = (bf16[512,256]{1,0:T(8,128)(2,1)S(1)}, bf16[512,256]{1,0:T(8,128)(2,1)S(1)}, u32[]{:S(2)}, u32[]{:S(2)}) collective-permute-start(bf16[512,256]{1,0:T(8,128)(2,1)S(1)} %tile.6), channel_id=1, source_target_pairs={{0,2},{1,3},{2,0},{3,1},{4,6},{5,7},{6,4},{7,5},{8,10},{9,11},{10,... | collective-permute-start | bytes 786440 | tf_op jit(solution)/shard_map/ppermute | solution.py:182
  56.0 2.6 %tile.7 = bf16[512,256]{1,0:T(8,128)(2,1)S(1)} custom-call(bf16[128,128]{1,0:T(8,128)(2,1)S(1)} %copy-done, bf16[512,384]{1,0:T(8,128)(2,1)S(1)} %collective-permute-done.9.rows_ref, bf16[512,384]{1,0:T(8,128)(2,1)S(1)} %constant_dynamic-update-slice_fusion.refs_0_, bf16[512,384]{1,0:T(8,128)(2,1)S(1)} %collective-permute-done.5.refs_1_, ...), custom_call_target="tpu_custom_call" | custom-call | tf_op jit(solution)/shard_map/tile/pallas_call | solution.py:232
  58.6 1.2 %collective-permute-start.14 = (bf16[512,256]{1,0:T(8,128)(2,1)S(1)}, bf16[512,256]{1,0:T(8,128)(2,1)S(1)}, u32[]{:S(2)}, u32[]{:S(2)}) collective-permute-start(bf16[512,256]{1,0:T(8,128)(2,1)S(1)} %tile.7), channel_id=1, source_target_pairs={{0,3},{1,0},{2,1},{3,2},{4,7},{5,4},{6,5},{7,6},{8,11},{9,8},{10,9... | collective-permute-start | bytes 786440 | tf_op jit(solution)/shard_map/ppermute | solution.py:182
  59.8 2.6 %tile.4.refs_0_ = f32[512,256]{1,0:T(8,128)S(1)} custom-call(bf16[128,128]{1,0:T(8,128)(2,1)S(1)} %copy-done, bf16[512,384]{1,0:T(8,128)(2,1)S(1)} %get-tuple-element.29.rows_ref, bf16[512,384]{1,0:T(8,128)(2,1)S(1)} %constant_dynamic-update-slice_fusion.refs_0_, bf16[512,384]{1,0:T(8,128)(2,1)S(1)} %collective-permute-done.5.refs_1_, ...), custom_call_target="tpu_custom_call" | custom-call | tf_op jit(solution)/shard_map/tile/pallas_call | solution.py:232
  62.4 2.2 %collective-permute-done.14.refs_3_ = bf16[512,256]{1,0:T(8,128)(2,1)S(1)} collective-permute-done((bf16[512,256]{1,0:T(8,128)(2,1)S(1)}, bf16[512,256]{1,0:T(8,128)(2,1)S(1)}, u32[]{:S(2)}, u32[]{:S(2)}) %collective-permute-start.14) | collective-permute-done | bytes 262176 | tf_op jit(solution)/shard_map/ppermute | solution.py:182
  64.6 1.2 %sum_rows.1 = (bf16[512,256]{1,0:T(8,128)(2,1)}, f32[128,256]{1,0:T(8,128)S(1)}, bf16[128,256]{1,0:T(8,128)(2,1)S(1)}, bf16[128,256]{1,0:T(8,128)(2,1)S(1)}, bf16[128,256]{1,0:T(8,128)(2,1)S(1)}) custom-call(f32[512,256]{1,0:T(8,128)S(1)} %tile.4.refs_0_, bf16[512,256]{1,0:T(8,128)(2,1)S(1)} %collective-permute-done.12.refs_1_, ...), custom_call_target="tpu_custom_call" | custom-call | tf_op jit(solution)/shard_map/sum_rows/pallas_call | solution.py:242
  65.8 6.5 %all-to-all-start = ((bf16[32,16,256]{2,1,0:T(8,128)(2,1)}), bf16[32,16,256]{2,1,0:T(8,128)(2,1)S(1)}, u32[]{:S(2)}, u32[]{:S(2)}) async-start(bf16[32,16,256]{2,1,0:T(8,128)(2,1)} %bitcast.3), calls=%async_computation | async-start | bytes 524288 | tf_op jit(solution)/shard_map/all_to_all | solution.py:190
  72.3 1.5 %collective-permute-start.15 = (bf16[128,256]{1,0:T(8,128)(2,1)S(1)}, bf16[128,256]{1,0:T(8,128)(2,1)S(1)}, u32[]{:S(2)}, u32[]{:S(2)}) collective-permute-start(bf16[128,256]{1,0:T(8,128)(2,1)S(1)} %get-tuple-element.38), channel_id=1, source_target_pairs={{0,64},{1,65},{2,66},{3,67},{4,68},{5,69},{6,70},{7,71},{8,72},{9,... | collective-permute-start | bytes 196616 | tf_op jit(solution)/shard_map/ppermute | solution.py:182
  73.8 2.4 %collective-permute-start.16 = (bf16[128,256]{1,0:T(8,128)(2,1)S(1)}, bf16[128,256]{1,0:T(8,128)(2,1)S(1)}, u32[]{:S(2)}, u32[]{:S(2)}) collective-permute-start(bf16[128,256]{1,0:T(8,128)(2,1)S(1)} %get-tuple-element.39), channel_id=1, source_target_pairs={{0,128},{1,129},{2,130},{3,131},{4,132},{5,133},{6,134},{7,135},{8... | collective-permute-start | bytes 196616 | tf_op jit(solution)/shard_map/ppermute | solution.py:182
  76.2 3.6 %collective-permute-done.15.b = bf16[128,256]{1,0:T(8,128)(2,1)S(1)} collective-permute-done((bf16[128,256]{1,0:T(8,128)(2,1)S(1)}, bf16[128,256]{1,0:T(8,128)(2,1)S(1)}, u32[]{:S(2)}, u32[]{:S(2)}) %collective-permute-start.15) | collective-permute-done | bytes 65568 | tf_op jit(solution)/shard_map/ppermute | solution.py:182
  79.8 1.0 collective-permute-done.16.c
  80.8 0.7 all-to-all-done.parts
  81.4 0.7 sum_spread.2
  82.1 5.4 %all-to-all-start.1 = ((f32[8,16,256]{2,1,0:T(8,128)}), f32[8,16,256]{2,1,0:T(8,128)S(1)}, u32[]{:S(2)}, u32[]{:S(2)}) async-start(f32[8,16,256]{2,1,0:T(8,128)} %sum_spread.2), calls=%async_computation.1 | async-start | bytes 262144 | tf_op jit(solution)/shard_map/all_to_all | solution.py:190
  87.5 1.1 collective-permute-start.17
  88.6 2.0 %collective-permute-done.17.d = bf16[128,256]{1,0:T(8,128)(2,1)S(1)} collective-permute-done((bf16[128,256]{1,0:T(8,128)(2,1)S(1)}, bf16[128,256]{1,0:T(8,128)(2,1)S(1)}, u32[]{:S(2)}, u32[]{:S(2)}) %collective-permute-start.17) | collective-permute-done | bytes 65568 | tf_op jit(solution)/shard_map/ppermute | solution.py:182
  90.6 4.7 %all-to-all-done.1.parts = f32[8,16,256]{2,1,0:T(8,128)S(1)} async-done(((f32[8,16,256]{2,1,0:T(8,128)}), f32[8,16,256]{2,1,0:T(8,128)S(1)}, u32[]{:S(2)}, u32[]{:S(2)}) %all-to-all-start.1) | async-done | bytes 131104 | tf_op jit(solution)/shard_map/all_to_all | solution.py:190
  95.3 0.7 sum_spread.3
  96.0 6.9 %all-to-all-start.2 = ((bf16[32,16,256]{2,1,0:T(8,128)(2,1)}), bf16[32,16,256]{2,1,0:T(8,128)(2,1)S(1)}, u32[]{:S(2)}, u32[]{:S(2)}) async-start(bf16[32,16,256]{2,1,0:T(8,128)(2,1)} %sum_spread.3), calls=%async_computation.2 | async-start | bytes 524288 | tf_op jit(solution)/shard_map/all_to_all | solution.py:190
  102.9 0.7 finish_rows.1
  103.6 8.2 %all-to-all-done.2 = bf16[32,16,256]{2,1,0:T(8,128)(2,1)S(1)} async-done(((bf16[32,16,256]{2,1,0:T(8,128)(2,1)}), bf16[32,16,256]{2,1,0:T(8,128)(2,1)S(1)}, u32[]{:S(2)}, u32[]{:S(2)}) %all-to-all-start.2) | async-done | bytes 262176 | tf_op jit(solution)/shard_map/all_to_all | solution.py:190
  111.8 0.9 convert_multiply_fusion
  (20 shorter events, 0.1 us)
Async XLA Ops:
  0.6 0.7 copy-start.5
  1.3 0.9 copy-start.1
  2.2 0.9 copy-start.2
  3.1 0.7 copy-start.3
  3.8 0.7 copy-start.4
  5.0 14.7 %collective-permute-start.3 = (bf16[128,896]{1,0:T(8,128)(2,1)S(1)}, bf16[128,896]{1,0:T(8,128)(2,1)S(1)}, u32[]{:S(2)}, u32[]{:S(2)}) collective-permute-start(bf16[128,896]{1,0:T(8,128)(2,1)S(1)} %get-tuple-element.25.refs_0_), channel_id=1, source_target_pairs={{0,64},{1,65},{2,66},{3,67},{4,68},{5,69},{6,70},{7,71},{8,72},{9,... | collective-permute-start | bytes 688136 | tf_op jit(solution)/shard_map/ppermute | solution.py:182
  7.1 12.7 %collective-permute-start.2 = (bf16[128,896]{1,0:T(8,128)(2,1)S(1)}, bf16[128,896]{1,0:T(8,128)(2,1)S(1)}, u32[]{:S(2)}, u32[]{:S(2)}) collective-permute-start(bf16[128,896]{1,0:T(8,128)(2,1)S(1)} %get-tuple-element.25.refs_0_), channel_id=1, source_target_pairs={{0,128},{1,129},{2,130},{3,131},{4,132},{5,133},{6,134},{7,135},{8... | collective-permute-start | bytes 688136 | tf_op jit(solution)/shard_map/ppermute | solution.py:182
  9.6 10.2 %collective-permute-start.1 = (bf16[128,896]{1,0:T(8,128)(2,1)S(1)}, bf16[128,896]{1,0:T(8,128)(2,1)S(1)}, u32[]{:S(2)}, u32[]{:S(2)}) collective-permute-start(bf16[128,896]{1,0:T(8,128)(2,1)S(1)} %get-tuple-element.25.refs_0_), channel_id=1, source_target_pairs={{0,192},{1,193},{2,194},{3,195},{4,196},{5,197},{6,198},{7,199},{8... | collective-permute-start | bytes 688136 | tf_op jit(solution)/shard_map/ppermute | solution.py:182
  10.7 9.0 %collective-permute-start = (bf16[128,384]{1,0:T(8,128)(2,1)S(1)}, bf16[128,384]{1,0:T(8,128)(2,1)S(1)}, u32[]{:S(2)}, u32[]{:S(2)}) collective-permute-start(bf16[128,384]{1,0:T(8,128)(2,1)S(1)} %get-tuple-element.24), channel_id=1, source_target_pairs={{0,32},{4,36},{8,40},{12,44},{32,0},{36,4},{40,8},{44,12},{1,33},{... | collective-permute-start | bytes 294920 | tf_op jit(solution)/shard_map/ppermute | solution.py:167
  19.9 6.3 %collective-permute-start.4 = (bf16[256,384]{1,0:T(8,128)(2,1)S(1)}, bf16[256,384]{1,0:T(8,128)(2,1)S(1)}, u32[]{:S(2)}, u32[]{:S(2)}) collective-permute-start(bf16[256,384]{1,0:T(8,128)(2,1)S(1)} %pad_maximum_fusion), channel_id=1, source_target_pairs={{0,16},{16,0},{1,17},{17,1},{2,18},{18,2},{3,19},{19,3},{4,20},{20... | collective-permute-start | bytes 589832 | tf_op jit(solution)/shard_map/ppermute | solution.py:167
  22.6 18.9 %collective-permute-start.9 = (bf16[512,384]{1,0:T(8,128)(2,1)S(1)}, bf16[512,384]{1,0:T(8,128)(2,1)S(1)}, u32[]{:S(2)}, u32[]{:S(2)}) collective-permute-start(bf16[512,384]{1,0:T(8,128)(2,1)S(1)} %get-tuple-element.29.rows_ref), channel_id=1, source_target_pairs={{0,1},{1,2},{2,3},{3,0},{4,5},{5,6},{6,7},{7,4},{8,9},{9,10},{10,1... | collective-permute-start | bytes 1179656 | tf_op jit(solution)/shard_map/ppermute | solution.py:182
  23.8 17.8 %collective-permute-start.8 = (bf16[512,384]{1,0:T(8,128)(2,1)S(1)}, bf16[512,384]{1,0:T(8,128)(2,1)S(1)}, u32[]{:S(2)}, u32[]{:S(2)}) collective-permute-start(bf16[512,384]{1,0:T(8,128)(2,1)S(1)} %get-tuple-element.29.rows_ref), channel_id=1, source_target_pairs={{0,2},{1,3},{2,0},{3,1},{4,6},{5,7},{6,4},{7,5},{8,10},{9,11},{10,... | collective-permute-start | bytes 1179656 | tf_op jit(solution)/shard_map/ppermute | solution.py:182
  25.3 16.3 %collective-permute-start.7 = (bf16[512,384]{1,0:T(8,128)(2,1)S(1)}, bf16[512,384]{1,0:T(8,128)(2,1)S(1)}, u32[]{:S(2)}, u32[]{:S(2)}) collective-permute-start(bf16[512,384]{1,0:T(8,128)(2,1)S(1)} %get-tuple-element.29.rows_ref), channel_id=1, source_target_pairs={{0,3},{1,0},{2,1},{3,2},{4,7},{5,4},{6,5},{7,6},{8,11},{9,8},{10,9... | collective-permute-start | bytes 1179656 | tf_op jit(solution)/shard_map/ppermute | solution.py:182
  26.2 22.8 %copy-start = (bf16[128,128]{1,0:T(8,128)(2,1)S(1)}, bf16[128,128]{1,0:T(8,128)(2,1)}, u32[]{:S(2)}) copy-start(bf16[128,128]{1,0:T(8,128)(2,1)} %constant.4.clone.table) | copy-start | bytes 98308
  26.2 15.3 %collective-permute-start.5 = (bf16[512,384]{1,0:T(8,128)(2,1)S(1)}, bf16[512,384]{1,0:T(8,128)(2,1)S(1)}, u32[]{:S(2)}, u32[]{:S(2)}) collective-permute-start(bf16[512,384]{1,0:T(8,128)(2,1)S(1)} %constant_dynamic-update-slice_fusion.refs_0_), channel_id=1, source_target_pairs={{0,4},{1,5},{2,6},{3,7},{4,8},{5,9},{6,10},{7,11},{8,12},{9,13},{1... | collective-permute-start | bytes 1179656 | tf_op jit(solution)/shard_map/ppermute | solution.py:182
  30.7 10.8 %collective-permute-start.6 = (bf16[256,384]{1,0:T(8,128)(2,1)S(1)}, bf16[256,384]{1,0:T(8,128)(2,1)S(1)}, u32[]{:S(2)}, u32[]{:S(2)}) collective-permute-start(bf16[256,384]{1,0:T(8,128)(2,1)S(1)} %pad_maximum_fusion), channel_id=1, source_target_pairs={{0,8},{4,12},{8,32},{12,36},{32,40},{36,44},{40,0},{44,4},{1,9},{5... | collective-permute-start | bytes 589832 | tf_op jit(solution)/shard_map/ppermute | solution.py:167
  41.5 7.5 %collective-permute-start.10 = (bf16[512,384]{1,0:T(8,128)(2,1)S(1)}, bf16[512,384]{1,0:T(8,128)(2,1)S(1)}, u32[]{:S(2)}, u32[]{:S(2)}) collective-permute-start(bf16[512,384]{1,0:T(8,128)(2,1)S(1)} %collective-permute-done.5.refs_1_), channel_id=1, source_target_pairs={{0,16},{16,0},{1,17},{17,1},{2,18},{18,2},{3,19},{19,3},{4,20},{20... | collective-permute-start | bytes 1179656 | tf_op jit(solution)/shard_map/ppermute | solution.py:167
  47.4 1.6 %collective-permute-start.11 = (bf16[256,384]{1,0:T(8,128)(2,1)S(1)}, bf16[256,384]{1,0:T(8,128)(2,1)S(1)}, u32[]{:S(2)}, u32[]{:S(2)}) collective-permute-start(bf16[256,384]{1,0:T(8,128)(2,1)S(1)} %collective-permute-done.6.refs_2_), channel_id=1, source_target_pairs={{0,16},{16,0},{1,17},{17,1},{2,18},{18,2},{3,19},{19,3},{4,20},{20... | collective-permute-start | bytes 589832 | tf_op jit(solution)/shard_map/ppermute | solution.py:167
  51.6 10.8 %collective-permute-start.12 = (bf16[512,256]{1,0:T(8,128)(2,1)S(1)}, bf16[512,256]{1,0:T(8,128)(2,1)S(1)}, u32[]{:S(2)}, u32[]{:S(2)}) collective-permute-start(bf16[512,256]{1,0:T(8,128)(2,1)S(1)} %tile.5), channel_id=1, source_target_pairs={{0,1},{1,2},{2,3},{3,0},{4,5},{5,6},{6,7},{7,4},{8,9},{9,10},{10,1... | collective-permute-start | bytes 786440 | tf_op jit(solution)/shard_map/ppermute | solution.py:182
  54.5 7.8 %collective-permute-start.13 = (bf16[512,256]{1,0:T(8,128)(2,1)S(1)}, bf16[512,256]{1,0:T(8,128)(2,1)S(1)}, u32[]{:S(2)}, u32[]{:S(2)}) collective-permute-start(bf16[512,256]{1,0:T(8,128)(2,1)S(1)} %tile.6), channel_id=1, source_target_pairs={{0,2},{1,3},{2,0},{3,1},{4,6},{5,7},{6,4},{7,5},{8,10},{9,11},{10,... | collective-permute-start | bytes 786440 | tf_op jit(solution)/shard_map/ppermute | solution.py:182
  58.6 6.0 %collective-permute-start.14 = (bf16[512,256]{1,0:T(8,128)(2,1)S(1)}, bf16[512,256]{1,0:T(8,128)(2,1)S(1)}, u32[]{:S(2)}, u32[]{:S(2)}) collective-permute-start(bf16[512,256]{1,0:T(8,128)(2,1)S(1)} %tile.7), channel_id=1, source_target_pairs={{0,3},{1,0},{2,1},{3,2},{4,7},{5,4},{6,5},{7,6},{8,11},{9,8},{10,9... | collective-permute-start | bytes 786440 | tf_op jit(solution)/shard_map/ppermute | solution.py:182
  65.8 15.6 %all-to-all-start = ((bf16[32,16,256]{2,1,0:T(8,128)(2,1)}), bf16[32,16,256]{2,1,0:T(8,128)(2,1)S(1)}, u32[]{:S(2)}, u32[]{:S(2)}) async-start(bf16[32,16,256]{2,1,0:T(8,128)(2,1)} %bitcast.3), calls=%async_computation | async-start | bytes 524288 | tf_op jit(solution)/shard_map/all_to_all | solution.py:190
  72.3 7.4 %collective-permute-start.15 = (bf16[128,256]{1,0:T(8,128)(2,1)S(1)}, bf16[128,256]{1,0:T(8,128)(2,1)S(1)}, u32[]{:S(2)}, u32[]{:S(2)}) collective-permute-start(bf16[128,256]{1,0:T(8,128)(2,1)S(1)} %get-tuple-element.38), channel_id=1, source_target_pairs={{0,64},{1,65},{2,66},{3,67},{4,68},{5,69},{6,70},{7,71},{8,72},{9,... | collective-permute-start | bytes 196616 | tf_op jit(solution)/shard_map/ppermute | solution.py:182
  73.8 7.0 %collective-permute-start.16 = (bf16[128,256]{1,0:T(8,128)(2,1)S(1)}, bf16[128,256]{1,0:T(8,128)(2,1)S(1)}, u32[]{:S(2)}, u32[]{:S(2)}) collective-permute-start(bf16[128,256]{1,0:T(8,128)(2,1)S(1)} %get-tuple-element.39), channel_id=1, source_target_pairs={{0,128},{1,129},{2,130},{3,131},{4,132},{5,133},{6,134},{7,135},{8... | collective-permute-start | bytes 196616 | tf_op jit(solution)/shard_map/ppermute | solution.py:182
  82.1 13.1 %all-to-all-start.1 = ((f32[8,16,256]{2,1,0:T(8,128)}), f32[8,16,256]{2,1,0:T(8,128)S(1)}, u32[]{:S(2)}, u32[]{:S(2)}) async-start(f32[8,16,256]{2,1,0:T(8,128)} %sum_spread.2), calls=%async_computation.1 | async-start | bytes 262144 | tf_op jit(solution)/shard_map/all_to_all | solution.py:190
  87.5 3.1 %collective-permute-start.17 = (bf16[128,256]{1,0:T(8,128)(2,1)S(1)}, bf16[128,256]{1,0:T(8,128)(2,1)S(1)}, u32[]{:S(2)}, u32[]{:S(2)}) collective-permute-start(bf16[128,256]{1,0:T(8,128)(2,1)S(1)} %get-tuple-element.43), channel_id=1, source_target_pairs={{0,192},{1,193},{2,194},{3,195},{4,196},{5,197},{6,198},{7,199},{8... | collective-permute-start | bytes 196616 | tf_op jit(solution)/shard_map/ppermute | solution.py:182
  96.0 15.8 %all-to-all-start.2 = ((bf16[32,16,256]{2,1,0:T(8,128)(2,1)}), bf16[32,16,256]{2,1,0:T(8,128)(2,1)S(1)}, u32[]{:S(2)}, u32[]{:S(2)}) async-start(bf16[32,16,256]{2,1,0:T(8,128)(2,1)} %sum_spread.3), calls=%async_computation.2 | async-start | bytes 524288 | tf_op jit(solution)/shard_map/all_to_all | solution.py:190

commit v4 on v3

--- a/solution.py
+++ b/solution.py
@@ -31,31 +31,26 @@
     return lax.dot_general(a, b, (((0,), (0,)), ((), ())), preferred_element_type=F32)
 
 
-def pack_kernel(embeds, weight, solve, probes, probe_solves, out, extended):
+def pack_kernel(embeds, weight, factors, copies, extended):
     rows, width = embeds.shape[0], weight.shape[1]
-    count = probes.shape[0]
     feats = jnp.dot(embeds[...], weight[...], preferred_element_type=F32).astype(BF16)
-    out[:, :width] = feats
     wide = feats.astype(F32)
     sq = jnp.sum(wide * wide, axis=1, keepdims=True)
     sq_hi = sq.astype(BF16).astype(F32)
     sq_mid = (sq - sq_hi).astype(BF16).astype(F32)
     sq_lo = sq - sq_hi - sq_mid
-    fold = math.sqrt(5.0 / 3.0 * ROOT5)
-    scale = (2.0 * count) ** (-0.5) * fold
-    factors = jnp.concatenate(
-        [solve[...] * fold, probes[...] * -scale, probe_solves[...] * -scale, jnp.zeros((1, rows), F32)],
-        axis=0,
-    ).T
-    hi = factors.astype(BF16).astype(F32)
-    lo = factors - hi
+    both = factors[...].T
+    hi = both.astype(BF16).astype(F32)
+    lo = both - hi
     lane = lax.broadcasted_iota(jnp.int32, (rows, 32), 1)
     tail = jnp.where(lane == 0, sq_hi, jnp.where(lane == 1, sq_mid, jnp.where(lane == 2, sq_lo, 0.0)))
     tail = jnp.concatenate([hi, lo, hi, tail], axis=1).astype(BF16)
-    out[:, width:] = tail
     extended[:, :width] = feats
     extended[:, width : width + 128] = tail
     extended[:, width + 128 :] = embeds[...]
+    for k in range(copies.shape[0]):
+        copies[k, :, :width] = feats
+        copies[k, :, width:] = tail
 
 
 def split_kernel(count, *refs):
@@ -193,17 +188,23 @@
 def shards(sizes, embeds, weight, solve, probes, probe_solves):
     rows, width = embeds.shape[0], weight.shape[1]
     n_side, n_z = sizes["x"], sizes["zh"] * sizes["zl"]
-    pack, extended = pl.pallas_call(
+    fold = math.sqrt(5.0 / 3.0 * ROOT5)
+    scale = (2.0 * probes.shape[1]) ** (-0.5) * fold
+    factors = jnp.concatenate(
+        [solve[None, :] * fold, probes.T * -scale, probe_solves.T * -scale, jnp.zeros((1, rows), F32)],
+        axis=0,
+    )
+    copies, extended = pl.pallas_call(
         pack_kernel,
         out_shape=[
-            jax.ShapeDtypeStruct((rows, width + 128), BF16),
+            jax.ShapeDtypeStruct((n_z, rows, width + 128), BF16),
             jax.ShapeDtypeStruct((rows, width + 128 + embeds.shape[1]), BF16),
         ],
-        in_specs=[VMEM] * 5,
+        in_specs=[VMEM] * 3,
         out_specs=[VMEM] * 2,
         compiler_params=params(16),
         name="pack",
-    )(embeds, weight, solve[None, :], probes.T, probe_solves.T)
+    )(embeds, weight, factors)
 
     blocks = [extended] + [turn(extended, sizes, 0, -d) for d in range(1, n_side)]
     line, embeds_line = pl.pallas_call(
@@ -217,18 +218,16 @@
         compiler_params=params(8),
         name="split",
     )(*blocks)
-    pair = jnp.concatenate([pack, ring(pack, DEPTH, n_z, n_z // 2)], axis=0)
-    pair, line = lax.optimization_barrier((pair, line))
-    four = jnp.concatenate([pair, ring(pair, "core", 2, 1)], axis=0)
-    near = move(four, sizes, lambda core: {"z": 1 - 2 * core})
-    far = ring(pair, DEPTH, n_z, 2)
+    stack = exchange(copies, DEPTH).reshape(n_z * rows, width + 128)
+    stack, line = lax.optimization_barrier((stack, line))
     lines = [line] + [turn(line, sizes, 1, -d) for d in range(1, n_side)]
-    near, far, lines = lax.optimization_barrier((near, far, lines))
-    columns = [four, near, far, ring(near, "core", 2, 1), ring(far, "core", 2, 1)]
+    columns = [stack, ring(stack, "core", 2, 1)]
 
     table = left_map(probes.shape[1])
     back = {}
     for d in (0, 3, 1, 2):
+        if d != 0:
+            lines[d], _ = lax.optimization_barrier((lines[d], back[0]))
         part = pl.pallas_call(
             functools.partial(tile_kernel, 256, 256),
             out_shape=jax.ShapeDtypeStruct((n_side * rows, width), F32 if d == 0 else BF16),
@@ -254,12 +253,10 @@
     arrived = [turn(block, sizes, 0, d + 1) for d, block in enumerate(other_rows)]
     n_plane = n_side * n_side * 2
     pieces = exchange(partial.reshape(n_plane, -1, width), PLANE)
-    pieces, arrived[0], arrived[1] = lax.optimization_barrier((pieces, arrived[0], arrived[1]))
+    pieces, arrived[0] = lax.optimization_barrier((pieces, arrived[0]))
     pieces = exchange(sum_spread(pieces, n_z, F32), DEPTH)
-    pieces, arrived[2] = lax.optimization_barrier((pieces, arrived[2]))
+    pieces, arrived[1] = lax.optimization_barrier((pieces, arrived[1]))
     pieces = exchange(sum_spread(pieces, n_plane, BF16), PLANE)
-    total_points = rows * n_plane * n_z
-    grad_weight = pieces.reshape(-1, width).astype(F32) * (1.0 / math.sqrt(total_points))
     grad_rows = pl.pallas_call(
         finish_rows_kernel,
         out_shape=jax.ShapeDtypeStruct((rows, width), F32),
@@ -268,6 +265,9 @@
         compiler_params=params(16),
         name="finish_rows",
     )(own_rows, *arrived)
+    pieces, grad_rows = lax.optimization_barrier((pieces, grad_rows))
+    total_points = rows * n_plane * n_z
+    grad_weight = pieces.reshape(-1, width).astype(F32) * (1.0 / math.sqrt(total_points))
     return grad_rows, grad_weight
 
 

time: 113 us -> 111 us (0.982)
  starting transfers between devices: 56.2 us -> 42.7 us
  waiting for transfers between devices: 36.8 us -> 47.7 us
  local copies, waits for them, and re-layouts: 3.95 us -> 1.93 us
  other arithmetic: 0.88 us -> 2.31 us
    ppermute x13 -> x12, waiting for transfers between devices: 8.82 us -> 28.9 us  [move(): return lax.ppermute(array, ALL, perm)]
    ppermute x5 -> x1, starting transfers between devices: 15.6 us -> 0.49 us  [ring(): lax.ppermute(array, axis, [(i, (i + shift) % size) for i in range(size)])]
    ppermute x5 -> x1, waiting for transfers between devices: 14.4 us -> 0.01 us  [ring(): lax.ppermute(array, axis, [(i, (i + shift) % size) for i in range(size)])]
    all_to_all x3 -> x4, waiting for transfers between devices: 13.5 us -> 18.9 us  [exchange(): return lax.all_to_all(array, axes, split_axis=0, concat_axis=0, tiled=True)]
    all_to_all x3 -> x4, starting transfers between devices: 18.8 us -> 22.7 us  [exchange(): return lax.all_to_all(array, axes, split_axis=0, concat_axis=0, tiled=True)]
    ppermute x13 -> x12, starting transfers between devices: 21.8 us -> 19.6 us  [move(): return lax.ppermute(array, ALL, perm)]
    unnamed x13 -> x6, local copies, waits for them, and re-layouts: 3.92 us -> 1.86 us
    mul x0 -> x2, other arithmetic: none -> 1.37 us  [the longest x1 0.72 us: shards(): probe_solves.T * -scale]
  transfers between devices with their start and end apart: 21 -> 17, of which waited for: 10 -> 14; matrix products, arithmetic and copies ran while one was open for 0% -> 0% of each run, Pallas kernels for 7% -> 10%
where the time goes in v4:
time: 111 us; the launch traced here: 110 us
  waiting for transfers between devices  47.7 us (43%)
  starting transfers between devices  42.7 us (38%)
  Pallas kernels  15 us (14%)
  other arithmetic  2.31 us (2%)
  local copies, waits for them, and re-layouts  1.93 us (2%)
    ppermute x12, waiting for transfers between devices, move(): return lax.ppermute(array, ALL, perm)  28.9 us
    all_to_all x4, starting transfers between devices, exchange(): return lax.all_to_all(array, axes, split_axis=0, concat_axis=0, tiled=True)  22.7 us
    ppermute x12, starting transfers between devices, move(): return lax.ppermute(array, ALL, perm)  19.6 us
    all_to_all x4, waiting for transfers between devices, exchange(): return lax.all_to_all(array, axes, split_axis=0, concat_axis=0, tiled=True)  18.9 us
    pallas_call x4, Pallas kernels, shards(): pl.pallas_call(functools.partial(tile_kernel, 256, 256), out_shape=jax.Sh...  10.2 us
  transfers between devices with their start and end apart: 17, of which 14 were waited for; matrix products, arithmetic and copies ran while one was open for 0% of the time, Pallas kernels for 10%

profile of v4, /device:TPU:1, one launch (start us, length us, event | category | flops | bytes accessed | tf_op | source)
XLA Modules:
  0.0 110.4 jit_solution(8463922384587145110)
XLA Ops:
  0.6 0.7 multiply_bitcast_fusion.2
  1.3 0.7 multiply_bitcast_fusion
  2.0 0.1 pad.3.clone
  2.1 0.1 maximum_maximum_fusion.factors
  2.2 0.9 copy-done.1
  3.1 0.9 copy-done.2
  4.0 1.4 %pack.1 = (bf16[8,128,384]{2,1,0:T(8,128)(2,1)}, bf16[128,896]{1,0:T(8,128)(2,1)S(1)}) custom-call(bf16[128,512]{1,0:T(8,128)(2,1)S(1)} %copy-done.2, bf16[512,256]{1,0:T(8,128)(2,1)S(1)} %copy-done.1, f32[32,128]{1,0:T(8,128)S(1)} %maximum_maximum_fusion.factors), custom_call_target="tpu_custom_call" | custom-call | tf_op jit(solution)/shard_map/pack/pallas_call | solution.py:197
  5.4 9.0 %all-to-all-start = ((bf16[8,128,384]{2,1,0:T(8,128)(2,1)}), bf16[8,128,384]{2,1,0:T(8,128)(2,1)S(1)}, u32[]{:S(2)}, u32[]{:S(2)}) async-start(bf16[8,128,384]{2,1,0:T(8,128)(2,1)} %get-tuple-element.22), calls=%async_computation | async-start | bytes 1572864 | tf_op jit(solution)/shard_map/all_to_all | solution.py:185
  14.4 2.6 %collective-permute-start = (bf16[128,896]{1,0:T(8,128)(2,1)S(1)}, bf16[128,896]{1,0:T(8,128)(2,1)S(1)}, u32[]{:S(2)}, u32[]{:S(2)}) collective-permute-start(bf16[128,896]{1,0:T(8,128)(2,1)S(1)} %get-tuple-element.23.refs_0_), channel_id=1, source_target_pairs={{0,192},{1,193},{2,194},{3,195},{4,196},{5,197},{6,198},{7,199},{8... | collective-permute-start | bytes 688136 | tf_op jit(solution)/shard_map/ppermute | solution.py:177
  17.0 0.5 collective-permute-start.1
  17.5 0.6 collective-permute-start.2
  18.1 4.3 %collective-permute-done.refs_1_ = bf16[128,896]{1,0:T(8,128)(2,1)S(1)} collective-permute-done((bf16[128,896]{1,0:T(8,128)(2,1)S(1)}, bf16[128,896]{1,0:T(8,128)(2,1)S(1)}, u32[]{:S(2)}, u32[]{:S(2)}) %collective-permute-start) | collective-permute-done | bytes 229408 | tf_op jit(solution)/shard_map/ppermute | solution.py:177
  22.4 1.3 %collective-permute-done.1.refs_2_ = bf16[128,896]{1,0:T(8,128)(2,1)S(1)} collective-permute-done((bf16[128,896]{1,0:T(8,128)(2,1)S(1)}, bf16[128,896]{1,0:T(8,128)(2,1)S(1)}, u32[]{:S(2)}, u32[]{:S(2)}) %collective-permute-start.1) | collective-permute-done | bytes 229408 | tf_op jit(solution)/shard_map/ppermute | solution.py:177
  23.7 2.4 %collective-permute-done.2.refs_3_ = bf16[128,896]{1,0:T(8,128)(2,1)S(1)} collective-permute-done((bf16[128,896]{1,0:T(8,128)(2,1)S(1)}, bf16[128,896]{1,0:T(8,128)(2,1)S(1)}, u32[]{:S(2)}, u32[]{:S(2)}) %collective-permute-start.2) | collective-permute-done | bytes 229408 | tf_op jit(solution)/shard_map/ppermute | solution.py:177
  26.1 0.1 split.1
  26.2 11.8 %all-to-all-done = bf16[8,128,384]{2,1,0:T(8,128)(2,1)S(1)} async-done(((bf16[8,128,384]{2,1,0:T(8,128)(2,1)}), bf16[8,128,384]{2,1,0:T(8,128)(2,1)S(1)}, u32[]{:S(2)}, u32[]{:S(2)}) %all-to-all-start) | async-done | bytes 786464 | tf_op jit(solution)/shard_map/all_to_all | solution.py:185
  38.0 0.5 collective-permute-start.3
  38.5 1.3 %collective-permute-start.8 = (bf16[512,384]{1,0:T(8,128)(2,1)S(1)}, bf16[512,384]{1,0:T(8,128)(2,1)S(1)}, u32[]{:S(2)}, u32[]{:S(2)}) collective-permute-start(bf16[512,384]{1,0:T(8,128)(2,1)S(1)} %get-tuple-element.25.rows_ref), channel_id=1, source_target_pairs={{0,1},{1,2},{2,3},{3,0},{4,5},{5,6},{6,7},{7,4},{8,9},{9,10},{10,1... | collective-permute-start | bytes 1179656 | tf_op jit(solution)/shard_map/ppermute | solution.py:177
  39.8 2.6 %collective-permute-start.6 = (bf16[512,384]{1,0:T(8,128)(2,1)S(1)}, bf16[512,384]{1,0:T(8,128)(2,1)S(1)}, u32[]{:S(2)}, u32[]{:S(2)}) collective-permute-start(bf16[512,384]{1,0:T(8,128)(2,1)S(1)} %get-tuple-element.25.rows_ref), channel_id=1, source_target_pairs={{0,2},{1,3},{2,0},{3,1},{4,6},{5,7},{6,4},{7,5},{8,10},{9,11},{10,... | collective-permute-start | bytes 1179656 | tf_op jit(solution)/shard_map/ppermute | solution.py:177
  42.4 1.1 collective-permute-start.4
  43.5 2.5 %tile.4.refs_0_ = f32[512,256]{1,0:T(8,128)S(1)} custom-call(bf16[128,128]{1,0:T(8,128)(2,1)S(1)} %copy-done, bf16[512,384]{1,0:T(8,128)(2,1)S(1)} %get-tuple-element.25.rows_ref, bf16[1024,384]{1,0:T(8,128)(2,1)S(1)} %bitcast.11, bf16[1024,384]{1,0:T(8,128)(2,1)S(1)} %collective-permute-done.3.refs_1_), custom_call_target="tpu_custom_call" | custom-call | tf_op jit(solution)/shard_map/tile/pallas_call | solution.py:231
  46.0 0.6 collective-permute-done.8.rows_ref
  46.7 2.5 %tile.7 = bf16[512,256]{1,0:T(8,128)(2,1)S(1)} custom-call(bf16[128,128]{1,0:T(8,128)(2,1)S(1)} %copy-done, bf16[512,384]{1,0:T(8,128)(2,1)S(1)} %collective-permute-done.8.rows_ref, bf16[1024,384]{1,0:T(8,128)(2,1)S(1)} %bitcast.12, bf16[1024,384]{1,0:T(8,128)(2,1)S(1)} %collective-permute-done.3.refs_1_), custom_call_target="tpu_custom_call" | custom-call | tf_op jit(solution)/shard_map/tile/pallas_call | solution.py:231
  49.2 1.7 %collective-permute-start.9 = (bf16[512,256]{1,0:T(8,128)(2,1)S(1)}, bf16[512,256]{1,0:T(8,128)(2,1)S(1)}, u32[]{:S(2)}, u32[]{:S(2)}) collective-permute-start(bf16[512,256]{1,0:T(8,128)(2,1)S(1)} %tile.7), channel_id=1, source_target_pairs={{0,3},{1,0},{2,1},{3,2},{4,7},{5,4},{6,5},{7,6},{8,11},{9,8},{10,9... | collective-permute-start | bytes 786440 | tf_op jit(solution)/shard_map/ppermute | solution.py:177
  51.0 1.1 %collective-permute-done.6.rows_ref = bf16[512,384]{1,0:T(8,128)(2,1)S(1)} collective-permute-done((bf16[512,384]{1,0:T(8,128)(2,1)S(1)}, bf16[512,384]{1,0:T(8,128)(2,1)S(1)}, u32[]{:S(2)}, u32[]{:S(2)}) %collective-permute-start.6) | collective-permute-done | bytes 393248 | tf_op jit(solution)/shard_map/ppermute | solution.py:177
  52.1 2.5 %tile.6 = bf16[512,256]{1,0:T(8,128)(2,1)S(1)} custom-call(bf16[128,128]{1,0:T(8,128)(2,1)S(1)} %copy-done, bf16[512,384]{1,0:T(8,128)(2,1)S(1)} %collective-permute-done.6.rows_ref, bf16[1024,384]{1,0:T(8,128)(2,1)S(1)} %bitcast.13, bf16[1024,384]{1,0:T(8,128)(2,1)S(1)} %collective-permute-done.3.refs_1_), custom_call_target="tpu_custom_call" | custom-call | tf_op jit(solution)/shard_map/tile/pallas_call | solution.py:231
  54.6 3.4 %collective-permute-start.7 = (bf16[512,256]{1,0:T(8,128)(2,1)S(1)}, bf16[512,256]{1,0:T(8,128)(2,1)S(1)}, u32[]{:S(2)}, u32[]{:S(2)}) collective-permute-start(bf16[512,256]{1,0:T(8,128)(2,1)S(1)} %tile.6), channel_id=1, source_target_pairs={{0,2},{1,3},{2,0},{3,1},{4,6},{5,7},{6,4},{7,5},{8,10},{9,11},{10,... | collective-permute-start | bytes 786440 | tf_op jit(solution)/shard_map/ppermute | solution.py:177
  58.0 2.5 %tile.5 = bf16[512,256]{1,0:T(8,128)(2,1)S(1)} custom-call(bf16[128,128]{1,0:T(8,128)(2,1)S(1)} %copy-done, bf16[512,384]{1,0:T(8,128)(2,1)S(1)} %collective-permute-done.4.rows_ref, bf16[1024,384]{1,0:T(8,128)(2,1)S(1)} %bitcast.14, bf16[1024,384]{1,0:T(8,128)(2,1)S(1)} %collective-permute-done.3.refs_1_), custom_call_target="tpu_custom_call" | custom-call | tf_op jit(solution)/shard_map/tile/pallas_call | solution.py:231
  60.6 0.9 collective-permute-start.5
  61.5 0.6 collective-permute-done.7.refs_2_
  62.1 5.0 %collective-permute-done.5.refs_1_ = bf16[512,256]{1,0:T(8,128)(2,1)S(1)} collective-permute-done((bf16[512,256]{1,0:T(8,128)(2,1)S(1)}, bf16[512,256]{1,0:T(8,128)(2,1)S(1)}, u32[]{:S(2)}, u32[]{:S(2)}) %collective-permute-start.5) | collective-permute-done | bytes 262176 | tf_op jit(solution)/shard_map/ppermute | solution.py:177
  67.1 1.2 %sum_rows.1 = (bf16[512,256]{1,0:T(8,128)(2,1)}, f32[128,256]{1,0:T(8,128)S(1)}, bf16[128,256]{1,0:T(8,128)(2,1)S(1)}, bf16[128,256]{1,0:T(8,128)(2,1)S(1)}, bf16[128,256]{1,0:T(8,128)(2,1)S(1)}) custom-call(f32[512,256]{1,0:T(8,128)S(1)} %tile.4.refs_0_, bf16[512,256]{1,0:T(8,128)(2,1)S(1)} %collective-permute-done.5.refs_1_, ...), custom_call_target="tpu_custom_call" | custom-call | tf_op jit(solution)/shard_map/sum_rows/pallas_call | solution.py:241
  68.3 4.8 %all-to-all-start.1 = ((bf16[32,16,256]{2,1,0:T(8,128)(2,1)}), bf16[32,16,256]{2,1,0:T(8,128)(2,1)S(1)}, u32[]{:S(2)}, u32[]{:S(2)}) async-start(bf16[32,16,256]{2,1,0:T(8,128)(2,1)} %bitcast.4), calls=%async_computation.1 | async-start | bytes 524288 | tf_op jit(solution)/shard_map/all_to_all | solution.py:185
  73.1 1.5 %collective-permute-start.10 = (bf16[128,256]{1,0:T(8,128)(2,1)S(1)}, bf16[128,256]{1,0:T(8,128)(2,1)S(1)}, u32[]{:S(2)}, u32[]{:S(2)}) collective-permute-start(bf16[128,256]{1,0:T(8,128)(2,1)S(1)} %get-tuple-element.32), channel_id=1, source_target_pairs={{0,64},{1,65},{2,66},{3,67},{4,68},{5,69},{6,70},{7,71},{8,72},{9,... | collective-permute-start | bytes 196616 | tf_op jit(solution)/shard_map/ppermute | solution.py:177
  74.6 6.0 %collective-permute-done.10.b = bf16[128,256]{1,0:T(8,128)(2,1)S(1)} collective-permute-done((bf16[128,256]{1,0:T(8,128)(2,1)S(1)}, bf16[128,256]{1,0:T(8,128)(2,1)S(1)}, u32[]{:S(2)}, u32[]{:S(2)}) %collective-permute-start.10) | collective-permute-done | bytes 65568 | tf_op jit(solution)/shard_map/ppermute | solution.py:177
  80.6 1.7 %all-to-all-done.1.parts = bf16[32,16,256]{2,1,0:T(8,128)(2,1)S(1)} async-done(((bf16[32,16,256]{2,1,0:T(8,128)(2,1)}), bf16[32,16,256]{2,1,0:T(8,128)(2,1)S(1)}, u32[]{:S(2)}, u32[]{:S(2)}) %all-to-all-start.1) | async-done | bytes 262176 | tf_op jit(solution)/shard_map/all_to_all | solution.py:185
  82.2 0.7 sum_spread.2
  83.0 3.4 %all-to-all-start.2 = ((f32[8,16,256]{2,1,0:T(8,128)}), f32[8,16,256]{2,1,0:T(8,128)S(1)}, u32[]{:S(2)}, u32[]{:S(2)}) async-start(f32[8,16,256]{2,1,0:T(8,128)} %sum_spread.2), calls=%async_computation.2 | async-start | bytes 262144 | tf_op jit(solution)/shard_map/all_to_all | solution.py:185
  86.3 0.7 collective-permute-start.11
  87.1 4.0 %collective-permute-done.11.c = bf16[128,256]{1,0:T(8,128)(2,1)S(1)} collective-permute-done((bf16[128,256]{1,0:T(8,128)(2,1)S(1)}, bf16[128,256]{1,0:T(8,128)(2,1)S(1)}, u32[]{:S(2)}, u32[]{:S(2)}) %collective-permute-start.11) | collective-permute-done | bytes 65568 | tf_op jit(solution)/shard_map/ppermute | solution.py:177
  91.0 3.3 %all-to-all-done.2.parts = f32[8,16,256]{2,1,0:T(8,128)S(1)} async-done(((f32[8,16,256]{2,1,0:T(8,128)}), f32[8,16,256]{2,1,0:T(8,128)S(1)}, u32[]{:S(2)}, u32[]{:S(2)}) %all-to-all-start.2) | async-done | bytes 131104 | tf_op jit(solution)/shard_map/all_to_all | solution.py:185
  94.4 0.7 sum_spread.3
  95.1 5.4 %all-to-all-start.3 = ((bf16[32,16,256]{2,1,0:T(8,128)(2,1)}), bf16[32,16,256]{2,1,0:T(8,128)(2,1)S(1)}, u32[]{:S(2)}, u32[]{:S(2)}) async-start(bf16[32,16,256]{2,1,0:T(8,128)(2,1)} %sum_spread.3), calls=%async_computation.3 | async-start | bytes 524288 | tf_op jit(solution)/shard_map/all_to_all | solution.py:185
  100.5 2.7 %collective-permute-start.12 = (bf16[128,256]{1,0:T(8,128)(2,1)S(1)}, bf16[128,256]{1,0:T(8,128)(2,1)S(1)}, u32[]{:S(2)}, u32[]{:S(2)}) collective-permute-start(bf16[128,256]{1,0:T(8,128)(2,1)S(1)} %get-tuple-element.39), channel_id=1, source_target_pairs={{0,192},{1,193},{2,194},{3,195},{4,196},{5,197},{6,198},{7,199},{8... | collective-permute-start | bytes 196616 | tf_op jit(solution)/shard_map/ppermute | solution.py:177
  103.2 3.5 %collective-permute-done.12.d = bf16[128,256]{1,0:T(8,128)(2,1)S(1)} collective-permute-done((bf16[128,256]{1,0:T(8,128)(2,1)S(1)}, bf16[128,256]{1,0:T(8,128)(2,1)S(1)}, u32[]{:S(2)}, u32[]{:S(2)}) %collective-permute-start.12) | collective-permute-done | bytes 65568 | tf_op jit(solution)/shard_map/ppermute | solution.py:177
  106.8 0.7 finish_rows.1
  107.4 2.1 %all-to-all-done.3 = bf16[32,16,256]{2,1,0:T(8,128)(2,1)S(1)} async-done(((bf16[32,16,256]{2,1,0:T(8,128)(2,1)}), bf16[32,16,256]{2,1,0:T(8,128)(2,1)S(1)}, u32[]{:S(2)}, u32[]{:S(2)}) %all-to-all-start.3) | async-done | bytes 262176 | tf_op jit(solution)/shard_map/all_to_all | solution.py:185
  109.5 0.9 convert_multiply_fusion
  (7 shorter events, 0.0 us)
Async XLA Ops:
  2.2 0.9 copy-start.1
  3.1 0.9 copy-start.2
  5.4 32.6 %all-to-all-start = ((bf16[8,128,384]{2,1,0:T(8,128)(2,1)}), bf16[8,128,384]{2,1,0:T(8,128)(2,1)S(1)}, u32[]{:S(2)}, u32[]{:S(2)}) async-start(bf16[8,128,384]{2,1,0:T(8,128)(2,1)} %get-tuple-element.22), calls=%async_computation | async-start | bytes 1572864 | tf_op jit(solution)/shard_map/all_to_all | solution.py:185
  14.4 29.1 %copy-start = (bf16[128,128]{1,0:T(8,128)(2,1)S(1)}, bf16[128,128]{1,0:T(8,128)(2,1)}, u32[]{:S(2)}) copy-start(bf16[128,128]{1,0:T(8,128)(2,1)} %constant.10.clone.table) | copy-start | bytes 98308
  14.4 8.0 %collective-permute-start = (bf16[128,896]{1,0:T(8,128)(2,1)S(1)}, bf16[128,896]{1,0:T(8,128)(2,1)S(1)}, u32[]{:S(2)}, u32[]{:S(2)}) collective-permute-start(bf16[128,896]{1,0:T(8,128)(2,1)S(1)} %get-tuple-element.23.refs_0_), channel_id=1, source_target_pairs={{0,192},{1,193},{2,194},{3,195},{4,196},{5,197},{6,198},{7,199},{8... | collective-permute-start | bytes 688136 | tf_op jit(solution)/shard_map/ppermute | solution.py:177
  17.0 6.7 %collective-permute-start.1 = (bf16[128,896]{1,0:T(8,128)(2,1)S(1)}, bf16[128,896]{1,0:T(8,128)(2,1)S(1)}, u32[]{:S(2)}, u32[]{:S(2)}) collective-permute-start(bf16[128,896]{1,0:T(8,128)(2,1)S(1)} %get-tuple-element.23.refs_0_), channel_id=1, source_target_pairs={{0,128},{1,129},{2,130},{3,131},{4,132},{5,133},{6,134},{7,135},{8... | collective-permute-start | bytes 688136 | tf_op jit(solution)/shard_map/ppermute | solution.py:177
  17.5 8.6 %collective-permute-start.2 = (bf16[128,896]{1,0:T(8,128)(2,1)S(1)}, bf16[128,896]{1,0:T(8,128)(2,1)S(1)}, u32[]{:S(2)}, u32[]{:S(2)}) collective-permute-start(bf16[128,896]{1,0:T(8,128)(2,1)S(1)} %get-tuple-element.23.refs_0_), channel_id=1, source_target_pairs={{0,64},{1,65},{2,66},{3,67},{4,68},{5,69},{6,70},{7,71},{8,72},{9,... | collective-permute-start | bytes 688136 | tf_op jit(solution)/shard_map/ppermute | solution.py:177
  38.0 5.5 %collective-permute-start.3 = (bf16[1024,384]{1,0:T(8,128)(2,1)S(1)}, bf16[1024,384]{1,0:T(8,128)(2,1)S(1)}, u32[]{:S(2)}, u32[]{:S(2)}) collective-permute-start(bf16[1024,384]{1,0:T(8,128)(2,1)S(1)} %bitcast.10), channel_id=1, source_target_pairs={{0,16},{16,0},{1,17},{17,1},{2,18},{18,2},{3,19},{19,3},{4,20},{20... | collective-permute-start | bytes 2359304 | tf_op jit(solution)/shard_map/ppermute | solution.py:162
  38.5 8.2 %collective-permute-start.8 = (bf16[512,384]{1,0:T(8,128)(2,1)S(1)}, bf16[512,384]{1,0:T(8,128)(2,1)S(1)}, u32[]{:S(2)}, u32[]{:S(2)}) collective-permute-start(bf16[512,384]{1,0:T(8,128)(2,1)S(1)} %get-tuple-element.25.rows_ref), channel_id=1, source_target_pairs={{0,1},{1,2},{2,3},{3,0},{4,5},{5,6},{6,7},{7,4},{8,9},{9,10},{10,1... | collective-permute-start | bytes 1179656 | tf_op jit(solution)/shard_map/ppermute | solution.py:177
  39.8 12.3 %collective-permute-start.6 = (bf16[512,384]{1,0:T(8,128)(2,1)S(1)}, bf16[512,384]{1,0:T(8,128)(2,1)S(1)}, u32[]{:S(2)}, u32[]{:S(2)}) collective-permute-start(bf16[512,384]{1,0:T(8,128)(2,1)S(1)} %get-tuple-element.25.rows_ref), channel_id=1, source_target_pairs={{0,2},{1,3},{2,0},{3,1},{4,6},{5,7},{6,4},{7,5},{8,10},{9,11},{10,... | collective-permute-start | bytes 1179656 | tf_op jit(solution)/shard_map/ppermute | solution.py:177
  42.4 15.6 %collective-permute-start.4 = (bf16[512,384]{1,0:T(8,128)(2,1)S(1)}, bf16[512,384]{1,0:T(8,128)(2,1)S(1)}, u32[]{:S(2)}, u32[]{:S(2)}) collective-permute-start(bf16[512,384]{1,0:T(8,128)(2,1)S(1)} %get-tuple-element.25.rows_ref), channel_id=1, source_target_pairs={{0,3},{1,0},{2,1},{3,2},{4,7},{5,4},{6,5},{7,6},{8,11},{9,8},{10,9... | collective-permute-start | bytes 1179656 | tf_op jit(solution)/shard_map/ppermute | solution.py:177
  49.2 12.3 %collective-permute-start.9 = (bf16[512,256]{1,0:T(8,128)(2,1)S(1)}, bf16[512,256]{1,0:T(8,128)(2,1)S(1)}, u32[]{:S(2)}, u32[]{:S(2)}) collective-permute-start(bf16[512,256]{1,0:T(8,128)(2,1)S(1)} %tile.7), channel_id=1, source_target_pairs={{0,3},{1,0},{2,1},{3,2},{4,7},{5,4},{6,5},{7,6},{8,11},{9,8},{10,9... | collective-permute-start | bytes 786440 | tf_op jit(solution)/shard_map/ppermute | solution.py:177
  54.6 7.4 %collective-permute-start.7 = (bf16[512,256]{1,0:T(8,128)(2,1)S(1)}, bf16[512,256]{1,0:T(8,128)(2,1)S(1)}, u32[]{:S(2)}, u32[]{:S(2)}) collective-permute-start(bf16[512,256]{1,0:T(8,128)(2,1)S(1)} %tile.6), channel_id=1, source_target_pairs={{0,2},{1,3},{2,0},{3,1},{4,6},{5,7},{6,4},{7,5},{8,10},{9,11},{10,... | collective-permute-start | bytes 786440 | tf_op jit(solution)/shard_map/ppermute | solution.py:177
  60.6 6.5 %collective-permute-start.5 = (bf16[512,256]{1,0:T(8,128)(2,1)S(1)}, bf16[512,256]{1,0:T(8,128)(2,1)S(1)}, u32[]{:S(2)}, u32[]{:S(2)}) collective-permute-start(bf16[512,256]{1,0:T(8,128)(2,1)S(1)} %tile.5), channel_id=1, source_target_pairs={{0,1},{1,2},{2,3},{3,0},{4,5},{5,6},{6,7},{7,4},{8,9},{9,10},{10,1... | collective-permute-start | bytes 786440 | tf_op jit(solution)/shard_map/ppermute | solution.py:177
  68.3 14.0 %all-to-all-start.1 = ((bf16[32,16,256]{2,1,0:T(8,128)(2,1)}), bf16[32,16,256]{2,1,0:T(8,128)(2,1)S(1)}, u32[]{:S(2)}, u32[]{:S(2)}) async-start(bf16[32,16,256]{2,1,0:T(8,128)(2,1)} %bitcast.4), calls=%async_computation.1 | async-start | bytes 524288 | tf_op jit(solution)/shard_map/all_to_all | solution.py:185
  73.1 7.4 %collective-permute-start.10 = (bf16[128,256]{1,0:T(8,128)(2,1)S(1)}, bf16[128,256]{1,0:T(8,128)(2,1)S(1)}, u32[]{:S(2)}, u32[]{:S(2)}) collective-permute-start(bf16[128,256]{1,0:T(8,128)(2,1)S(1)} %get-tuple-element.32), channel_id=1, source_target_pairs={{0,64},{1,65},{2,66},{3,67},{4,68},{5,69},{6,70},{7,71},{8,72},{9,... | collective-permute-start | bytes 196616 | tf_op jit(solution)/shard_map/ppermute | solution.py:177
  83.0 11.4 %all-to-all-start.2 = ((f32[8,16,256]{2,1,0:T(8,128)}), f32[8,16,256]{2,1,0:T(8,128)S(1)}, u32[]{:S(2)}, u32[]{:S(2)}) async-start(f32[8,16,256]{2,1,0:T(8,128)} %sum_spread.2), calls=%async_computation.2 | async-start | bytes 262144 | tf_op jit(solution)/shard_map/all_to_all | solution.py:185
  86.3 4.7 %collective-permute-start.11 = (bf16[128,256]{1,0:T(8,128)(2,1)S(1)}, bf16[128,256]{1,0:T(8,128)(2,1)S(1)}, u32[]{:S(2)}, u32[]{:S(2)}) collective-permute-start(bf16[128,256]{1,0:T(8,128)(2,1)S(1)} %get-tuple-element.34), channel_id=1, source_target_pairs={{0,128},{1,129},{2,130},{3,131},{4,132},{5,133},{6,134},{7,135},{8... | collective-permute-start | bytes 196616 | tf_op jit(solution)/shard_map/ppermute | solution.py:177
  95.1 14.4 %all-to-all-start.3 = ((bf16[32,16,256]{2,1,0:T(8,128)(2,1)}), bf16[32,16,256]{2,1,0:T(8,128)(2,1)S(1)}, u32[]{:S(2)}, u32[]{:S(2)}) async-start(bf16[32,16,256]{2,1,0:T(8,128)(2,1)} %sum_spread.3), calls=%async_computation.3 | async-start | bytes 524288 | tf_op jit(solution)/shard_map/all_to_all | solution.py:185
  100.5 6.2 %collective-permute-start.12 = (bf16[128,256]{1,0:T(8,128)(2,1)S(1)}, bf16[128,256]{1,0:T(8,128)(2,1)S(1)}, u32[]{:S(2)}, u32[]{:S(2)}) collective-permute-start(bf16[128,256]{1,0:T(8,128)(2,1)S(1)} %get-tuple-element.39), channel_id=1, source_target_pairs={{0,192},{1,193},{2,194},{3,195},{4,196},{5,197},{6,198},{7,199},{8... | collective-permute-start | bytes 196616 | tf_op jit(solution)/shard_map/ppermute | solution.py:177

commit v5 on v4

--- a/solution.py
+++ b/solution.py
@@ -31,15 +31,37 @@
     return lax.dot_general(a, b, (((0,), (0,)), ((), ())), preferred_element_type=F32)
 
 
-def pack_kernel(embeds, weight, factors, copies, extended):
+def pack_kernel(embeds, weight, solve, probes, probe_solves, packed, extended, weight_in, solve_in, probes_in, probe_solves_in, sems):
     rows, width = embeds.shape[0], weight.shape[1]
-    feats = jnp.dot(embeds[...], weight[...], preferred_element_type=F32).astype(BF16)
+    embeds_in = extended.at[:, width + 128 :]
+    loads = [
+        pltpu.make_async_copy(source, target, sems.at[k])
+        for k, (source, target) in enumerate(
+            (
+                (weight, weight_in),
+                (embeds, embeds_in),
+                (probes, probes_in),
+                (probe_solves, probe_solves_in),
+                (solve, solve_in),
+            )
+        )
+    ]
+    for load in loads:
+        load.start()
+    for load in loads:
+        load.wait()
+    feats = jnp.dot(embeds_in[...], weight_in[...], preferred_element_type=F32).astype(BF16)
     wide = feats.astype(F32)
     sq = jnp.sum(wide * wide, axis=1, keepdims=True)
     sq_hi = sq.astype(BF16).astype(F32)
     sq_mid = (sq - sq_hi).astype(BF16).astype(F32)
     sq_lo = sq - sq_hi - sq_mid
-    both = factors[...].T
+    fold = math.sqrt(5.0 / 3.0 * ROOT5)
+    scale = (2.0 * probes.shape[0]) ** (-0.5) * fold
+    both = jnp.concatenate(
+        [solve_in[...] * fold, probes_in[...] * -scale, probe_solves_in[...] * -scale, jnp.zeros((1, rows), F32)],
+        axis=0,
+    ).T
     hi = both.astype(BF16).astype(F32)
     lo = both - hi
     lane = lax.broadcasted_iota(jnp.int32, (rows, 32), 1)
@@ -47,10 +69,8 @@
     tail = jnp.concatenate([hi, lo, hi, tail], axis=1).astype(BF16)
     extended[:, :width] = feats
     extended[:, width : width + 128] = tail
-    extended[:, width + 128 :] = embeds[...]
-    for k in range(copies.shape[0]):
-        copies[k, :, :width] = feats
-        copies[k, :, width:] = tail
+    packed[:, :width] = feats
+    packed[:, width:] = tail
 
 
 def split_kernel(count, *refs):
@@ -188,23 +208,24 @@
 def shards(sizes, embeds, weight, solve, probes, probe_solves):
     rows, width = embeds.shape[0], weight.shape[1]
     n_side, n_z = sizes["x"], sizes["zh"] * sizes["zl"]
-    fold = math.sqrt(5.0 / 3.0 * ROOT5)
-    scale = (2.0 * probes.shape[1]) ** (-0.5) * fold
-    factors = jnp.concatenate(
-        [solve[None, :] * fold, probes.T * -scale, probe_solves.T * -scale, jnp.zeros((1, rows), F32)],
-        axis=0,
-    )
-    copies, extended = pl.pallas_call(
+    pack, extended = pl.pallas_call(
         pack_kernel,
         out_shape=[
-            jax.ShapeDtypeStruct((n_z, rows, width + 128), BF16),
+            jax.ShapeDtypeStruct((rows, width + 128), BF16),
             jax.ShapeDtypeStruct((rows, width + 128 + embeds.shape[1]), BF16),
         ],
-        in_specs=[VMEM] * 3,
+        in_specs=[pl.BlockSpec(memory_space=pl.ANY)] * 5,
         out_specs=[VMEM] * 2,
-        compiler_params=params(16),
+        scratch_shapes=[
+            pltpu.VMEM(weight.shape, BF16),
+            pltpu.VMEM((1, rows), F32),
+            pltpu.VMEM(probes.shape[::-1], F32),
+            pltpu.VMEM(probes.shape[::-1], F32),
+            pltpu.SemaphoreType.DMA((5,)),
+        ],
+        compiler_params=params(48),
         name="pack",
-    )(embeds, weight, factors)
+    )(embeds, weight, solve[None, :], probes.T, probe_solves.T)
 
     blocks = [extended] + [turn(extended, sizes, 0, -d) for d in range(1, n_side)]
     line, embeds_line = pl.pallas_call(
@@ -218,10 +239,13 @@
         compiler_params=params(8),
         name="split",
     )(*blocks)
-    stack = exchange(copies, DEPTH).reshape(n_z * rows, width + 128)
-    stack, line = lax.optimization_barrier((stack, line))
+    pair = jnp.concatenate([pack, ring(pack, DEPTH, n_z, n_z // 2)], axis=0)
+    pair, line = lax.optimization_barrier((pair, line))
+    swap = ring(pair, "core", 2, 1)
+    far = move(pair, sizes, lambda core: {"z": 2 - 4 * core})
+    near = [move(part, sizes, lambda core: {"z": 1 - 2 * core}) for part in (pair, swap)]
     lines = [line] + [turn(line, sizes, 1, -d) for d in range(1, n_side)]
-    columns = [stack, ring(stack, "core", 2, 1)]
+    columns = [pair, swap, far, *near] + [ring(part, "core", 2, 1) for part in (far, *near)]
 
     table = left_map(probes.shape[1])
     back = {}

time: 111 us -> 109 us (0.982)
  waiting for transfers between devices: 47.7 us -> 32.8 us
  starting transfers between devices: 42.7 us -> 55.9 us
  local copies, waits for them, and re-layouts: 1.93 us -> 3.9 us
  other arithmetic: 2.31 us -> 0.88 us
    all_to_all x4 -> x3, waiting for transfers between devices: 18.9 us -> 6.89 us  [exchange(): return lax.all_to_all(array, axes, split_axis=0, concat_axis=0, tiled=True)]
    ppermute x1 -> x5, starting transfers between devices: 0.49 us -> 10.2 us  [ring(): lax.ppermute(array, axis, [(i, (i + shift) % size) for i in range(size)])]
    ppermute x12 -> x15, starting transfers between devices: 19.6 us -> 28.1 us  [move(): return lax.ppermute(array, ALL, perm)]
    ppermute x12 -> x15, waiting for transfers between devices: 28.9 us -> 22.6 us  [move(): return lax.ppermute(array, ALL, perm)]
    all_to_all x4 -> x3, starting transfers between devices: 22.7 us -> 17.7 us  [exchange(): return lax.all_to_all(array, axes, split_axis=0, concat_axis=0, tiled=True)]
    ppermute x1 -> x5, waiting for transfers between devices: 0.01 us -> 3.32 us  [ring(): lax.ppermute(array, axis, [(i, (i + shift) % size) for i in range(size)])]
    unnamed x6 -> x12, local copies, waits for them, and re-layouts: 1.86 us -> 3.9 us
    mul x2 -> x0, other arithmetic: 1.37 us -> none  [the longest x1 0.72 us: shards(): probe_solves.T * -scale]
  transfers between devices with their start and end apart: 17 -> 23, of which waited for: 14 -> 12; matrix products, arithmetic and copies ran while one was open for 0% -> 0% of each run, Pallas kernels for 10% -> 10%
where the time goes in v5:
time: 109 us
  starting transfers between devices  55.9 us (51%)
  waiting for transfers between devices  32.8 us (30%)
  Pallas kernels  14.2 us (13%)
  local copies, waits for them, and re-layouts  3.9 us (4%)
    ppermute x15, starting transfers between devices, move(): return lax.ppermute(array, ALL, perm)  28.1 us
    ppermute x15, waiting for transfers between devices, move(): return lax.ppermute(array, ALL, perm)  22.6 us
    all_to_all x3, starting transfers between devices, exchange(): return lax.all_to_all(array, axes, split_axis=0, concat_axis=0, tiled=True)  17.7 us
    pallas_call x4, Pallas kernels, shards(): pl.pallas_call(functools.partial(tile_kernel, 256, 256), out_shape=jax.Sh...  10.2 us
    ppermute x5, starting transfers between devices, ring(): lax.ppermute(array, axis, [(i, (i + shift) % size) for i in range(size)])  10.2 us
    all_to_all x3, waiting for transfers between devices, exchange(): return lax.all_to_all(array, axes, split_axis=0, concat_axis=0, tiled=True)  6.89 us
    unnamed x12, local copies, waits for them, and re-layouts  3.9 us
    ppermute x5, waiting for transfers between devices, ring(): lax.ppermute(array, axis, [(i, (i + shift) % size) for i in range(size)])  3.32 us
  transfers between devices with their start and end apart: 23, of which 12 were waited for; matrix products, arithmetic and copies ran while one was open for 0% of the time, Pallas kernels for 10%

profile of v5, /device:TPU:1, one launch (start us, length us, event | category | flops | bytes accessed | tf_op | source)
XLA Modules:
  0.0 108.5 jit_solution(14973046451355616651)
XLA Ops:
  0.6 0.6 copy-done.5
  1.3 0.9 copy-done.1
  2.2 0.9 copy-done.2
  3.1 0.7 copy-done.3
  3.8 0.7 copy-done.4
  4.5 0.6 pack.1
  5.1 3.4 %collective-permute-start.1 = (bf16[128,896]{1,0:T(8,128)(2,1)S(1)}, bf16[128,896]{1,0:T(8,128)(2,1)S(1)}, u32[]{:S(2)}, u32[]{:S(2)}) collective-permute-start(bf16[128,896]{1,0:T(8,128)(2,1)S(1)} %get-tuple-element.23.refs_0_), channel_id=1, source_target_pairs={{0,192},{1,193},{2,194},{3,195},{4,196},{5,197},{6,198},{7,199},{8... | collective-permute-start | bytes 688136 | tf_op jit(solution)/shard_map/ppermute | solution.py:197
  8.5 0.5 collective-permute-start.2
  9.0 0.6 collective-permute-start.3
  9.6 6.9 %collective-permute-start = (bf16[128,384]{1,0:T(8,128)(2,1)S(1)}, bf16[128,384]{1,0:T(8,128)(2,1)S(1)}, u32[]{:S(2)}, u32[]{:S(2)}) collective-permute-start(bf16[128,384]{1,0:T(8,128)(2,1)S(1)} %get-tuple-element.22), channel_id=1, source_target_pairs={{0,32},{4,36},{8,40},{12,44},{32,0},{36,4},{40,8},{44,12},{1,33},{... | collective-permute-start | bytes 294920 | tf_op jit(solution)/shard_map/ppermute | solution.py:182
  16.6 2.1 %collective-permute-done = bf16[128,384]{1,0:T(8,128)(2,1)S(1)} collective-permute-done((bf16[128,384]{1,0:T(8,128)(2,1)S(1)}, bf16[128,384]{1,0:T(8,128)(2,1)S(1)}, u32[]{:S(2)}, u32[]{:S(2)}) %collective-permute-start) | collective-permute-done | bytes 98336 | tf_op jit(solution)/shard_map/ppermute | solution.py:182
  18.8 2.7 %collective-permute-start.4 = (bf16[256,384]{1,0:T(8,128)(2,1)S(1)}, bf16[256,384]{1,0:T(8,128)(2,1)S(1)}, u32[]{:S(2)}, u32[]{:S(2)}) collective-permute-start(bf16[256,384]{1,0:T(8,128)(2,1)S(1)} %pad_maximum_fusion.refs_0_), channel_id=1, source_target_pairs={{0,16},{16,0},{1,17},{17,1},{2,18},{18,2},{3,19},{19,3},{4,20},{20... | collective-permute-start | bytes 589832 | tf_op jit(solution)/shard_map/ppermute | solution.py:182
  21.5 5.4 %collective-permute-start.5 = (bf16[256,384]{1,0:T(8,128)(2,1)S(1)}, bf16[256,384]{1,0:T(8,128)(2,1)S(1)}, u32[]{:S(2)}, u32[]{:S(2)}) collective-permute-start(bf16[256,384]{1,0:T(8,128)(2,1)S(1)} %pad_maximum_fusion.refs_0_), channel_id=1, source_target_pairs={{0,8},{1,9},{2,10},{3,11},{4,12},{5,13},{6,14},{7,15},{8,32},{9,33... | collective-permute-start | bytes 589832 | tf_op jit(solution)/shard_map/ppermute | solution.py:197
  26.9 0.1 collective-permute-start.6
  27.0 1.2 %collective-permute-start.7 = (bf16[256,384]{1,0:T(8,128)(2,1)S(1)}, bf16[256,384]{1,0:T(8,128)(2,1)S(1)}, u32[]{:S(2)}, u32[]{:S(2)}) collective-permute-start(bf16[256,384]{1,0:T(8,128)(2,1)S(1)} %collective-permute-done.4.refs_1_), channel_id=1, source_target_pairs={{0,4},{1,5},{2,6},{3,7},{4,8},{5,9},{6,10},{7,11},{8,12},{9,13},{1... | collective-permute-start | bytes 589832 | tf_op jit(solution)/shard_map/ppermute | solution.py:197
  28.2 3.4 %collective-permute-done.5.refs_2_ = bf16[256,384]{1,0:T(8,128)(2,1)S(1)} collective-permute-done((bf16[256,384]{1,0:T(8,128)(2,1)S(1)}, bf16[256,384]{1,0:T(8,128)(2,1)S(1)}, u32[]{:S(2)}, u32[]{:S(2)}) %collective-permute-start.5) | collective-permute-done | bytes 196640 | tf_op jit(solution)/shard_map/ppermute | solution.py:197
  31.6 1.6 %collective-permute-start.15 = (bf16[512,384]{1,0:T(8,128)(2,1)S(1)}, bf16[512,384]{1,0:T(8,128)(2,1)S(1)}, u32[]{:S(2)}, u32[]{:S(2)}) collective-permute-start(bf16[512,384]{1,0:T(8,128)(2,1)S(1)} %get-tuple-element.25.rows_ref), channel_id=1, source_target_pairs={{0,1},{1,2},{2,3},{3,0},{4,5},{5,6},{6,7},{7,4},{8,9},{9,10},{10,1... | collective-permute-start | bytes 1179656 | tf_op jit(solution)/shard_map/ppermute | solution.py:197
  33.2 2.7 %collective-permute-start.13 = (bf16[512,384]{1,0:T(8,128)(2,1)S(1)}, bf16[512,384]{1,0:T(8,128)(2,1)S(1)}, u32[]{:S(2)}, u32[]{:S(2)}) collective-permute-start(bf16[512,384]{1,0:T(8,128)(2,1)S(1)} %get-tuple-element.25.rows_ref), channel_id=1, source_target_pairs={{0,2},{1,3},{2,0},{3,1},{4,6},{5,7},{6,4},{7,5},{8,10},{9,11},{10,... | collective-permute-start | bytes 1179656 | tf_op jit(solution)/shard_map/ppermute | solution.py:197
  35.9 1.8 %collective-permute-start.11 = (bf16[512,384]{1,0:T(8,128)(2,1)S(1)}, bf16[512,384]{1,0:T(8,128)(2,1)S(1)}, u32[]{:S(2)}, u32[]{:S(2)}) collective-permute-start(bf16[512,384]{1,0:T(8,128)(2,1)S(1)} %get-tuple-element.25.rows_ref), channel_id=1, source_target_pairs={{0,3},{1,0},{2,1},{3,2},{4,7},{5,4},{6,5},{7,6},{8,11},{9,8},{10,9... | collective-permute-start | bytes 1179656 | tf_op jit(solution)/shard_map/ppermute | solution.py:197
  37.7 0.5 collective-permute-start.10
  38.2 0.9 collective-permute-done.9.refs_6_
  39.1 0.3 collective-permute-done.10.refs_7_
  39.4 2.6 %tile.4.refs_0_ = f32[512,256]{1,0:T(8,128)S(1)} custom-call(bf16[128,128]{1,0:T(8,128)(2,1)S(1)} %copy-done, bf16[512,384]{1,0:T(8,128)(2,1)S(1)} %get-tuple-element.25.rows_ref, bf16[256,384]{1,0:T(8,128)(2,1)S(1)} %pad_maximum_fusion.refs_0_, bf16[256,384]{1,0:T(8,128)(2,1)S(1)} %collective-permute-done.4.refs_1_, ...), custom_call_target="tpu_custom_call" | custom-call | tf_op jit(solution)/shard_map/tile/pallas_call | solution.py:255
  42.0 2.6 %tile.7 = bf16[512,256]{1,0:T(8,128)(2,1)S(1)} custom-call(bf16[128,128]{1,0:T(8,128)(2,1)S(1)} %copy-done, bf16[512,384]{1,0:T(8,128)(2,1)S(1)} %collective-permute-done.15.rows_ref, bf16[256,384]{1,0:T(8,128)(2,1)S(1)} %pad_maximum_fusion.refs_0_, bf16[256,384]{1,0:T(8,128)(2,1)S(1)} %collective-permute-done.4.refs_1_, ...), custom_call_target="tpu_custom_call" | custom-call | tf_op jit(solution)/shard_map/tile/pallas_call | solution.py:255
  44.6 2.0 %collective-permute-start.16 = (bf16[512,256]{1,0:T(8,128)(2,1)S(1)}, bf16[512,256]{1,0:T(8,128)(2,1)S(1)}, u32[]{:S(2)}, u32[]{:S(2)}) collective-permute-start(bf16[512,256]{1,0:T(8,128)(2,1)S(1)} %tile.7), channel_id=1, source_target_pairs={{0,3},{1,0},{2,1},{3,2},{4,7},{5,4},{6,5},{7,6},{8,11},{9,8},{10,9... | collective-permute-start | bytes 786440 | tf_op jit(solution)/shard_map/ppermute | solution.py:197
  46.5 2.6 %tile.6 = bf16[512,256]{1,0:T(8,128)(2,1)S(1)} custom-call(bf16[128,128]{1,0:T(8,128)(2,1)S(1)} %copy-done, bf16[512,384]{1,0:T(8,128)(2,1)S(1)} %collective-permute-done.13.rows_ref, bf16[256,384]{1,0:T(8,128)(2,1)S(1)} %pad_maximum_fusion.refs_0_, bf16[256,384]{1,0:T(8,128)(2,1)S(1)} %collective-permute-done.4.refs_1_, ...), custom_call_target="tpu_custom_call" | custom-call | tf_op jit(solution)/shard_map/tile/pallas_call | solution.py:255
  49.1 3.0 %collective-permute-start.14 = (bf16[512,256]{1,0:T(8,128)(2,1)S(1)}, bf16[512,256]{1,0:T(8,128)(2,1)S(1)}, u32[]{:S(2)}, u32[]{:S(2)}) collective-permute-start(bf16[512,256]{1,0:T(8,128)(2,1)S(1)} %tile.6), channel_id=1, source_target_pairs={{0,2},{1,3},{2,0},{3,1},{4,6},{5,7},{6,4},{7,5},{8,10},{9,11},{10,... | collective-permute-start | bytes 786440 | tf_op jit(solution)/shard_map/ppermute | solution.py:197
  52.1 2.6 %tile.5 = bf16[512,256]{1,0:T(8,128)(2,1)S(1)} custom-call(bf16[128,128]{1,0:T(8,128)(2,1)S(1)} %copy-done, bf16[512,384]{1,0:T(8,128)(2,1)S(1)} %collective-permute-done.11.rows_ref, bf16[256,384]{1,0:T(8,128)(2,1)S(1)} %pad_maximum_fusion.refs_0_, bf16[256,384]{1,0:T(8,128)(2,1)S(1)} %collective-permute-done.4.refs_1_, ...), custom_call_target="tpu_custom_call" | custom-call | tf_op jit(solution)/shard_map/tile/pallas_call | solution.py:255
  54.6 1.1 %collective-permute-start.12 = (bf16[512,256]{1,0:T(8,128)(2,1)S(1)}, bf16[512,256]{1,0:T(8,128)(2,1)S(1)}, u32[]{:S(2)}, u32[]{:S(2)}) collective-permute-start(bf16[512,256]{1,0:T(8,128)(2,1)S(1)} %tile.5), channel_id=1, source_target_pairs={{0,1},{1,2},{2,3},{3,0},{4,5},{5,6},{6,7},{7,4},{8,9},{9,10},{10,1... | collective-permute-start | bytes 786440 | tf_op jit(solution)/shard_map/ppermute | solution.py:197
  55.8 0.4 collective-permute-done.14.refs_2_
  56.2 5.3 %collective-permute-done.12.refs_1_ = bf16[512,256]{1,0:T(8,128)(2,1)S(1)} collective-permute-done((bf16[512,256]{1,0:T(8,128)(2,1)S(1)}, bf16[512,256]{1,0:T(8,128)(2,1)S(1)}, u32[]{:S(2)}, u32[]{:S(2)}) %collective-permute-start.12) | collective-permute-done | bytes 262176 | tf_op jit(solution)/shard_map/ppermute | solution.py:197
  61.4 1.2 %sum_rows.1 = (bf16[512,256]{1,0:T(8,128)(2,1)}, f32[128,256]{1,0:T(8,128)S(1)}, bf16[128,256]{1,0:T(8,128)(2,1)S(1)}, bf16[128,256]{1,0:T(8,128)(2,1)S(1)}, bf16[128,256]{1,0:T(8,128)(2,1)S(1)}) custom-call(f32[512,256]{1,0:T(8,128)S(1)} %tile.4.refs_0_, bf16[512,256]{1,0:T(8,128)(2,1)S(1)} %collective-permute-done.12.refs_1_, ...), custom_call_target="tpu_custom_call" | custom-call | tf_op jit(solution)/shard_map/sum_rows/pallas_call | solution.py:265
  62.7 4.3 %all-to-all-start = ((bf16[32,16,256]{2,1,0:T(8,128)(2,1)}), bf16[32,16,256]{2,1,0:T(8,128)(2,1)S(1)}, u32[]{:S(2)}, u32[]{:S(2)}) async-start(bf16[32,16,256]{2,1,0:T(8,128)(2,1)} %bitcast.3), calls=%async_computation | async-start | bytes 524288 | tf_op jit(solution)/shard_map/all_to_all | solution.py:205
  66.9 1.5 %collective-permute-start.17 = (bf16[128,256]{1,0:T(8,128)(2,1)S(1)}, bf16[128,256]{1,0:T(8,128)(2,1)S(1)}, u32[]{:S(2)}, u32[]{:S(2)}) collective-permute-start(bf16[128,256]{1,0:T(8,128)(2,1)S(1)} %get-tuple-element.32), channel_id=1, source_target_pairs={{0,64},{1,65},{2,66},{3,67},{4,68},{5,69},{6,70},{7,71},{8,72},{9,... | collective-permute-start | bytes 196616 | tf_op jit(solution)/shard_map/ppermute | solution.py:197
  68.4 6.0 %collective-permute-done.17.b = bf16[128,256]{1,0:T(8,128)(2,1)S(1)} collective-permute-done((bf16[128,256]{1,0:T(8,128)(2,1)S(1)}, bf16[128,256]{1,0:T(8,128)(2,1)S(1)}, u32[]{:S(2)}, u32[]{:S(2)}) %collective-permute-start.17) | collective-permute-done | bytes 65568 | tf_op jit(solution)/shard_map/ppermute | solution.py:197
  74.4 1.7 %all-to-all-done.parts = bf16[32,16,256]{2,1,0:T(8,128)(2,1)S(1)} async-done(((bf16[32,16,256]{2,1,0:T(8,128)(2,1)}), bf16[32,16,256]{2,1,0:T(8,128)(2,1)S(1)}, u32[]{:S(2)}, u32[]{:S(2)}) %all-to-all-start) | async-done | bytes 262176 | tf_op jit(solution)/shard_map/all_to_all | solution.py:205
  76.0 0.7 sum_spread.2
  76.8 7.6 %all-to-all-start.1 = ((f32[8,16,256]{2,1,0:T(8,128)}), f32[8,16,256]{2,1,0:T(8,128)S(1)}, u32[]{:S(2)}, u32[]{:S(2)}) async-start(f32[8,16,256]{2,1,0:T(8,128)} %sum_spread.2), calls=%async_computation.1 | async-start | bytes 262144 | tf_op jit(solution)/shard_map/all_to_all | solution.py:205
  84.4 0.7 collective-permute-start.18
  85.0 4.0 %collective-permute-done.18.c = bf16[128,256]{1,0:T(8,128)(2,1)S(1)} collective-permute-done((bf16[128,256]{1,0:T(8,128)(2,1)S(1)}, bf16[128,256]{1,0:T(8,128)(2,1)S(1)}, u32[]{:S(2)}, u32[]{:S(2)}) %collective-permute-start.18) | collective-permute-done | bytes 65568 | tf_op jit(solution)/shard_map/ppermute | solution.py:197
  89.0 3.1 %all-to-all-done.1.parts = f32[8,16,256]{2,1,0:T(8,128)S(1)} async-done(((f32[8,16,256]{2,1,0:T(8,128)}), f32[8,16,256]{2,1,0:T(8,128)S(1)}, u32[]{:S(2)}, u32[]{:S(2)}) %all-to-all-start.1) | async-done | bytes 131104 | tf_op jit(solution)/shard_map/all_to_all | solution.py:205
  92.1 0.7 sum_spread.3
  92.9 5.8 %all-to-all-start.2 = ((bf16[32,16,256]{2,1,0:T(8,128)(2,1)}), bf16[32,16,256]{2,1,0:T(8,128)(2,1)S(1)}, u32[]{:S(2)}, u32[]{:S(2)}) async-start(bf16[32,16,256]{2,1,0:T(8,128)(2,1)} %sum_spread.3), calls=%async_computation.2 | async-start | bytes 524288 | tf_op jit(solution)/shard_map/all_to_all | solution.py:205
  98.7 2.7 %collective-permute-start.19 = (bf16[128,256]{1,0:T(8,128)(2,1)S(1)}, bf16[128,256]{1,0:T(8,128)(2,1)S(1)}, u32[]{:S(2)}, u32[]{:S(2)}) collective-permute-start(bf16[128,256]{1,0:T(8,128)(2,1)S(1)} %get-tuple-element.39), channel_id=1, source_target_pairs={{0,192},{1,193},{2,194},{3,195},{4,196},{5,197},{6,198},{7,199},{8... | collective-permute-start | bytes 196616 | tf_op jit(solution)/shard_map/ppermute | solution.py:197
  101.4 3.5 %collective-permute-done.19.d = bf16[128,256]{1,0:T(8,128)(2,1)S(1)} collective-permute-done((bf16[128,256]{1,0:T(8,128)(2,1)S(1)}, bf16[128,256]{1,0:T(8,128)(2,1)S(1)}, u32[]{:S(2)}, u32[]{:S(2)}) %collective-permute-start.19) | collective-permute-done | bytes 65568 | tf_op jit(solution)/shard_map/ppermute | solution.py:197
  104.9 0.7 finish_rows.1
  105.6 2.1 %all-to-all-done.2 = bf16[32,16,256]{2,1,0:T(8,128)(2,1)S(1)} async-done(((bf16[32,16,256]{2,1,0:T(8,128)(2,1)}), bf16[32,16,256]{2,1,0:T(8,128)(2,1)S(1)}, u32[]{:S(2)}, u32[]{:S(2)}) %all-to-all-start.2) | async-done | bytes 262176 | tf_op jit(solution)/shard_map/all_to_all | solution.py:205
  107.7 0.9 convert_multiply_fusion
  (22 shorter events, 0.2 us)
Async XLA Ops:
  0.6 0.7 copy-start.5
  1.3 0.9 copy-start.1
  2.2 0.9 copy-start.2
  3.1 0.7 copy-start.3
  3.8 0.7 copy-start.4
  5.1 13.6 %collective-permute-start.1 = (bf16[128,896]{1,0:T(8,128)(2,1)S(1)}, bf16[128,896]{1,0:T(8,128)(2,1)S(1)}, u32[]{:S(2)}, u32[]{:S(2)}) collective-permute-start(bf16[128,896]{1,0:T(8,128)(2,1)S(1)} %get-tuple-element.23.refs_0_), channel_id=1, source_target_pairs={{0,192},{1,193},{2,194},{3,195},{4,196},{5,197},{6,198},{7,199},{8... | collective-permute-start | bytes 688136 | tf_op jit(solution)/shard_map/ppermute | solution.py:197
  8.5 10.2 %collective-permute-start.2 = (bf16[128,896]{1,0:T(8,128)(2,1)S(1)}, bf16[128,896]{1,0:T(8,128)(2,1)S(1)}, u32[]{:S(2)}, u32[]{:S(2)}) collective-permute-start(bf16[128,896]{1,0:T(8,128)(2,1)S(1)} %get-tuple-element.23.refs_0_), channel_id=1, source_target_pairs={{0,128},{1,129},{2,130},{3,131},{4,132},{5,133},{6,134},{7,135},{8... | collective-permute-start | bytes 688136 | tf_op jit(solution)/shard_map/ppermute | solution.py:197
  9.0 9.7 %collective-permute-start.3 = (bf16[128,896]{1,0:T(8,128)(2,1)S(1)}, bf16[128,896]{1,0:T(8,128)(2,1)S(1)}, u32[]{:S(2)}, u32[]{:S(2)}) collective-permute-start(bf16[128,896]{1,0:T(8,128)(2,1)S(1)} %get-tuple-element.23.refs_0_), channel_id=1, source_target_pairs={{0,64},{1,65},{2,66},{3,67},{4,68},{5,69},{6,70},{7,71},{8,72},{9,... | collective-permute-start | bytes 688136 | tf_op jit(solution)/shard_map/ppermute | solution.py:197
  9.6 9.0 %collective-permute-start = (bf16[128,384]{1,0:T(8,128)(2,1)S(1)}, bf16[128,384]{1,0:T(8,128)(2,1)S(1)}, u32[]{:S(2)}, u32[]{:S(2)}) collective-permute-start(bf16[128,384]{1,0:T(8,128)(2,1)S(1)} %get-tuple-element.22), channel_id=1, source_target_pairs={{0,32},{4,36},{8,40},{12,44},{32,0},{36,4},{40,8},{44,12},{1,33},{... | collective-permute-start | bytes 294920 | tf_op jit(solution)/shard_map/ppermute | solution.py:182
  18.7 20.7 %copy-start = (bf16[128,128]{1,0:T(8,128)(2,1)S(1)}, bf16[128,128]{1,0:T(8,128)(2,1)}, u32[]{:S(2)}) copy-start(bf16[128,128]{1,0:T(8,128)(2,1)} %constant.4.clone.table) | copy-start | bytes 98308
  18.8 8.2 %collective-permute-start.4 = (bf16[256,384]{1,0:T(8,128)(2,1)S(1)}, bf16[256,384]{1,0:T(8,128)(2,1)S(1)}, u32[]{:S(2)}, u32[]{:S(2)}) collective-permute-start(bf16[256,384]{1,0:T(8,128)(2,1)S(1)} %pad_maximum_fusion.refs_0_), channel_id=1, source_target_pairs={{0,16},{16,0},{1,17},{17,1},{2,18},{18,2},{3,19},{19,3},{4,20},{20... | collective-permute-start | bytes 589832 | tf_op jit(solution)/shard_map/ppermute | solution.py:182
  21.5 10.1 %collective-permute-start.5 = (bf16[256,384]{1,0:T(8,128)(2,1)S(1)}, bf16[256,384]{1,0:T(8,128)(2,1)S(1)}, u32[]{:S(2)}, u32[]{:S(2)}) collective-permute-start(bf16[256,384]{1,0:T(8,128)(2,1)S(1)} %pad_maximum_fusion.refs_0_), channel_id=1, source_target_pairs={{0,8},{1,9},{2,10},{3,11},{4,12},{5,13},{6,14},{7,15},{8,32},{9,33... | collective-permute-start | bytes 589832 | tf_op jit(solution)/shard_map/ppermute | solution.py:197
  26.9 9.0 %collective-permute-start.6 = (bf16[256,384]{1,0:T(8,128)(2,1)S(1)}, bf16[256,384]{1,0:T(8,128)(2,1)S(1)}, u32[]{:S(2)}, u32[]{:S(2)}) collective-permute-start(bf16[256,384]{1,0:T(8,128)(2,1)S(1)} %pad_maximum_fusion.refs_0_), channel_id=1, source_target_pairs={{0,4},{1,5},{2,6},{3,7},{4,8},{5,9},{6,10},{7,11},{8,12},{9,13},{1... | collective-permute-start | bytes 589832 | tf_op jit(solution)/shard_map/ppermute | solution.py:197
  27.0 10.7 %collective-permute-start.7 = (bf16[256,384]{1,0:T(8,128)(2,1)S(1)}, bf16[256,384]{1,0:T(8,128)(2,1)S(1)}, u32[]{:S(2)}, u32[]{:S(2)}) collective-permute-start(bf16[256,384]{1,0:T(8,128)(2,1)S(1)} %collective-permute-done.4.refs_1_), channel_id=1, source_target_pairs={{0,4},{1,5},{2,6},{3,7},{4,8},{5,9},{6,10},{7,11},{8,12},{9,13},{1... | collective-permute-start | bytes 589832 | tf_op jit(solution)/shard_map/ppermute | solution.py:197
  31.6 6.1 %collective-permute-start.8 = (bf16[256,384]{1,0:T(8,128)(2,1)S(1)}, bf16[256,384]{1,0:T(8,128)(2,1)S(1)}, u32[]{:S(2)}, u32[]{:S(2)}) collective-permute-start(bf16[256,384]{1,0:T(8,128)(2,1)S(1)} %collective-permute-done.5.refs_2_), channel_id=1, source_target_pairs={{0,16},{16,0},{1,17},{17,1},{2,18},{18,2},{3,19},{19,3},{4,20},{20... | collective-permute-start | bytes 589832 | tf_op jit(solution)/shard_map/ppermute | solution.py:182
  31.6 10.3 %collective-permute-start.15 = (bf16[512,384]{1,0:T(8,128)(2,1)S(1)}, bf16[512,384]{1,0:T(8,128)(2,1)S(1)}, u32[]{:S(2)}, u32[]{:S(2)}) collective-permute-start(bf16[512,384]{1,0:T(8,128)(2,1)S(1)} %get-tuple-element.25.rows_ref), channel_id=1, source_target_pairs={{0,1},{1,2},{2,3},{3,0},{4,5},{5,6},{6,7},{7,4},{8,9},{9,10},{10,1... | collective-permute-start | bytes 1179656 | tf_op jit(solution)/shard_map/ppermute | solution.py:197
  33.2 13.3 %collective-permute-start.13 = (bf16[512,384]{1,0:T(8,128)(2,1)S(1)}, bf16[512,384]{1,0:T(8,128)(2,1)S(1)}, u32[]{:S(2)}, u32[]{:S(2)}) collective-permute-start(bf16[512,384]{1,0:T(8,128)(2,1)S(1)} %get-tuple-element.25.rows_ref), channel_id=1, source_target_pairs={{0,2},{1,3},{2,0},{3,1},{4,6},{5,7},{6,4},{7,5},{8,10},{9,11},{10,... | collective-permute-start | bytes 1179656 | tf_op jit(solution)/shard_map/ppermute | solution.py:197
  35.9 16.2 %collective-permute-start.11 = (bf16[512,384]{1,0:T(8,128)(2,1)S(1)}, bf16[512,384]{1,0:T(8,128)(2,1)S(1)}, u32[]{:S(2)}, u32[]{:S(2)}) collective-permute-start(bf16[512,384]{1,0:T(8,128)(2,1)S(1)} %get-tuple-element.25.rows_ref), channel_id=1, source_target_pairs={{0,3},{1,0},{2,1},{3,2},{4,7},{5,4},{6,5},{7,6},{8,11},{9,8},{10,9... | collective-permute-start | bytes 1179656 | tf_op jit(solution)/shard_map/ppermute | solution.py:197
  37.7 1.4 %collective-permute-start.9 = (bf16[256,384]{1,0:T(8,128)(2,1)S(1)}, bf16[256,384]{1,0:T(8,128)(2,1)S(1)}, u32[]{:S(2)}, u32[]{:S(2)}) collective-permute-start(bf16[256,384]{1,0:T(8,128)(2,1)S(1)} %collective-permute-done.6.refs_3_), channel_id=1, source_target_pairs={{0,16},{16,0},{1,17},{17,1},{2,18},{18,2},{3,19},{19,3},{4,20},{20... | collective-permute-start | bytes 589832 | tf_op jit(solution)/shard_map/ppermute | solution.py:182
  37.7 1.7 %collective-permute-start.10 = (bf16[256,384]{1,0:T(8,128)(2,1)S(1)}, bf16[256,384]{1,0:T(8,128)(2,1)S(1)}, u32[]{:S(2)}, u32[]{:S(2)}) collective-permute-start(bf16[256,384]{1,0:T(8,128)(2,1)S(1)} %collective-permute-done.7.refs_4_), channel_id=1, source_target_pairs={{0,16},{16,0},{1,17},{17,1},{2,18},{18,2},{3,19},{19,3},{4,20},{20... | collective-permute-start | bytes 589832 | tf_op jit(solution)/shard_map/ppermute | solution.py:182
  44.6 11.2 %collective-permute-start.16 = (bf16[512,256]{1,0:T(8,128)(2,1)S(1)}, bf16[512,256]{1,0:T(8,128)(2,1)S(1)}, u32[]{:S(2)}, u32[]{:S(2)}) collective-permute-start(bf16[512,256]{1,0:T(8,128)(2,1)S(1)} %tile.7), channel_id=1, source_target_pairs={{0,3},{1,0},{2,1},{3,2},{4,7},{5,4},{6,5},{7,6},{8,11},{9,8},{10,9... | collective-permute-start | bytes 786440 | tf_op jit(solution)/shard_map/ppermute | solution.py:197
  49.1 7.1 %collective-permute-start.14 = (bf16[512,256]{1,0:T(8,128)(2,1)S(1)}, bf16[512,256]{1,0:T(8,128)(2,1)S(1)}, u32[]{:S(2)}, u32[]{:S(2)}) collective-permute-start(bf16[512,256]{1,0:T(8,128)(2,1)S(1)} %tile.6), channel_id=1, source_target_pairs={{0,2},{1,3},{2,0},{3,1},{4,6},{5,7},{6,4},{7,5},{8,10},{9,11},{10,... | collective-permute-start | bytes 786440 | tf_op jit(solution)/shard_map/ppermute | solution.py:197
  54.6 6.8 %collective-permute-start.12 = (bf16[512,256]{1,0:T(8,128)(2,1)S(1)}, bf16[512,256]{1,0:T(8,128)(2,1)S(1)}, u32[]{:S(2)}, u32[]{:S(2)}) collective-permute-start(bf16[512,256]{1,0:T(8,128)(2,1)S(1)} %tile.5), channel_id=1, source_target_pairs={{0,1},{1,2},{2,3},{3,0},{4,5},{5,6},{6,7},{7,4},{8,9},{9,10},{10,1... | collective-permute-start | bytes 786440 | tf_op jit(solution)/shard_map/ppermute | solution.py:197
  62.7 13.4 %all-to-all-start = ((bf16[32,16,256]{2,1,0:T(8,128)(2,1)}), bf16[32,16,256]{2,1,0:T(8,128)(2,1)S(1)}, u32[]{:S(2)}, u32[]{:S(2)}) async-start(bf16[32,16,256]{2,1,0:T(8,128)(2,1)} %bitcast.3), calls=%async_computation | async-start | bytes 524288 | tf_op jit(solution)/shard_map/all_to_all | solution.py:205
  66.9 7.4 %collective-permute-start.17 = (bf16[128,256]{1,0:T(8,128)(2,1)S(1)}, bf16[128,256]{1,0:T(8,128)(2,1)S(1)}, u32[]{:S(2)}, u32[]{:S(2)}) collective-permute-start(bf16[128,256]{1,0:T(8,128)(2,1)S(1)} %get-tuple-element.32), channel_id=1, source_target_pairs={{0,64},{1,65},{2,66},{3,67},{4,68},{5,69},{6,70},{7,71},{8,72},{9,... | collective-permute-start | bytes 196616 | tf_op jit(solution)/shard_map/ppermute | solution.py:197
  76.8 15.4 %all-to-all-start.1 = ((f32[8,16,256]{2,1,0:T(8,128)}), f32[8,16,256]{2,1,0:T(8,128)S(1)}, u32[]{:S(2)}, u32[]{:S(2)}) async-start(f32[8,16,256]{2,1,0:T(8,128)} %sum_spread.2), calls=%async_computation.1 | async-start | bytes 262144 | tf_op jit(solution)/shard_map/all_to_all | solution.py:205
  84.4 4.6 %collective-permute-start.18 = (bf16[128,256]{1,0:T(8,128)(2,1)S(1)}, bf16[128,256]{1,0:T(8,128)(2,1)S(1)}, u32[]{:S(2)}, u32[]{:S(2)}) collective-permute-start(bf16[128,256]{1,0:T(8,128)(2,1)S(1)} %get-tuple-element.34), channel_id=1, source_target_pairs={{0,128},{1,129},{2,130},{3,131},{4,132},{5,133},{6,134},{7,135},{8... | collective-permute-start | bytes 196616 | tf_op jit(solution)/shard_map/ppermute | solution.py:197
  92.9 14.8 %all-to-all-start.2 = ((bf16[32,16,256]{2,1,0:T(8,128)(2,1)}), bf16[32,16,256]{2,1,0:T(8,128)(2,1)S(1)}, u32[]{:S(2)}, u32[]{:S(2)}) async-start(bf16[32,16,256]{2,1,0:T(8,128)(2,1)} %sum_spread.3), calls=%async_computation.2 | async-start | bytes 524288 | tf_op jit(solution)/shard_map/all_to_all | solution.py:205
  98.7 6.2 %collective-permute-start.19 = (bf16[128,256]{1,0:T(8,128)(2,1)S(1)}, bf16[128,256]{1,0:T(8,128)(2,1)S(1)}, u32[]{:S(2)}, u32[]{:S(2)}) collective-permute-start(bf16[128,256]{1,0:T(8,128)(2,1)S(1)} %get-tuple-element.39), channel_id=1, source_target_pairs={{0,192},{1,193},{2,194},{3,195},{4,196},{5,197},{6,198},{7,199},{8... | collective-permute-start | bytes 196616 | tf_op jit(solution)/shard_map/ppermute | solution.py:197

commit v6 on v5

--- a/solution.py
+++ b/solution.py
@@ -12,7 +12,7 @@
 LOG2E = math.log2(math.e)
 ROOT5 = math.sqrt(5.0)
 ALL = ("y", "zh", "core", "zl", "x")
-PLANE = ("y", "core", "x")
+PLANE = ("y", "x")
 DEPTH = ("zh", "zl")
 F32 = jnp.float32
 BF16 = jnp.bfloat16
@@ -95,8 +95,10 @@
     return jnp.asarray(table, BF16)
 
 
-def tile_kernel(sub, step, table, rows_ref, *refs):
+def tile_kernel(sub, step, adds, table, rows_ref, *refs):
     *columns, out = refs
+    if adds:
+        begin, *columns = columns
     width = out.shape[1]
     rows = rows_ref.shape[0]
     u_rows = rows_ref[:, :width]
@@ -109,7 +111,7 @@
     lane = lax.broadcasted_iota(jnp.int32, (8, 128), 1)
     pick_cols = jnp.where((lane >= 96) & (lane < 99), 1.0, 0.0).astype(BF16)
     blocks = [slice(k, k + sub) for k in range(0, rows, sub)]
-    acc = [jnp.zeros((sub, width), F32) for _ in blocks]
+    acc = [begin[block, :] if adds else jnp.zeros((sub, width), F32) for block in blocks]
     total = [jnp.zeros((sub, 128), F32) for _ in blocks]
     work = [
         (ref, start, k)
@@ -158,10 +160,13 @@
     grad_rows[...] = (own[...] + b[...].astype(F32)) + (c[...].astype(F32) + d[...].astype(F32))
 
 
-def sum_spread_kernel(parts, out):
-    total = parts[0].astype(F32)
-    for k in range(1, parts.shape[0]):
-        total = total + parts[k].astype(F32)
+def sum_spread_kernel(*refs):
+    *parts, out = refs
+    total = None
+    for ref in parts:
+        for k in range(ref.shape[0]):
+            term = ref[k].astype(F32)
+            total = term if total is None else total + term
     low = total.astype(out.dtype)
     for k in range(out.shape[0]):
         out[k] = low
@@ -170,12 +175,12 @@
 def sum_spread(parts, copies, dtype):
     return pl.pallas_call(
         sum_spread_kernel,
-        out_shape=jax.ShapeDtypeStruct((copies,) + parts.shape[1:], dtype),
-        in_specs=[VMEM],
+        out_shape=jax.ShapeDtypeStruct((copies,) + parts[0].shape[1:], dtype),
+        in_specs=[VMEM] * len(parts),
         out_specs=VMEM,
         compiler_params=params(16),
         name="sum_spread",
-    )(parts)
+    )(*parts)
 
 
 def ring(array, axis, size, shift):
@@ -214,7 +219,7 @@
             jax.ShapeDtypeStruct((rows, width + 128), BF16),
             jax.ShapeDtypeStruct((rows, width + 128 + embeds.shape[1]), BF16),
         ],
-        in_specs=[pl.BlockSpec(memory_space=pl.ANY)] * 5,
+        in_specs=[pl.BlockSpec(memory_space=pltpu.HBM)] * 5,
         out_specs=[VMEM] * 2,
         scratch_shapes=[
             pltpu.VMEM(weight.shape, BF16),
@@ -225,7 +230,7 @@
         ],
         compiler_params=params(48),
         name="pack",
-    )(embeds, weight, solve[None, :], probes.T, probe_solves.T)
+    )(*(pltpu.with_memory_space_constraint(a, pltpu.HBM) for a in (embeds, weight, solve[None, :], probes.T, probe_solves.T)))
 
     blocks = [extended] + [turn(extended, sizes, 0, -d) for d in range(1, n_side)]
     line, embeds_line = pl.pallas_call(
@@ -241,25 +246,31 @@
     )(*blocks)
     pair = jnp.concatenate([pack, ring(pack, DEPTH, n_z, n_z // 2)], axis=0)
     pair, line = lax.optimization_barrier((pair, line))
-    swap = ring(pair, "core", 2, 1)
+    four = jnp.concatenate([pair, ring(pair, "core", 2, 1)], axis=0)
+    near = move(four, sizes, lambda core: {"z": 1 - 2 * core})
     far = move(pair, sizes, lambda core: {"z": 2 - 4 * core})
-    near = [move(part, sizes, lambda core: {"z": 1 - 2 * core}) for part in (pair, swap)]
     lines = [line] + [turn(line, sizes, 1, -d) for d in range(1, n_side)]
-    columns = [pair, swap, far, *near] + [ring(part, "core", 2, 1) for part in (far, *near)]
+    near, far, lines = lax.optimization_barrier((near, far, lines))
+    columns = [four, near, far, ring(near, "core", 2, 1), ring(far, "core", 2, 1)]
 
     table = left_map(probes.shape[1])
-    back = {}
-    for d in (0, 3, 1, 2):
-        if d != 0:
-            lines[d], _ = lax.optimization_barrier((lines[d], back[0]))
-        part = pl.pallas_call(
-            functools.partial(tile_kernel, 256, 256),
-            out_shape=jax.ShapeDtypeStruct((n_side * rows, width), F32 if d == 0 else BF16),
-            in_specs=[VMEM] * (2 + len(columns)),
+
+    def tile(rows_in, columns, dtype, start=None):
+        return pl.pallas_call(
+            functools.partial(tile_kernel, 256, 256, start is not None),
+            out_shape=jax.ShapeDtypeStruct((rows_in.shape[0], width), dtype),
+            in_specs=[VMEM] * (2 + len(columns) + (start is not None)),
             out_specs=VMEM,
             compiler_params=params(16),
             name="tile",
-        )(table, lines[d], *columns)
+        )(table, rows_in, *([] if start is None else [start]), *columns)
+
+    back = {}
+    for d in (0, 3, 1, 2):
+        if d == 2:
+            part = tile(lines[d], columns[3:], BF16, tile(lines[d], columns[:3], F32))
+        else:
+            part = tile(lines[d], columns, F32 if d == 0 else BF16)
         back[d] = part if d == 0 else turn(part, sizes, 1, d)
 
     partial, own_rows, *other_rows = pl.pallas_call(
@@ -274,13 +285,20 @@
         compiler_params=params(16),
         name="sum_rows",
     )(*(back[d] for d in range(n_side)), embeds_line)
-    arrived = [turn(block, sizes, 0, d + 1) for d, block in enumerate(other_rows)]
-    n_plane = n_side * n_side * 2
+    arrived = [turn(other_rows[0], sizes, 0, 1)]
+    n_plane = n_side * n_side
     pieces = exchange(partial.reshape(n_plane, -1, width), PLANE)
     pieces, arrived[0] = lax.optimization_barrier((pieces, arrived[0]))
-    pieces = exchange(sum_spread(pieces, n_z, F32), DEPTH)
+    piece = sum_spread([pieces], 1, F32)
+    spread = sum_spread([piece, ring(piece, "core", 2, 1)], n_z, F32)
+    spread, other_rows[1] = lax.optimization_barrier((spread, other_rows[1]))
+    pieces = exchange(spread, DEPTH)
+    arrived.append(turn(other_rows[1], sizes, 0, 2))
     pieces, arrived[1] = lax.optimization_barrier((pieces, arrived[1]))
-    pieces = exchange(sum_spread(pieces, n_plane, BF16), PLANE)
+    spread = sum_spread([pieces], n_plane, BF16)
+    spread, other_rows[2] = lax.optimization_barrier((spread, other_rows[2]))
+    pieces = exchange(spread, PLANE)
+    arrived.append(turn(other_rows[2], sizes, 0, 3))
     grad_rows = pl.pallas_call(
         finish_rows_kernel,
         out_shape=jax.ShapeDtypeStruct((rows, width), F32),
@@ -290,7 +308,7 @@
         name="finish_rows",
     )(own_rows, *arrived)
     pieces, grad_rows = lax.optimization_barrier((pieces, grad_rows))
-    total_points = rows * n_plane * n_z
+    total_points = rows * n_plane * n_z * 2
     grad_weight = pieces.reshape(-1, width).astype(F32) * (1.0 / math.sqrt(total_points))
     return grad_rows, grad_weight
 

time: 109 us -> 106 us (0.972)
  local copies, waits for them, and re-layouts: 3.9 us -> 0.06 us
  Pallas kernels: 14.2 us -> 15.5 us
    ppermute x5, starting transfers between devices: 10.2 us -> 17.6 us  [ring(): lax.ppermute(array, axis, [(i, (i + shift) % size) for i in range(size)])]
    ppermute x15 -> x14, waiting for transfers between devices: 22.6 us -> 18.4 us  [move(): return lax.ppermute(array, ALL, perm)]
    ppermute x15 -> x14, starting transfers between devices: 28.1 us -> 23.9 us  [move(): return lax.ppermute(array, ALL, perm)]
    unnamed x12 -> x3, local copies, waits for them, and re-layouts: 3.9 us -> 0.03 us
    all_to_all x3, waiting for transfers between devices: 6.89 us -> 10.6 us  [exchange(): return lax.all_to_all(array, axes, split_axis=0, concat_axis=0, tiled=True)]
    all_to_all x3, starting transfers between devices: 17.7 us -> 14.1 us  [exchange(): return lax.all_to_all(array, axes, split_axis=0, concat_axis=0, tiled=True)]
    pallas_call x4 -> x5, Pallas kernels: 10.2 us -> 10.5 us  [tile(): pl.pallas_call(functools.partial(tile_kernel, 256, 256, start is not None...]
  transfers between devices with their start and end apart: 23 -> 22, of which waited for: 12 -> 10; matrix products, arithmetic and copies ran while one was open for 0% -> 0% of each run, Pallas kernels for 10% -> 10%
where the time goes in v6:
time: 106 us; the launch traced here: 105 us
  starting transfers between devices  55.6 us (52%)
  waiting for transfers between devices  32 us (30%)
  Pallas kernels  15.5 us (15%)
    ppermute x14, starting transfers between devices, move(): return lax.ppermute(array, ALL, perm)  23.9 us
    ppermute x14, waiting for transfers between devices, move(): return lax.ppermute(array, ALL, perm)  18.4 us
    ppermute x5, starting transfers between devices, ring(): lax.ppermute(array, axis, [(i, (i + shift) % size) for i in range(size)])  17.6 us
    all_to_all x3, starting transfers between devices, exchange(): return lax.all_to_all(array, axes, split_axis=0, concat_axis=0, tiled=True)  14.1 us
    all_to_all x3, waiting for transfers between devices, exchange(): return lax.all_to_all(array, axes, split_axis=0, concat_axis=0, tiled=True)  10.6 us
    pallas_call x5, Pallas kernels, tile(): pl.pallas_call(functools.partial(tile_kernel, 256, 256, start is not None...  10.5 us
    ppermute x5, waiting for transfers between devices, ring(): lax.ppermute(array, axis, [(i, (i + shift) % size) for i in range(size)])  2.97 us
  transfers between devices with their start and end apart: 22, of which 10 were waited for; matrix products, arithmetic and copies ran while one was open for 0% of the time, Pallas kernels for 10%

profile of v6, /device:TPU:1, one launch (start us, length us, event | category | flops | bytes accessed | tf_op | source)
XLA Modules:
  0.0 104.8 jit_solution(17393658495737538633)
XLA Ops:
  0.6 1.5 %pack.1 = (bf16[128,384]{1,0:T(8,128)(2,1)S(1)}, bf16[128,896]{1,0:T(8,128)(2,1)S(1)}) custom-call(bf16[128,512]{1,0:T(8,128)(2,1)} %embeds.1, bf16[512,256]{1,0:T(8,128)(2,1)} %weight.1, f32[1,128]{1,0:T(1,128)} %bitcast.8, f32[15,128]{1,0:T(8,128)} %bitcast.6, f32[15,128]{1,0:T(8,128)} %bitcast.7), custom_call_target="tpu_custom_call" | custom-call | tf_op jit(solution)/shard_map/pack/pallas_call | solution.py:216
  2.2 2.1 %collective-permute-start.3 = (bf16[128,896]{1,0:T(8,128)(2,1)S(1)}, bf16[128,896]{1,0:T(8,128)(2,1)S(1)}, u32[]{:S(2)}, u32[]{:S(2)}) collective-permute-start(bf16[128,896]{1,0:T(8,128)(2,1)S(1)} %get-tuple-element.30.refs_0_), channel_id=1, source_target_pairs={{0,64},{1,65},{2,66},{3,67},{4,68},{5,69},{6,70},{7,71},{8,72},{9,... | collective-permute-start | bytes 688136 | tf_op jit(solution)/shard_map/ppermute | solution.py:202
  4.3 2.5 %collective-permute-start.2 = (bf16[128,896]{1,0:T(8,128)(2,1)S(1)}, bf16[128,896]{1,0:T(8,128)(2,1)S(1)}, u32[]{:S(2)}, u32[]{:S(2)}) collective-permute-start(bf16[128,896]{1,0:T(8,128)(2,1)S(1)} %get-tuple-element.30.refs_0_), channel_id=1, source_target_pairs={{0,128},{1,129},{2,130},{3,131},{4,132},{5,133},{6,134},{7,135},{8... | collective-permute-start | bytes 688136 | tf_op jit(solution)/shard_map/ppermute | solution.py:202
  6.7 1.2 %collective-permute-start.1 = (bf16[128,896]{1,0:T(8,128)(2,1)S(1)}, bf16[128,896]{1,0:T(8,128)(2,1)S(1)}, u32[]{:S(2)}, u32[]{:S(2)}) collective-permute-start(bf16[128,896]{1,0:T(8,128)(2,1)S(1)} %get-tuple-element.30.refs_0_), channel_id=1, source_target_pairs={{0,192},{1,193},{2,194},{3,195},{4,196},{5,197},{6,198},{7,199},{8... | collective-permute-start | bytes 688136 | tf_op jit(solution)/shard_map/ppermute | solution.py:202
  7.9 6.9 %collective-permute-start = (bf16[128,384]{1,0:T(8,128)(2,1)S(1)}, bf16[128,384]{1,0:T(8,128)(2,1)S(1)}, u32[]{:S(2)}, u32[]{:S(2)}) collective-permute-start(bf16[128,384]{1,0:T(8,128)(2,1)S(1)} %get-tuple-element.29), channel_id=1, source_target_pairs={{0,32},{4,36},{8,40},{12,44},{32,0},{36,4},{40,8},{44,12},{1,33},{... | collective-permute-start | bytes 294920 | tf_op jit(solution)/shard_map/ppermute | solution.py:187
  14.8 2.1 %collective-permute-done = bf16[128,384]{1,0:T(8,128)(2,1)S(1)} collective-permute-done((bf16[128,384]{1,0:T(8,128)(2,1)S(1)}, bf16[128,384]{1,0:T(8,128)(2,1)S(1)}, u32[]{:S(2)}, u32[]{:S(2)}) %collective-permute-start) | collective-permute-done | bytes 98336 | tf_op jit(solution)/shard_map/ppermute | solution.py:187
  16.9 0.0 collective-permute-done.2.refs_2_
  17.0 0.0 collective-permute-done.1.refs_1_
  17.0 0.1 split.1
  17.0 2.7 %collective-permute-start.4 = (bf16[256,384]{1,0:T(8,128)(2,1)S(1)}, bf16[256,384]{1,0:T(8,128)(2,1)S(1)}, u32[]{:S(2)}, u32[]{:S(2)}) collective-permute-start(bf16[256,384]{1,0:T(8,128)(2,1)S(1)} %pad_maximum_fusion), channel_id=1, source_target_pairs={{0,16},{16,0},{1,17},{17,1},{2,18},{18,2},{3,19},{19,3},{4,20},{20... | collective-permute-start | bytes 589832 | tf_op jit(solution)/shard_map/ppermute | solution.py:187
  19.8 1.2 %collective-permute-start.9 = (bf16[512,384]{1,0:T(8,128)(2,1)S(1)}, bf16[512,384]{1,0:T(8,128)(2,1)S(1)}, u32[]{:S(2)}, u32[]{:S(2)}) collective-permute-start(bf16[512,384]{1,0:T(8,128)(2,1)S(1)} %get-tuple-element.34.rows_ref), channel_id=1, source_target_pairs={{0,1},{1,2},{2,3},{3,0},{4,5},{5,6},{6,7},{7,4},{8,9},{9,10},{10,1... | collective-permute-start | bytes 1179656 | tf_op jit(solution)/shard_map/ppermute | solution.py:202
  20.9 1.5 %collective-permute-start.8 = (bf16[512,384]{1,0:T(8,128)(2,1)S(1)}, bf16[512,384]{1,0:T(8,128)(2,1)S(1)}, u32[]{:S(2)}, u32[]{:S(2)}) collective-permute-start(bf16[512,384]{1,0:T(8,128)(2,1)S(1)} %get-tuple-element.34.rows_ref), channel_id=1, source_target_pairs={{0,2},{1,3},{2,0},{3,1},{4,6},{5,7},{6,4},{7,5},{8,10},{9,11},{10,... | collective-permute-start | bytes 1179656 | tf_op jit(solution)/shard_map/ppermute | solution.py:202
  22.4 0.9 collective-permute-start.7
  23.3 0.0 copy-start
  23.4 0.0 collective-permute-done.4
  23.4 4.5 %collective-permute-start.5 = (bf16[512,384]{1,0:T(8,128)(2,1)S(1)}, bf16[512,384]{1,0:T(8,128)(2,1)S(1)}, u32[]{:S(2)}, u32[]{:S(2)}) collective-permute-start(bf16[512,384]{1,0:T(8,128)(2,1)S(1)} %constant_dynamic-update-slice_fusion.refs_0_), channel_id=1, source_target_pairs={{0,4},{1,5},{2,6},{3,7},{4,8},{5,9},{6,10},{7,11},{8,12},{9,13},{1... | collective-permute-start | bytes 1179656 | tf_op jit(solution)/shard_map/ppermute | solution.py:202
  27.9 2.2 %collective-permute-start.6 = (bf16[256,384]{1,0:T(8,128)(2,1)S(1)}, bf16[256,384]{1,0:T(8,128)(2,1)S(1)}, u32[]{:S(2)}, u32[]{:S(2)}) collective-permute-start(bf16[256,384]{1,0:T(8,128)(2,1)S(1)} %pad_maximum_fusion), channel_id=1, source_target_pairs={{0,8},{1,9},{2,10},{3,11},{4,12},{5,13},{6,14},{7,15},{8,32},{9,33... | collective-permute-start | bytes 589832 | tf_op jit(solution)/shard_map/ppermute | solution.py:202
  30.1 6.7 %collective-permute-done.6.refs_2_ = bf16[256,384]{1,0:T(8,128)(2,1)S(1)} collective-permute-done((bf16[256,384]{1,0:T(8,128)(2,1)S(1)}, bf16[256,384]{1,0:T(8,128)(2,1)S(1)}, u32[]{:S(2)}, u32[]{:S(2)}) %collective-permute-start.6) | collective-permute-done | bytes 196640 | tf_op jit(solution)/shard_map/ppermute | solution.py:202
  36.9 4.3 %collective-permute-start.10 = (bf16[512,384]{1,0:T(8,128)(2,1)S(1)}, bf16[512,384]{1,0:T(8,128)(2,1)S(1)}, u32[]{:S(2)}, u32[]{:S(2)}) collective-permute-start(bf16[512,384]{1,0:T(8,128)(2,1)S(1)} %collective-permute-done.5.refs_1_), channel_id=1, source_target_pairs={{0,16},{16,0},{1,17},{17,1},{2,18},{18,2},{3,19},{19,3},{4,20},{20... | collective-permute-start | bytes 1179656 | tf_op jit(solution)/shard_map/ppermute | solution.py:187
  41.1 0.1 collective-permute-start.11
  41.2 1.7 %tile.7.refs_0_ = f32[512,256]{1,0:T(8,128)S(1)} custom-call(bf16[128,128]{1,0:T(8,128)(2,1)S(1)} %copy-done, bf16[512,384]{1,0:T(8,128)(2,1)S(1)} %collective-permute-done.8.rows_ref, bf16[512,384]{1,0:T(8,128)(2,1)S(1)} %constant_dynamic-update-slice_fusion.refs_0_, bf16[512,384]{1,0:T(8,128)(2,1)S(1)} %collective-permute-done.5.refs_1_, ...), custom_call_target="tpu_custom_call" | custom-call | tf_op jit(solution)/shard_map/tile/pallas_call | solution.py:259
  43.0 1.1 %tile.8 = bf16[512,256]{1,0:T(8,128)(2,1)S(1)} custom-call(bf16[128,128]{1,0:T(8,128)(2,1)S(1)} %copy-done, bf16[512,384]{1,0:T(8,128)(2,1)S(1)} %collective-permute-done.8.rows_ref, f32[512,256]{1,0:T(8,128)S(1)} %tile.7.refs_0_, bf16[512,384]{1,0:T(8,128)(2,1)S(1)} %collective-permute-done.10.refs_3_.refs_1_, ...), custom_call_target="tpu_custom_call" | custom-call | tf_op jit(solution)/shard_map/tile/pallas_call | solution.py:259
  44.1 0.3 collective-permute-start.13
  44.4 2.6 %tile.6 = bf16[512,256]{1,0:T(8,128)(2,1)S(1)} custom-call(bf16[128,128]{1,0:T(8,128)(2,1)S(1)} %copy-done, bf16[512,384]{1,0:T(8,128)(2,1)S(1)} %collective-permute-done.7.rows_ref, bf16[512,384]{1,0:T(8,128)(2,1)S(1)} %constant_dynamic-update-slice_fusion.refs_0_, bf16[512,384]{1,0:T(8,128)(2,1)S(1)} %collective-permute-done.5.refs_1_, ...), custom_call_target="tpu_custom_call" | custom-call | tf_op jit(solution)/shard_map/tile/pallas_call | solution.py:259
  47.0 0.2 collective-permute-start.12
  47.2 2.6 %tile.9 = bf16[512,256]{1,0:T(8,128)(2,1)S(1)} custom-call(bf16[128,128]{1,0:T(8,128)(2,1)S(1)} %copy-done, bf16[512,384]{1,0:T(8,128)(2,1)S(1)} %collective-permute-done.9.rows_ref, bf16[512,384]{1,0:T(8,128)(2,1)S(1)} %constant_dynamic-update-slice_fusion.refs_0_, bf16[512,384]{1,0:T(8,128)(2,1)S(1)} %collective-permute-done.5.refs_1_, ...), custom_call_target="tpu_custom_call" | custom-call | tf_op jit(solution)/shard_map/tile/pallas_call | solution.py:259
  49.8 2.6 %collective-permute-start.14 = (bf16[512,256]{1,0:T(8,128)(2,1)S(1)}, bf16[512,256]{1,0:T(8,128)(2,1)S(1)}, u32[]{:S(2)}, u32[]{:S(2)}) collective-permute-start(bf16[512,256]{1,0:T(8,128)(2,1)S(1)} %tile.9), channel_id=1, source_target_pairs={{0,3},{1,0},{2,1},{3,2},{4,7},{5,4},{6,5},{7,6},{8,11},{9,8},{10,9... | collective-permute-start | bytes 786440 | tf_op jit(solution)/shard_map/ppermute | solution.py:202
  52.4 2.6 %tile.5.refs_0_ = f32[512,256]{1,0:T(8,128)S(1)} custom-call(bf16[128,128]{1,0:T(8,128)(2,1)S(1)} %copy-done, bf16[512,384]{1,0:T(8,128)(2,1)S(1)} %get-tuple-element.34.rows_ref, bf16[512,384]{1,0:T(8,128)(2,1)S(1)} %constant_dynamic-update-slice_fusion.refs_0_, bf16[512,384]{1,0:T(8,128)(2,1)S(1)} %collective-permute-done.5.refs_1_, ...), custom_call_target="tpu_custom_call" | custom-call | tf_op jit(solution)/shard_map/tile/pallas_call | solution.py:259
  54.9 1.4 %collective-permute-done.14.refs_3_ = bf16[512,256]{1,0:T(8,128)(2,1)S(1)} collective-permute-done((bf16[512,256]{1,0:T(8,128)(2,1)S(1)}, bf16[512,256]{1,0:T(8,128)(2,1)S(1)}, u32[]{:S(2)}, u32[]{:S(2)}) %collective-permute-start.14) | collective-permute-done | bytes 262176 | tf_op jit(solution)/shard_map/ppermute | solution.py:202
  56.4 1.2 %sum_rows.1 = (bf16[512,256]{1,0:T(8,128)(2,1)}, f32[128,256]{1,0:T(8,128)S(1)}, bf16[128,256]{1,0:T(8,128)(2,1)S(1)}, bf16[128,256]{1,0:T(8,128)(2,1)S(1)}, bf16[128,256]{1,0:T(8,128)(2,1)S(1)}) custom-call(f32[512,256]{1,0:T(8,128)S(1)} %tile.5.refs_0_, bf16[512,256]{1,0:T(8,128)(2,1)S(1)} %collective-permute-done.12.refs_1_, ...), custom_call_target="tpu_custom_call" | custom-call | tf_op jit(solution)/shard_map/sum_rows/pallas_call | solution.py:276
  57.6 4.6 %all-to-all-start = ((bf16[16,32,256]{2,1,0:T(8,128)(2,1)}), bf16[16,32,256]{2,1,0:T(8,128)(2,1)S(1)}, u32[]{:S(2)}, u32[]{:S(2)}) async-start(bf16[16,32,256]{2,1,0:T(8,128)(2,1)} %bitcast.3), calls=%async_computation | async-start | bytes 524288 | tf_op jit(solution)/shard_map/all_to_all | solution.py:210
  62.2 1.4 %collective-permute-start.15 = (bf16[128,256]{1,0:T(8,128)(2,1)S(1)}, bf16[128,256]{1,0:T(8,128)(2,1)S(1)}, u32[]{:S(2)}, u32[]{:S(2)}) collective-permute-start(bf16[128,256]{1,0:T(8,128)(2,1)S(1)} %get-tuple-element.42), channel_id=1, source_target_pairs={{0,64},{1,65},{2,66},{3,67},{4,68},{5,69},{6,70},{7,71},{8,72},{9,... | collective-permute-start | bytes 196616 | tf_op jit(solution)/shard_map/ppermute | solution.py:202
  63.6 4.5 %collective-permute-done.15.b = bf16[128,256]{1,0:T(8,128)(2,1)S(1)} collective-permute-done((bf16[128,256]{1,0:T(8,128)(2,1)S(1)}, bf16[128,256]{1,0:T(8,128)(2,1)S(1)}, u32[]{:S(2)}, u32[]{:S(2)}) %collective-permute-start.15) | collective-permute-done | bytes 65568 | tf_op jit(solution)/shard_map/ppermute | solution.py:202
  68.1 1.7 %all-to-all-done.refs_0_ = bf16[16,32,256]{2,1,0:T(8,128)(2,1)S(1)} async-done(((bf16[16,32,256]{2,1,0:T(8,128)(2,1)}), bf16[16,32,256]{2,1,0:T(8,128)(2,1)S(1)}, u32[]{:S(2)}, u32[]{:S(2)}) %all-to-all-start) | async-done | bytes 262176 | tf_op jit(solution)/shard_map/all_to_all | solution.py:210
  69.8 3.6 %collective-permute-start.16 = (f32[1,32,256]{2,1,0:T(8,128)S(1)}, f32[1,32,256]{2,1,0:T(8,128)S(1)}, u32[]{:S(2)}, u32[]{:S(2)}) collective-permute-start(f32[1,32,256]{2,1,0:T(8,128)S(1)} %sum_spread.3.refs_0_), channel_id=1, source_target_pairs={{0,16},{16,0},{1,17},{17,1},{2,18},{18,2},{3,19},{19,3},{4,20},{20... | collective-permute-start | bytes 98312 | tf_op jit(solution)/shard_map/ppermute | solution.py:187
  73.4 0.9 collective-permute-done.16.refs_1_
  74.3 0.7 sum_spread.4
  75.0 5.9 %all-to-all-start.1 = ((f32[8,32,256]{2,1,0:T(8,128)}), f32[8,32,256]{2,1,0:T(8,128)S(1)}, u32[]{:S(2)}, u32[]{:S(2)}) async-start(f32[8,32,256]{2,1,0:T(8,128)} %sum_spread.4), calls=%async_computation.1 | async-start | bytes 524288 | tf_op jit(solution)/shard_map/all_to_all | solution.py:210
  80.9 1.0 collective-permute-start.17
  81.9 3.6 %collective-permute-done.17.c = bf16[128,256]{1,0:T(8,128)(2,1)S(1)} collective-permute-done((bf16[128,256]{1,0:T(8,128)(2,1)S(1)}, bf16[128,256]{1,0:T(8,128)(2,1)S(1)}, u32[]{:S(2)}, u32[]{:S(2)}) %collective-permute-start.17) | collective-permute-done | bytes 65568 | tf_op jit(solution)/shard_map/ppermute | solution.py:202
  85.5 6.6 %all-to-all-done.1.refs_0_ = f32[8,32,256]{2,1,0:T(8,128)S(1)} async-done(((f32[8,32,256]{2,1,0:T(8,128)}), f32[8,32,256]{2,1,0:T(8,128)S(1)}, u32[]{:S(2)}, u32[]{:S(2)}) %all-to-all-start.1) | async-done | bytes 262176 | tf_op jit(solution)/shard_map/all_to_all | solution.py:210
  92.1 0.7 sum_spread.5
  92.8 3.5 %all-to-all-start.2 = ((bf16[16,32,256]{2,1,0:T(8,128)(2,1)}), bf16[16,32,256]{2,1,0:T(8,128)(2,1)S(1)}, u32[]{:S(2)}, u32[]{:S(2)}) async-start(bf16[16,32,256]{2,1,0:T(8,128)(2,1)} %sum_spread.5), calls=%async_computation.2 | async-start | bytes 524288 | tf_op jit(solution)/shard_map/all_to_all | solution.py:210
  96.4 2.5 %collective-permute-start.18 = (bf16[128,256]{1,0:T(8,128)(2,1)S(1)}, bf16[128,256]{1,0:T(8,128)(2,1)S(1)}, u32[]{:S(2)}, u32[]{:S(2)}) collective-permute-start(bf16[128,256]{1,0:T(8,128)(2,1)S(1)} %get-tuple-element.53), channel_id=1, source_target_pairs={{0,192},{1,193},{2,194},{3,195},{4,196},{5,197},{6,198},{7,199},{8... | collective-permute-start | bytes 196616 | tf_op jit(solution)/shard_map/ppermute | solution.py:202
  98.9 2.1 %collective-permute-done.18.d = bf16[128,256]{1,0:T(8,128)(2,1)S(1)} collective-permute-done((bf16[128,256]{1,0:T(8,128)(2,1)S(1)}, bf16[128,256]{1,0:T(8,128)(2,1)S(1)}, u32[]{:S(2)}, u32[]{:S(2)}) %collective-permute-start.18) | collective-permute-done | bytes 65568 | tf_op jit(solution)/shard_map/ppermute | solution.py:202
  101.0 0.7 finish_rows.1
  101.7 2.3 %all-to-all-done.2 = bf16[16,32,256]{2,1,0:T(8,128)(2,1)S(1)} async-done(((bf16[16,32,256]{2,1,0:T(8,128)(2,1)}), bf16[16,32,256]{2,1,0:T(8,128)(2,1)S(1)}, u32[]{:S(2)}, u32[]{:S(2)}) %all-to-all-start.2) | async-done | bytes 262176 | tf_op jit(solution)/shard_map/all_to_all | solution.py:210
  104.0 0.8 convert_multiply_fusion
  (14 shorter events, 0.1 us)
Async XLA Ops:
  2.2 14.8 %collective-permute-start.3 = (bf16[128,896]{1,0:T(8,128)(2,1)S(1)}, bf16[128,896]{1,0:T(8,128)(2,1)S(1)}, u32[]{:S(2)}, u32[]{:S(2)}) collective-permute-start(bf16[128,896]{1,0:T(8,128)(2,1)S(1)} %get-tuple-element.30.refs_0_), channel_id=1, source_target_pairs={{0,64},{1,65},{2,66},{3,67},{4,68},{5,69},{6,70},{7,71},{8,72},{9,... | collective-permute-start | bytes 688136 | tf_op jit(solution)/shard_map/ppermute | solution.py:202
  4.3 12.7 %collective-permute-start.2 = (bf16[128,896]{1,0:T(8,128)(2,1)S(1)}, bf16[128,896]{1,0:T(8,128)(2,1)S(1)}, u32[]{:S(2)}, u32[]{:S(2)}) collective-permute-start(bf16[128,896]{1,0:T(8,128)(2,1)S(1)} %get-tuple-element.30.refs_0_), channel_id=1, source_target_pairs={{0,128},{1,129},{2,130},{3,131},{4,132},{5,133},{6,134},{7,135},{8... | collective-permute-start | bytes 688136 | tf_op jit(solution)/shard_map/ppermute | solution.py:202
  6.7 10.2 %collective-permute-start.1 = (bf16[128,896]{1,0:T(8,128)(2,1)S(1)}, bf16[128,896]{1,0:T(8,128)(2,1)S(1)}, u32[]{:S(2)}, u32[]{:S(2)}) collective-permute-start(bf16[128,896]{1,0:T(8,128)(2,1)S(1)} %get-tuple-element.30.refs_0_), channel_id=1, source_target_pairs={{0,192},{1,193},{2,194},{3,195},{4,196},{5,197},{6,198},{7,199},{8... | collective-permute-start | bytes 688136 | tf_op jit(solution)/shard_map/ppermute | solution.py:202
  7.9 9.0 %collective-permute-start = (bf16[128,384]{1,0:T(8,128)(2,1)S(1)}, bf16[128,384]{1,0:T(8,128)(2,1)S(1)}, u32[]{:S(2)}, u32[]{:S(2)}) collective-permute-start(bf16[128,384]{1,0:T(8,128)(2,1)S(1)} %get-tuple-element.29), channel_id=1, source_target_pairs={{0,32},{4,36},{8,40},{12,44},{32,0},{36,4},{40,8},{44,12},{1,33},{... | collective-permute-start | bytes 294920 | tf_op jit(solution)/shard_map/ppermute | solution.py:187
  17.0 6.3 %collective-permute-start.4 = (bf16[256,384]{1,0:T(8,128)(2,1)S(1)}, bf16[256,384]{1,0:T(8,128)(2,1)S(1)}, u32[]{:S(2)}, u32[]{:S(2)}) collective-permute-start(bf16[256,384]{1,0:T(8,128)(2,1)S(1)} %pad_maximum_fusion), channel_id=1, source_target_pairs={{0,16},{16,0},{1,17},{17,1},{2,18},{18,2},{3,19},{19,3},{4,20},{20... | collective-permute-start | bytes 589832 | tf_op jit(solution)/shard_map/ppermute | solution.py:187
  19.8 17.1 %collective-permute-start.9 = (bf16[512,384]{1,0:T(8,128)(2,1)S(1)}, bf16[512,384]{1,0:T(8,128)(2,1)S(1)}, u32[]{:S(2)}, u32[]{:S(2)}) collective-permute-start(bf16[512,384]{1,0:T(8,128)(2,1)S(1)} %get-tuple-element.34.rows_ref), channel_id=1, source_target_pairs={{0,1},{1,2},{2,3},{3,0},{4,5},{5,6},{6,7},{7,4},{8,9},{9,10},{10,1... | collective-permute-start | bytes 1179656 | tf_op jit(solution)/shard_map/ppermute | solution.py:202
  20.9 15.9 %collective-permute-start.8 = (bf16[512,384]{1,0:T(8,128)(2,1)S(1)}, bf16[512,384]{1,0:T(8,128)(2,1)S(1)}, u32[]{:S(2)}, u32[]{:S(2)}) collective-permute-start(bf16[512,384]{1,0:T(8,128)(2,1)S(1)} %get-tuple-element.34.rows_ref), channel_id=1, source_target_pairs={{0,2},{1,3},{2,0},{3,1},{4,6},{5,7},{6,4},{7,5},{8,10},{9,11},{10,... | collective-permute-start | bytes 1179656 | tf_op jit(solution)/shard_map/ppermute | solution.py:202
  22.4 14.4 %collective-permute-start.7 = (bf16[512,384]{1,0:T(8,128)(2,1)S(1)}, bf16[512,384]{1,0:T(8,128)(2,1)S(1)}, u32[]{:S(2)}, u32[]{:S(2)}) collective-permute-start(bf16[512,384]{1,0:T(8,128)(2,1)S(1)} %get-tuple-element.34.rows_ref), channel_id=1, source_target_pairs={{0,3},{1,0},{2,1},{3,2},{4,7},{5,4},{6,5},{7,6},{8,11},{9,8},{10,9... | collective-permute-start | bytes 1179656 | tf_op jit(solution)/shard_map/ppermute | solution.py:202
  23.3 17.9 %copy-start = (bf16[128,128]{1,0:T(8,128)(2,1)S(1)}, bf16[128,128]{1,0:T(8,128)(2,1)}, u32[]{:S(2)}) copy-start(bf16[128,128]{1,0:T(8,128)(2,1)} %constant.4.clone.table) | copy-start | bytes 98308
  23.4 13.4 %collective-permute-start.5 = (bf16[512,384]{1,0:T(8,128)(2,1)S(1)}, bf16[512,384]{1,0:T(8,128)(2,1)S(1)}, u32[]{:S(2)}, u32[]{:S(2)}) collective-permute-start(bf16[512,384]{1,0:T(8,128)(2,1)S(1)} %constant_dynamic-update-slice_fusion.refs_0_), channel_id=1, source_target_pairs={{0,4},{1,5},{2,6},{3,7},{4,8},{5,9},{6,10},{7,11},{8,12},{9,13},{1... | collective-permute-start | bytes 1179656 | tf_op jit(solution)/shard_map/ppermute | solution.py:202
  27.9 8.9 %collective-permute-start.6 = (bf16[256,384]{1,0:T(8,128)(2,1)S(1)}, bf16[256,384]{1,0:T(8,128)(2,1)S(1)}, u32[]{:S(2)}, u32[]{:S(2)}) collective-permute-start(bf16[256,384]{1,0:T(8,128)(2,1)S(1)} %pad_maximum_fusion), channel_id=1, source_target_pairs={{0,8},{1,9},{2,10},{3,11},{4,12},{5,13},{6,14},{7,15},{8,32},{9,33... | collective-permute-start | bytes 589832 | tf_op jit(solution)/shard_map/ppermute | solution.py:202
  36.9 6.1 %collective-permute-start.10 = (bf16[512,384]{1,0:T(8,128)(2,1)S(1)}, bf16[512,384]{1,0:T(8,128)(2,1)S(1)}, u32[]{:S(2)}, u32[]{:S(2)}) collective-permute-start(bf16[512,384]{1,0:T(8,128)(2,1)S(1)} %collective-permute-done.5.refs_1_), channel_id=1, source_target_pairs={{0,16},{16,0},{1,17},{17,1},{2,18},{18,2},{3,19},{19,3},{4,20},{20... | collective-permute-start | bytes 1179656 | tf_op jit(solution)/shard_map/ppermute | solution.py:187
  41.1 1.8 %collective-permute-start.11 = (bf16[256,384]{1,0:T(8,128)(2,1)S(1)}, bf16[256,384]{1,0:T(8,128)(2,1)S(1)}, u32[]{:S(2)}, u32[]{:S(2)}) collective-permute-start(bf16[256,384]{1,0:T(8,128)(2,1)S(1)} %collective-permute-done.6.refs_2_), channel_id=1, source_target_pairs={{0,16},{16,0},{1,17},{17,1},{2,18},{18,2},{3,19},{19,3},{4,20},{20... | collective-permute-start | bytes 589832 | tf_op jit(solution)/shard_map/ppermute | solution.py:187
  44.1 10.8 %collective-permute-start.13 = (bf16[512,256]{1,0:T(8,128)(2,1)S(1)}, bf16[512,256]{1,0:T(8,128)(2,1)S(1)}, u32[]{:S(2)}, u32[]{:S(2)}) collective-permute-start(bf16[512,256]{1,0:T(8,128)(2,1)S(1)} %tile.8), channel_id=1, source_target_pairs={{0,2},{1,3},{2,0},{3,1},{4,6},{5,7},{6,4},{7,5},{8,10},{9,11},{10,... | collective-permute-start | bytes 786440 | tf_op jit(solution)/shard_map/ppermute | solution.py:202
  47.0 8.0 %collective-permute-start.12 = (bf16[512,256]{1,0:T(8,128)(2,1)S(1)}, bf16[512,256]{1,0:T(8,128)(2,1)S(1)}, u32[]{:S(2)}, u32[]{:S(2)}) collective-permute-start(bf16[512,256]{1,0:T(8,128)(2,1)S(1)} %tile.6), channel_id=1, source_target_pairs={{0,1},{1,2},{2,3},{3,0},{4,5},{5,6},{6,7},{7,4},{8,9},{9,10},{10,1... | collective-permute-start | bytes 786440 | tf_op jit(solution)/shard_map/ppermute | solution.py:202
  49.8 6.6 %collective-permute-start.14 = (bf16[512,256]{1,0:T(8,128)(2,1)S(1)}, bf16[512,256]{1,0:T(8,128)(2,1)S(1)}, u32[]{:S(2)}, u32[]{:S(2)}) collective-permute-start(bf16[512,256]{1,0:T(8,128)(2,1)S(1)} %tile.9), channel_id=1, source_target_pairs={{0,3},{1,0},{2,1},{3,2},{4,7},{5,4},{6,5},{7,6},{8,11},{9,8},{10,9... | collective-permute-start | bytes 786440 | tf_op jit(solution)/shard_map/ppermute | solution.py:202
  57.6 12.2 %all-to-all-start = ((bf16[16,32,256]{2,1,0:T(8,128)(2,1)}), bf16[16,32,256]{2,1,0:T(8,128)(2,1)S(1)}, u32[]{:S(2)}, u32[]{:S(2)}) async-start(bf16[16,32,256]{2,1,0:T(8,128)(2,1)} %bitcast.3), calls=%async_computation | async-start | bytes 524288 | tf_op jit(solution)/shard_map/all_to_all | solution.py:210
  62.2 5.8 %collective-permute-start.15 = (bf16[128,256]{1,0:T(8,128)(2,1)S(1)}, bf16[128,256]{1,0:T(8,128)(2,1)S(1)}, u32[]{:S(2)}, u32[]{:S(2)}) collective-permute-start(bf16[128,256]{1,0:T(8,128)(2,1)S(1)} %get-tuple-element.42), channel_id=1, source_target_pairs={{0,64},{1,65},{2,66},{3,67},{4,68},{5,69},{6,70},{7,71},{8,72},{9,... | collective-permute-start | bytes 196616 | tf_op jit(solution)/shard_map/ppermute | solution.py:202
  69.8 4.5 %collective-permute-start.16 = (f32[1,32,256]{2,1,0:T(8,128)S(1)}, f32[1,32,256]{2,1,0:T(8,128)S(1)}, u32[]{:S(2)}, u32[]{:S(2)}) collective-permute-start(f32[1,32,256]{2,1,0:T(8,128)S(1)} %sum_spread.3.refs_0_), channel_id=1, source_target_pairs={{0,16},{16,0},{1,17},{17,1},{2,18},{18,2},{3,19},{19,3},{4,20},{20... | collective-permute-start | bytes 98312 | tf_op jit(solution)/shard_map/ppermute | solution.py:187
  75.0 17.1 %all-to-all-start.1 = ((f32[8,32,256]{2,1,0:T(8,128)}), f32[8,32,256]{2,1,0:T(8,128)S(1)}, u32[]{:S(2)}, u32[]{:S(2)}) async-start(f32[8,32,256]{2,1,0:T(8,128)} %sum_spread.4), calls=%async_computation.1 | async-start | bytes 524288 | tf_op jit(solution)/shard_map/all_to_all | solution.py:210
  80.9 4.6 %collective-permute-start.17 = (bf16[128,256]{1,0:T(8,128)(2,1)S(1)}, bf16[128,256]{1,0:T(8,128)(2,1)S(1)}, u32[]{:S(2)}, u32[]{:S(2)}) collective-permute-start(bf16[128,256]{1,0:T(8,128)(2,1)S(1)} %get-tuple-element.46), channel_id=1, source_target_pairs={{0,128},{1,129},{2,130},{3,131},{4,132},{5,133},{6,134},{7,135},{8... | collective-permute-start | bytes 196616 | tf_op jit(solution)/shard_map/ppermute | solution.py:202
  92.8 11.1 %all-to-all-start.2 = ((bf16[16,32,256]{2,1,0:T(8,128)(2,1)}), bf16[16,32,256]{2,1,0:T(8,128)(2,1)S(1)}, u32[]{:S(2)}, u32[]{:S(2)}) async-start(bf16[16,32,256]{2,1,0:T(8,128)(2,1)} %sum_spread.5), calls=%async_computation.2 | async-start | bytes 524288 | tf_op jit(solution)/shard_map/all_to_all | solution.py:210
  96.4 4.6 %collective-permute-start.18 = (bf16[128,256]{1,0:T(8,128)(2,1)S(1)}, bf16[128,256]{1,0:T(8,128)(2,1)S(1)}, u32[]{:S(2)}, u32[]{:S(2)}) collective-permute-start(bf16[128,256]{1,0:T(8,128)(2,1)S(1)} %get-tuple-element.53), channel_id=1, source_target_pairs={{0,192},{1,193},{2,194},{3,195},{4,196},{5,197},{6,198},{7,199},{8... | collective-permute-start | bytes 196616 | tf_op jit(solution)/shard_map/ppermute | solution.py:202

commit v7 on v6

--- a/solution.py
+++ b/solution.py
@@ -142,9 +142,9 @@
         out[block, :] = (acc[k] - row_total * u_rows[block].astype(F32)).astype(out.dtype)
 
 
-def sum_rows_kernel(count, *refs):
-    parts, (embeds, partial, own, *others) = refs[:count], refs[count:]
-    rows = own.shape[0]
+def sum_rows_kernel(count, core, *refs):
+    parts, (embeds, keep, send, own, *others, weight) = refs[:count], refs[count:]
+    rows, half = own.shape[0], keep.shape[0]
     total = parts[0][...]
     for ref in parts[1:]:
         total = total + ref[...].astype(F32)
@@ -153,20 +153,29 @@
     own[...] = total[:rows]
     for k, ref in enumerate(others):
         ref[...] = hi[(k + 1) * rows : (k + 2) * rows]
-    partial[...] = (dot_tn(embeds[...], hi) + dot_tn(embeds[...], lo)).astype(BF16)
+    weight[...] = dot_tn(embeds[...], hi) + dot_tn(embeds[...], lo)
+    keep[...] = weight[pl.ds(pl.multiple_of(core[0] * half, half), half), :]
+    send[...] = weight[pl.ds(pl.multiple_of((1 - core[0]) * half, half), half), :]
+
+
+def add_halves_kernel(a, b, out):
+    out[...] = (a[...] + b[...]).astype(out.dtype)
+
+
+def join_halves_kernel(scale, core, a, b, out):
+    half = a.shape[0]
+    out[pl.ds(pl.multiple_of(core[0] * half, half), half), :] = a[...].astype(F32) * scale
+    out[pl.ds(pl.multiple_of((1 - core[0]) * half, half), half), :] = b[...].astype(F32) * scale
 
 
 def finish_rows_kernel(own, b, c, d, grad_rows):
     grad_rows[...] = (own[...] + b[...].astype(F32)) + (c[...].astype(F32) + d[...].astype(F32))
 
 
-def sum_spread_kernel(*refs):
-    *parts, out = refs
-    total = None
-    for ref in parts:
-        for k in range(ref.shape[0]):
-            term = ref[k].astype(F32)
-            total = term if total is None else total + term
+def sum_spread_kernel(parts, out):
+    total = parts[0].astype(F32)
+    for k in range(1, parts.shape[0]):
+        total = total + parts[k].astype(F32)
     low = total.astype(out.dtype)
     for k in range(out.shape[0]):
         out[k] = low
@@ -175,12 +184,12 @@
 def sum_spread(parts, copies, dtype):
     return pl.pallas_call(
         sum_spread_kernel,
-        out_shape=jax.ShapeDtypeStruct((copies,) + parts[0].shape[1:], dtype),
-        in_specs=[VMEM] * len(parts),
+        out_shape=jax.ShapeDtypeStruct((copies,) + parts.shape[1:], dtype),
+        in_specs=[VMEM],
         out_specs=VMEM,
         compiler_params=params(16),
         name="sum_spread",
-    )(*parts)
+    )(parts)
 
 
 def ring(array, axis, size, shift):
@@ -247,9 +256,10 @@
     pair = jnp.concatenate([pack, ring(pack, DEPTH, n_z, n_z // 2)], axis=0)
     pair, line = lax.optimization_barrier((pair, line))
     four = jnp.concatenate([pair, ring(pair, "core", 2, 1)], axis=0)
-    near = move(four, sizes, lambda core: {"z": 1 - 2 * core})
+    four, line = lax.optimization_barrier((four, line))
     far = move(pair, sizes, lambda core: {"z": 2 - 4 * core})
     lines = [line] + [turn(line, sizes, 1, -d) for d in range(1, n_side)]
+    near = move(four, sizes, lambda core: {"z": 1 - 2 * core})
     near, far, lines = lax.optimization_barrier((near, far, lines))
     columns = [four, near, far, ring(near, "core", 2, 1), ring(far, "core", 2, 1)]
 
@@ -273,29 +283,40 @@
             part = tile(lines[d], columns, F32 if d == 0 else BF16)
         back[d] = part if d == 0 else turn(part, sizes, 1, d)
 
-    partial, own_rows, *other_rows = pl.pallas_call(
+    core = lax.axis_index("core")[None]
+    scalar = pl.BlockSpec(memory_space=pltpu.SMEM)
+    half = embeds.shape[1] // 2
+    keep, send, own_rows, *other_rows = pl.pallas_call(
         functools.partial(sum_rows_kernel, n_side),
-        out_shape=[
-            jax.ShapeDtypeStruct((embeds.shape[1], width), BF16),
-            jax.ShapeDtypeStruct((rows, width), F32),
-        ]
+        out_shape=[jax.ShapeDtypeStruct((half, width), F32)] * 2
+        + [jax.ShapeDtypeStruct((rows, width), F32)]
         + [jax.ShapeDtypeStruct((rows, width), BF16)] * (n_side - 1),
-        in_specs=[VMEM] * (n_side + 1),
-        out_specs=[VMEM] * (n_side + 1),
+        in_specs=[scalar] + [VMEM] * (n_side + 1),
+        out_specs=[VMEM] * (n_side + 2),
+        scratch_shapes=[pltpu.VMEM((2 * half, width), F32)],
         compiler_params=params(16),
         name="sum_rows",
-    )(*(back[d] for d in range(n_side)), embeds_line)
-    arrived = [turn(other_rows[0], sizes, 0, 1)]
+    )(core, *(back[d] for d in range(n_side)), embeds_line)
+    partial = pl.pallas_call(
+        add_halves_kernel,
+        out_shape=jax.ShapeDtypeStruct((half, width), BF16),
+        in_specs=[VMEM] * 2,
+        out_specs=VMEM,
+        compiler_params=params(16),
+        name="add_halves",
+    )(keep, ring(send, "core", 2, 1))
+    partial, other_rows[0] = lax.optimization_barrier((partial, other_rows[0]))
+
     n_plane = n_side * n_side
     pieces = exchange(partial.reshape(n_plane, -1, width), PLANE)
+    arrived = [turn(other_rows[0], sizes, 0, 1)]
     pieces, arrived[0] = lax.optimization_barrier((pieces, arrived[0]))
-    piece = sum_spread([pieces], 1, F32)
-    spread = sum_spread([piece, ring(piece, "core", 2, 1)], n_z, F32)
+    spread = sum_spread(pieces, n_z, F32)
     spread, other_rows[1] = lax.optimization_barrier((spread, other_rows[1]))
     pieces = exchange(spread, DEPTH)
     arrived.append(turn(other_rows[1], sizes, 0, 2))
     pieces, arrived[1] = lax.optimization_barrier((pieces, arrived[1]))
-    spread = sum_spread([pieces], n_plane, BF16)
+    spread = sum_spread(pieces, n_plane, BF16)
     spread, other_rows[2] = lax.optimization_barrier((spread, other_rows[2]))
     pieces = exchange(spread, PLANE)
     arrived.append(turn(other_rows[2], sizes, 0, 3))
@@ -308,8 +329,15 @@
         name="finish_rows",
     )(own_rows, *arrived)
     pieces, grad_rows = lax.optimization_barrier((pieces, grad_rows))
-    total_points = rows * n_plane * n_z * 2
-    grad_weight = pieces.reshape(-1, width).astype(F32) * (1.0 / math.sqrt(total_points))
+    pieces = pieces.reshape(half, width)
+    grad_weight = pl.pallas_call(
+        functools.partial(join_halves_kernel, 1.0 / math.sqrt(rows * n_plane * n_z * 2)),
+        out_shape=jax.ShapeDtypeStruct((2 * half, width), F32),
+        in_specs=[scalar] + [VMEM] * 2,
+        out_specs=VMEM,
+        compiler_params=params(16),
+        name="join_halves",
+    )(core, pieces, ring(pieces, "core", 2, 1))
     return grad_rows, grad_weight
 
 

time: 106 us -> 107 us (level)
  starting transfers between devices: 55.6 us -> 59.1 us
  waiting for transfers between devices: 32 us -> 29.4 us
  Pallas kernels: 15.5 us -> 17.3 us
    all_to_all x3, waiting for transfers between devices: 10.6 us -> 6.52 us  [exchange(): return lax.all_to_all(array, axes, split_axis=0, concat_axis=0, tiled=True)]
    ppermute x5 -> x6, starting transfers between devices: 17.6 us -> 20.1 us  [ring(): lax.ppermute(array, axis, [(i, (i + shift) % size) for i in range(size)])]
    ppermute x5 -> x6, waiting for transfers between devices: 2.97 us -> 5.33 us  [ring(): lax.ppermute(array, axis, [(i, (i + shift) % size) for i in range(size)])]
    pallas_call x0 -> x2, Pallas kernels: none -> 1.51 us  [the longest x1 0.83 us: shards(): pl.pallas_call(functools.partial(join_halves_kernel, 1.0 / math.sqrt(rows...]
  transfers between devices with their start and end apart: 22 -> 23, of which waited for: 10 -> 12; matrix products, arithmetic and copies ran while one was open for 0% -> 0% of each run, Pallas kernels for 10% -> 9%
where the time goes in v7:
time: 107 us
  starting transfers between devices  59.1 us (55%)
  waiting for transfers between devices  29.4 us (27%)
  Pallas kernels  17.3 us (16%)
    ppermute x14, starting transfers between devices, move(): return lax.ppermute(array, ALL, perm)  24.3 us
    ppermute x6, starting transfers between devices, ring(): lax.ppermute(array, axis, [(i, (i + shift) % size) for i in range(size)])  20.1 us
    ppermute x14, waiting for transfers between devices, move(): return lax.ppermute(array, ALL, perm)  17.5 us
    all_to_all x3, starting transfers between devices, exchange(): return lax.all_to_all(array, axes, split_axis=0, concat_axis=0, tiled=True)  14.7 us
    pallas_call x5, Pallas kernels, tile(): pl.pallas_call(functools.partial(tile_kernel, 256, 256, start is not None...  10.5 us
    all_to_all x3, waiting for transfers between devices, exchange(): return lax.all_to_all(array, axes, split_axis=0, concat_axis=0, tiled=True)  6.52 us
    ppermute x6, waiting for transfers between devices, ring(): lax.ppermute(array, axis, [(i, (i + shift) % size) for i in range(size)])  5.33 us
  transfers between devices with their start and end apart: 23, of which 12 were waited for; matrix products, arithmetic and copies ran while one was open for 0% of the time, Pallas kernels for 9%

profile of v7, /device:TPU:1, one launch (start us, length us, event | category | flops | bytes accessed | tf_op | source)
XLA Modules:
  0.0 106.7 jit_solution(1131688985960625291)
XLA Ops:
  0.6 1.5 %pack.1 = (bf16[128,384]{1,0:T(8,128)(2,1)S(1)}, bf16[128,896]{1,0:T(8,128)(2,1)S(1)}) custom-call(bf16[128,512]{1,0:T(8,128)(2,1)} %embeds.1, bf16[512,256]{1,0:T(8,128)(2,1)} %weight.1, f32[1,128]{1,0:T(1,128)} %bitcast.10, f32[15,128]{1,0:T(8,128)} %bitcast.8, f32[15,128]{1,0:T(8,128)} %bitcast.9), custom_call_target="tpu_custom_call" | custom-call | tf_op jit(solution)/shard_map/pack/pallas_call | solution.py:225
  2.2 2.1 %collective-permute-start.3 = (bf16[128,896]{1,0:T(8,128)(2,1)S(1)}, bf16[128,896]{1,0:T(8,128)(2,1)S(1)}, u32[]{:S(2)}, u32[]{:S(2)}) collective-permute-start(bf16[128,896]{1,0:T(8,128)(2,1)S(1)} %get-tuple-element.35.refs_0_), channel_id=1, source_target_pairs={{0,64},{1,65},{2,66},{3,67},{4,68},{5,69},{6,70},{7,71},{8,72},{9,... | collective-permute-start | bytes 688136 | tf_op jit(solution)/shard_map/ppermute | solution.py:211
  4.3 2.5 %collective-permute-start.2 = (bf16[128,896]{1,0:T(8,128)(2,1)S(1)}, bf16[128,896]{1,0:T(8,128)(2,1)S(1)}, u32[]{:S(2)}, u32[]{:S(2)}) collective-permute-start(bf16[128,896]{1,0:T(8,128)(2,1)S(1)} %get-tuple-element.35.refs_0_), channel_id=1, source_target_pairs={{0,128},{1,129},{2,130},{3,131},{4,132},{5,133},{6,134},{7,135},{8... | collective-permute-start | bytes 688136 | tf_op jit(solution)/shard_map/ppermute | solution.py:211
  6.7 1.2 %collective-permute-start.1 = (bf16[128,896]{1,0:T(8,128)(2,1)S(1)}, bf16[128,896]{1,0:T(8,128)(2,1)S(1)}, u32[]{:S(2)}, u32[]{:S(2)}) collective-permute-start(bf16[128,896]{1,0:T(8,128)(2,1)S(1)} %get-tuple-element.35.refs_0_), channel_id=1, source_target_pairs={{0,192},{1,193},{2,194},{3,195},{4,196},{5,197},{6,198},{7,199},{8... | collective-permute-start | bytes 688136 | tf_op jit(solution)/shard_map/ppermute | solution.py:211
  7.9 6.9 %collective-permute-start = (bf16[128,384]{1,0:T(8,128)(2,1)S(1)}, bf16[128,384]{1,0:T(8,128)(2,1)S(1)}, u32[]{:S(2)}, u32[]{:S(2)}) collective-permute-start(bf16[128,384]{1,0:T(8,128)(2,1)S(1)} %get-tuple-element.34), channel_id=1, source_target_pairs={{0,32},{4,36},{8,40},{12,44},{32,0},{36,4},{40,8},{44,12},{1,33},{... | collective-permute-start | bytes 294920 | tf_op jit(solution)/shard_map/ppermute | solution.py:196
  14.8 2.1 %collective-permute-done = bf16[128,384]{1,0:T(8,128)(2,1)S(1)} collective-permute-done((bf16[128,384]{1,0:T(8,128)(2,1)S(1)}, bf16[128,384]{1,0:T(8,128)(2,1)S(1)}, u32[]{:S(2)}, u32[]{:S(2)}) %collective-permute-start) | collective-permute-done | bytes 98336 | tf_op jit(solution)/shard_map/ppermute | solution.py:196
  17.0 0.1 split.1
  17.1 2.7 %collective-permute-start.4 = (bf16[256,384]{1,0:T(8,128)(2,1)S(1)}, bf16[256,384]{1,0:T(8,128)(2,1)S(1)}, u32[]{:S(2)}, u32[]{:S(2)}) collective-permute-start(bf16[256,384]{1,0:T(8,128)(2,1)S(1)} %pad_maximum_fusion.1), channel_id=1, source_target_pairs={{0,16},{16,0},{1,17},{17,1},{2,18},{18,2},{3,19},{19,3},{4,20},{20... | collective-permute-start | bytes 589832 | tf_op jit(solution)/shard_map/ppermute | solution.py:196
  19.8 1.1 %collective-permute-done.4 = bf16[256,384]{1,0:T(8,128)(2,1)S(1)} collective-permute-done((bf16[256,384]{1,0:T(8,128)(2,1)S(1)}, bf16[256,384]{1,0:T(8,128)(2,1)S(1)}, u32[]{:S(2)}, u32[]{:S(2)}) %collective-permute-start.4) | collective-permute-done | bytes 196640 | tf_op jit(solution)/shard_map/ppermute | solution.py:196
  20.9 1.2 %collective-permute-start.9 = (bf16[512,384]{1,0:T(8,128)(2,1)S(1)}, bf16[512,384]{1,0:T(8,128)(2,1)S(1)}, u32[]{:S(2)}, u32[]{:S(2)}) collective-permute-start(bf16[512,384]{1,0:T(8,128)(2,1)S(1)} %get-tuple-element.41.rows_ref), channel_id=1, source_target_pairs={{0,1},{1,2},{2,3},{3,0},{4,5},{5,6},{6,7},{7,4},{8,9},{9,10},{10,1... | collective-permute-start | bytes 1179656 | tf_op jit(solution)/shard_map/ppermute | solution.py:211
  22.1 1.8 %collective-permute-start.8 = (bf16[512,384]{1,0:T(8,128)(2,1)S(1)}, bf16[512,384]{1,0:T(8,128)(2,1)S(1)}, u32[]{:S(2)}, u32[]{:S(2)}) collective-permute-start(bf16[512,384]{1,0:T(8,128)(2,1)S(1)} %get-tuple-element.41.rows_ref), channel_id=1, source_target_pairs={{0,2},{1,3},{2,0},{3,1},{4,6},{5,7},{6,4},{7,5},{8,10},{9,11},{10,... | collective-permute-start | bytes 1179656 | tf_op jit(solution)/shard_map/ppermute | solution.py:211
  23.9 0.7 collective-permute-start.7
  24.6 4.3 %collective-permute-start.5 = (bf16[512,384]{1,0:T(8,128)(2,1)S(1)}, bf16[512,384]{1,0:T(8,128)(2,1)S(1)}, u32[]{:S(2)}, u32[]{:S(2)}) collective-permute-start(bf16[512,384]{1,0:T(8,128)(2,1)S(1)} %pad_maximum_fusion.refs_0_), channel_id=1, source_target_pairs={{0,4},{1,5},{2,6},{3,7},{4,8},{5,9},{6,10},{7,11},{8,12},{9,13},{1... | collective-permute-start | bytes 1179656 | tf_op jit(solution)/shard_map/ppermute | solution.py:211
  28.9 2.3 %collective-permute-start.6 = (bf16[256,384]{1,0:T(8,128)(2,1)S(1)}, bf16[256,384]{1,0:T(8,128)(2,1)S(1)}, u32[]{:S(2)}, u32[]{:S(2)}) collective-permute-start(bf16[256,384]{1,0:T(8,128)(2,1)S(1)} %pad_maximum_fusion.1), channel_id=1, source_target_pairs={{0,8},{1,9},{2,10},{3,11},{4,12},{5,13},{6,14},{7,15},{8,32},{9,33... | collective-permute-start | bytes 589832 | tf_op jit(solution)/shard_map/ppermute | solution.py:211
  31.2 6.6 %collective-permute-done.6.refs_2_ = bf16[256,384]{1,0:T(8,128)(2,1)S(1)} collective-permute-done((bf16[256,384]{1,0:T(8,128)(2,1)S(1)}, bf16[256,384]{1,0:T(8,128)(2,1)S(1)}, u32[]{:S(2)}, u32[]{:S(2)}) %collective-permute-start.6) | collective-permute-done | bytes 196640 | tf_op jit(solution)/shard_map/ppermute | solution.py:211
  37.9 4.6 %collective-permute-start.10 = (bf16[512,384]{1,0:T(8,128)(2,1)S(1)}, bf16[512,384]{1,0:T(8,128)(2,1)S(1)}, u32[]{:S(2)}, u32[]{:S(2)}) collective-permute-start(bf16[512,384]{1,0:T(8,128)(2,1)S(1)} %collective-permute-done.5.refs_1_), channel_id=1, source_target_pairs={{0,16},{16,0},{1,17},{17,1},{2,18},{18,2},{3,19},{19,3},{4,20},{20... | collective-permute-start | bytes 1179656 | tf_op jit(solution)/shard_map/ppermute | solution.py:196
  42.5 0.1 collective-permute-start.11
  42.6 1.7 %tile.7.refs_0_ = f32[512,256]{1,0:T(8,128)S(1)} custom-call(bf16[128,128]{1,0:T(8,128)(2,1)S(1)} %copy-done, bf16[512,384]{1,0:T(8,128)(2,1)S(1)} %collective-permute-done.8.rows_ref, bf16[512,384]{1,0:T(8,128)(2,1)S(1)} %pad_maximum_fusion.refs_0_, bf16[512,384]{1,0:T(8,128)(2,1)S(1)} %collective-permute-done.5.refs_1_, ...), custom_call_target="tpu_custom_call" | custom-call | tf_op jit(solution)/shard_map/tile/pallas_call | solution.py:269
  44.3 1.1 %tile.8 = bf16[512,256]{1,0:T(8,128)(2,1)S(1)} custom-call(bf16[128,128]{1,0:T(8,128)(2,1)S(1)} %copy-done, bf16[512,384]{1,0:T(8,128)(2,1)S(1)} %collective-permute-done.8.rows_ref, f32[512,256]{1,0:T(8,128)S(1)} %tile.7.refs_0_, bf16[512,384]{1,0:T(8,128)(2,1)S(1)} %collective-permute-done.10.refs_3_.refs_1_, ...), custom_call_target="tpu_custom_call" | custom-call | tf_op jit(solution)/shard_map/tile/pallas_call | solution.py:269
  45.4 0.3 collective-permute-start.13
  45.7 2.6 %tile.6 = bf16[512,256]{1,0:T(8,128)(2,1)S(1)} custom-call(bf16[128,128]{1,0:T(8,128)(2,1)S(1)} %copy-done, bf16[512,384]{1,0:T(8,128)(2,1)S(1)} %collective-permute-done.7.rows_ref, bf16[512,384]{1,0:T(8,128)(2,1)S(1)} %pad_maximum_fusion.refs_0_, bf16[512,384]{1,0:T(8,128)(2,1)S(1)} %collective-permute-done.5.refs_1_, ...), custom_call_target="tpu_custom_call" | custom-call | tf_op jit(solution)/shard_map/tile/pallas_call | solution.py:269
  48.3 0.2 collective-permute-start.12
  48.5 2.6 %tile.9 = bf16[512,256]{1,0:T(8,128)(2,1)S(1)} custom-call(bf16[128,128]{1,0:T(8,128)(2,1)S(1)} %copy-done, bf16[512,384]{1,0:T(8,128)(2,1)S(1)} %collective-permute-done.9.rows_ref, bf16[512,384]{1,0:T(8,128)(2,1)S(1)} %pad_maximum_fusion.refs_0_, bf16[512,384]{1,0:T(8,128)(2,1)S(1)} %collective-permute-done.5.refs_1_, ...), custom_call_target="tpu_custom_call" | custom-call | tf_op jit(solution)/shard_map/tile/pallas_call | solution.py:269
  51.1 2.6 %collective-permute-start.14 = (bf16[512,256]{1,0:T(8,128)(2,1)S(1)}, bf16[512,256]{1,0:T(8,128)(2,1)}, u32[]{:S(2)}, u32[]{:S(2)}) collective-permute-start(bf16[512,256]{1,0:T(8,128)(2,1)S(1)} %tile.9), channel_id=1, source_target_pairs={{0,3},{1,0},{2,1},{3,2},{4,7},{5,4},{6,5},{7,6},{8,11},{9,8},{10,9... | collective-permute-start | bytes 786440 | tf_op jit(solution)/shard_map/ppermute | solution.py:211
  53.7 2.6 %tile.5.refs_0_ = f32[512,256]{1,0:T(8,128)S(1)} custom-call(bf16[128,128]{1,0:T(8,128)(2,1)S(1)} %copy-done, bf16[512,384]{1,0:T(8,128)(2,1)S(1)} %get-tuple-element.41.rows_ref, bf16[512,384]{1,0:T(8,128)(2,1)S(1)} %pad_maximum_fusion.refs_0_, bf16[512,384]{1,0:T(8,128)(2,1)S(1)} %collective-permute-done.5.refs_1_, ...), custom_call_target="tpu_custom_call" | custom-call | tf_op jit(solution)/shard_map/tile/pallas_call | solution.py:269
  56.3 1.5 %collective-permute-done.14.refs_3_ = bf16[512,256]{1,0:T(8,128)(2,1)} collective-permute-done((bf16[512,256]{1,0:T(8,128)(2,1)S(1)}, bf16[512,256]{1,0:T(8,128)(2,1)}, u32[]{:S(2)}, u32[]{:S(2)}) %collective-permute-start.14) | collective-permute-done | bytes 262176 | tf_op jit(solution)/shard_map/ppermute | solution.py:211
  57.8 1.6 %sum_rows.1 = (f32[256,256]{1,0:T(8,128)S(1)}, f32[256,256]{1,0:T(8,128)S(1)}, f32[128,256]{1,0:T(8,128)S(1)}, bf16[128,256]{1,0:T(8,128)(2,1)S(1)}, bf16[128,25...) custom-call(s32[1]{0:T(128)} %bitcast.core, f32[512,256]{1,0:T(8,128)S(1)} %tile.5.refs_0_, ...), custom_call_target="tpu_custom_call" | custom-call | tf_op jit(solution)/shard_map/sum_rows/pallas_call | solution.py:289
  59.4 1.6 %collective-permute-start.15 = (f32[256,256]{1,0:T(8,128)S(1)}, f32[256,256]{1,0:T(8,128)S(1)}, u32[]{:S(2)}, u32[]{:S(2)}) collective-permute-start(f32[256,256]{1,0:T(8,128)S(1)} %get-tuple-element.49), channel_id=1, source_target_pairs={{0,16},{16,0},{1,17},{17,1},{2,18},{18,2},{3,19},{19,3},{4,20},{20... | collective-permute-start | bytes 786440 | tf_op jit(solution)/shard_map/ppermute | solution.py:196
  61.1 1.2 %collective-permute-done.15.b = f32[256,256]{1,0:T(8,128)S(1)} collective-permute-done((f32[256,256]{1,0:T(8,128)S(1)}, f32[256,256]{1,0:T(8,128)S(1)}, u32[]{:S(2)}, u32[]{:S(2)}) %collective-permute-start.15) | collective-permute-done | bytes 262176 | tf_op jit(solution)/shard_map/ppermute | solution.py:196
  62.2 0.7 add_halves.1
  62.9 5.1 %all-to-all-start = ((bf16[16,16,256]{2,1,0:T(8,128)(2,1)}), bf16[16,16,256]{2,1,0:T(8,128)(2,1)S(1)}, u32[]{:S(2)}, u32[]{:S(2)}) async-start(bf16[16,16,256]{2,1,0:T(8,128)(2,1)} %bitcast.4), calls=%async_computation | async-start | bytes 262144 | tf_op jit(solution)/shard_map/all_to_all | solution.py:219
  68.0 1.4 %collective-permute-start.16 = (bf16[128,256]{1,0:T(8,128)(2,1)S(1)}, bf16[128,256]{1,0:T(8,128)(2,1)S(1)}, u32[]{:S(2)}, u32[]{:S(2)}) collective-permute-start(bf16[128,256]{1,0:T(8,128)(2,1)S(1)} %get-tuple-element.52), channel_id=1, source_target_pairs={{0,64},{1,65},{2,66},{3,67},{4,68},{5,69},{6,70},{7,71},{8,72},{9,... | collective-permute-start | bytes 196616 | tf_op jit(solution)/shard_map/ppermute | solution.py:211
  69.4 4.6 %collective-permute-done.16.b = bf16[128,256]{1,0:T(8,128)(2,1)S(1)} collective-permute-done((bf16[128,256]{1,0:T(8,128)(2,1)S(1)}, bf16[128,256]{1,0:T(8,128)(2,1)S(1)}, u32[]{:S(2)}, u32[]{:S(2)}) %collective-permute-start.16) | collective-permute-done | bytes 65568 | tf_op jit(solution)/shard_map/ppermute | solution.py:211
  74.0 0.9 all-to-all-done.parts
  74.8 0.7 sum_spread.2
  75.5 5.8 %all-to-all-start.1 = ((f32[8,16,256]{2,1,0:T(8,128)}), f32[8,16,256]{2,1,0:T(8,128)S(1)}, u32[]{:S(2)}, u32[]{:S(2)}) async-start(f32[8,16,256]{2,1,0:T(8,128)} %sum_spread.2), calls=%async_computation.1 | async-start | bytes 262144 | tf_op jit(solution)/shard_map/all_to_all | solution.py:219
  81.3 1.2 %collective-permute-start.17 = (bf16[128,256]{1,0:T(8,128)(2,1)S(1)}, bf16[128,256]{1,0:T(8,128)(2,1)S(1)}, u32[]{:S(2)}, u32[]{:S(2)}) collective-permute-start(bf16[128,256]{1,0:T(8,128)(2,1)S(1)} %get-tuple-element.56), channel_id=1, source_target_pairs={{0,128},{1,129},{2,130},{3,131},{4,132},{5,133},{6,134},{7,135},{8... | collective-permute-start | bytes 196616 | tf_op jit(solution)/shard_map/ppermute | solution.py:211
  82.5 3.4 %collective-permute-done.17.c = bf16[128,256]{1,0:T(8,128)(2,1)S(1)} collective-permute-done((bf16[128,256]{1,0:T(8,128)(2,1)S(1)}, bf16[128,256]{1,0:T(8,128)(2,1)S(1)}, u32[]{:S(2)}, u32[]{:S(2)}) %collective-permute-start.17) | collective-permute-done | bytes 65568 | tf_op jit(solution)/shard_map/ppermute | solution.py:211
  85.9 3.4 %all-to-all-done.1.parts = f32[8,16,256]{2,1,0:T(8,128)S(1)} async-done(((f32[8,16,256]{2,1,0:T(8,128)}), f32[8,16,256]{2,1,0:T(8,128)S(1)}, u32[]{:S(2)}, u32[]{:S(2)}) %all-to-all-start.1) | async-done | bytes 131104 | tf_op jit(solution)/shard_map/all_to_all | solution.py:219
  89.3 0.7 sum_spread.3
  90.0 3.8 %all-to-all-start.2 = ((bf16[16,16,256]{2,1,0:T(8,128)(2,1)}), bf16[16,16,256]{2,1,0:T(8,128)(2,1)S(1)}, u32[]{:S(2)}, u32[]{:S(2)}) async-start(bf16[16,16,256]{2,1,0:T(8,128)(2,1)} %sum_spread.3), calls=%async_computation.2 | async-start | bytes 262144 | tf_op jit(solution)/shard_map/all_to_all | solution.py:219
  93.8 2.6 %collective-permute-start.18 = (bf16[128,256]{1,0:T(8,128)(2,1)S(1)}, bf16[128,256]{1,0:T(8,128)(2,1)S(1)}, u32[]{:S(2)}, u32[]{:S(2)}) collective-permute-start(bf16[128,256]{1,0:T(8,128)(2,1)S(1)} %get-tuple-element.63), channel_id=1, source_target_pairs={{0,192},{1,193},{2,194},{3,195},{4,196},{5,197},{6,198},{7,199},{8... | collective-permute-start | bytes 196616 | tf_op jit(solution)/shard_map/ppermute | solution.py:211
  96.4 1.3 %collective-permute-done.18.d = bf16[128,256]{1,0:T(8,128)(2,1)S(1)} collective-permute-done((bf16[128,256]{1,0:T(8,128)(2,1)S(1)}, bf16[128,256]{1,0:T(8,128)(2,1)S(1)}, u32[]{:S(2)}, u32[]{:S(2)}) %collective-permute-start.18) | collective-permute-done | bytes 65568 | tf_op jit(solution)/shard_map/ppermute | solution.py:211
  97.7 0.7 finish_rows.1
  98.4 2.2 %all-to-all-done.2 = bf16[16,16,256]{2,1,0:T(8,128)(2,1)S(1)} async-done(((bf16[16,16,256]{2,1,0:T(8,128)(2,1)}), bf16[16,16,256]{2,1,0:T(8,128)(2,1)S(1)}, u32[]{:S(2)}, u32[]{:S(2)}) %all-to-all-start.2) | async-done | bytes 131104 | tf_op jit(solution)/shard_map/all_to_all | solution.py:219
  100.7 4.2 %collective-permute-start.19 = (bf16[256,256]{1,0:T(8,128)(2,1)S(1)}, bf16[256,256]{1,0:T(8,128)(2,1)S(1)}, u32[]{:S(2)}, u32[]{:S(2)}) collective-permute-start(bf16[256,256]{1,0:T(8,128)(2,1)S(1)} %bitcast.6), channel_id=1, source_target_pairs={{0,16},{16,0},{1,17},{17,1},{2,18},{18,2},{3,19},{19,3},{4,20},{20... | collective-permute-start | bytes 393224 | tf_op jit(solution)/shard_map/ppermute | solution.py:196
  104.9 1.0 collective-permute-done.19.b
  105.9 0.8 join_halves.1
  (15 shorter events, 0.1 us)
Async XLA Ops:
  2.2 14.8 %collective-permute-start.3 = (bf16[128,896]{1,0:T(8,128)(2,1)S(1)}, bf16[128,896]{1,0:T(8,128)(2,1)S(1)}, u32[]{:S(2)}, u32[]{:S(2)}) collective-permute-start(bf16[128,896]{1,0:T(8,128)(2,1)S(1)} %get-tuple-element.35.refs_0_), channel_id=1, source_target_pairs={{0,64},{1,65},{2,66},{3,67},{4,68},{5,69},{6,70},{7,71},{8,72},{9,... | collective-permute-start | bytes 688136 | tf_op jit(solution)/shard_map/ppermute | solution.py:211
  4.3 12.7 %collective-permute-start.2 = (bf16[128,896]{1,0:T(8,128)(2,1)S(1)}, bf16[128,896]{1,0:T(8,128)(2,1)S(1)}, u32[]{:S(2)}, u32[]{:S(2)}) collective-permute-start(bf16[128,896]{1,0:T(8,128)(2,1)S(1)} %get-tuple-element.35.refs_0_), channel_id=1, source_target_pairs={{0,128},{1,129},{2,130},{3,131},{4,132},{5,133},{6,134},{7,135},{8... | collective-permute-start | bytes 688136 | tf_op jit(solution)/shard_map/ppermute | solution.py:211
  6.7 10.2 %collective-permute-start.1 = (bf16[128,896]{1,0:T(8,128)(2,1)S(1)}, bf16[128,896]{1,0:T(8,128)(2,1)S(1)}, u32[]{:S(2)}, u32[]{:S(2)}) collective-permute-start(bf16[128,896]{1,0:T(8,128)(2,1)S(1)} %get-tuple-element.35.refs_0_), channel_id=1, source_target_pairs={{0,192},{1,193},{2,194},{3,195},{4,196},{5,197},{6,198},{7,199},{8... | collective-permute-start | bytes 688136 | tf_op jit(solution)/shard_map/ppermute | solution.py:211
  7.9 9.0 %collective-permute-start = (bf16[128,384]{1,0:T(8,128)(2,1)S(1)}, bf16[128,384]{1,0:T(8,128)(2,1)S(1)}, u32[]{:S(2)}, u32[]{:S(2)}) collective-permute-start(bf16[128,384]{1,0:T(8,128)(2,1)S(1)} %get-tuple-element.34), channel_id=1, source_target_pairs={{0,32},{4,36},{8,40},{12,44},{32,0},{36,4},{40,8},{44,12},{1,33},{... | collective-permute-start | bytes 294920 | tf_op jit(solution)/shard_map/ppermute | solution.py:196
  17.0 25.5 %copy-start = (bf16[128,128]{1,0:T(8,128)(2,1)S(1)}, bf16[128,128]{1,0:T(8,128)(2,1)}, u32[]{:S(2)}) copy-start(bf16[128,128]{1,0:T(8,128)(2,1)} %constant.8.clone.table) | copy-start | bytes 98308
  17.1 3.8 %collective-permute-start.4 = (bf16[256,384]{1,0:T(8,128)(2,1)S(1)}, bf16[256,384]{1,0:T(8,128)(2,1)S(1)}, u32[]{:S(2)}, u32[]{:S(2)}) collective-permute-start(bf16[256,384]{1,0:T(8,128)(2,1)S(1)} %pad_maximum_fusion.1), channel_id=1, source_target_pairs={{0,16},{16,0},{1,17},{17,1},{2,18},{18,2},{3,19},{19,3},{4,20},{20... | collective-permute-start | bytes 589832 | tf_op jit(solution)/shard_map/ppermute | solution.py:196
  20.9 17.0 %collective-permute-start.9 = (bf16[512,384]{1,0:T(8,128)(2,1)S(1)}, bf16[512,384]{1,0:T(8,128)(2,1)S(1)}, u32[]{:S(2)}, u32[]{:S(2)}) collective-permute-start(bf16[512,384]{1,0:T(8,128)(2,1)S(1)} %get-tuple-element.41.rows_ref), channel_id=1, source_target_pairs={{0,1},{1,2},{2,3},{3,0},{4,5},{5,6},{6,7},{7,4},{8,9},{9,10},{10,1... | collective-permute-start | bytes 1179656 | tf_op jit(solution)/shard_map/ppermute | solution.py:211
  22.1 15.8 %collective-permute-start.8 = (bf16[512,384]{1,0:T(8,128)(2,1)S(1)}, bf16[512,384]{1,0:T(8,128)(2,1)S(1)}, u32[]{:S(2)}, u32[]{:S(2)}) collective-permute-start(bf16[512,384]{1,0:T(8,128)(2,1)S(1)} %get-tuple-element.41.rows_ref), channel_id=1, source_target_pairs={{0,2},{1,3},{2,0},{3,1},{4,6},{5,7},{6,4},{7,5},{8,10},{9,11},{10,... | collective-permute-start | bytes 1179656 | tf_op jit(solution)/shard_map/ppermute | solution.py:211
  23.9 14.0 %collective-permute-start.7 = (bf16[512,384]{1,0:T(8,128)(2,1)S(1)}, bf16[512,384]{1,0:T(8,128)(2,1)S(1)}, u32[]{:S(2)}, u32[]{:S(2)}) collective-permute-start(bf16[512,384]{1,0:T(8,128)(2,1)S(1)} %get-tuple-element.41.rows_ref), channel_id=1, source_target_pairs={{0,3},{1,0},{2,1},{3,2},{4,7},{5,4},{6,5},{7,6},{8,11},{9,8},{10,9... | collective-permute-start | bytes 1179656 | tf_op jit(solution)/shard_map/ppermute | solution.py:211
  24.6 13.3 %collective-permute-start.5 = (bf16[512,384]{1,0:T(8,128)(2,1)S(1)}, bf16[512,384]{1,0:T(8,128)(2,1)S(1)}, u32[]{:S(2)}, u32[]{:S(2)}) collective-permute-start(bf16[512,384]{1,0:T(8,128)(2,1)S(1)} %pad_maximum_fusion.refs_0_), channel_id=1, source_target_pairs={{0,4},{1,5},{2,6},{3,7},{4,8},{5,9},{6,10},{7,11},{8,12},{9,13},{1... | collective-permute-start | bytes 1179656 | tf_op jit(solution)/shard_map/ppermute | solution.py:211
  28.9 8.9 %collective-permute-start.6 = (bf16[256,384]{1,0:T(8,128)(2,1)S(1)}, bf16[256,384]{1,0:T(8,128)(2,1)S(1)}, u32[]{:S(2)}, u32[]{:S(2)}) collective-permute-start(bf16[256,384]{1,0:T(8,128)(2,1)S(1)} %pad_maximum_fusion.1), channel_id=1, source_target_pairs={{0,8},{1,9},{2,10},{3,11},{4,12},{5,13},{6,14},{7,15},{8,32},{9,33... | collective-permute-start | bytes 589832 | tf_op jit(solution)/shard_map/ppermute | solution.py:211
  37.9 6.4 %collective-permute-start.10 = (bf16[512,384]{1,0:T(8,128)(2,1)S(1)}, bf16[512,384]{1,0:T(8,128)(2,1)S(1)}, u32[]{:S(2)}, u32[]{:S(2)}) collective-permute-start(bf16[512,384]{1,0:T(8,128)(2,1)S(1)} %collective-permute-done.5.refs_1_), channel_id=1, source_target_pairs={{0,16},{16,0},{1,17},{17,1},{2,18},{18,2},{3,19},{19,3},{4,20},{20... | collective-permute-start | bytes 1179656 | tf_op jit(solution)/shard_map/ppermute | solution.py:196
  42.5 1.8 %collective-permute-start.11 = (bf16[256,384]{1,0:T(8,128)(2,1)S(1)}, bf16[256,384]{1,0:T(8,128)(2,1)S(1)}, u32[]{:S(2)}, u32[]{:S(2)}) collective-permute-start(bf16[256,384]{1,0:T(8,128)(2,1)S(1)} %collective-permute-done.6.refs_2_), channel_id=1, source_target_pairs={{0,16},{16,0},{1,17},{17,1},{2,18},{18,2},{3,19},{19,3},{4,20},{20... | collective-permute-start | bytes 589832 | tf_op jit(solution)/shard_map/ppermute | solution.py:196
  45.4 10.8 %collective-permute-start.13 = (bf16[512,256]{1,0:T(8,128)(2,1)S(1)}, bf16[512,256]{1,0:T(8,128)(2,1)}, u32[]{:S(2)}, u32[]{:S(2)}) collective-permute-start(bf16[512,256]{1,0:T(8,128)(2,1)S(1)} %tile.8), channel_id=1, source_target_pairs={{0,2},{1,3},{2,0},{3,1},{4,6},{5,7},{6,4},{7,5},{8,10},{9,11},{10,... | collective-permute-start | bytes 786440 | tf_op jit(solution)/shard_map/ppermute | solution.py:211
  48.3 8.0 %collective-permute-start.12 = (bf16[512,256]{1,0:T(8,128)(2,1)S(1)}, bf16[512,256]{1,0:T(8,128)(2,1)}, u32[]{:S(2)}, u32[]{:S(2)}) collective-permute-start(bf16[512,256]{1,0:T(8,128)(2,1)S(1)} %tile.6), channel_id=1, source_target_pairs={{0,1},{1,2},{2,3},{3,0},{4,5},{5,6},{6,7},{7,4},{8,9},{9,10},{10,1... | collective-permute-start | bytes 786440 | tf_op jit(solution)/shard_map/ppermute | solution.py:211
  51.1 6.7 %collective-permute-start.14 = (bf16[512,256]{1,0:T(8,128)(2,1)S(1)}, bf16[512,256]{1,0:T(8,128)(2,1)}, u32[]{:S(2)}, u32[]{:S(2)}) collective-permute-start(bf16[512,256]{1,0:T(8,128)(2,1)S(1)} %tile.9), channel_id=1, source_target_pairs={{0,3},{1,0},{2,1},{3,2},{4,7},{5,4},{6,5},{7,6},{8,11},{9,8},{10,9... | collective-permute-start | bytes 786440 | tf_op jit(solution)/shard_map/ppermute | solution.py:211
  59.4 2.8 %collective-permute-start.15 = (f32[256,256]{1,0:T(8,128)S(1)}, f32[256,256]{1,0:T(8,128)S(1)}, u32[]{:S(2)}, u32[]{:S(2)}) collective-permute-start(f32[256,256]{1,0:T(8,128)S(1)} %get-tuple-element.49), channel_id=1, source_target_pairs={{0,16},{16,0},{1,17},{17,1},{2,18},{18,2},{3,19},{19,3},{4,20},{20... | collective-permute-start | bytes 786440 | tf_op jit(solution)/shard_map/ppermute | solution.py:196
  62.9 11.9 %all-to-all-start = ((bf16[16,16,256]{2,1,0:T(8,128)(2,1)}), bf16[16,16,256]{2,1,0:T(8,128)(2,1)S(1)}, u32[]{:S(2)}, u32[]{:S(2)}) async-start(bf16[16,16,256]{2,1,0:T(8,128)(2,1)} %bitcast.4), calls=%async_computation | async-start | bytes 262144 | tf_op jit(solution)/shard_map/all_to_all | solution.py:219
  68.0 6.0 %collective-permute-start.16 = (bf16[128,256]{1,0:T(8,128)(2,1)S(1)}, bf16[128,256]{1,0:T(8,128)(2,1)S(1)}, u32[]{:S(2)}, u32[]{:S(2)}) collective-permute-start(bf16[128,256]{1,0:T(8,128)(2,1)S(1)} %get-tuple-element.52), channel_id=1, source_target_pairs={{0,64},{1,65},{2,66},{3,67},{4,68},{5,69},{6,70},{7,71},{8,72},{9,... | collective-permute-start | bytes 196616 | tf_op jit(solution)/shard_map/ppermute | solution.py:211
  75.5 13.8 %all-to-all-start.1 = ((f32[8,16,256]{2,1,0:T(8,128)}), f32[8,16,256]{2,1,0:T(8,128)S(1)}, u32[]{:S(2)}, u32[]{:S(2)}) async-start(f32[8,16,256]{2,1,0:T(8,128)} %sum_spread.2), calls=%async_computation.1 | async-start | bytes 262144 | tf_op jit(solution)/shard_map/all_to_all | solution.py:219
  81.3 4.6 %collective-permute-start.17 = (bf16[128,256]{1,0:T(8,128)(2,1)S(1)}, bf16[128,256]{1,0:T(8,128)(2,1)S(1)}, u32[]{:S(2)}, u32[]{:S(2)}) collective-permute-start(bf16[128,256]{1,0:T(8,128)(2,1)S(1)} %get-tuple-element.56), channel_id=1, source_target_pairs={{0,128},{1,129},{2,130},{3,131},{4,132},{5,133},{6,134},{7,135},{8... | collective-permute-start | bytes 196616 | tf_op jit(solution)/shard_map/ppermute | solution.py:211
  90.0 10.7 %all-to-all-start.2 = ((bf16[16,16,256]{2,1,0:T(8,128)(2,1)}), bf16[16,16,256]{2,1,0:T(8,128)(2,1)S(1)}, u32[]{:S(2)}, u32[]{:S(2)}) async-start(bf16[16,16,256]{2,1,0:T(8,128)(2,1)} %sum_spread.3), calls=%async_computation.2 | async-start | bytes 262144 | tf_op jit(solution)/shard_map/all_to_all | solution.py:219
  93.8 3.9 %collective-permute-start.18 = (bf16[128,256]{1,0:T(8,128)(2,1)S(1)}, bf16[128,256]{1,0:T(8,128)(2,1)S(1)}, u32[]{:S(2)}, u32[]{:S(2)}) collective-permute-start(bf16[128,256]{1,0:T(8,128)(2,1)S(1)} %get-tuple-element.63), channel_id=1, source_target_pairs={{0,192},{1,193},{2,194},{3,195},{4,196},{5,197},{6,198},{7,199},{8... | collective-permute-start | bytes 196616 | tf_op jit(solution)/shard_map/ppermute | solution.py:211
  100.7 5.2 %collective-permute-start.19 = (bf16[256,256]{1,0:T(8,128)(2,1)S(1)}, bf16[256,256]{1,0:T(8,128)(2,1)S(1)}, u32[]{:S(2)}, u32[]{:S(2)}) collective-permute-start(bf16[256,256]{1,0:T(8,128)(2,1)S(1)} %bitcast.6), channel_id=1, source_target_pairs={{0,16},{16,0},{1,17},{17,1},{2,18},{18,2},{3,19},{19,3},{4,20},{20... | collective-permute-start | bytes 393224 | tf_op jit(solution)/shard_map/ppermute | solution.py:196

commit v8 on v5

--- a/solution.py
+++ b/solution.py
@@ -73,11 +73,10 @@
     packed[:, width:] = tail
 
 
-def split_kernel(count, *refs):
-    line, embeds = refs[count:]
-    rows, width = refs[0].shape[0], line.shape[1]
-    for k, ref in enumerate(refs[:count]):
-        line[k * rows : (k + 1) * rows, :] = ref[:, :width]
+def split_kernel(own, other, pair, embeds):
+    rows, width = own.shape[0], pair.shape[1]
+    for k, ref in enumerate((own, other)):
+        pair[k * rows : (k + 1) * rows, :] = ref[:, :width]
         embeds[k * rows : (k + 1) * rows, :] = ref[:, width:]
 
 
@@ -95,8 +94,10 @@
     return jnp.asarray(table, BF16)
 
 
-def tile_kernel(sub, step, table, rows_ref, *refs):
+def tile_kernel(sub, step, adds, table, rows_ref, *refs):
     *columns, out = refs
+    if adds:
+        begin, *columns = columns
     width = out.shape[1]
     rows = rows_ref.shape[0]
     u_rows = rows_ref[:, :width]
@@ -109,7 +110,7 @@
     lane = lax.broadcasted_iota(jnp.int32, (8, 128), 1)
     pick_cols = jnp.where((lane >= 96) & (lane < 99), 1.0, 0.0).astype(BF16)
     blocks = [slice(k, k + sub) for k in range(0, rows, sub)]
-    acc = [jnp.zeros((sub, width), F32) for _ in blocks]
+    acc = [begin[block, :] if adds else jnp.zeros((sub, width), F32) for block in blocks]
     total = [jnp.zeros((sub, 128), F32) for _ in blocks]
     work = [
         (ref, start, k)
@@ -140,22 +141,18 @@
         out[block, :] = (acc[k] - row_total * u_rows[block].astype(F32)).astype(out.dtype)
 
 
-def sum_rows_kernel(count, *refs):
-    parts, (embeds, partial, own, *others) = refs[:count], refs[count:]
+def sum_rows_kernel(a, b, c, d, embeds, partial, own, other):
     rows = own.shape[0]
-    total = parts[0][...]
-    for ref in parts[1:]:
-        total = total + ref[...].astype(F32)
+    total = (a[...] + b[...].astype(F32)) + (c[...].astype(F32) + d[...].astype(F32))
     hi = total.astype(BF16)
     lo = (total - hi.astype(F32)).astype(BF16)
     own[...] = total[:rows]
-    for k, ref in enumerate(others):
-        ref[...] = hi[(k + 1) * rows : (k + 2) * rows]
+    other[...] = hi[rows:]
     partial[...] = (dot_tn(embeds[...], hi) + dot_tn(embeds[...], lo)).astype(BF16)
 
 
-def finish_rows_kernel(own, b, c, d, grad_rows):
-    grad_rows[...] = (own[...] + b[...].astype(F32)) + (c[...].astype(F32) + d[...].astype(F32))
+def finish_rows_kernel(own, arrived, grad_rows):
+    grad_rows[...] = own[...] + arrived[...].astype(F32)
 
 
 def sum_spread_kernel(parts, out):
@@ -214,7 +211,7 @@
             jax.ShapeDtypeStruct((rows, width + 128), BF16),
             jax.ShapeDtypeStruct((rows, width + 128 + embeds.shape[1]), BF16),
         ],
-        in_specs=[pl.BlockSpec(memory_space=pl.ANY)] * 5,
+        in_specs=[pl.BlockSpec(memory_space=pltpu.HBM)] * 5,
         out_specs=[VMEM] * 2,
         scratch_shapes=[
             pltpu.VMEM(weight.shape, BF16),
@@ -225,71 +222,79 @@
         ],
         compiler_params=params(48),
         name="pack",
-    )(embeds, weight, solve[None, :], probes.T, probe_solves.T)
-
-    blocks = [extended] + [turn(extended, sizes, 0, -d) for d in range(1, n_side)]
-    line, embeds_line = pl.pallas_call(
-        functools.partial(split_kernel, n_side),
+    )(*(pltpu.with_memory_space_constraint(a, pltpu.HBM) for a in (embeds, weight, solve[None, :], probes.T, probe_solves.T)))
+
+    line = jnp.concatenate([pack] + [turn(pack, sizes, 0, d) for d in range(1, n_side)], axis=0)
+    pair, embeds_pair = pl.pallas_call(
+        split_kernel,
         out_shape=[
-            jax.ShapeDtypeStruct((n_side * rows, width + 128), BF16),
-            jax.ShapeDtypeStruct((n_side * rows, embeds.shape[1]), BF16),
+            jax.ShapeDtypeStruct((2 * rows, width + 128), BF16),
+            jax.ShapeDtypeStruct((2 * rows, embeds.shape[1]), BF16),
         ],
-        in_specs=[VMEM] * n_side,
+        in_specs=[VMEM] * 2,
         out_specs=[VMEM] * 2,
         compiler_params=params(8),
         name="split",
-    )(*blocks)
-    pair = jnp.concatenate([pack, ring(pack, DEPTH, n_z, n_z // 2)], axis=0)
-    pair, line = lax.optimization_barrier((pair, line))
-    swap = ring(pair, "core", 2, 1)
-    far = move(pair, sizes, lambda core: {"z": 2 - 4 * core})
-    near = [move(part, sizes, lambda core: {"z": 1 - 2 * core}) for part in (pair, swap)]
-    lines = [line] + [turn(line, sizes, 1, -d) for d in range(1, n_side)]
-    columns = [pair, swap, far, *near] + [ring(part, "core", 2, 1) for part in (far, *near)]
+    )(extended, ring(extended, DEPTH, n_z, n_z // 2))
+    line, pair = lax.optimization_barrier((line, pair))
+
+    def along(array, step):
+        return move(array, sizes, lambda core: {"z": step if abs(step) == 1 else step * (1 - 2 * core)})
+
+    steps = (1, -1, 2)
+    columns = [line] + [turn(line, sizes, 1, d) for d in range(1, n_side)]
+    lines = [along(pair, step) for step in steps]
+    columns, lines = lax.optimization_barrier((columns, lines))
+    swapped = [ring(part, "core", 2, 1) for part in columns]
 
     table = left_map(probes.shape[1])
-    back = {}
-    for d in (0, 3, 1, 2):
-        if d != 0:
-            lines[d], _ = lax.optimization_barrier((lines[d], back[0]))
-        part = pl.pallas_call(
-            functools.partial(tile_kernel, 256, 256),
-            out_shape=jax.ShapeDtypeStruct((n_side * rows, width), F32 if d == 0 else BF16),
-            in_specs=[VMEM] * (2 + len(columns)),
+
+    def tile(rows_in, columns, dtype, start=None):
+        return pl.pallas_call(
+            functools.partial(tile_kernel, 256, 256, start is not None),
+            out_shape=jax.ShapeDtypeStruct((rows_in.shape[0], width), dtype),
+            in_specs=[VMEM] * (2 + len(columns) + (start is not None)),
             out_specs=VMEM,
             compiler_params=params(16),
             name="tile",
-        )(table, lines[d], *columns)
-        back[d] = part if d == 0 else turn(part, sizes, 1, d)
-
-    partial, own_rows, *other_rows = pl.pallas_call(
-        functools.partial(sum_rows_kernel, n_side),
+        )(table, rows_in, *([] if start is None else [start]), *columns)
+
+    own = tile(pair, columns, F32)
+    first = tile(lines[0], columns, F32)
+    swapped, own, first = lax.optimization_barrier((swapped, own, first))
+    own = tile(pair, swapped, F32, own)
+    back = [None] * len(steps)
+    for k in (1, 2):
+        back[k] = along(tile(lines[k], columns + swapped, BF16), -steps[k])
+    back[0] = along(tile(lines[0], swapped, BF16, first), -steps[0])
+
+    partial, own_rows, other_rows = pl.pallas_call(
+        sum_rows_kernel,
         out_shape=[
             jax.ShapeDtypeStruct((embeds.shape[1], width), BF16),
             jax.ShapeDtypeStruct((rows, width), F32),
-        ]
-        + [jax.ShapeDtypeStruct((rows, width), BF16)] * (n_side - 1),
-        in_specs=[VMEM] * (n_side + 1),
-        out_specs=[VMEM] * (n_side + 1),
+            jax.ShapeDtypeStruct((rows, width), BF16),
+        ],
+        in_specs=[VMEM] * 5,
+        out_specs=[VMEM] * 3,
         compiler_params=params(16),
         name="sum_rows",
-    )(*(back[d] for d in range(n_side)), embeds_line)
-    arrived = [turn(block, sizes, 0, d + 1) for d, block in enumerate(other_rows)]
+    )(own, *back, embeds_pair)
+
     n_plane = n_side * n_side * 2
     pieces = exchange(partial.reshape(n_plane, -1, width), PLANE)
-    pieces, arrived[0] = lax.optimization_barrier((pieces, arrived[0]))
-    pieces = exchange(sum_spread(pieces, n_z, F32), DEPTH)
-    pieces, arrived[1] = lax.optimization_barrier((pieces, arrived[1]))
-    pieces = exchange(sum_spread(pieces, n_plane, BF16), PLANE)
+    arrived = ring(other_rows, DEPTH, n_z, n_z // 2)
     grad_rows = pl.pallas_call(
         finish_rows_kernel,
         out_shape=jax.ShapeDtypeStruct((rows, width), F32),
-        in_specs=[VMEM] * 4,
+        in_specs=[VMEM] * 2,
         out_specs=VMEM,
         compiler_params=params(16),
         name="finish_rows",
-    )(own_rows, *arrived)
+    )(own_rows, arrived)
     pieces, grad_rows = lax.optimization_barrier((pieces, grad_rows))
+    pieces = exchange(sum_spread(pieces, n_z, F32), DEPTH)
+    pieces = exchange(sum_spread(pieces, n_plane, BF16), PLANE)
     total_points = rows * n_plane * n_z
     grad_weight = pieces.reshape(-1, width).astype(F32) * (1.0 / math.sqrt(total_points))
     return grad_rows, grad_weight

time: 109 us -> 111 us (1.018)
  blocking collectives: 0 us -> 32.1 us
  starting transfers between devices: 55.9 us -> 38.1 us
  waiting for transfers between devices: 32.8 us -> 23.3 us
  local copies, waits for them, and re-layouts: 3.9 us -> 0.01 us
  Pallas kernels: 14.2 us -> 15.6 us
    all_to_all x0 -> x2, blocking collectives: none -> 32.1 us  [exchange(): return lax.all_to_all(array, axes, split_axis=0, concat_axis=0, tiled=True)]
    all_to_all x3 -> x1, starting transfers between devices: 17.7 us -> 6.42 us  [exchange(): return lax.all_to_all(array, axes, split_axis=0, concat_axis=0, tiled=True)]
    ppermute x15 -> x12, starting transfers between devices: 28.1 us -> 18.1 us  [move(): return lax.ppermute(array, ALL, perm)]
    all_to_all x3 -> x1, waiting for transfers between devices: 6.89 us -> 0.77 us  [exchange(): return lax.all_to_all(array, axes, split_axis=0, concat_axis=0, tiled=True)]
    unnamed x12 -> x2, local copies, waits for them, and re-layouts: 3.9 us -> 0.01 us
    ppermute x5 -> x6, starting transfers between devices: 10.2 us -> 13.6 us  [ring(): lax.ppermute(array, axis, [(i, (i + shift) % size) for i in range(size)])]
    ppermute x15 -> x12, waiting for transfers between devices: 22.6 us -> 19.8 us  [move(): return lax.ppermute(array, ALL, perm)]
    pallas_call x6 -> x8, Pallas kernels: 11.5 us -> 13.3 us  [the longest x6 12.2 us: tile(): pl.pallas_call(functools.partial(tile_kernel, 256, 256, start is not None...]
  transfers between devices with their start and end apart: 23 -> 19, of which waited for: 12 -> 11; matrix products, arithmetic and copies ran while one was open for 0% -> 0% of each run, Pallas kernels for 10% -> 5%
where the time goes in v8:
time: 111 us
  starting transfers between devices  38.1 us (34%)
  blocking collectives  32.1 us (29%)
  waiting for transfers between devices  23.3 us (21%)
  Pallas kernels  15.6 us (14%)
    all_to_all x2, blocking collectives, exchange(): return lax.all_to_all(array, axes, split_axis=0, concat_axis=0, tiled=True)  32.1 us
    ppermute x12, waiting for transfers between devices, move(): return lax.ppermute(array, ALL, perm)  19.8 us
    ppermute x12, starting transfers between devices, move(): return lax.ppermute(array, ALL, perm)  18.1 us
    ppermute x6, starting transfers between devices, ring(): lax.ppermute(array, axis, [(i, (i + shift) % size) for i in range(size)])  13.6 us
    pallas_call x6, Pallas kernels, tile(): pl.pallas_call(functools.partial(tile_kernel, 256, 256, start is not None...  12.2 us
    all_to_all x1, starting transfers between devices, exchange(): return lax.all_to_all(array, axes, split_axis=0, concat_axis=0, tiled=True)  6.42 us
    ppermute x6, waiting for transfers between devices, ring(): lax.ppermute(array, axis, [(i, (i + shift) % size) for i in range(size)])  2.75 us
  transfers between devices with their start and end apart: 19, of which 11 were waited for; matrix products, arithmetic and copies ran while one was open for 0% of the time, Pallas kernels for 5%

profile of v8, /device:TPU:1, one launch (start us, length us, event | category | flops | bytes accessed | tf_op | source)
XLA Modules:
  0.0 110.7 jit_solution(16793368381305924853)
XLA Ops:
  0.6 1.5 %pack.1 = (bf16[128,384]{1,0:T(8,128)(2,1)S(1)}, bf16[128,896]{1,0:T(8,128)(2,1)S(1)}) custom-call(bf16[128,512]{1,0:T(8,128)(2,1)} %embeds.1, bf16[512,256]{1,0:T(8,128)(2,1)} %weight.1, f32[1,128]{1,0:T(1,128)} %bitcast.8, f32[15,128]{1,0:T(8,128)} %bitcast.6, f32[15,128]{1,0:T(8,128)} %bitcast.7), custom_call_target="tpu_custom_call" | custom-call | tf_op jit(solution)/shard_map/pack/pallas_call | solution.py:208
  2.2 7.8 %collective-permute-start.3 = (bf16[128,896]{1,0:T(8,128)(2,1)S(1)}, bf16[128,896]{1,0:T(8,128)(2,1)S(1)}, u32[]{:S(2)}, u32[]{:S(2)}) collective-permute-start(bf16[128,896]{1,0:T(8,128)(2,1)S(1)} %get-tuple-element.27.own), channel_id=1, source_target_pairs={{0,32},{4,36},{8,40},{12,44},{32,0},{36,4},{40,8},{44,12},{1,33},{... | collective-permute-start | bytes 688136 | tf_op jit(solution)/shard_map/ppermute | solution.py:179
  10.0 2.5 %collective-permute-start.2 = (bf16[128,384]{1,0:T(8,128)(2,1)S(1)}, bf16[128,384]{1,0:T(8,128)(2,1)S(1)}, u32[]{:S(2)}, u32[]{:S(2)}) collective-permute-start(bf16[128,384]{1,0:T(8,128)(2,1)S(1)} %get-tuple-element.26), channel_id=1, source_target_pairs={{0,192},{1,193},{2,194},{3,195},{4,196},{5,197},{6,198},{7,199},{8... | collective-permute-start | bytes 294920 | tf_op jit(solution)/shard_map/ppermute | solution.py:194
  12.5 0.5 collective-permute-start.1
  13.0 0.6 collective-permute-start
  13.6 0.5 collective-permute-done.2
  14.1 3.4 %collective-permute-done.1 = bf16[128,384]{1,0:T(8,128)(2,1)S(1)} collective-permute-done((bf16[128,384]{1,0:T(8,128)(2,1)S(1)}, bf16[128,384]{1,0:T(8,128)(2,1)S(1)}, u32[]{:S(2)}, u32[]{:S(2)}) %collective-permute-start.1) | collective-permute-done | bytes 98336 | tf_op jit(solution)/shard_map/ppermute | solution.py:194
  17.5 1.3 %collective-permute-done = bf16[128,384]{1,0:T(8,128)(2,1)S(1)} collective-permute-done((bf16[128,384]{1,0:T(8,128)(2,1)S(1)}, bf16[128,384]{1,0:T(8,128)(2,1)S(1)}, u32[]{:S(2)}, u32[]{:S(2)}) %collective-permute-start) | collective-permute-done | bytes 98336 | tf_op jit(solution)/shard_map/ppermute | solution.py:194
  18.8 0.0 copy-start
  18.9 5.7 %collective-permute-start.9 = (bf16[256,384]{1,0:T(8,128)(2,1)S(1)}, bf16[256,384]{1,0:T(8,128)(2,1)S(1)}, u32[]{:S(2)}, u32[]{:S(2)}) collective-permute-start(bf16[256,384]{1,0:T(8,128)(2,1)S(1)} %get-tuple-element.29.rows_ref), channel_id=1, source_target_pairs={{0,8},{1,9},{2,10},{3,11},{4,12},{5,13},{6,14},{7,15},{8,32},{9,33... | collective-permute-start | bytes 589832 | tf_op jit(solution)/shard_map/ppermute | solution.py:194
  24.6 2.7 %collective-permute-start.6 = (bf16[512,384]{1,0:T(8,128)(2,1)S(1)}, bf16[512,384]{1,0:T(8,128)(2,1)S(1)}, u32[]{:S(2)}, u32[]{:S(2)}) collective-permute-start(bf16[512,384]{1,0:T(8,128)(2,1)S(1)} %pad_maximum_fusion.refs_0_), channel_id=1, source_target_pairs={{0,3},{1,0},{2,1},{3,2},{4,7},{5,4},{6,5},{7,6},{8,11},{9,8},{10,9... | collective-permute-start | bytes 1179656 | tf_op jit(solution)/shard_map/ppermute | solution.py:194
  27.3 0.3 collective-permute-start.5
  27.7 0.7 collective-permute-start.4
  28.4 0.0 collective-permute-start.8
  28.4 0.9 collective-permute-done.9.rows_ref
  29.3 0.6 collective-permute-start.7
  29.8 5.4 %collective-permute-done.8.rows_ref = bf16[256,384]{1,0:T(8,128)(2,1)S(1)} collective-permute-done((bf16[256,384]{1,0:T(8,128)(2,1)S(1)}, bf16[256,384]{1,0:T(8,128)(2,1)S(1)}, u32[]{:S(2)}, u32[]{:S(2)}) %collective-permute-start.8) | collective-permute-done | bytes 196640 | tf_op jit(solution)/shard_map/ppermute | solution.py:194
  35.3 0.0 collective-permute-done.7.rows_ref
  35.3 1.0 collective-permute-done.6.refs_3_
  36.3 0.0 collective-permute-done.5.refs_2_
  36.3 3.4 %collective-permute-done.4.refs_1_ = bf16[512,384]{1,0:T(8,128)(2,1)S(1)} collective-permute-done((bf16[512,384]{1,0:T(8,128)(2,1)S(1)}, bf16[512,384]{1,0:T(8,128)(2,1)S(1)}, u32[]{:S(2)}, u32[]{:S(2)}) %collective-permute-start.4) | collective-permute-done | bytes 393248 | tf_op jit(solution)/shard_map/ppermute | solution.py:194
  39.7 0.0 collective-permute-start.10
  39.7 0.5 collective-permute-start.11
  40.2 0.0 collective-permute-start.12
  40.2 0.5 collective-permute-start.13
  40.7 1.6 %tile.6.refs_0_ = f32[256,256]{1,0:T(8,128)S(1)} custom-call(bf16[128,128]{1,0:T(8,128)(2,1)S(1)} %copy-done, bf16[256,384]{1,0:T(8,128)(2,1)S(1)} %get-tuple-element.29.rows_ref, bf16[512,384]{1,0:T(8,128)(2,1)S(1)} %pad_maximum_fusion.refs_0_, bf16[512,384]{1,0:T(8,128)(2,1)S(1)} %collective-permute-done.4.refs_1_, ...), custom_call_target="tpu_custom_call" | custom-call | tf_op jit(solution)/shard_map/tile/pallas_call | solution.py:253
  42.3 1.6 %tile.7.refs_0_ = f32[256,256]{1,0:T(8,128)S(1)} custom-call(bf16[128,128]{1,0:T(8,128)(2,1)S(1)} %copy-done, bf16[256,384]{1,0:T(8,128)(2,1)S(1)} %collective-permute-done.7.rows_ref, bf16[512,384]{1,0:T(8,128)(2,1)S(1)} %pad_maximum_fusion.refs_0_, bf16[512,384]{1,0:T(8,128)(2,1)S(1)} %collective-permute-done.4.refs_1_, ...), custom_call_target="tpu_custom_call" | custom-call | tf_op jit(solution)/shard_map/tile/pallas_call | solution.py:253
  44.0 0.0 collective-permute-done.10.refs_1_.refs_4_
  44.0 0.0 collective-permute-done.13.refs_4_.refs_7_
  44.0 2.9 %tile.11 = bf16[256,256]{1,0:T(8,128)(2,1)S(1)} custom-call(bf16[128,128]{1,0:T(8,128)(2,1)S(1)} %copy-done, bf16[256,384]{1,0:T(8,128)(2,1)S(1)} %collective-permute-done.9.rows_ref, bf16[512,384]{1,0:T(8,128)(2,1)S(1)} %pad_maximum_fusion.refs_0_, bf16[512,384]{1,0:T(8,128)(2,1)S(1)} %collective-permute-done.4.refs_1_, ...), custom_call_target="tpu_custom_call" | custom-call | tf_op jit(solution)/shard_map/tile/pallas_call | solution.py:253
  46.9 2.9 %tile.10 = bf16[256,256]{1,0:T(8,128)(2,1)S(1)} custom-call(bf16[128,128]{1,0:T(8,128)(2,1)S(1)} %copy-done, bf16[256,384]{1,0:T(8,128)(2,1)S(1)} %collective-permute-done.8.rows_ref, bf16[512,384]{1,0:T(8,128)(2,1)S(1)} %pad_maximum_fusion.refs_0_, bf16[512,384]{1,0:T(8,128)(2,1)S(1)} %collective-permute-done.4.refs_1_, ...), custom_call_target="tpu_custom_call" | custom-call | tf_op jit(solution)/shard_map/tile/pallas_call | solution.py:253
  49.7 1.6 %tile.9 = bf16[256,256]{1,0:T(8,128)(2,1)S(1)} custom-call(bf16[128,128]{1,0:T(8,128)(2,1)S(1)} %copy-done, bf16[256,384]{1,0:T(8,128)(2,1)S(1)} %collective-permute-done.7.rows_ref, f32[256,256]{1,0:T(8,128)S(1)} %tile.7.refs_0_, bf16[512,384]{1,0:T(8,128)(2,1)S(1)} %collective-permute-done.10.refs_1_.refs_4_, ...), custom_call_target="tpu_custom_call" | custom-call | tf_op jit(solution)/shard_map/tile/pallas_call | solution.py:253
  51.4 1.2 %collective-permute-start.14 = (bf16[256,256]{1,0:T(8,128)(2,1)S(1)}, bf16[256,256]{1,0:T(8,128)(2,1)S(1)}, u32[]{:S(2)}, u32[]{:S(2)}) collective-permute-start(bf16[256,256]{1,0:T(8,128)(2,1)S(1)} %tile.9), channel_id=1, source_target_pairs={{0,44},{1,45},{2,46},{3,47},{4,0},{5,1},{6,2},{7,3},{8,4},{9,5},{1... | collective-permute-start | bytes 393224 | tf_op jit(solution)/shard_map/ppermute | solution.py:194
  52.6 0.3 collective-permute-start.15
  52.9 3.0 %collective-permute-start.16 = (bf16[256,256]{1,0:T(8,128)(2,1)S(1)}, bf16[256,256]{1,0:T(8,128)(2,1)S(1)}, u32[]{:S(2)}, u32[]{:S(2)}) collective-permute-start(bf16[256,256]{1,0:T(8,128)(2,1)S(1)} %tile.11), channel_id=1, source_target_pairs={{0,40},{1,41},{2,42},{3,43},{4,44},{5,45},{6,46},{7,47},{8,0},{9,1... | collective-permute-start | bytes 393224 | tf_op jit(solution)/shard_map/ppermute | solution.py:194
  55.9 1.6 %tile.8.a = f32[256,256]{1,0:T(8,128)S(1)} custom-call(bf16[128,128]{1,0:T(8,128)(2,1)S(1)} %copy-done, bf16[256,384]{1,0:T(8,128)(2,1)S(1)} %get-tuple-element.29.rows_ref, f32[256,256]{1,0:T(8,128)S(1)} %tile.6.refs_0_, bf16[512,384]{1,0:T(8,128)(2,1)S(1)} %collective-permute-done.10.refs_1_.refs_4_, ...), custom_call_target="tpu_custom_call" | custom-call | tf_op jit(solution)/shard_map/tile/pallas_call | solution.py:253
  57.5 0.0 collective-permute-done.14.b
  57.5 0.8 collective-permute-done.15.c
  58.2 3.1 %collective-permute-done.16.d = bf16[256,256]{1,0:T(8,128)(2,1)S(1)} collective-permute-done((bf16[256,256]{1,0:T(8,128)(2,1)S(1)}, bf16[256,256]{1,0:T(8,128)(2,1)S(1)}, u32[]{:S(2)}, u32[]{:S(2)}) %collective-permute-start.16) | collective-permute-done | bytes 131104 | tf_op jit(solution)/shard_map/ppermute | solution.py:194
  61.3 1.1 sum_rows.1
  62.4 6.4 %all-to-all-start = ((bf16[32,16,256]{2,1,0:T(8,128)(2,1)}), bf16[32,16,256]{2,1,0:T(8,128)(2,1)S(1)}, u32[]{:S(2)}, u32[]{:S(2)}) async-start(bf16[32,16,256]{2,1,0:T(8,128)(2,1)} %bitcast.3), calls=%async_computation | async-start | bytes 524288 | tf_op jit(solution)/shard_map/all_to_all | solution.py:202
  68.8 4.7 %collective-permute-start.17 = (bf16[128,256]{1,0:T(8,128)(2,1)S(1)}, bf16[128,256]{1,0:T(8,128)(2,1)S(1)}, u32[]{:S(2)}, u32[]{:S(2)}) collective-permute-start(bf16[128,256]{1,0:T(8,128)(2,1)S(1)} %get-tuple-element.47), channel_id=1, source_target_pairs={{0,32},{4,36},{8,40},{12,44},{32,0},{36,4},{40,8},{44,12},{1,33},{... | collective-permute-start | bytes 196616 | tf_op jit(solution)/shard_map/ppermute | solution.py:179
  73.5 2.7 %collective-permute-done.17.arrived = bf16[128,256]{1,0:T(8,128)(2,1)S(1)} collective-permute-done((bf16[128,256]{1,0:T(8,128)(2,1)S(1)}, bf16[128,256]{1,0:T(8,128)(2,1)S(1)}, u32[]{:S(2)}, u32[]{:S(2)}) %collective-permute-start.17) | collective-permute-done | bytes 65568 | tf_op jit(solution)/shard_map/ppermute | solution.py:179
  76.3 0.7 finish_rows.1
  76.9 0.8 all-to-all-done.parts
  77.8 13.8 %all_to_all.15.parts = f32[8,16,256]{2,1,0:T(8,128)S(1)} all-to-all(f32[8,16,256]{2,1,0:T(8,128)S(1)} %sum_spread.2), channel_id=1, replica_groups=mesh['y'=4,'zh'=2,'core'=2,'zl'=4,'x'=4] {'zh','zl'}, dimensions={0} | all-to-all | bytes 262144 | tf_op jit(solution)/shard_map/all_to_all | solution.py:202
  91.6 18.3 %all_to_all.16 = bf16[32,16,256]{2,1,0:T(8,128)(2,1)S(1)} all-to-all(bf16[32,16,256]{2,1,0:T(8,128)(2,1)S(1)} %sum_spread.3), channel_id=1, replica_groups=mesh['y'=4,'zh'=2,'core'=2,'zl'=4,'x'=4] {'y','core','x'}, dimensions={0} | all-to-all | bytes 524288 | tf_op jit(solution)/shard_map/all_to_all | solution.py:202
  109.8 0.9 convert_multiply_fusion
  (8 shorter events, 0.2 us)
Async XLA Ops:
  2.2 16.7 %collective-permute-start.3 = (bf16[128,896]{1,0:T(8,128)(2,1)S(1)}, bf16[128,896]{1,0:T(8,128)(2,1)S(1)}, u32[]{:S(2)}, u32[]{:S(2)}) collective-permute-start(bf16[128,896]{1,0:T(8,128)(2,1)S(1)} %get-tuple-element.27.own), channel_id=1, source_target_pairs={{0,32},{4,36},{8,40},{12,44},{32,0},{36,4},{40,8},{44,12},{1,33},{... | collective-permute-start | bytes 688136 | tf_op jit(solution)/shard_map/ppermute | solution.py:179
  10.0 4.1 %collective-permute-start.2 = (bf16[128,384]{1,0:T(8,128)(2,1)S(1)}, bf16[128,384]{1,0:T(8,128)(2,1)S(1)}, u32[]{:S(2)}, u32[]{:S(2)}) collective-permute-start(bf16[128,384]{1,0:T(8,128)(2,1)S(1)} %get-tuple-element.26), channel_id=1, source_target_pairs={{0,192},{1,193},{2,194},{3,195},{4,196},{5,197},{6,198},{7,199},{8... | collective-permute-start | bytes 294920 | tf_op jit(solution)/shard_map/ppermute | solution.py:194
  12.5 5.1 %collective-permute-start.1 = (bf16[128,384]{1,0:T(8,128)(2,1)S(1)}, bf16[128,384]{1,0:T(8,128)(2,1)S(1)}, u32[]{:S(2)}, u32[]{:S(2)}) collective-permute-start(bf16[128,384]{1,0:T(8,128)(2,1)S(1)} %get-tuple-element.26), channel_id=1, source_target_pairs={{0,128},{1,129},{2,130},{3,131},{4,132},{5,133},{6,134},{7,135},{8... | collective-permute-start | bytes 294920 | tf_op jit(solution)/shard_map/ppermute | solution.py:194
  13.0 5.8 %collective-permute-start = (bf16[128,384]{1,0:T(8,128)(2,1)S(1)}, bf16[128,384]{1,0:T(8,128)(2,1)S(1)}, u32[]{:S(2)}, u32[]{:S(2)}) collective-permute-start(bf16[128,384]{1,0:T(8,128)(2,1)S(1)} %get-tuple-element.26), channel_id=1, source_target_pairs={{0,64},{1,65},{2,66},{3,67},{4,68},{5,69},{6,70},{7,71},{8,72},{9,... | collective-permute-start | bytes 294920 | tf_op jit(solution)/shard_map/ppermute | solution.py:194
  18.8 21.9 %copy-start = (bf16[128,128]{1,0:T(8,128)(2,1)S(1)}, bf16[128,128]{1,0:T(8,128)(2,1)}, u32[]{:S(2)}) copy-start(bf16[128,128]{1,0:T(8,128)(2,1)} %constant.4.clone.table) | copy-start | bytes 98308
  18.9 10.4 %collective-permute-start.9 = (bf16[256,384]{1,0:T(8,128)(2,1)S(1)}, bf16[256,384]{1,0:T(8,128)(2,1)S(1)}, u32[]{:S(2)}, u32[]{:S(2)}) collective-permute-start(bf16[256,384]{1,0:T(8,128)(2,1)S(1)} %get-tuple-element.29.rows_ref), channel_id=1, source_target_pairs={{0,8},{1,9},{2,10},{3,11},{4,12},{5,13},{6,14},{7,15},{8,32},{9,33... | collective-permute-start | bytes 589832 | tf_op jit(solution)/shard_map/ppermute | solution.py:194
  24.6 11.7 %collective-permute-start.6 = (bf16[512,384]{1,0:T(8,128)(2,1)S(1)}, bf16[512,384]{1,0:T(8,128)(2,1)S(1)}, u32[]{:S(2)}, u32[]{:S(2)}) collective-permute-start(bf16[512,384]{1,0:T(8,128)(2,1)S(1)} %pad_maximum_fusion.refs_0_), channel_id=1, source_target_pairs={{0,3},{1,0},{2,1},{3,2},{4,7},{5,4},{6,5},{7,6},{8,11},{9,8},{10,9... | collective-permute-start | bytes 1179656 | tf_op jit(solution)/shard_map/ppermute | solution.py:194
  27.3 8.9 %collective-permute-start.5 = (bf16[512,384]{1,0:T(8,128)(2,1)S(1)}, bf16[512,384]{1,0:T(8,128)(2,1)S(1)}, u32[]{:S(2)}, u32[]{:S(2)}) collective-permute-start(bf16[512,384]{1,0:T(8,128)(2,1)S(1)} %pad_maximum_fusion.refs_0_), channel_id=1, source_target_pairs={{0,2},{1,3},{2,0},{3,1},{4,6},{5,7},{6,4},{7,5},{8,10},{9,11},{10,... | collective-permute-start | bytes 1179656 | tf_op jit(solution)/shard_map/ppermute | solution.py:194
  27.7 12.0 %collective-permute-start.4 = (bf16[512,384]{1,0:T(8,128)(2,1)S(1)}, bf16[512,384]{1,0:T(8,128)(2,1)S(1)}, u32[]{:S(2)}, u32[]{:S(2)}) collective-permute-start(bf16[512,384]{1,0:T(8,128)(2,1)S(1)} %pad_maximum_fusion.refs_0_), channel_id=1, source_target_pairs={{0,1},{1,2},{2,3},{3,0},{4,5},{5,6},{6,7},{7,4},{8,9},{9,10},{10,1... | collective-permute-start | bytes 1179656 | tf_op jit(solution)/shard_map/ppermute | solution.py:194
  28.4 6.9 %collective-permute-start.8 = (bf16[256,384]{1,0:T(8,128)(2,1)S(1)}, bf16[256,384]{1,0:T(8,128)(2,1)S(1)}, u32[]{:S(2)}, u32[]{:S(2)}) collective-permute-start(bf16[256,384]{1,0:T(8,128)(2,1)S(1)} %get-tuple-element.29.rows_ref), channel_id=1, source_target_pairs={{0,44},{1,45},{2,46},{3,47},{4,0},{5,1},{6,2},{7,3},{8,4},{9,5},{1... | collective-permute-start | bytes 589832 | tf_op jit(solution)/shard_map/ppermute | solution.py:194
  29.3 6.0 %collective-permute-start.7 = (bf16[256,384]{1,0:T(8,128)(2,1)S(1)}, bf16[256,384]{1,0:T(8,128)(2,1)S(1)}, u32[]{:S(2)}, u32[]{:S(2)}) collective-permute-start(bf16[256,384]{1,0:T(8,128)(2,1)S(1)} %get-tuple-element.29.rows_ref), channel_id=1, source_target_pairs={{0,4},{1,5},{2,6},{3,7},{4,8},{5,9},{6,10},{7,11},{8,12},{9,13},{1... | collective-permute-start | bytes 589832 | tf_op jit(solution)/shard_map/ppermute | solution.py:194
  39.7 4.3 %collective-permute-start.10 = (bf16[512,384]{1,0:T(8,128)(2,1)S(1)}, bf16[512,384]{1,0:T(8,128)(2,1)S(1)}, u32[]{:S(2)}, u32[]{:S(2)}) collective-permute-start(bf16[512,384]{1,0:T(8,128)(2,1)S(1)} %pad_maximum_fusion.refs_0_), channel_id=1, source_target_pairs={{0,16},{16,0},{1,17},{17,1},{2,18},{18,2},{3,19},{19,3},{4,20},{20... | collective-permute-start | bytes 1179656 | tf_op jit(solution)/shard_map/ppermute | solution.py:179
  39.7 4.3 %collective-permute-start.11 = (bf16[512,384]{1,0:T(8,128)(2,1)S(1)}, bf16[512,384]{1,0:T(8,128)(2,1)S(1)}, u32[]{:S(2)}, u32[]{:S(2)}) collective-permute-start(bf16[512,384]{1,0:T(8,128)(2,1)S(1)} %collective-permute-done.4.refs_1_), channel_id=1, source_target_pairs={{0,16},{16,0},{1,17},{17,1},{2,18},{18,2},{3,19},{19,3},{4,20},{20... | collective-permute-start | bytes 1179656 | tf_op jit(solution)/shard_map/ppermute | solution.py:179
  40.2 3.8 %collective-permute-start.12 = (bf16[512,384]{1,0:T(8,128)(2,1)S(1)}, bf16[512,384]{1,0:T(8,128)(2,1)S(1)}, u32[]{:S(2)}, u32[]{:S(2)}) collective-permute-start(bf16[512,384]{1,0:T(8,128)(2,1)S(1)} %collective-permute-done.5.refs_2_), channel_id=1, source_target_pairs={{0,16},{16,0},{1,17},{17,1},{2,18},{18,2},{3,19},{19,3},{4,20},{20... | collective-permute-start | bytes 1179656 | tf_op jit(solution)/shard_map/ppermute | solution.py:179
  40.2 3.8 %collective-permute-start.13 = (bf16[512,384]{1,0:T(8,128)(2,1)S(1)}, bf16[512,384]{1,0:T(8,128)(2,1)S(1)}, u32[]{:S(2)}, u32[]{:S(2)}) collective-permute-start(bf16[512,384]{1,0:T(8,128)(2,1)S(1)} %collective-permute-done.6.refs_3_), channel_id=1, source_target_pairs={{0,16},{16,0},{1,17},{17,1},{2,18},{18,2},{3,19},{19,3},{4,20},{20... | collective-permute-start | bytes 1179656 | tf_op jit(solution)/shard_map/ppermute | solution.py:179
  51.4 6.1 %collective-permute-start.14 = (bf16[256,256]{1,0:T(8,128)(2,1)S(1)}, bf16[256,256]{1,0:T(8,128)(2,1)S(1)}, u32[]{:S(2)}, u32[]{:S(2)}) collective-permute-start(bf16[256,256]{1,0:T(8,128)(2,1)S(1)} %tile.9), channel_id=1, source_target_pairs={{0,44},{1,45},{2,46},{3,47},{4,0},{5,1},{6,2},{7,3},{8,4},{9,5},{1... | collective-permute-start | bytes 393224 | tf_op jit(solution)/shard_map/ppermute | solution.py:194
  52.6 5.7 %collective-permute-start.15 = (bf16[256,256]{1,0:T(8,128)(2,1)S(1)}, bf16[256,256]{1,0:T(8,128)(2,1)S(1)}, u32[]{:S(2)}, u32[]{:S(2)}) collective-permute-start(bf16[256,256]{1,0:T(8,128)(2,1)S(1)} %tile.10), channel_id=1, source_target_pairs={{0,4},{1,5},{2,6},{3,7},{4,8},{5,9},{6,10},{7,11},{8,12},{9,13},{1... | collective-permute-start | bytes 393224 | tf_op jit(solution)/shard_map/ppermute | solution.py:194
  52.9 8.4 %collective-permute-start.16 = (bf16[256,256]{1,0:T(8,128)(2,1)S(1)}, bf16[256,256]{1,0:T(8,128)(2,1)S(1)}, u32[]{:S(2)}, u32[]{:S(2)}) collective-permute-start(bf16[256,256]{1,0:T(8,128)(2,1)S(1)} %tile.11), channel_id=1, source_target_pairs={{0,40},{1,41},{2,42},{3,43},{4,44},{5,45},{6,46},{7,47},{8,0},{9,1... | collective-permute-start | bytes 393224 | tf_op jit(solution)/shard_map/ppermute | solution.py:194
  62.4 15.3 %all-to-all-start = ((bf16[32,16,256]{2,1,0:T(8,128)(2,1)}), bf16[32,16,256]{2,1,0:T(8,128)(2,1)S(1)}, u32[]{:S(2)}, u32[]{:S(2)}) async-start(bf16[32,16,256]{2,1,0:T(8,128)(2,1)} %bitcast.3), calls=%async_computation | async-start | bytes 524288 | tf_op jit(solution)/shard_map/all_to_all | solution.py:202
  68.8 7.5 %collective-permute-start.17 = (bf16[128,256]{1,0:T(8,128)(2,1)S(1)}, bf16[128,256]{1,0:T(8,128)(2,1)S(1)}, u32[]{:S(2)}, u32[]{:S(2)}) collective-permute-start(bf16[128,256]{1,0:T(8,128)(2,1)S(1)} %get-tuple-element.47), channel_id=1, source_target_pairs={{0,32},{4,36},{8,40},{12,44},{32,0},{36,4},{40,8},{44,12},{1,33},{... | collective-permute-start | bytes 196616 | tf_op jit(solution)/shard_map/ppermute | solution.py:179

commit v9 on v6

--- a/solution.py
+++ b/solution.py
@@ -13,6 +13,7 @@
 ROOT5 = math.sqrt(5.0)
 ALL = ("y", "zh", "core", "zl", "x")
 PLANE = ("y", "x")
+STACK = ("zh", "core", "zl")
 DEPTH = ("zh", "zl")
 F32 = jnp.float32
 BF16 = jnp.bfloat16
@@ -33,7 +34,7 @@
 
 def pack_kernel(embeds, weight, solve, probes, probe_solves, packed, extended, weight_in, solve_in, probes_in, probe_solves_in, sems):
     rows, width = embeds.shape[0], weight.shape[1]
-    embeds_in = extended.at[:, width + 128 :]
+    embeds_in = extended.at[:, 128:]
     loads = [
         pltpu.make_async_copy(source, target, sems.at[k])
         for k, (source, target) in enumerate(
@@ -67,18 +68,20 @@
     lane = lax.broadcasted_iota(jnp.int32, (rows, 32), 1)
     tail = jnp.where(lane == 0, sq_hi, jnp.where(lane == 1, sq_mid, jnp.where(lane == 2, sq_lo, 0.0)))
     tail = jnp.concatenate([hi, lo, hi, tail], axis=1).astype(BF16)
-    extended[:, :width] = feats
-    extended[:, width : width + 128] = tail
+    extended[:, :128] = tail
     packed[:, :width] = feats
     packed[:, width:] = tail
 
 
-def split_kernel(count, *refs):
+def split_kernel(count, weight, *refs):
     line, embeds = refs[count:]
-    rows, width = refs[0].shape[0], line.shape[1]
+    rows, width = refs[0].shape[0], weight.shape[1]
     for k, ref in enumerate(refs[:count]):
-        line[k * rows : (k + 1) * rows, :] = ref[:, :width]
-        embeds[k * rows : (k + 1) * rows, :] = ref[:, width:]
+        block = slice(k * rows, (k + 1) * rows)
+        own = ref[:, 128:]
+        line[block, :width] = jnp.dot(own, weight[...], preferred_element_type=F32).astype(BF16)
+        line[block, width:] = ref[:, :128]
+        embeds[block, :] = own
 
 
 def left_map(count):
@@ -217,7 +220,7 @@
         pack_kernel,
         out_shape=[
             jax.ShapeDtypeStruct((rows, width + 128), BF16),
-            jax.ShapeDtypeStruct((rows, width + 128 + embeds.shape[1]), BF16),
+            jax.ShapeDtypeStruct((rows, 128 + embeds.shape[1]), BF16),
         ],
         in_specs=[pl.BlockSpec(memory_space=pltpu.HBM)] * 5,
         out_specs=[VMEM] * 2,
@@ -239,20 +242,17 @@
             jax.ShapeDtypeStruct((n_side * rows, width + 128), BF16),
             jax.ShapeDtypeStruct((n_side * rows, embeds.shape[1]), BF16),
         ],
-        in_specs=[VMEM] * n_side,
+        in_specs=[VMEM] * (n_side + 1),
         out_specs=[VMEM] * 2,
         compiler_params=params(8),
         name="split",
-    )(*blocks)
+    )(weight, *blocks)
     pair = jnp.concatenate([pack, ring(pack, DEPTH, n_z, n_z // 2)], axis=0)
     pair, line = lax.optimization_barrier((pair, line))
     four = jnp.concatenate([pair, ring(pair, "core", 2, 1)], axis=0)
     near = move(four, sizes, lambda core: {"z": 1 - 2 * core})
     far = move(pair, sizes, lambda core: {"z": 2 - 4 * core})
     lines = [line] + [turn(line, sizes, 1, -d) for d in range(1, n_side)]
-    near, far, lines = lax.optimization_barrier((near, far, lines))
-    columns = [four, near, far, ring(near, "core", 2, 1), ring(far, "core", 2, 1)]
-
     table = left_map(probes.shape[1])
 
     def tile(rows_in, columns, dtype, start=None):
@@ -265,12 +265,18 @@
             name="tile",
         )(table, rows_in, *([] if start is None else [start]), *columns)
 
+    begin = tile(line, [four], F32)
+    near, far, lines, begin = lax.optimization_barrier((near, far, lines, begin))
+    columns = [four, near, far, ring(near, "core", 2, 1), ring(far, "core", 2, 1)]
+
     back = {}
     for d in (0, 3, 1, 2):
         if d == 2:
             part = tile(lines[d], columns[3:], BF16, tile(lines[d], columns[:3], F32))
+        elif d == 0:
+            part = tile(line, columns[1:], F32, begin)
         else:
-            part = tile(lines[d], columns, F32 if d == 0 else BF16)
+            part = tile(lines[d], columns, BF16)
         back[d] = part if d == 0 else turn(part, sizes, 1, d)
 
     partial, own_rows, *other_rows = pl.pallas_call(
@@ -289,10 +295,9 @@
     n_plane = n_side * n_side
     pieces = exchange(partial.reshape(n_plane, -1, width), PLANE)
     pieces, arrived[0] = lax.optimization_barrier((pieces, arrived[0]))
-    piece = sum_spread([pieces], 1, F32)
-    spread = sum_spread([piece, ring(piece, "core", 2, 1)], n_z, F32)
+    spread = sum_spread([pieces], n_z * 2, BF16)
     spread, other_rows[1] = lax.optimization_barrier((spread, other_rows[1]))
-    pieces = exchange(spread, DEPTH)
+    pieces = exchange(spread, STACK)
     arrived.append(turn(other_rows[1], sizes, 0, 2))
     pieces, arrived[1] = lax.optimization_barrier((pieces, arrived[1]))
     spread = sum_spread([pieces], n_plane, BF16)

time: 106 us -> 102 us (0.962)
  starting transfers between devices: 55.6 us -> 48.2 us
  waiting for transfers between devices: 32 us -> 34.6 us
    ppermute x14, waiting for transfers between devices: 18.4 us -> 26.6 us  [move(): return lax.ppermute(array, ALL, perm)]
    ppermute x5 -> x4, starting transfers between devices: 17.6 us -> 12.1 us  [ring(): lax.ppermute(array, axis, [(i, (i + shift) % size) for i in range(size)])]
    ppermute x14, starting transfers between devices: 23.9 us -> 20.5 us  [move(): return lax.ppermute(array, ALL, perm)]
    ppermute x5 -> x4, waiting for transfers between devices: 2.97 us -> 0.01 us  [ring(): lax.ppermute(array, axis, [(i, (i + shift) % size) for i in range(size)])]
    all_to_all x3, waiting for transfers between devices: 10.6 us -> 7.99 us  [exchange(): return lax.all_to_all(array, axes, split_axis=0, concat_axis=0, tiled=True)]
    all_to_all x3, starting transfers between devices: 14.1 us -> 15.6 us  [exchange(): return lax.all_to_all(array, axes, split_axis=0, concat_axis=0, tiled=True)]
    pallas_call x5 -> x6, Pallas kernels: 10.5 us -> 10.8 us  [tile(): pl.pallas_call(functools.partial(tile_kernel, 256, 256, start is not None...]
  transfers between devices with their start and end apart: 22 -> 21, of which waited for: 10 -> 10; matrix products, arithmetic and copies ran while one was open for 0% -> 0% of each run, Pallas kernels for 10% -> 10%
where the time goes in v9:
time: 102 us; the launch traced here: 101 us
  starting transfers between devices  48.2 us (47%)
  waiting for transfers between devices  34.6 us (34%)
  Pallas kernels  16.1 us (16%)
    ppermute x14, waiting for transfers between devices, move(): return lax.ppermute(array, ALL, perm)  26.6 us
    ppermute x14, starting transfers between devices, move(): return lax.ppermute(array, ALL, perm)  20.5 us
    all_to_all x3, starting transfers between devices, exchange(): return lax.all_to_all(array, axes, split_axis=0, concat_axis=0, tiled=True)  15.6 us
    ppermute x4, starting transfers between devices, ring(): lax.ppermute(array, axis, [(i, (i + shift) % size) for i in range(size)])  12.1 us
    pallas_call x6, Pallas kernels, tile(): pl.pallas_call(functools.partial(tile_kernel, 256, 256, start is not None...  10.8 us
    all_to_all x3, waiting for transfers between devices, exchange(): return lax.all_to_all(array, axes, split_axis=0, concat_axis=0, tiled=True)  7.99 us
  transfers between devices with their start and end apart: 21, of which 10 were waited for; matrix products, arithmetic and copies ran while one was open for 0% of the time, Pallas kernels for 10%

profile of v9, /device:TPU:1, one launch (start us, length us, event | category | flops | bytes accessed | tf_op | source)
XLA Modules:
  0.0 100.6 jit_solution(13596777024702911837)
XLA Ops:
  0.6 1.5 %pack.1 = (bf16[128,384]{1,0:T(8,128)(2,1)S(1)}, bf16[128,640]{1,0:T(8,128)(2,1)S(1)}) custom-call(bf16[128,512]{1,0:T(8,128)(2,1)} %embeds.1, bf16[512,256]{1,0:T(8,128)(2,1)} %weight.3, f32[1,128]{1,0:T(1,128)} %bitcast.8, f32[15,128]{1,0:T(8,128)} %bitcast.6, f32[15,128]{1,0:T(8,128)} %bitcast.7), custom_call_target="tpu_custom_call" | custom-call | tf_op jit(solution)/shard_map/pack/pallas_call | solution.py:219
  2.2 0.0 copy-start.1
  2.2 7.8 %collective-permute-start = (bf16[128,384]{1,0:T(8,128)(2,1)S(1)}, bf16[128,384]{1,0:T(8,128)(2,1)S(1)}, u32[]{:S(2)}, u32[]{:S(2)}) collective-permute-start(bf16[128,384]{1,0:T(8,128)(2,1)S(1)} %get-tuple-element.29), channel_id=1, source_target_pairs={{0,32},{4,36},{8,40},{12,44},{32,0},{36,4},{40,8},{44,12},{1,33},{... | collective-permute-start | bytes 294920 | tf_op jit(solution)/shard_map/ppermute | solution.py:190
  10.0 1.2 %collective-permute-start.3 = (bf16[128,640]{1,0:T(8,128)(2,1)S(1)}, bf16[128,640]{1,0:T(8,128)(2,1)S(1)}, u32[]{:S(2)}, u32[]{:S(2)}) collective-permute-start(bf16[128,640]{1,0:T(8,128)(2,1)S(1)} %get-tuple-element.30.refs_0_), channel_id=1, source_target_pairs={{0,64},{1,65},{2,66},{3,67},{4,68},{5,69},{6,70},{7,71},{8,72},{9,... | collective-permute-start | bytes 491528 | tf_op jit(solution)/shard_map/ppermute | solution.py:205
  11.2 2.5 %collective-permute-start.2 = (bf16[128,640]{1,0:T(8,128)(2,1)S(1)}, bf16[128,640]{1,0:T(8,128)(2,1)S(1)}, u32[]{:S(2)}, u32[]{:S(2)}) collective-permute-start(bf16[128,640]{1,0:T(8,128)(2,1)S(1)} %get-tuple-element.30.refs_0_), channel_id=1, source_target_pairs={{0,128},{1,129},{2,130},{3,131},{4,132},{5,133},{6,134},{7,135},{8... | collective-permute-start | bytes 491528 | tf_op jit(solution)/shard_map/ppermute | solution.py:205
  13.7 1.2 %collective-permute-start.1 = (bf16[128,640]{1,0:T(8,128)(2,1)S(1)}, bf16[128,640]{1,0:T(8,128)(2,1)S(1)}, u32[]{:S(2)}, u32[]{:S(2)}) collective-permute-start(bf16[128,640]{1,0:T(8,128)(2,1)S(1)} %get-tuple-element.30.refs_0_), channel_id=1, source_target_pairs={{0,192},{1,193},{2,194},{3,195},{4,196},{5,197},{6,198},{7,199},{8... | collective-permute-start | bytes 491528 | tf_op jit(solution)/shard_map/ppermute | solution.py:205
  14.8 0.0 collective-permute-done
  14.9 0.8 collective-permute-done.3.refs_3_
  15.7 2.7 %collective-permute-done.2.refs_2_ = bf16[128,640]{1,0:T(8,128)(2,1)S(1)} collective-permute-done((bf16[128,640]{1,0:T(8,128)(2,1)S(1)}, bf16[128,640]{1,0:T(8,128)(2,1)S(1)}, u32[]{:S(2)}, u32[]{:S(2)}) %collective-permute-start.2) | collective-permute-done | bytes 163872 | tf_op jit(solution)/shard_map/ppermute | solution.py:205
  18.4 0.0 collective-permute-done.1.refs_1_
  18.4 0.3 split.1
  18.8 2.4 %collective-permute-start.4 = (bf16[256,384]{1,0:T(8,128)(2,1)S(1)}, bf16[256,384]{1,0:T(8,128)(2,1)S(1)}, u32[]{:S(2)}, u32[]{:S(2)}) collective-permute-start(bf16[256,384]{1,0:T(8,128)(2,1)S(1)} %pad_maximum_fusion), channel_id=1, source_target_pairs={{0,16},{16,0},{1,17},{17,1},{2,18},{18,2},{3,19},{19,3},{4,20},{20... | collective-permute-start | bytes 589832 | tf_op jit(solution)/shard_map/ppermute | solution.py:190
  21.2 1.1 %collective-permute-start.9 = (bf16[512,384]{1,0:T(8,128)(2,1)S(1)}, bf16[512,384]{1,0:T(8,128)(2,1)S(1)}, u32[]{:S(2)}, u32[]{:S(2)}) collective-permute-start(bf16[512,384]{1,0:T(8,128)(2,1)S(1)} %get-tuple-element.32.rows_ref), channel_id=1, source_target_pairs={{0,1},{1,2},{2,3},{3,0},{4,5},{5,6},{6,7},{7,4},{8,9},{9,10},{10,1... | collective-permute-start | bytes 1179656 | tf_op jit(solution)/shard_map/ppermute | solution.py:205
  22.3 2.4 %collective-permute-start.8 = (bf16[512,384]{1,0:T(8,128)(2,1)S(1)}, bf16[512,384]{1,0:T(8,128)(2,1)S(1)}, u32[]{:S(2)}, u32[]{:S(2)}) collective-permute-start(bf16[512,384]{1,0:T(8,128)(2,1)S(1)} %get-tuple-element.32.rows_ref), channel_id=1, source_target_pairs={{0,2},{1,3},{2,0},{3,1},{4,6},{5,7},{6,4},{7,5},{8,10},{9,11},{10,... | collective-permute-start | bytes 1179656 | tf_op jit(solution)/shard_map/ppermute | solution.py:205
  24.6 0.9 collective-permute-start.7
  25.6 0.0 copy-start
  25.6 0.1 collective-permute-start.5
  25.7 1.0 %collective-permute-start.6 = (bf16[256,384]{1,0:T(8,128)(2,1)S(1)}, bf16[256,384]{1,0:T(8,128)(2,1)S(1)}, u32[]{:S(2)}, u32[]{:S(2)}) collective-permute-start(bf16[256,384]{1,0:T(8,128)(2,1)S(1)} %pad_maximum_fusion), channel_id=1, source_target_pairs={{0,8},{1,9},{2,10},{3,11},{4,12},{5,13},{6,14},{7,15},{8,32},{9,33... | collective-permute-start | bytes 589832 | tf_op jit(solution)/shard_map/ppermute | solution.py:205
  26.8 0.9 tile.6.refs_0_
  27.7 9.6 %collective-permute-done.6.refs_2_ = bf16[256,384]{1,0:T(8,128)(2,1)S(1)} collective-permute-done((bf16[256,384]{1,0:T(8,128)(2,1)S(1)}, bf16[256,384]{1,0:T(8,128)(2,1)S(1)}, u32[]{:S(2)}, u32[]{:S(2)}) %collective-permute-start.6) | collective-permute-done | bytes 196640 | tf_op jit(solution)/shard_map/ppermute | solution.py:205
  37.3 1.5 %collective-permute-start.10 = (bf16[512,384]{1,0:T(8,128)(2,1)S(1)}, bf16[512,384]{1,0:T(8,128)(2,1)S(1)}, u32[]{:S(2)}, u32[]{:S(2)}) collective-permute-start(bf16[512,384]{1,0:T(8,128)(2,1)S(1)} %collective-permute-done.5.refs_1_), channel_id=1, source_target_pairs={{0,16},{16,0},{1,17},{17,1},{2,18},{18,2},{3,19},{19,3},{4,20},{20... | collective-permute-start | bytes 1179656 | tf_op jit(solution)/shard_map/ppermute | solution.py:190
  38.9 0.3 collective-permute-start.11
  39.2 1.7 %tile.9.refs_0_ = f32[512,256]{1,0:T(8,128)S(1)} custom-call(bf16[128,128]{1,0:T(8,128)(2,1)S(1)} %copy-done, bf16[512,384]{1,0:T(8,128)(2,1)S(1)} %collective-permute-done.8.rows_ref, bf16[512,384]{1,0:T(8,128)(2,1)S(1)} %constant_dynamic-update-slice_fusion.refs_0_, bf16[512,384]{1,0:T(8,128)(2,1)S(1)} %collective-permute-done.5.refs_1_, ...), custom_call_target="tpu_custom_call" | custom-call | tf_op jit(solution)/shard_map/tile/pallas_call | solution.py:259
  40.9 1.1 %tile.10 = bf16[512,256]{1,0:T(8,128)(2,1)S(1)} custom-call(bf16[128,128]{1,0:T(8,128)(2,1)S(1)} %copy-done, bf16[512,384]{1,0:T(8,128)(2,1)S(1)} %collective-permute-done.8.rows_ref, f32[512,256]{1,0:T(8,128)S(1)} %tile.9.refs_0_, bf16[512,384]{1,0:T(8,128)(2,1)S(1)} %collective-permute-done.10.refs_3_.refs_1_, ...), custom_call_target="tpu_custom_call" | custom-call | tf_op jit(solution)/shard_map/tile/pallas_call | solution.py:259
  42.0 2.3 %collective-permute-start.13 = (bf16[512,256]{1,0:T(8,128)(2,1)S(1)}, bf16[512,256]{1,0:T(8,128)(2,1)S(1)}, u32[]{:S(2)}, u32[]{:S(2)}) collective-permute-start(bf16[512,256]{1,0:T(8,128)(2,1)S(1)} %tile.10), channel_id=1, source_target_pairs={{0,2},{1,3},{2,0},{3,1},{4,6},{5,7},{6,4},{7,5},{8,10},{9,11},{10,... | collective-permute-start | bytes 786440 | tf_op jit(solution)/shard_map/ppermute | solution.py:205
  44.4 2.6 %tile.8 = bf16[512,256]{1,0:T(8,128)(2,1)S(1)} custom-call(bf16[128,128]{1,0:T(8,128)(2,1)S(1)} %copy-done, bf16[512,384]{1,0:T(8,128)(2,1)S(1)} %collective-permute-done.7.rows_ref, bf16[512,384]{1,0:T(8,128)(2,1)S(1)} %constant_dynamic-update-slice_fusion.refs_0_, bf16[512,384]{1,0:T(8,128)(2,1)S(1)} %collective-permute-done.5.refs_1_, ...), custom_call_target="tpu_custom_call" | custom-call | tf_op jit(solution)/shard_map/tile/pallas_call | solution.py:259
  46.9 0.6 collective-permute-start.12
  47.6 2.6 %tile.11 = bf16[512,256]{1,0:T(8,128)(2,1)S(1)} custom-call(bf16[128,128]{1,0:T(8,128)(2,1)S(1)} %copy-done, bf16[512,384]{1,0:T(8,128)(2,1)S(1)} %collective-permute-done.9.rows_ref, bf16[512,384]{1,0:T(8,128)(2,1)S(1)} %constant_dynamic-update-slice_fusion.refs_0_, bf16[512,384]{1,0:T(8,128)(2,1)S(1)} %collective-permute-done.5.refs_1_, ...), custom_call_target="tpu_custom_call" | custom-call | tf_op jit(solution)/shard_map/tile/pallas_call | solution.py:259
  50.1 2.4 %collective-permute-start.14 = (bf16[512,256]{1,0:T(8,128)(2,1)S(1)}, bf16[512,256]{1,0:T(8,128)(2,1)S(1)}, u32[]{:S(2)}, u32[]{:S(2)}) collective-permute-start(bf16[512,256]{1,0:T(8,128)(2,1)S(1)} %tile.11), channel_id=1, source_target_pairs={{0,3},{1,0},{2,1},{3,2},{4,7},{5,4},{6,5},{7,6},{8,11},{9,8},{10,9... | collective-permute-start | bytes 786440 | tf_op jit(solution)/shard_map/ppermute | solution.py:205
  52.6 2.0 %tile.7.refs_0_ = f32[512,256]{1,0:T(8,128)S(1)} custom-call(bf16[128,128]{1,0:T(8,128)(2,1)S(1)} %copy-done, bf16[512,384]{1,0:T(8,128)(2,1)S(1)} %get-tuple-element.32.rows_ref, f32[512,256]{1,0:T(8,128)S(1)} %tile.6.refs_0_, bf16[512,384]{1,0:T(8,128)(2,1)S(1)} %collective-permute-done.5.refs_1_, bf16[256,384]{1,0:T(8,128)(2,1)S(1)} %collective-permute-done.6.refs_2_, ...), custom_call_target="tpu_custom_call" | custom-call | tf_op jit(solution)/shard_map/tile/pallas_call | solution.py:259
  54.6 1.4 %collective-permute-done.14.refs_3_ = bf16[512,256]{1,0:T(8,128)(2,1)S(1)} collective-permute-done((bf16[512,256]{1,0:T(8,128)(2,1)S(1)}, bf16[512,256]{1,0:T(8,128)(2,1)S(1)}, u32[]{:S(2)}, u32[]{:S(2)}) %collective-permute-start.14) | collective-permute-done | bytes 262176 | tf_op jit(solution)/shard_map/ppermute | solution.py:205
  55.9 1.2 %sum_rows.1 = (bf16[512,256]{1,0:T(8,128)(2,1)}, f32[128,256]{1,0:T(8,128)S(1)}, bf16[128,256]{1,0:T(8,128)(2,1)S(1)}, bf16[128,256]{1,0:T(8,128)(2,1)S(1)}, bf16[128,256]{1,0:T(8,128)(2,1)S(1)}) custom-call(f32[512,256]{1,0:T(8,128)S(1)} %tile.7.refs_0_, bf16[512,256]{1,0:T(8,128)(2,1)S(1)} %collective-permute-done.12.refs_1_, ...), custom_call_target="tpu_custom_call" | custom-call | tf_op jit(solution)/shard_map/sum_rows/pallas_call | solution.py:282
  57.2 4.4 %all-to-all-start = ((bf16[16,32,256]{2,1,0:T(8,128)(2,1)}), bf16[16,32,256]{2,1,0:T(8,128)(2,1)S(1)}, u32[]{:S(2)}, u32[]{:S(2)}) async-start(bf16[16,32,256]{2,1,0:T(8,128)(2,1)} %bitcast.3), calls=%async_computation | async-start | bytes 524288 | tf_op jit(solution)/shard_map/all_to_all | solution.py:213
  61.6 1.4 %collective-permute-start.15 = (bf16[128,256]{1,0:T(8,128)(2,1)S(1)}, bf16[128,256]{1,0:T(8,128)(2,1)S(1)}, u32[]{:S(2)}, u32[]{:S(2)}) collective-permute-start(bf16[128,256]{1,0:T(8,128)(2,1)S(1)} %get-tuple-element.42), channel_id=1, source_target_pairs={{0,64},{1,65},{2,66},{3,67},{4,68},{5,69},{6,70},{7,71},{8,72},{9,... | collective-permute-start | bytes 196616 | tf_op jit(solution)/shard_map/ppermute | solution.py:205
  63.0 4.5 %collective-permute-done.15.b = bf16[128,256]{1,0:T(8,128)(2,1)S(1)} collective-permute-done((bf16[128,256]{1,0:T(8,128)(2,1)S(1)}, bf16[128,256]{1,0:T(8,128)(2,1)S(1)}, u32[]{:S(2)}, u32[]{:S(2)}) %collective-permute-start.15) | collective-permute-done | bytes 65568 | tf_op jit(solution)/shard_map/ppermute | solution.py:205
  67.4 1.7 %all-to-all-done.refs_0_ = bf16[16,32,256]{2,1,0:T(8,128)(2,1)S(1)} async-done(((bf16[16,32,256]{2,1,0:T(8,128)(2,1)}), bf16[16,32,256]{2,1,0:T(8,128)(2,1)S(1)}, u32[]{:S(2)}, u32[]{:S(2)}) %all-to-all-start) | async-done | bytes 262176 | tf_op jit(solution)/shard_map/all_to_all | solution.py:213
  69.2 0.8 sum_spread.2
  69.9 7.6 %all-to-all-start.1 = ((bf16[16,32,256]{2,1,0:T(8,128)(2,1)}), bf16[16,32,256]{2,1,0:T(8,128)(2,1)S(1)}, u32[]{:S(2)}, u32[]{:S(2)}) async-start(bf16[16,32,256]{2,1,0:T(8,128)(2,1)} %sum_spread.2), calls=%async_computation.1 | async-start | bytes 524288 | tf_op jit(solution)/shard_map/all_to_all | solution.py:213
  77.5 1.0 collective-permute-start.16
  78.5 3.9 %collective-permute-done.16.c = bf16[128,256]{1,0:T(8,128)(2,1)S(1)} collective-permute-done((bf16[128,256]{1,0:T(8,128)(2,1)S(1)}, bf16[128,256]{1,0:T(8,128)(2,1)S(1)}, u32[]{:S(2)}, u32[]{:S(2)}) %collective-permute-start.16) | collective-permute-done | bytes 65568 | tf_op jit(solution)/shard_map/ppermute | solution.py:205
  82.4 4.7 %all-to-all-done.1.refs_0_ = bf16[16,32,256]{2,1,0:T(8,128)(2,1)S(1)} async-done(((bf16[16,32,256]{2,1,0:T(8,128)(2,1)}), bf16[16,32,256]{2,1,0:T(8,128)(2,1)S(1)}, u32[]{:S(2)}, u32[]{:S(2)}) %all-to-all-start.1) | async-done | bytes 262176 | tf_op jit(solution)/shard_map/all_to_all | solution.py:213
  87.1 0.8 sum_spread.3
  87.8 3.5 %all-to-all-start.2 = ((bf16[16,32,256]{2,1,0:T(8,128)(2,1)}), bf16[16,32,256]{2,1,0:T(8,128)(2,1)S(1)}, u32[]{:S(2)}, u32[]{:S(2)}) async-start(bf16[16,32,256]{2,1,0:T(8,128)(2,1)} %sum_spread.3), calls=%async_computation.2 | async-start | bytes 524288 | tf_op jit(solution)/shard_map/all_to_all | solution.py:213
  91.4 2.5 %collective-permute-start.17 = (bf16[128,256]{1,0:T(8,128)(2,1)S(1)}, bf16[128,256]{1,0:T(8,128)(2,1)S(1)}, u32[]{:S(2)}, u32[]{:S(2)}) collective-permute-start(bf16[128,256]{1,0:T(8,128)(2,1)S(1)} %get-tuple-element.53), channel_id=1, source_target_pairs={{0,192},{1,193},{2,194},{3,195},{4,196},{5,197},{6,198},{7,199},{8... | collective-permute-start | bytes 196616 | tf_op jit(solution)/shard_map/ppermute | solution.py:205
  93.9 3.6 %collective-permute-done.17.d = bf16[128,256]{1,0:T(8,128)(2,1)S(1)} collective-permute-done((bf16[128,256]{1,0:T(8,128)(2,1)S(1)}, bf16[128,256]{1,0:T(8,128)(2,1)S(1)}, u32[]{:S(2)}, u32[]{:S(2)}) %collective-permute-start.17) | collective-permute-done | bytes 65568 | tf_op jit(solution)/shard_map/ppermute | solution.py:205
  97.5 0.7 finish_rows.1
  98.1 1.6 %all-to-all-done.2 = bf16[16,32,256]{2,1,0:T(8,128)(2,1)S(1)} async-done(((bf16[16,32,256]{2,1,0:T(8,128)(2,1)}), bf16[16,32,256]{2,1,0:T(8,128)(2,1)S(1)}, u32[]{:S(2)}, u32[]{:S(2)}) %all-to-all-start.2) | async-done | bytes 262176 | tf_op jit(solution)/shard_map/all_to_all | solution.py:213
  99.8 0.8 convert_multiply_fusion
  (14 shorter events, 0.1 us)
Async XLA Ops:
  2.2 16.3 %copy-start.1 = (bf16[512,256]{1,0:T(8,128)(2,1)S(1)}, bf16[512,256]{1,0:T(8,128)(2,1)}, u32[]{:S(2)}) copy-start(bf16[512,256]{1,0:T(8,128)(2,1)} %weight.3) | copy-start | bytes 786436
  2.2 12.6 %collective-permute-start = (bf16[128,384]{1,0:T(8,128)(2,1)S(1)}, bf16[128,384]{1,0:T(8,128)(2,1)S(1)}, u32[]{:S(2)}, u32[]{:S(2)}) collective-permute-start(bf16[128,384]{1,0:T(8,128)(2,1)S(1)} %get-tuple-element.29), channel_id=1, source_target_pairs={{0,32},{4,36},{8,40},{12,44},{32,0},{36,4},{40,8},{44,12},{1,33},{... | collective-permute-start | bytes 294920 | tf_op jit(solution)/shard_map/ppermute | solution.py:190
  10.0 5.7 %collective-permute-start.3 = (bf16[128,640]{1,0:T(8,128)(2,1)S(1)}, bf16[128,640]{1,0:T(8,128)(2,1)S(1)}, u32[]{:S(2)}, u32[]{:S(2)}) collective-permute-start(bf16[128,640]{1,0:T(8,128)(2,1)S(1)} %get-tuple-element.30.refs_0_), channel_id=1, source_target_pairs={{0,64},{1,65},{2,66},{3,67},{4,68},{5,69},{6,70},{7,71},{8,72},{9,... | collective-permute-start | bytes 491528 | tf_op jit(solution)/shard_map/ppermute | solution.py:205
  11.2 7.2 %collective-permute-start.2 = (bf16[128,640]{1,0:T(8,128)(2,1)S(1)}, bf16[128,640]{1,0:T(8,128)(2,1)S(1)}, u32[]{:S(2)}, u32[]{:S(2)}) collective-permute-start(bf16[128,640]{1,0:T(8,128)(2,1)S(1)} %get-tuple-element.30.refs_0_), channel_id=1, source_target_pairs={{0,128},{1,129},{2,130},{3,131},{4,132},{5,133},{6,134},{7,135},{8... | collective-permute-start | bytes 491528 | tf_op jit(solution)/shard_map/ppermute | solution.py:205
  13.7 4.8 %collective-permute-start.1 = (bf16[128,640]{1,0:T(8,128)(2,1)S(1)}, bf16[128,640]{1,0:T(8,128)(2,1)S(1)}, u32[]{:S(2)}, u32[]{:S(2)}) collective-permute-start(bf16[128,640]{1,0:T(8,128)(2,1)S(1)} %get-tuple-element.30.refs_0_), channel_id=1, source_target_pairs={{0,192},{1,193},{2,194},{3,195},{4,196},{5,197},{6,198},{7,199},{8... | collective-permute-start | bytes 491528 | tf_op jit(solution)/shard_map/ppermute | solution.py:205
  18.8 6.8 %collective-permute-start.4 = (bf16[256,384]{1,0:T(8,128)(2,1)S(1)}, bf16[256,384]{1,0:T(8,128)(2,1)S(1)}, u32[]{:S(2)}, u32[]{:S(2)}) collective-permute-start(bf16[256,384]{1,0:T(8,128)(2,1)S(1)} %pad_maximum_fusion), channel_id=1, source_target_pairs={{0,16},{16,0},{1,17},{17,1},{2,18},{18,2},{3,19},{19,3},{4,20},{20... | collective-permute-start | bytes 589832 | tf_op jit(solution)/shard_map/ppermute | solution.py:190
  21.2 16.1 %collective-permute-start.9 = (bf16[512,384]{1,0:T(8,128)(2,1)S(1)}, bf16[512,384]{1,0:T(8,128)(2,1)S(1)}, u32[]{:S(2)}, u32[]{:S(2)}) collective-permute-start(bf16[512,384]{1,0:T(8,128)(2,1)S(1)} %get-tuple-element.32.rows_ref), channel_id=1, source_target_pairs={{0,1},{1,2},{2,3},{3,0},{4,5},{5,6},{6,7},{7,4},{8,9},{9,10},{10,1... | collective-permute-start | bytes 1179656 | tf_op jit(solution)/shard_map/ppermute | solution.py:205
  22.3 15.0 %collective-permute-start.8 = (bf16[512,384]{1,0:T(8,128)(2,1)S(1)}, bf16[512,384]{1,0:T(8,128)(2,1)S(1)}, u32[]{:S(2)}, u32[]{:S(2)}) collective-permute-start(bf16[512,384]{1,0:T(8,128)(2,1)S(1)} %get-tuple-element.32.rows_ref), channel_id=1, source_target_pairs={{0,2},{1,3},{2,0},{3,1},{4,6},{5,7},{6,4},{7,5},{8,10},{9,11},{10,... | collective-permute-start | bytes 1179656 | tf_op jit(solution)/shard_map/ppermute | solution.py:205
  24.6 12.7 %collective-permute-start.7 = (bf16[512,384]{1,0:T(8,128)(2,1)S(1)}, bf16[512,384]{1,0:T(8,128)(2,1)S(1)}, u32[]{:S(2)}, u32[]{:S(2)}) collective-permute-start(bf16[512,384]{1,0:T(8,128)(2,1)S(1)} %get-tuple-element.32.rows_ref), channel_id=1, source_target_pairs={{0,3},{1,0},{2,1},{3,2},{4,7},{5,4},{6,5},{7,6},{8,11},{9,8},{10,9... | collective-permute-start | bytes 1179656 | tf_op jit(solution)/shard_map/ppermute | solution.py:205
  25.6 1.2 %copy-start = (bf16[128,128]{1,0:T(8,128)(2,1)S(1)}, bf16[128,128]{1,0:T(8,128)(2,1)}, u32[]{:S(2)}) copy-start(bf16[128,128]{1,0:T(8,128)(2,1)} %constant.4.clone.table) | copy-start | bytes 98308
  25.6 11.7 %collective-permute-start.5 = (bf16[512,384]{1,0:T(8,128)(2,1)S(1)}, bf16[512,384]{1,0:T(8,128)(2,1)S(1)}, u32[]{:S(2)}, u32[]{:S(2)}) collective-permute-start(bf16[512,384]{1,0:T(8,128)(2,1)S(1)} %constant_dynamic-update-slice_fusion.refs_0_), channel_id=1, source_target_pairs={{0,4},{1,5},{2,6},{3,7},{4,8},{5,9},{6,10},{7,11},{8,12},{9,13},{1... | collective-permute-start | bytes 1179656 | tf_op jit(solution)/shard_map/ppermute | solution.py:205
  25.7 11.6 %collective-permute-start.6 = (bf16[256,384]{1,0:T(8,128)(2,1)S(1)}, bf16[256,384]{1,0:T(8,128)(2,1)S(1)}, u32[]{:S(2)}, u32[]{:S(2)}) collective-permute-start(bf16[256,384]{1,0:T(8,128)(2,1)S(1)} %pad_maximum_fusion), channel_id=1, source_target_pairs={{0,8},{1,9},{2,10},{3,11},{4,12},{5,13},{6,14},{7,15},{8,32},{9,33... | collective-permute-start | bytes 589832 | tf_op jit(solution)/shard_map/ppermute | solution.py:205
  37.3 3.6 %collective-permute-start.10 = (bf16[512,384]{1,0:T(8,128)(2,1)S(1)}, bf16[512,384]{1,0:T(8,128)(2,1)S(1)}, u32[]{:S(2)}, u32[]{:S(2)}) collective-permute-start(bf16[512,384]{1,0:T(8,128)(2,1)S(1)} %collective-permute-done.5.refs_1_), channel_id=1, source_target_pairs={{0,16},{16,0},{1,17},{17,1},{2,18},{18,2},{3,19},{19,3},{4,20},{20... | collective-permute-start | bytes 1179656 | tf_op jit(solution)/shard_map/ppermute | solution.py:190
  38.9 2.0 %collective-permute-start.11 = (bf16[256,384]{1,0:T(8,128)(2,1)S(1)}, bf16[256,384]{1,0:T(8,128)(2,1)S(1)}, u32[]{:S(2)}, u32[]{:S(2)}) collective-permute-start(bf16[256,384]{1,0:T(8,128)(2,1)S(1)} %collective-permute-done.6.refs_2_), channel_id=1, source_target_pairs={{0,16},{16,0},{1,17},{17,1},{2,18},{18,2},{3,19},{19,3},{4,20},{20... | collective-permute-start | bytes 589832 | tf_op jit(solution)/shard_map/ppermute | solution.py:190
  42.0 12.5 %collective-permute-start.13 = (bf16[512,256]{1,0:T(8,128)(2,1)S(1)}, bf16[512,256]{1,0:T(8,128)(2,1)S(1)}, u32[]{:S(2)}, u32[]{:S(2)}) collective-permute-start(bf16[512,256]{1,0:T(8,128)(2,1)S(1)} %tile.10), channel_id=1, source_target_pairs={{0,2},{1,3},{2,0},{3,1},{4,6},{5,7},{6,4},{7,5},{8,10},{9,11},{10,... | collective-permute-start | bytes 786440 | tf_op jit(solution)/shard_map/ppermute | solution.py:205
  46.9 7.6 %collective-permute-start.12 = (bf16[512,256]{1,0:T(8,128)(2,1)S(1)}, bf16[512,256]{1,0:T(8,128)(2,1)S(1)}, u32[]{:S(2)}, u32[]{:S(2)}) collective-permute-start(bf16[512,256]{1,0:T(8,128)(2,1)S(1)} %tile.8), channel_id=1, source_target_pairs={{0,1},{1,2},{2,3},{3,0},{4,5},{5,6},{6,7},{7,4},{8,9},{9,10},{10,1... | collective-permute-start | bytes 786440 | tf_op jit(solution)/shard_map/ppermute | solution.py:205
  50.1 5.8 %collective-permute-start.14 = (bf16[512,256]{1,0:T(8,128)(2,1)S(1)}, bf16[512,256]{1,0:T(8,128)(2,1)S(1)}, u32[]{:S(2)}, u32[]{:S(2)}) collective-permute-start(bf16[512,256]{1,0:T(8,128)(2,1)S(1)} %tile.11), channel_id=1, source_target_pairs={{0,3},{1,0},{2,1},{3,2},{4,7},{5,4},{6,5},{7,6},{8,11},{9,8},{10,9... | collective-permute-start | bytes 786440 | tf_op jit(solution)/shard_map/ppermute | solution.py:205
  57.2 12.0 %all-to-all-start = ((bf16[16,32,256]{2,1,0:T(8,128)(2,1)}), bf16[16,32,256]{2,1,0:T(8,128)(2,1)S(1)}, u32[]{:S(2)}, u32[]{:S(2)}) async-start(bf16[16,32,256]{2,1,0:T(8,128)(2,1)} %bitcast.3), calls=%async_computation | async-start | bytes 524288 | tf_op jit(solution)/shard_map/all_to_all | solution.py:213
  61.6 5.8 %collective-permute-start.15 = (bf16[128,256]{1,0:T(8,128)(2,1)S(1)}, bf16[128,256]{1,0:T(8,128)(2,1)S(1)}, u32[]{:S(2)}, u32[]{:S(2)}) collective-permute-start(bf16[128,256]{1,0:T(8,128)(2,1)S(1)} %get-tuple-element.42), channel_id=1, source_target_pairs={{0,64},{1,65},{2,66},{3,67},{4,68},{5,69},{6,70},{7,71},{8,72},{9,... | collective-permute-start | bytes 196616 | tf_op jit(solution)/shard_map/ppermute | solution.py:205
  69.9 17.2 %all-to-all-start.1 = ((bf16[16,32,256]{2,1,0:T(8,128)(2,1)}), bf16[16,32,256]{2,1,0:T(8,128)(2,1)S(1)}, u32[]{:S(2)}, u32[]{:S(2)}) async-start(bf16[16,32,256]{2,1,0:T(8,128)(2,1)} %sum_spread.2), calls=%async_computation.1 | async-start | bytes 524288 | tf_op jit(solution)/shard_map/all_to_all | solution.py:213
  77.5 4.9 %collective-permute-start.16 = (bf16[128,256]{1,0:T(8,128)(2,1)S(1)}, bf16[128,256]{1,0:T(8,128)(2,1)S(1)}, u32[]{:S(2)}, u32[]{:S(2)}) collective-permute-start(bf16[128,256]{1,0:T(8,128)(2,1)S(1)} %get-tuple-element.46), channel_id=1, source_target_pairs={{0,128},{1,129},{2,130},{3,131},{4,132},{5,133},{6,134},{7,135},{8... | collective-permute-start | bytes 196616 | tf_op jit(solution)/shard_map/ppermute | solution.py:205
  87.8 11.9 %all-to-all-start.2 = ((bf16[16,32,256]{2,1,0:T(8,128)(2,1)}), bf16[16,32,256]{2,1,0:T(8,128)(2,1)S(1)}, u32[]{:S(2)}, u32[]{:S(2)}) async-start(bf16[16,32,256]{2,1,0:T(8,128)(2,1)} %sum_spread.3), calls=%async_computation.2 | async-start | bytes 524288 | tf_op jit(solution)/shard_map/all_to_all | solution.py:213
  91.4 6.1 %collective-permute-start.17 = (bf16[128,256]{1,0:T(8,128)(2,1)S(1)}, bf16[128,256]{1,0:T(8,128)(2,1)S(1)}, u32[]{:S(2)}, u32[]{:S(2)}) collective-permute-start(bf16[128,256]{1,0:T(8,128)(2,1)S(1)} %get-tuple-element.53), channel_id=1, source_target_pairs={{0,192},{1,193},{2,194},{3,195},{4,196},{5,197},{6,198},{7,199},{8... | collective-permute-start | bytes 196616 | tf_op jit(solution)/shard_map/ppermute | solution.py:205

commit v10 on v9

--- a/solution.py
+++ b/solution.py
@@ -79,9 +79,11 @@
     for k, ref in enumerate(refs[:count]):
         block = slice(k * rows, (k + 1) * rows)
         own = ref[:, 128:]
-        line[block, :width] = jnp.dot(own, weight[...], preferred_element_type=F32).astype(BF16)
-        line[block, width:] = ref[:, :128]
+        line[block, :] = jnp.dot(own, weight[...], preferred_element_type=F32).astype(BF16)
         embeds[block, :] = own
+    for k in range(0, count, 2):
+        both = [ref[:, :64].astype(F32) for ref in refs[k : k + 2]]
+        line[count * rows :, k * 64 : k * 64 + 128] = jnp.concatenate(both, axis=1).astype(BF16)
 
 
 def left_map(count):
@@ -91,10 +93,11 @@
     for k in range(count):
         source[1 + k], sign[1 + k] = 1 + count + k, -1.0
         source[1 + count + k], sign[1 + count + k] = 1 + k, -1.0
-    table = np.zeros((128, 128), np.float32)
-    for group, offset in ((0, 0), (1, 0), (2, 32)):
-        for k in range(32):
-            table[offset + source[k], 32 * group + k] = sign[k]
+    table = np.zeros((2, 128, 128), np.float32)
+    for half in range(2):
+        for group, offset in ((0, 0), (1, 0), (2, 32)):
+            for k in range(32):
+                table[half, 64 * half + offset + source[k], 32 * group + k] = sign[k]
     return jnp.asarray(table, BF16)
 
 
@@ -103,14 +106,18 @@
     if adds:
         begin, *columns = columns
     width = out.shape[1]
-    rows = rows_ref.shape[0]
-    u_rows = rows_ref[:, :width]
-    fac = rows_ref[:, width:]
-    twice = (u_rows.astype(F32) * -2.0).astype(BF16)
-    left = jnp.dot(fac, table[...], preferred_element_type=F32).astype(BF16)
-    lane = lax.broadcasted_iota(jnp.int32, (128, 128), 0)
-    pick = jnp.where((lane >= 96) & (lane < 99), 1.0, 0.0).astype(BF16)
-    sq_rows = jnp.dot(fac, pick, preferred_element_type=F32)[:, :1]
+    block = rows_ref.shape[0] // 5
+    rows = 4 * block
+    u_rows = rows_ref[:rows, :]
+    wide = u_rows.astype(F32)
+    twice = (wide * -2.0).astype(BF16)
+    left = []
+    for k in range(4):
+        start = k // 2 * 128
+        fac = rows_ref[rows:, start : start + 128]
+        left.append(jnp.dot(fac, table[k % 2], preferred_element_type=F32).astype(BF16))
+    left = jnp.concatenate(left, axis=0)
+    sq_rows = jnp.sum(wide * wide, axis=1, keepdims=True)
     lane = lax.broadcasted_iota(jnp.int32, (8, 128), 1)
     pick_cols = jnp.where((lane >= 96) & (lane < 99), 1.0, 0.0).astype(BF16)
     blocks = [slice(k, k + sub) for k in range(0, rows, sub)]
@@ -239,7 +246,7 @@
     line, embeds_line = pl.pallas_call(
         functools.partial(split_kernel, n_side),
         out_shape=[
-            jax.ShapeDtypeStruct((n_side * rows, width + 128), BF16),
+            jax.ShapeDtypeStruct(((n_side + 1) * rows, width), BF16),
             jax.ShapeDtypeStruct((n_side * rows, embeds.shape[1]), BF16),
         ],
         in_specs=[VMEM] * (n_side + 1),
@@ -258,7 +265,7 @@
     def tile(rows_in, columns, dtype, start=None):
         return pl.pallas_call(
             functools.partial(tile_kernel, 256, 256, start is not None),
-            out_shape=jax.ShapeDtypeStruct((rows_in.shape[0], width), dtype),
+            out_shape=jax.ShapeDtypeStruct((n_side * rows, width), dtype),
             in_specs=[VMEM] * (2 + len(columns) + (start is not None)),
             out_specs=VMEM,
             compiler_params=params(16),
@@ -296,14 +303,9 @@
     pieces = exchange(partial.reshape(n_plane, -1, width), PLANE)
     pieces, arrived[0] = lax.optimization_barrier((pieces, arrived[0]))
     spread = sum_spread([pieces], n_z * 2, BF16)
-    spread, other_rows[1] = lax.optimization_barrier((spread, other_rows[1]))
+    spread, other_rows[1], other_rows[2] = lax.optimization_barrier((spread, other_rows[1], other_rows[2]))
     pieces = exchange(spread, STACK)
-    arrived.append(turn(other_rows[1], sizes, 0, 2))
-    pieces, arrived[1] = lax.optimization_barrier((pieces, arrived[1]))
-    spread = sum_spread([pieces], n_plane, BF16)
-    spread, other_rows[2] = lax.optimization_barrier((spread, other_rows[2]))
-    pieces = exchange(spread, PLANE)
-    arrived.append(turn(other_rows[2], sizes, 0, 3))
+    arrived += [turn(other_rows[d], sizes, 0, d + 1) for d in (1, 2)]
     grad_rows = pl.pallas_call(
         finish_rows_kernel,
         out_shape=jax.ShapeDtypeStruct((rows, width), F32),
@@ -313,6 +315,7 @@
         name="finish_rows",
     )(own_rows, *arrived)
     pieces, grad_rows = lax.optimization_barrier((pieces, grad_rows))
+    pieces = exchange(sum_spread([pieces], n_plane, BF16), PLANE)
     total_points = rows * n_plane * n_z * 2
     grad_weight = pieces.reshape(-1, width).astype(F32) * (1.0 / math.sqrt(total_points))
     return grad_rows, grad_weight

time: 102 us -> 100 us (0.980)
  blocking collectives: 0 us -> 10.7 us
  waiting for transfers between devices: 34.6 us -> 24.3 us
  starting transfers between devices: 48.2 us -> 46.1 us
    all_to_all x0 -> x1, blocking collectives: none -> 10.7 us  [exchange(): return lax.all_to_all(array, axes, split_axis=0, concat_axis=0, tiled=True)]
    ppermute x14, waiting for transfers between devices: 26.6 us -> 17.2 us  [move(): return lax.ppermute(array, ALL, perm)]
    all_to_all x3 -> x2, starting transfers between devices: 15.6 us -> 11.1 us  [exchange(): return lax.all_to_all(array, axes, split_axis=0, concat_axis=0, tiled=True)]
    ppermute x4, starting transfers between devices: 12.1 us -> 15.2 us  [ring(): lax.ppermute(array, axis, [(i, (i + shift) % size) for i in range(size)])]
    all_to_all x3 -> x2, waiting for transfers between devices: 7.99 us -> 6.03 us  [exchange(): return lax.all_to_all(array, axes, split_axis=0, concat_axis=0, tiled=True)]
    ppermute x4, waiting for transfers between devices: 0.01 us -> 1.04 us  [ring(): lax.ppermute(array, axis, [(i, (i + shift) % size) for i in range(size)])]
  transfers between devices with their start and end apart: 21 -> 20, of which waited for: 10 -> 9; matrix products, arithmetic and copies ran while one was open for 0% -> 0% of each run, Pallas kernels for 10% -> 11%
where the time goes in v10:
time: 100 us; the launch traced here: 98.8 us
  starting transfers between devices  46.1 us (46%)
  waiting for transfers between devices  24.3 us (24%)
  Pallas kernels  15.9 us (16%)
  blocking collectives  10.7 us (11%)
    ppermute x14, starting transfers between devices, move(): return lax.ppermute(array, ALL, perm)  19.8 us
    ppermute x14, waiting for transfers between devices, move(): return lax.ppermute(array, ALL, perm)  17.2 us
    ppermute x4, starting transfers between devices, ring(): lax.ppermute(array, axis, [(i, (i + shift) % size) for i in range(size)])  15.2 us
    pallas_call x6, Pallas kernels, tile(): pl.pallas_call(functools.partial(tile_kernel, 256, 256, start is not None...  11.4 us
    all_to_all x2, starting transfers between devices, exchange(): return lax.all_to_all(array, axes, split_axis=0, concat_axis=0, tiled=True)  11.1 us
    all_to_all x1, blocking collectives, exchange(): return lax.all_to_all(array, axes, split_axis=0, concat_axis=0, tiled=True)  10.7 us
    all_to_all x2, waiting for transfers between devices, exchange(): return lax.all_to_all(array, axes, split_axis=0, concat_axis=0, tiled=True)  6.03 us
  transfers between devices with their start and end apart: 20, of which 9 were waited for; matrix products, arithmetic and copies ran while one was open for 0% of the time, Pallas kernels for 11%

profile of v10, /device:TPU:1, one launch (start us, length us, event | category | flops | bytes accessed | tf_op | source)
XLA Modules:
  0.0 98.8 jit_solution(18289299104166323491)
XLA Ops:
  0.6 1.5 %pack.1 = (bf16[128,384]{1,0:T(8,128)(2,1)S(1)}, bf16[128,640]{1,0:T(8,128)(2,1)S(1)}) custom-call(bf16[128,512]{1,0:T(8,128)(2,1)} %embeds.1, bf16[512,256]{1,0:T(8,128)(2,1)} %weight.3, f32[1,128]{1,0:T(1,128)} %bitcast.8, f32[15,128]{1,0:T(8,128)} %bitcast.6, f32[15,128]{1,0:T(8,128)} %bitcast.7), custom_call_target="tpu_custom_call" | custom-call | tf_op jit(solution)/shard_map/pack/pallas_call | solution.py:226
  2.2 0.0 copy-start.1
  2.2 7.8 %collective-permute-start = (bf16[128,384]{1,0:T(8,128)(2,1)S(1)}, bf16[128,384]{1,0:T(8,128)(2,1)S(1)}, u32[]{:S(2)}, u32[]{:S(2)}) collective-permute-start(bf16[128,384]{1,0:T(8,128)(2,1)S(1)} %get-tuple-element.26), channel_id=1, source_target_pairs={{0,32},{4,36},{8,40},{12,44},{32,0},{36,4},{40,8},{44,12},{1,33},{... | collective-permute-start | bytes 294920 | tf_op jit(solution)/shard_map/ppermute | solution.py:197
  10.0 1.2 %collective-permute-start.3 = (bf16[128,640]{1,0:T(8,128)(2,1)S(1)}, bf16[128,640]{1,0:T(8,128)(2,1)S(1)}, u32[]{:S(2)}, u32[]{:S(2)}) collective-permute-start(bf16[128,640]{1,0:T(8,128)(2,1)S(1)} %get-tuple-element.27.refs_0_), channel_id=1, source_target_pairs={{0,64},{1,65},{2,66},{3,67},{4,68},{5,69},{6,70},{7,71},{8,72},{9,... | collective-permute-start | bytes 491528 | tf_op jit(solution)/shard_map/ppermute | solution.py:212
  11.2 2.5 %collective-permute-start.2 = (bf16[128,640]{1,0:T(8,128)(2,1)S(1)}, bf16[128,640]{1,0:T(8,128)(2,1)S(1)}, u32[]{:S(2)}, u32[]{:S(2)}) collective-permute-start(bf16[128,640]{1,0:T(8,128)(2,1)S(1)} %get-tuple-element.27.refs_0_), channel_id=1, source_target_pairs={{0,128},{1,129},{2,130},{3,131},{4,132},{5,133},{6,134},{7,135},{8... | collective-permute-start | bytes 491528 | tf_op jit(solution)/shard_map/ppermute | solution.py:212
  13.7 1.2 %collective-permute-start.1 = (bf16[128,640]{1,0:T(8,128)(2,1)S(1)}, bf16[128,640]{1,0:T(8,128)(2,1)S(1)}, u32[]{:S(2)}, u32[]{:S(2)}) collective-permute-start(bf16[128,640]{1,0:T(8,128)(2,1)S(1)} %get-tuple-element.27.refs_0_), channel_id=1, source_target_pairs={{0,192},{1,193},{2,194},{3,195},{4,196},{5,197},{6,198},{7,199},{8... | collective-permute-start | bytes 491528 | tf_op jit(solution)/shard_map/ppermute | solution.py:212
  14.8 0.0 collective-permute-done
  14.9 0.8 collective-permute-done.3.refs_3_
  15.7 2.7 %collective-permute-done.2.refs_2_ = bf16[128,640]{1,0:T(8,128)(2,1)S(1)} collective-permute-done((bf16[128,640]{1,0:T(8,128)(2,1)S(1)}, bf16[128,640]{1,0:T(8,128)(2,1)S(1)}, u32[]{:S(2)}, u32[]{:S(2)}) %collective-permute-start.2) | collective-permute-done | bytes 163872 | tf_op jit(solution)/shard_map/ppermute | solution.py:212
  18.4 0.0 collective-permute-done.1.refs_1_
  18.4 0.3 split.1
  18.8 2.4 %collective-permute-start.4 = (bf16[256,384]{1,0:T(8,128)(2,1)S(1)}, bf16[256,384]{1,0:T(8,128)(2,1)S(1)}, u32[]{:S(2)}, u32[]{:S(2)}) collective-permute-start(bf16[256,384]{1,0:T(8,128)(2,1)S(1)} %pad_maximum_fusion), channel_id=1, source_target_pairs={{0,16},{16,0},{1,17},{17,1},{2,18},{18,2},{3,19},{19,3},{4,20},{20... | collective-permute-start | bytes 589832 | tf_op jit(solution)/shard_map/ppermute | solution.py:197
  21.2 0.0 copy-start
  21.2 1.0 %collective-permute-done.4 = bf16[256,384]{1,0:T(8,128)(2,1)S(1)} collective-permute-done((bf16[256,384]{1,0:T(8,128)(2,1)S(1)}, bf16[256,384]{1,0:T(8,128)(2,1)S(1)}, u32[]{:S(2)}, u32[]{:S(2)}) %collective-permute-start.4) | collective-permute-done | bytes 196640 | tf_op jit(solution)/shard_map/ppermute | solution.py:197
  22.3 0.1 collective-permute-start.5
  22.4 1.2 %collective-permute-start.9 = (bf16[640,256]{1,0:T(8,128)(2,1)S(1)}, bf16[640,256]{1,0:T(8,128)(2,1)S(1)}, u32[]{:S(2)}, u32[]{:S(2)}) collective-permute-start(bf16[640,256]{1,0:T(8,128)(2,1)S(1)} %get-tuple-element.29.rows_ref), channel_id=1, source_target_pairs={{0,1},{1,2},{2,3},{3,0},{4,5},{5,6},{6,7},{7,4},{8,9},{9,10},{10,1... | collective-permute-start | bytes 983048 | tf_op jit(solution)/shard_map/ppermute | solution.py:212
  23.5 2.4 %collective-permute-start.8 = (bf16[640,256]{1,0:T(8,128)(2,1)S(1)}, bf16[640,256]{1,0:T(8,128)(2,1)S(1)}, u32[]{:S(2)}, u32[]{:S(2)}) collective-permute-start(bf16[640,256]{1,0:T(8,128)(2,1)S(1)} %get-tuple-element.29.rows_ref), channel_id=1, source_target_pairs={{0,2},{1,3},{2,0},{3,1},{4,6},{5,7},{6,4},{7,5},{8,10},{9,11},{10,... | collective-permute-start | bytes 983048 | tf_op jit(solution)/shard_map/ppermute | solution.py:212
  25.9 0.9 collective-permute-start.7
  26.8 1.0 collective-permute-start.6
  27.8 0.9 tile.6.refs_0_
  28.7 6.0 %collective-permute-done.6.refs_2_ = bf16[256,384]{1,0:T(8,128)(2,1)S(1)} collective-permute-done((bf16[256,384]{1,0:T(8,128)(2,1)S(1)}, bf16[256,384]{1,0:T(8,128)(2,1)S(1)}, u32[]{:S(2)}, u32[]{:S(2)}) %collective-permute-start.6) | collective-permute-done | bytes 196640 | tf_op jit(solution)/shard_map/ppermute | solution.py:212
  34.7 0.0 collective-permute-done.5.refs_1_
  34.7 4.7 %collective-permute-start.10 = (bf16[512,384]{1,0:T(8,128)(2,1)S(1)}, bf16[512,384]{1,0:T(8,128)(2,1)S(1)}, u32[]{:S(2)}, u32[]{:S(2)}) collective-permute-start(bf16[512,384]{1,0:T(8,128)(2,1)S(1)} %collective-permute-done.5.refs_1_), channel_id=1, source_target_pairs={{0,16},{16,0},{1,17},{17,1},{2,18},{18,2},{3,19},{19,3},{4,20},{20... | collective-permute-start | bytes 1179656 | tf_op jit(solution)/shard_map/ppermute | solution.py:197
  39.4 0.3 collective-permute-start.11
  39.7 1.8 %tile.9.refs_0_ = f32[512,256]{1,0:T(8,128)S(1)} custom-call(bf16[2,128,128]{2,1,0:T(8,128)(2,1)S(1)} %copy-done, bf16[640,256]{1,0:T(8,128)(2,1)S(1)} %collective-permute-done.8.rows_ref, bf16[512,384]{1,0:T(8,128)(2,1)S(1)} %constant_dynamic-update-slice_fusion.refs_0_, bf16[512,384]{1,0:T(8,128)(2,1)S(1)} %collective-permute-done.5.refs_1_, ...), custom_call_target="tpu_custom_call" | custom-call | tf_op jit(solution)/shard_map/tile/pallas_call | solution.py:266
  41.5 0.0 collective-permute-done.10.refs_3_.refs_1_
  41.5 1.2 %tile.10 = bf16[512,256]{1,0:T(8,128)(2,1)S(1)} custom-call(bf16[2,128,128]{2,1,0:T(8,128)(2,1)S(1)} %copy-done, bf16[640,256]{1,0:T(8,128)(2,1)S(1)} %collective-permute-done.8.rows_ref, f32[512,256]{1,0:T(8,128)S(1)} %tile.9.refs_0_, bf16[512,384]{1,0:T(8,128)(2,1)S(1)} %collective-permute-done.10.refs_3_.refs_1_, ...), custom_call_target="tpu_custom_call" | custom-call | tf_op jit(solution)/shard_map/tile/pallas_call | solution.py:266
  42.8 2.4 %collective-permute-start.13 = (bf16[512,256]{1,0:T(8,128)(2,1)S(1)}, bf16[512,256]{1,0:T(8,128)(2,1)S(1)}, u32[]{:S(2)}, u32[]{:S(2)}) collective-permute-start(bf16[512,256]{1,0:T(8,128)(2,1)S(1)} %tile.10), channel_id=1, source_target_pairs={{0,2},{1,3},{2,0},{3,1},{4,6},{5,7},{6,4},{7,5},{8,10},{9,11},{10,... | collective-permute-start | bytes 786440 | tf_op jit(solution)/shard_map/ppermute | solution.py:212
  45.2 2.7 %tile.8 = bf16[512,256]{1,0:T(8,128)(2,1)S(1)} custom-call(bf16[2,128,128]{2,1,0:T(8,128)(2,1)S(1)} %copy-done, bf16[640,256]{1,0:T(8,128)(2,1)S(1)} %collective-permute-done.7.rows_ref, bf16[512,384]{1,0:T(8,128)(2,1)S(1)} %constant_dynamic-update-slice_fusion.refs_0_, bf16[512,384]{1,0:T(8,128)(2,1)S(1)} %collective-permute-done.5.refs_1_, ...), custom_call_target="tpu_custom_call" | custom-call | tf_op jit(solution)/shard_map/tile/pallas_call | solution.py:266
  47.8 0.6 collective-permute-start.12
  48.5 2.7 %tile.11 = bf16[512,256]{1,0:T(8,128)(2,1)S(1)} custom-call(bf16[2,128,128]{2,1,0:T(8,128)(2,1)S(1)} %copy-done, bf16[640,256]{1,0:T(8,128)(2,1)S(1)} %collective-permute-done.9.rows_ref, bf16[512,384]{1,0:T(8,128)(2,1)S(1)} %constant_dynamic-update-slice_fusion.refs_0_, bf16[512,384]{1,0:T(8,128)(2,1)S(1)} %collective-permute-done.5.refs_1_, ...), custom_call_target="tpu_custom_call" | custom-call | tf_op jit(solution)/shard_map/tile/pallas_call | solution.py:266
  51.2 2.4 %collective-permute-start.14 = (bf16[512,256]{1,0:T(8,128)(2,1)S(1)}, bf16[512,256]{1,0:T(8,128)(2,1)S(1)}, u32[]{:S(2)}, u32[]{:S(2)}) collective-permute-start(bf16[512,256]{1,0:T(8,128)(2,1)S(1)} %tile.11), channel_id=1, source_target_pairs={{0,3},{1,0},{2,1},{3,2},{4,7},{5,4},{6,5},{7,6},{8,11},{9,8},{10,9... | collective-permute-start | bytes 786440 | tf_op jit(solution)/shard_map/ppermute | solution.py:212
  53.6 2.1 %tile.7.refs_0_ = f32[512,256]{1,0:T(8,128)S(1)} custom-call(bf16[2,128,128]{2,1,0:T(8,128)(2,1)S(1)} %copy-done, bf16[640,256]{1,0:T(8,128)(2,1)S(1)} %get-tuple-element.29.rows_ref, f32[512,256]{1,0:T(8,128)S(1)} %tile.6.refs_0_, bf16[512,384]{1,0:T(8,128)(2,1)S(1)} %collective-permute-done.5.refs_1_, bf16[256,384]{1,0:T(8,128)(2,1)S(1)} %collective-permute-done.6.refs_2_, ...), custom_call_target="tpu_custom_call" | custom-call | tf_op jit(solution)/shard_map/tile/pallas_call | solution.py:266
  55.7 1.2 %collective-permute-done.14.refs_3_ = bf16[512,256]{1,0:T(8,128)(2,1)S(1)} collective-permute-done((bf16[512,256]{1,0:T(8,128)(2,1)S(1)}, bf16[512,256]{1,0:T(8,128)(2,1)S(1)}, u32[]{:S(2)}, u32[]{:S(2)}) %collective-permute-start.14) | collective-permute-done | bytes 262176 | tf_op jit(solution)/shard_map/ppermute | solution.py:212
  56.9 1.2 %sum_rows.1 = (bf16[512,256]{1,0:T(8,128)(2,1)}, f32[128,256]{1,0:T(8,128)S(1)}, bf16[128,256]{1,0:T(8,128)(2,1)S(1)}, bf16[128,256]{1,0:T(8,128)(2,1)S(1)}, bf16[128,256]{1,0:T(8,128)(2,1)S(1)}) custom-call(f32[512,256]{1,0:T(8,128)S(1)} %tile.7.refs_0_, bf16[512,256]{1,0:T(8,128)(2,1)S(1)} %collective-permute-done.12.refs_1_, ...), custom_call_target="tpu_custom_call" | custom-call | tf_op jit(solution)/shard_map/sum_rows/pallas_call | solution.py:289
  58.1 4.5 %all-to-all-start = ((bf16[16,32,256]{2,1,0:T(8,128)(2,1)}), bf16[16,32,256]{2,1,0:T(8,128)(2,1)S(1)}, u32[]{:S(2)}, u32[]{:S(2)}) async-start(bf16[16,32,256]{2,1,0:T(8,128)(2,1)} %bitcast.3), calls=%async_computation | async-start | bytes 524288 | tf_op jit(solution)/shard_map/all_to_all | solution.py:220
  62.6 1.4 %collective-permute-start.15 = (bf16[128,256]{1,0:T(8,128)(2,1)S(1)}, bf16[128,256]{1,0:T(8,128)(2,1)S(1)}, u32[]{:S(2)}, u32[]{:S(2)}) collective-permute-start(bf16[128,256]{1,0:T(8,128)(2,1)S(1)} %get-tuple-element.39), channel_id=1, source_target_pairs={{0,64},{1,65},{2,66},{3,67},{4,68},{5,69},{6,70},{7,71},{8,72},{9,... | collective-permute-start | bytes 196616 | tf_op jit(solution)/shard_map/ppermute | solution.py:212
  64.0 4.5 %collective-permute-done.15.b = bf16[128,256]{1,0:T(8,128)(2,1)S(1)} collective-permute-done((bf16[128,256]{1,0:T(8,128)(2,1)S(1)}, bf16[128,256]{1,0:T(8,128)(2,1)S(1)}, u32[]{:S(2)}, u32[]{:S(2)}) %collective-permute-start.15) | collective-permute-done | bytes 65568 | tf_op jit(solution)/shard_map/ppermute | solution.py:212
  68.5 1.7 %all-to-all-done.refs_0_ = bf16[16,32,256]{2,1,0:T(8,128)(2,1)S(1)} async-done(((bf16[16,32,256]{2,1,0:T(8,128)(2,1)}), bf16[16,32,256]{2,1,0:T(8,128)(2,1)S(1)}, u32[]{:S(2)}, u32[]{:S(2)}) %all-to-all-start) | async-done | bytes 262176 | tf_op jit(solution)/shard_map/all_to_all | solution.py:220
  70.2 0.8 sum_spread.2
  71.0 6.6 %all-to-all-start.1 = ((bf16[16,32,256]{2,1,0:T(8,128)(2,1)}), bf16[16,32,256]{2,1,0:T(8,128)(2,1)S(1)}, u32[]{:S(2)}, u32[]{:S(2)}) async-start(bf16[16,32,256]{2,1,0:T(8,128)(2,1)} %sum_spread.2), calls=%async_computation.1 | async-start | bytes 524288 | tf_op jit(solution)/shard_map/all_to_all | solution.py:220
  77.6 1.0 %collective-permute-start.16 = (bf16[128,256]{1,0:T(8,128)(2,1)S(1)}, bf16[128,256]{1,0:T(8,128)(2,1)S(1)}, u32[]{:S(2)}, u32[]{:S(2)}) collective-permute-start(bf16[128,256]{1,0:T(8,128)(2,1)S(1)} %get-tuple-element.46), channel_id=1, source_target_pairs={{0,128},{1,129},{2,130},{3,131},{4,132},{5,133},{6,134},{7,135},{8... | collective-permute-start | bytes 196616 | tf_op jit(solution)/shard_map/ppermute | solution.py:212
  78.6 1.7 %collective-permute-start.17 = (bf16[128,256]{1,0:T(8,128)(2,1)S(1)}, bf16[128,256]{1,0:T(8,128)(2,1)S(1)}, u32[]{:S(2)}, u32[]{:S(2)}) collective-permute-start(bf16[128,256]{1,0:T(8,128)(2,1)S(1)} %get-tuple-element.47), channel_id=1, source_target_pairs={{0,192},{1,193},{2,194},{3,195},{4,196},{5,197},{6,198},{7,199},{8... | collective-permute-start | bytes 196616 | tf_op jit(solution)/shard_map/ppermute | solution.py:212
  80.2 1.9 %collective-permute-done.16.c = bf16[128,256]{1,0:T(8,128)(2,1)S(1)} collective-permute-done((bf16[128,256]{1,0:T(8,128)(2,1)S(1)}, bf16[128,256]{1,0:T(8,128)(2,1)S(1)}, u32[]{:S(2)}, u32[]{:S(2)}) %collective-permute-start.16) | collective-permute-done | bytes 65568 | tf_op jit(solution)/shard_map/ppermute | solution.py:212
  82.2 0.7 finish_rows.1
  82.9 4.3 %all-to-all-done.1.refs_0_ = bf16[16,32,256]{2,1,0:T(8,128)(2,1)S(1)} async-done(((bf16[16,32,256]{2,1,0:T(8,128)(2,1)}), bf16[16,32,256]{2,1,0:T(8,128)(2,1)S(1)}, u32[]{:S(2)}, u32[]{:S(2)}) %all-to-all-start.1) | async-done | bytes 262176 | tf_op jit(solution)/shard_map/all_to_all | solution.py:220
  87.2 10.7 %all_to_all.15 = bf16[16,32,256]{2,1,0:T(8,128)(2,1)S(1)} all-to-all(bf16[16,32,256]{2,1,0:T(8,128)(2,1)S(1)} %sum_spread.3), channel_id=1, replica_groups=mesh['y'=4,'zh'=2,'core'=2,'zl'=4,'x'=4] {'y','x'}, dimensions={0} | all-to-all | bytes 524288 | tf_op jit(solution)/shard_map/all_to_all | solution.py:220
  97.9 0.8 convert_multiply_fusion
  (13 shorter events, 0.1 us)
Async XLA Ops:
  2.2 16.3 %copy-start.1 = (bf16[512,256]{1,0:T(8,128)(2,1)S(1)}, bf16[512,256]{1,0:T(8,128)(2,1)}, u32[]{:S(2)}) copy-start(bf16[512,256]{1,0:T(8,128)(2,1)} %weight.3) | copy-start | bytes 786436
  2.2 12.6 %collective-permute-start = (bf16[128,384]{1,0:T(8,128)(2,1)S(1)}, bf16[128,384]{1,0:T(8,128)(2,1)S(1)}, u32[]{:S(2)}, u32[]{:S(2)}) collective-permute-start(bf16[128,384]{1,0:T(8,128)(2,1)S(1)} %get-tuple-element.26), channel_id=1, source_target_pairs={{0,32},{4,36},{8,40},{12,44},{32,0},{36,4},{40,8},{44,12},{1,33},{... | collective-permute-start | bytes 294920 | tf_op jit(solution)/shard_map/ppermute | solution.py:197
  10.0 5.7 %collective-permute-start.3 = (bf16[128,640]{1,0:T(8,128)(2,1)S(1)}, bf16[128,640]{1,0:T(8,128)(2,1)S(1)}, u32[]{:S(2)}, u32[]{:S(2)}) collective-permute-start(bf16[128,640]{1,0:T(8,128)(2,1)S(1)} %get-tuple-element.27.refs_0_), channel_id=1, source_target_pairs={{0,64},{1,65},{2,66},{3,67},{4,68},{5,69},{6,70},{7,71},{8,72},{9,... | collective-permute-start | bytes 491528 | tf_op jit(solution)/shard_map/ppermute | solution.py:212
  11.2 7.2 %collective-permute-start.2 = (bf16[128,640]{1,0:T(8,128)(2,1)S(1)}, bf16[128,640]{1,0:T(8,128)(2,1)S(1)}, u32[]{:S(2)}, u32[]{:S(2)}) collective-permute-start(bf16[128,640]{1,0:T(8,128)(2,1)S(1)} %get-tuple-element.27.refs_0_), channel_id=1, source_target_pairs={{0,128},{1,129},{2,130},{3,131},{4,132},{5,133},{6,134},{7,135},{8... | collective-permute-start | bytes 491528 | tf_op jit(solution)/shard_map/ppermute | solution.py:212
  13.7 4.8 %collective-permute-start.1 = (bf16[128,640]{1,0:T(8,128)(2,1)S(1)}, bf16[128,640]{1,0:T(8,128)(2,1)S(1)}, u32[]{:S(2)}, u32[]{:S(2)}) collective-permute-start(bf16[128,640]{1,0:T(8,128)(2,1)S(1)} %get-tuple-element.27.refs_0_), channel_id=1, source_target_pairs={{0,192},{1,193},{2,194},{3,195},{4,196},{5,197},{6,198},{7,199},{8... | collective-permute-start | bytes 491528 | tf_op jit(solution)/shard_map/ppermute | solution.py:212
  18.8 3.5 %collective-permute-start.4 = (bf16[256,384]{1,0:T(8,128)(2,1)S(1)}, bf16[256,384]{1,0:T(8,128)(2,1)S(1)}, u32[]{:S(2)}, u32[]{:S(2)}) collective-permute-start(bf16[256,384]{1,0:T(8,128)(2,1)S(1)} %pad_maximum_fusion), channel_id=1, source_target_pairs={{0,16},{16,0},{1,17},{17,1},{2,18},{18,2},{3,19},{19,3},{4,20},{20... | collective-permute-start | bytes 589832 | tf_op jit(solution)/shard_map/ppermute | solution.py:197
  21.2 6.6 %copy-start = (bf16[2,128,128]{2,1,0:T(8,128)(2,1)S(1)}, bf16[2,128,128]{2,1,0:T(8,128)(2,1)}, u32[]{:S(2)}) copy-start(bf16[2,128,128]{2,1,0:T(8,128)(2,1)} %constant.4.clone.table) | copy-start | bytes 196612
  22.3 12.4 %collective-permute-start.5 = (bf16[512,384]{1,0:T(8,128)(2,1)S(1)}, bf16[512,384]{1,0:T(8,128)(2,1)S(1)}, u32[]{:S(2)}, u32[]{:S(2)}) collective-permute-start(bf16[512,384]{1,0:T(8,128)(2,1)S(1)} %constant_dynamic-update-slice_fusion.refs_0_), channel_id=1, source_target_pairs={{0,4},{1,5},{2,6},{3,7},{4,8},{5,9},{6,10},{7,11},{8,12},{9,13},{1... | collective-permute-start | bytes 1179656 | tf_op jit(solution)/shard_map/ppermute | solution.py:212
  22.4 12.3 %collective-permute-start.9 = (bf16[640,256]{1,0:T(8,128)(2,1)S(1)}, bf16[640,256]{1,0:T(8,128)(2,1)S(1)}, u32[]{:S(2)}, u32[]{:S(2)}) collective-permute-start(bf16[640,256]{1,0:T(8,128)(2,1)S(1)} %get-tuple-element.29.rows_ref), channel_id=1, source_target_pairs={{0,1},{1,2},{2,3},{3,0},{4,5},{5,6},{6,7},{7,4},{8,9},{9,10},{10,1... | collective-permute-start | bytes 983048 | tf_op jit(solution)/shard_map/ppermute | solution.py:212
  23.5 11.2 %collective-permute-start.8 = (bf16[640,256]{1,0:T(8,128)(2,1)S(1)}, bf16[640,256]{1,0:T(8,128)(2,1)S(1)}, u32[]{:S(2)}, u32[]{:S(2)}) collective-permute-start(bf16[640,256]{1,0:T(8,128)(2,1)S(1)} %get-tuple-element.29.rows_ref), channel_id=1, source_target_pairs={{0,2},{1,3},{2,0},{3,1},{4,6},{5,7},{6,4},{7,5},{8,10},{9,11},{10,... | collective-permute-start | bytes 983048 | tf_op jit(solution)/shard_map/ppermute | solution.py:212
  25.9 8.8 %collective-permute-start.7 = (bf16[640,256]{1,0:T(8,128)(2,1)S(1)}, bf16[640,256]{1,0:T(8,128)(2,1)S(1)}, u32[]{:S(2)}, u32[]{:S(2)}) collective-permute-start(bf16[640,256]{1,0:T(8,128)(2,1)S(1)} %get-tuple-element.29.rows_ref), channel_id=1, source_target_pairs={{0,3},{1,0},{2,1},{3,2},{4,7},{5,4},{6,5},{7,6},{8,11},{9,8},{10,9... | collective-permute-start | bytes 983048 | tf_op jit(solution)/shard_map/ppermute | solution.py:212
  26.8 7.9 %collective-permute-start.6 = (bf16[256,384]{1,0:T(8,128)(2,1)S(1)}, bf16[256,384]{1,0:T(8,128)(2,1)S(1)}, u32[]{:S(2)}, u32[]{:S(2)}) collective-permute-start(bf16[256,384]{1,0:T(8,128)(2,1)S(1)} %pad_maximum_fusion), channel_id=1, source_target_pairs={{0,8},{1,9},{2,10},{3,11},{4,12},{5,13},{6,14},{7,15},{8,32},{9,33... | collective-permute-start | bytes 589832 | tf_op jit(solution)/shard_map/ppermute | solution.py:212
  34.7 6.8 %collective-permute-start.10 = (bf16[512,384]{1,0:T(8,128)(2,1)S(1)}, bf16[512,384]{1,0:T(8,128)(2,1)S(1)}, u32[]{:S(2)}, u32[]{:S(2)}) collective-permute-start(bf16[512,384]{1,0:T(8,128)(2,1)S(1)} %collective-permute-done.5.refs_1_), channel_id=1, source_target_pairs={{0,16},{16,0},{1,17},{17,1},{2,18},{18,2},{3,19},{19,3},{4,20},{20... | collective-permute-start | bytes 1179656 | tf_op jit(solution)/shard_map/ppermute | solution.py:197
  39.4 2.1 %collective-permute-start.11 = (bf16[256,384]{1,0:T(8,128)(2,1)S(1)}, bf16[256,384]{1,0:T(8,128)(2,1)S(1)}, u32[]{:S(2)}, u32[]{:S(2)}) collective-permute-start(bf16[256,384]{1,0:T(8,128)(2,1)S(1)} %collective-permute-done.6.refs_2_), channel_id=1, source_target_pairs={{0,16},{16,0},{1,17},{17,1},{2,18},{18,2},{3,19},{19,3},{4,20},{20... | collective-permute-start | bytes 589832 | tf_op jit(solution)/shard_map/ppermute | solution.py:197
  42.8 12.9 %collective-permute-start.13 = (bf16[512,256]{1,0:T(8,128)(2,1)S(1)}, bf16[512,256]{1,0:T(8,128)(2,1)S(1)}, u32[]{:S(2)}, u32[]{:S(2)}) collective-permute-start(bf16[512,256]{1,0:T(8,128)(2,1)S(1)} %tile.10), channel_id=1, source_target_pairs={{0,2},{1,3},{2,0},{3,1},{4,6},{5,7},{6,4},{7,5},{8,10},{9,11},{10,... | collective-permute-start | bytes 786440 | tf_op jit(solution)/shard_map/ppermute | solution.py:212
  47.8 7.8 %collective-permute-start.12 = (bf16[512,256]{1,0:T(8,128)(2,1)S(1)}, bf16[512,256]{1,0:T(8,128)(2,1)S(1)}, u32[]{:S(2)}, u32[]{:S(2)}) collective-permute-start(bf16[512,256]{1,0:T(8,128)(2,1)S(1)} %tile.8), channel_id=1, source_target_pairs={{0,1},{1,2},{2,3},{3,0},{4,5},{5,6},{6,7},{7,4},{8,9},{9,10},{10,1... | collective-permute-start | bytes 786440 | tf_op jit(solution)/shard_map/ppermute | solution.py:212
  51.2 5.7 %collective-permute-start.14 = (bf16[512,256]{1,0:T(8,128)(2,1)S(1)}, bf16[512,256]{1,0:T(8,128)(2,1)S(1)}, u32[]{:S(2)}, u32[]{:S(2)}) collective-permute-start(bf16[512,256]{1,0:T(8,128)(2,1)S(1)} %tile.11), channel_id=1, source_target_pairs={{0,3},{1,0},{2,1},{3,2},{4,7},{5,4},{6,5},{7,6},{8,11},{9,8},{10,9... | collective-permute-start | bytes 786440 | tf_op jit(solution)/shard_map/ppermute | solution.py:212
  58.1 12.1 %all-to-all-start = ((bf16[16,32,256]{2,1,0:T(8,128)(2,1)}), bf16[16,32,256]{2,1,0:T(8,128)(2,1)S(1)}, u32[]{:S(2)}, u32[]{:S(2)}) async-start(bf16[16,32,256]{2,1,0:T(8,128)(2,1)} %bitcast.3), calls=%async_computation | async-start | bytes 524288 | tf_op jit(solution)/shard_map/all_to_all | solution.py:220
  62.6 5.8 %collective-permute-start.15 = (bf16[128,256]{1,0:T(8,128)(2,1)S(1)}, bf16[128,256]{1,0:T(8,128)(2,1)S(1)}, u32[]{:S(2)}, u32[]{:S(2)}) collective-permute-start(bf16[128,256]{1,0:T(8,128)(2,1)S(1)} %get-tuple-element.39), channel_id=1, source_target_pairs={{0,64},{1,65},{2,66},{3,67},{4,68},{5,69},{6,70},{7,71},{8,72},{9,... | collective-permute-start | bytes 196616 | tf_op jit(solution)/shard_map/ppermute | solution.py:212
  71.0 16.2 %all-to-all-start.1 = ((bf16[16,32,256]{2,1,0:T(8,128)(2,1)}), bf16[16,32,256]{2,1,0:T(8,128)(2,1)S(1)}, u32[]{:S(2)}, u32[]{:S(2)}) async-start(bf16[16,32,256]{2,1,0:T(8,128)(2,1)} %sum_spread.2), calls=%async_computation.1 | async-start | bytes 524288 | tf_op jit(solution)/shard_map/all_to_all | solution.py:220
  77.6 4.6 %collective-permute-start.16 = (bf16[128,256]{1,0:T(8,128)(2,1)S(1)}, bf16[128,256]{1,0:T(8,128)(2,1)S(1)}, u32[]{:S(2)}, u32[]{:S(2)}) collective-permute-start(bf16[128,256]{1,0:T(8,128)(2,1)S(1)} %get-tuple-element.46), channel_id=1, source_target_pairs={{0,128},{1,129},{2,130},{3,131},{4,132},{5,133},{6,134},{7,135},{8... | collective-permute-start | bytes 196616 | tf_op jit(solution)/shard_map/ppermute | solution.py:212
  78.6 3.6 %collective-permute-start.17 = (bf16[128,256]{1,0:T(8,128)(2,1)S(1)}, bf16[128,256]{1,0:T(8,128)(2,1)S(1)}, u32[]{:S(2)}, u32[]{:S(2)}) collective-permute-start(bf16[128,256]{1,0:T(8,128)(2,1)S(1)} %get-tuple-element.47), channel_id=1, source_target_pairs={{0,192},{1,193},{2,194},{3,195},{4,196},{5,197},{6,198},{7,199},{8... | collective-permute-start | bytes 196616 | tf_op jit(solution)/shard_map/ppermute | solution.py:212

commit v11 on v10

--- a/solution.py
+++ b/solution.py
@@ -152,18 +152,21 @@
         out[block, :] = (acc[k] - row_total * u_rows[block].astype(F32)).astype(out.dtype)
 
 
-def sum_rows_kernel(count, *refs):
-    parts, (embeds, partial, own, *others) = refs[:count], refs[count:]
+def sum_rows_kernel(a, b, c, embeds, total, weight):
+    rows = a[...] + (b[...].astype(F32) + c[...].astype(F32))
+    hi = rows.astype(BF16)
+    lo = (rows - hi.astype(F32)).astype(BF16)
+    total[...] = rows
+    weight[...] = dot_tn(embeds[...], hi) + dot_tn(embeds[...], lo)
+
+
+def last_rows_kernel(total, weight, last, embeds, partial, own, *others):
     rows = own.shape[0]
-    total = parts[0][...]
-    for ref in parts[1:]:
-        total = total + ref[...].astype(F32)
-    hi = total.astype(BF16)
-    lo = (total - hi.astype(F32)).astype(BF16)
-    own[...] = total[:rows]
+    partial[...] = (weight[...] + dot_tn(embeds[...], last[...])).astype(BF16)
+    own[...] = total[:rows] + last[:rows].astype(F32)
     for k, ref in enumerate(others):
-        ref[...] = hi[(k + 1) * rows : (k + 2) * rows]
-    partial[...] = (dot_tn(embeds[...], hi) + dot_tn(embeds[...], lo)).astype(BF16)
+        block = slice((k + 1) * rows, (k + 2) * rows)
+        ref[...] = (total[block] + last[block].astype(F32)).astype(BF16)
 
 
 def finish_rows_kernel(own, b, c, d, grad_rows):
@@ -256,9 +259,9 @@
     )(weight, *blocks)
     pair = jnp.concatenate([pack, ring(pack, DEPTH, n_z, n_z // 2)], axis=0)
     pair, line = lax.optimization_barrier((pair, line))
-    four = jnp.concatenate([pair, ring(pair, "core", 2, 1)], axis=0)
-    near = move(four, sizes, lambda core: {"z": 1 - 2 * core})
-    far = move(pair, sizes, lambda core: {"z": 2 - 4 * core})
+    near = [ring(pair, DEPTH, n_z, d) for d in (1, -1)]
+    near.append(move(pair, sizes, lambda core: {"z": 2 - 4 * core}))
+    four = [pair, ring(pair, "core", 2, 1)]
     lines = [line] + [turn(line, sizes, 1, -d) for d in range(1, n_side)]
     table = left_map(probes.shape[1])
 
@@ -272,33 +275,47 @@
             name="tile",
         )(table, rows_in, *([] if start is None else [start]), *columns)
 
-    begin = tile(line, [four], F32)
-    near, far, lines, begin = lax.optimization_barrier((near, far, lines, begin))
-    columns = [four, near, far, ring(near, "core", 2, 1), ring(far, "core", 2, 1)]
+    begin = tile(line, four, F32)
+    near, lines, begin = lax.optimization_barrier((near, lines, begin))
+    columns = four + near
+    count = len(columns)
+    columns += [ring(part, "core", 2, 1) for part in near]
 
     back = {}
     for d in (0, 3, 1, 2):
         if d == 2:
-            part = tile(lines[d], columns[3:], BF16, tile(lines[d], columns[:3], F32))
+            part = tile(lines[d], columns[count:], BF16, tile(lines[d], columns[:count], F32))
         elif d == 0:
-            part = tile(line, columns[1:], F32, begin)
+            part = tile(line, columns[len(four) :], F32, begin)
         else:
             part = tile(lines[d], columns, BF16)
         back[d] = part if d == 0 else turn(part, sizes, 1, d)
 
+    total, weight_sum = pl.pallas_call(
+        sum_rows_kernel,
+        out_shape=[
+            jax.ShapeDtypeStruct((n_side * rows, width), F32),
+            jax.ShapeDtypeStruct((embeds.shape[1], width), F32),
+        ],
+        in_specs=[VMEM] * 4,
+        out_specs=[VMEM] * 2,
+        compiler_params=params(16),
+        name="sum_rows",
+    )(back[0], back[1], back[2], embeds_line)
     partial, own_rows, *other_rows = pl.pallas_call(
-        functools.partial(sum_rows_kernel, n_side),
+        last_rows_kernel,
         out_shape=[
             jax.ShapeDtypeStruct((embeds.shape[1], width), BF16),
             jax.ShapeDtypeStruct((rows, width), F32),
         ]
         + [jax.ShapeDtypeStruct((rows, width), BF16)] * (n_side - 1),
-        in_specs=[VMEM] * (n_side + 1),
+        in_specs=[VMEM] * 4,
         out_specs=[VMEM] * (n_side + 1),
         compiler_params=params(16),
-        name="sum_rows",
-    )(*(back[d] for d in range(n_side)), embeds_line)
+        name="last_rows",
+    )(total, weight_sum, back[3], embeds_line)
     arrived = [turn(other_rows[0], sizes, 0, 1)]
+
     n_plane = n_side * n_side
     pieces = exchange(partial.reshape(n_plane, -1, width), PLANE)
     pieces, arrived[0] = lax.optimization_barrier((pieces, arrived[0]))

time: 100 us -> 101 us (1.010)
    ppermute x4 -> x7, waiting for transfers between devices: 1.04 us -> 5.11 us  [ring(): lax.ppermute(array, axis, [(i, (i + shift) % size) for i in range(size)])]
    ppermute x14 -> x13, waiting for transfers between devices: 17.2 us -> 13.3 us  [move(): return lax.ppermute(array, ALL, perm)]
    all_to_all x2, starting transfers between devices: 11.1 us -> 13.4 us  [exchange(): return lax.all_to_all(array, axes, split_axis=0, concat_axis=0, tiled=True)]
    ppermute x14 -> x13, starting transfers between devices: 19.8 us -> 18.5 us  [move(): return lax.ppermute(array, ALL, perm)]
    ppermute x4 -> x7, starting transfers between devices: 15.2 us -> 14.7 us  [ring(): lax.ppermute(array, axis, [(i, (i + shift) % size) for i in range(size)])]
  transfers between devices with their start and end apart: 20 -> 22, of which waited for: 9 -> 10; matrix products, arithmetic and copies ran while one was open for 0% -> 0% of each run, Pallas kernels for 11% -> 11%
where the time goes in v11:
time: 101 us; the launch traced here: 99.7 us
  starting transfers between devices  46.6 us (46%)
  waiting for transfers between devices  24.5 us (24%)
  Pallas kernels  16.3 us (16%)
  blocking collectives  10.7 us (11%)
    ppermute x13, starting transfers between devices, move(): return lax.ppermute(array, ALL, perm)  18.5 us
    ppermute x7, starting transfers between devices, ring(): lax.ppermute(array, axis, [(i, (i + shift) % size) for i in range(size)])  14.7 us
    all_to_all x2, starting transfers between devices, exchange(): return lax.all_to_all(array, axes, split_axis=0, concat_axis=0, tiled=True)  13.4 us
    ppermute x13, waiting for transfers between devices, move(): return lax.ppermute(array, ALL, perm)  13.3 us
    pallas_call x6, Pallas kernels, tile(): pl.pallas_call(functools.partial(tile_kernel, 256, 256, start is not None...  11.4 us
    all_to_all x1, blocking collectives, exchange(): return lax.all_to_all(array, axes, split_axis=0, concat_axis=0, tiled=True)  10.7 us
    all_to_all x2, waiting for transfers between devices, exchange(): return lax.all_to_all(array, axes, split_axis=0, concat_axis=0, tiled=True)  6.03 us
    ppermute x7, waiting for transfers between devices, ring(): lax.ppermute(array, axis, [(i, (i + shift) % size) for i in range(size)])  5.11 us
  transfers between devices with their start and end apart: 22, of which 10 were waited for; matrix products, arithmetic and copies ran while one was open for 0% of the time, Pallas kernels for 11%

profile of v11, /device:TPU:1, one launch (start us, length us, event | category | flops | bytes accessed | tf_op | source)
XLA Modules:
  0.0 99.7 jit_solution(1551955352913702351)
XLA Ops:
  0.6 1.5 %pack.1 = (bf16[128,384]{1,0:T(8,128)(2,1)S(1)}, bf16[128,640]{1,0:T(8,128)(2,1)S(1)}) custom-call(bf16[128,512]{1,0:T(8,128)(2,1)} %embeds.1, bf16[512,256]{1,0:T(8,128)(2,1)} %weight.3, f32[1,128]{1,0:T(1,128)} %bitcast.8, f32[15,128]{1,0:T(8,128)} %bitcast.6, f32[15,128]{1,0:T(8,128)} %bitcast.7), custom_call_target="tpu_custom_call" | custom-call | tf_op jit(solution)/shard_map/pack/pallas_call | solution.py:229
  2.2 0.0 copy-start.1
  2.2 7.8 %collective-permute-start = (bf16[128,384]{1,0:T(8,128)(2,1)S(1)}, bf16[128,384]{1,0:T(8,128)(2,1)S(1)}, u32[]{:S(2)}, u32[]{:S(2)}) collective-permute-start(bf16[128,384]{1,0:T(8,128)(2,1)S(1)} %get-tuple-element.29), channel_id=1, source_target_pairs={{0,32},{4,36},{8,40},{12,44},{32,0},{36,4},{40,8},{44,12},{1,33},{... | collective-permute-start | bytes 294920 | tf_op jit(solution)/shard_map/ppermute | solution.py:200
  10.0 1.2 %collective-permute-start.3 = (bf16[128,640]{1,0:T(8,128)(2,1)S(1)}, bf16[128,640]{1,0:T(8,128)(2,1)S(1)}, u32[]{:S(2)}, u32[]{:S(2)}) collective-permute-start(bf16[128,640]{1,0:T(8,128)(2,1)S(1)} %get-tuple-element.30.refs_0_), channel_id=1, source_target_pairs={{0,64},{1,65},{2,66},{3,67},{4,68},{5,69},{6,70},{7,71},{8,72},{9,... | collective-permute-start | bytes 491528 | tf_op jit(solution)/shard_map/ppermute | solution.py:215
  11.2 2.5 %collective-permute-start.2 = (bf16[128,640]{1,0:T(8,128)(2,1)S(1)}, bf16[128,640]{1,0:T(8,128)(2,1)S(1)}, u32[]{:S(2)}, u32[]{:S(2)}) collective-permute-start(bf16[128,640]{1,0:T(8,128)(2,1)S(1)} %get-tuple-element.30.refs_0_), channel_id=1, source_target_pairs={{0,128},{1,129},{2,130},{3,131},{4,132},{5,133},{6,134},{7,135},{8... | collective-permute-start | bytes 491528 | tf_op jit(solution)/shard_map/ppermute | solution.py:215
  13.7 1.2 %collective-permute-start.1 = (bf16[128,640]{1,0:T(8,128)(2,1)S(1)}, bf16[128,640]{1,0:T(8,128)(2,1)S(1)}, u32[]{:S(2)}, u32[]{:S(2)}) collective-permute-start(bf16[128,640]{1,0:T(8,128)(2,1)S(1)} %get-tuple-element.30.refs_0_), channel_id=1, source_target_pairs={{0,192},{1,193},{2,194},{3,195},{4,196},{5,197},{6,198},{7,199},{8... | collective-permute-start | bytes 491528 | tf_op jit(solution)/shard_map/ppermute | solution.py:215
  14.8 0.0 collective-permute-done
  14.9 0.0 copy-start
  14.9 0.8 collective-permute-done.3.refs_3_
  15.7 2.7 %collective-permute-done.2.refs_2_ = bf16[128,640]{1,0:T(8,128)(2,1)S(1)} collective-permute-done((bf16[128,640]{1,0:T(8,128)(2,1)S(1)}, bf16[128,640]{1,0:T(8,128)(2,1)S(1)}, u32[]{:S(2)}, u32[]{:S(2)}) %collective-permute-start.2) | collective-permute-done | bytes 163872 | tf_op jit(solution)/shard_map/ppermute | solution.py:215
  18.4 0.0 collective-permute-done.1.refs_1_
  18.4 0.3 split.1
  18.7 2.4 %collective-permute-start.10 = (bf16[256,384]{1,0:T(8,128)(2,1)S(1)}, bf16[256,384]{1,0:T(8,128)(2,1)S(1)}, u32[]{:S(2)}, u32[]{:S(2)}) collective-permute-start(bf16[256,384]{1,0:T(8,128)(2,1)S(1)} %pad_maximum_fusion.refs_0_), channel_id=1, source_target_pairs={{0,16},{16,0},{1,17},{17,1},{2,18},{18,2},{3,19},{19,3},{4,20},{20... | collective-permute-start | bytes 589832 | tf_op jit(solution)/shard_map/ppermute | solution.py:200
  21.2 1.1 %collective-permute-start.9 = (bf16[640,256]{1,0:T(8,128)(2,1)S(1)}, bf16[640,256]{1,0:T(8,128)(2,1)S(1)}, u32[]{:S(2)}, u32[]{:S(2)}) collective-permute-start(bf16[640,256]{1,0:T(8,128)(2,1)S(1)} %get-tuple-element.32.rows_ref), channel_id=1, source_target_pairs={{0,1},{1,2},{2,3},{3,0},{4,5},{5,6},{6,7},{7,4},{8,9},{9,10},{10,1... | collective-permute-start | bytes 983048 | tf_op jit(solution)/shard_map/ppermute | solution.py:215
  22.3 2.4 %collective-permute-start.8 = (bf16[640,256]{1,0:T(8,128)(2,1)S(1)}, bf16[640,256]{1,0:T(8,128)(2,1)S(1)}, u32[]{:S(2)}, u32[]{:S(2)}) collective-permute-start(bf16[640,256]{1,0:T(8,128)(2,1)S(1)} %get-tuple-element.32.rows_ref), channel_id=1, source_target_pairs={{0,2},{1,3},{2,0},{3,1},{4,6},{5,7},{6,4},{7,5},{8,10},{9,11},{10,... | collective-permute-start | bytes 983048 | tf_op jit(solution)/shard_map/ppermute | solution.py:215
  24.6 1.0 %collective-permute-start.7 = (bf16[640,256]{1,0:T(8,128)(2,1)S(1)}, bf16[640,256]{1,0:T(8,128)(2,1)S(1)}, u32[]{:S(2)}, u32[]{:S(2)}) collective-permute-start(bf16[640,256]{1,0:T(8,128)(2,1)S(1)} %get-tuple-element.32.rows_ref), channel_id=1, source_target_pairs={{0,3},{1,0},{2,1},{3,2},{4,7},{5,4},{6,5},{7,6},{8,11},{9,8},{10,9... | collective-permute-start | bytes 983048 | tf_op jit(solution)/shard_map/ppermute | solution.py:215
  25.7 0.9 collective-permute-start.5
  26.6 2.4 %collective-permute-done.6.refs_3_.refs_4_ = bf16[256,384]{1,0:T(8,128)(2,1)S(1)} collective-permute-done((bf16[256,384]{1,0:T(8,128)(2,1)S(1)}, bf16[256,384]{1,0:T(8,128)(2,1)S(1)}, u32[]{:S(2)}, u32[]{:S(2)}) %collective-permute-start.6) | collective-permute-done | bytes 196640 | tf_op jit(solution)/shard_map/ppermute | solution.py:215
  29.0 0.9 tile.6.refs_0_
  29.9 0.8 collective-permute-done.5.refs_2_.refs_3_
  30.7 4.3 %collective-permute-done.4.refs_1_.refs_2_ = bf16[256,384]{1,0:T(8,128)(2,1)S(1)} collective-permute-done((bf16[256,384]{1,0:T(8,128)(2,1)S(1)}, bf16[256,384]{1,0:T(8,128)(2,1)S(1)}, u32[]{:S(2)}, u32[]{:S(2)}) %collective-permute-start.4) | collective-permute-done | bytes 196640 | tf_op jit(solution)/shard_map/ppermute | solution.py:200
  35.0 3.0 %collective-permute-start.11 = (bf16[256,384]{1,0:T(8,128)(2,1)S(1)}, bf16[256,384]{1,0:T(8,128)(2,1)S(1)}, u32[]{:S(2)}, u32[]{:S(2)}) collective-permute-start(bf16[256,384]{1,0:T(8,128)(2,1)S(1)} %collective-permute-done.4.refs_1_.refs_2_), channel_id=1, source_target_pairs={{0,16},{16,0},{1,17},{17,1},{2,18},{18,2},{3,19},{19,3},{4,20},{20... | collective-permute-start | bytes 589832 | tf_op jit(solution)/shard_map/ppermute | solution.py:200
  38.0 0.1 collective-permute-start.12
  38.1 0.4 collective-permute-start.13
  38.5 1.8 %tile.9.refs_0_ = f32[512,256]{1,0:T(8,128)S(1)} custom-call(bf16[2,128,128]{2,1,0:T(8,128)(2,1)S(1)} %copy-done, bf16[640,256]{1,0:T(8,128)(2,1)S(1)} %collective-permute-done.8.rows_ref, bf16[256,384]{1,0:T(8,128)(2,1)S(1)} %pad_maximum_fusion.refs_0_, bf16[256,384]{1,0:T(8,128)(2,1)S(1)} %collective-permute-done.10.refs_1_, ...), custom_call_target="tpu_custom_call" | custom-call | tf_op jit(solution)/shard_map/tile/pallas_call | solution.py:269
  40.4 1.2 %tile.10 = bf16[512,256]{1,0:T(8,128)(2,1)S(1)} custom-call(bf16[2,128,128]{2,1,0:T(8,128)(2,1)S(1)} %copy-done, bf16[640,256]{1,0:T(8,128)(2,1)S(1)} %collective-permute-done.8.rows_ref, f32[512,256]{1,0:T(8,128)S(1)} %tile.9.refs_0_, bf16[256,384]{1,0:T(8,128)(2,1)S(1)} %collective-permute-done.11.refs_4_.refs_5_.refs_1_, ...), custom_call_target="tpu_custom_call" | custom-call | tf_op jit(solution)/shard_map/tile/pallas_call | solution.py:269
  41.6 2.1 %collective-permute-start.15 = (bf16[512,256]{1,0:T(8,128)(2,1)S(1)}, bf16[512,256]{1,0:T(8,128)(2,1)S(1)}, u32[]{:S(2)}, u32[]{:S(2)}) collective-permute-start(bf16[512,256]{1,0:T(8,128)(2,1)S(1)} %tile.10), channel_id=1, source_target_pairs={{0,2},{1,3},{2,0},{3,1},{4,6},{5,7},{6,4},{7,5},{8,10},{9,11},{10,... | collective-permute-start | bytes 786440 | tf_op jit(solution)/shard_map/ppermute | solution.py:215
  43.7 2.7 %tile.8 = bf16[512,256]{1,0:T(8,128)(2,1)S(1)} custom-call(bf16[2,128,128]{2,1,0:T(8,128)(2,1)S(1)} %copy-done, bf16[640,256]{1,0:T(8,128)(2,1)S(1)} %collective-permute-done.7.rows_ref, bf16[256,384]{1,0:T(8,128)(2,1)S(1)} %pad_maximum_fusion.refs_0_, bf16[256,384]{1,0:T(8,128)(2,1)S(1)} %collective-permute-done.10.refs_1_, ...), custom_call_target="tpu_custom_call" | custom-call | tf_op jit(solution)/shard_map/tile/pallas_call | solution.py:269
  46.4 0.8 collective-permute-start.14
  47.2 2.7 %tile.11 = bf16[512,256]{1,0:T(8,128)(2,1)S(1)} custom-call(bf16[2,128,128]{2,1,0:T(8,128)(2,1)S(1)} %copy-done, bf16[640,256]{1,0:T(8,128)(2,1)S(1)} %collective-permute-done.9.rows_ref, bf16[256,384]{1,0:T(8,128)(2,1)S(1)} %pad_maximum_fusion.refs_0_, bf16[256,384]{1,0:T(8,128)(2,1)S(1)} %collective-permute-done.10.refs_1_, ...), custom_call_target="tpu_custom_call" | custom-call | tf_op jit(solution)/shard_map/tile/pallas_call | solution.py:269
  49.9 2.3 %collective-permute-start.16 = (bf16[512,256]{1,0:T(8,128)(2,1)S(1)}, bf16[512,256]{1,0:T(8,128)(2,1)S(1)}, u32[]{:S(2)}, u32[]{:S(2)}) collective-permute-start(bf16[512,256]{1,0:T(8,128)(2,1)S(1)} %tile.11), channel_id=1, source_target_pairs={{0,3},{1,0},{2,1},{3,2},{4,7},{5,4},{6,5},{7,6},{8,11},{9,8},{10,9... | collective-permute-start | bytes 786440 | tf_op jit(solution)/shard_map/ppermute | solution.py:215
  52.2 2.1 %tile.7.a = f32[512,256]{1,0:T(8,128)S(1)} custom-call(bf16[2,128,128]{2,1,0:T(8,128)(2,1)S(1)} %copy-done, bf16[640,256]{1,0:T(8,128)(2,1)S(1)} %get-tuple-element.32.rows_ref, f32[512,256]{1,0:T(8,128)S(1)} %tile.6.refs_0_, bf16[256,384]{1,0:T(8,128)(2,1)S(1)} %collective-permute-done.4.refs_1_.refs_2_, ...), custom_call_target="tpu_custom_call" | custom-call | tf_op jit(solution)/shard_map/tile/pallas_call | solution.py:269
  54.3 0.5 sum_rows.1
  54.8 1.0 collective-permute-done.16.last
  55.7 1.1 %last_rows.1 = (bf16[512,256]{1,0:T(8,128)(2,1)}, f32[128,256]{1,0:T(8,128)S(1)}, bf16[128,256]{1,0:T(8,128)(2,1)S(1)}, bf16[128,256]{1,0:T(8,128)(2,1)S(1)}, bf16[128,256]{1,0:T(8,128)(2,1)S(1)}) custom-call(f32[512,256]{1,0:T(8,128)S(1)} %get-tuple-element.41.total, f32[512,256]{1,0:T(8,128)S(1)} %get-tuple-element.42.weight, ...), custom_call_target="tpu_custom_call" | custom-call | tf_op jit(solution)/shard_map/last_rows/pallas_call | solution.py:305
  56.8 6.7 %all-to-all-start = ((bf16[16,32,256]{2,1,0:T(8,128)(2,1)}), bf16[16,32,256]{2,1,0:T(8,128)(2,1)S(1)}, u32[]{:S(2)}, u32[]{:S(2)}) async-start(bf16[16,32,256]{2,1,0:T(8,128)(2,1)} %bitcast.3), calls=%async_computation | async-start | bytes 524288 | tf_op jit(solution)/shard_map/all_to_all | solution.py:223
  63.5 1.4 %collective-permute-start.17 = (bf16[128,256]{1,0:T(8,128)(2,1)S(1)}, bf16[128,256]{1,0:T(8,128)(2,1)S(1)}, u32[]{:S(2)}, u32[]{:S(2)}) collective-permute-start(bf16[128,256]{1,0:T(8,128)(2,1)S(1)} %get-tuple-element.45), channel_id=1, source_target_pairs={{0,64},{1,65},{2,66},{3,67},{4,68},{5,69},{6,70},{7,71},{8,72},{9,... | collective-permute-start | bytes 196616 | tf_op jit(solution)/shard_map/ppermute | solution.py:215
  64.9 4.5 %collective-permute-done.17.b = bf16[128,256]{1,0:T(8,128)(2,1)S(1)} collective-permute-done((bf16[128,256]{1,0:T(8,128)(2,1)S(1)}, bf16[128,256]{1,0:T(8,128)(2,1)S(1)}, u32[]{:S(2)}, u32[]{:S(2)}) %collective-permute-start.17) | collective-permute-done | bytes 65568 | tf_op jit(solution)/shard_map/ppermute | solution.py:215
  69.4 1.7 %all-to-all-done.refs_0_ = bf16[16,32,256]{2,1,0:T(8,128)(2,1)S(1)} async-done(((bf16[16,32,256]{2,1,0:T(8,128)(2,1)}), bf16[16,32,256]{2,1,0:T(8,128)(2,1)S(1)}, u32[]{:S(2)}, u32[]{:S(2)}) %all-to-all-start) | async-done | bytes 262176 | tf_op jit(solution)/shard_map/all_to_all | solution.py:223
  71.1 0.8 sum_spread.2
  71.8 6.7 %all-to-all-start.1 = ((bf16[16,32,256]{2,1,0:T(8,128)(2,1)}), bf16[16,32,256]{2,1,0:T(8,128)(2,1)S(1)}, u32[]{:S(2)}, u32[]{:S(2)}) async-start(bf16[16,32,256]{2,1,0:T(8,128)(2,1)} %sum_spread.2), calls=%async_computation.1 | async-start | bytes 524288 | tf_op jit(solution)/shard_map/all_to_all | solution.py:223
  78.5 1.0 collective-permute-start.18
  79.5 1.7 %collective-permute-start.19 = (bf16[128,256]{1,0:T(8,128)(2,1)S(1)}, bf16[128,256]{1,0:T(8,128)(2,1)S(1)}, u32[]{:S(2)}, u32[]{:S(2)}) collective-permute-start(bf16[128,256]{1,0:T(8,128)(2,1)S(1)} %get-tuple-element.53), channel_id=1, source_target_pairs={{0,192},{1,193},{2,194},{3,195},{4,196},{5,197},{6,198},{7,199},{8... | collective-permute-start | bytes 196616 | tf_op jit(solution)/shard_map/ppermute | solution.py:215
  81.2 1.9 %collective-permute-done.18.c = bf16[128,256]{1,0:T(8,128)(2,1)S(1)} collective-permute-done((bf16[128,256]{1,0:T(8,128)(2,1)S(1)}, bf16[128,256]{1,0:T(8,128)(2,1)S(1)}, u32[]{:S(2)}, u32[]{:S(2)}) %collective-permute-start.18) | collective-permute-done | bytes 65568 | tf_op jit(solution)/shard_map/ppermute | solution.py:215
  83.1 0.7 finish_rows.1
  83.8 4.3 %all-to-all-done.1.refs_0_ = bf16[16,32,256]{2,1,0:T(8,128)(2,1)S(1)} async-done(((bf16[16,32,256]{2,1,0:T(8,128)(2,1)}), bf16[16,32,256]{2,1,0:T(8,128)(2,1)S(1)}, u32[]{:S(2)}, u32[]{:S(2)}) %all-to-all-start.1) | async-done | bytes 262176 | tf_op jit(solution)/shard_map/all_to_all | solution.py:223
  88.2 10.7 %all_to_all.15 = bf16[16,32,256]{2,1,0:T(8,128)(2,1)S(1)} all-to-all(bf16[16,32,256]{2,1,0:T(8,128)(2,1)S(1)} %sum_spread.3), channel_id=1, replica_groups=mesh['y'=4,'zh'=2,'core'=2,'zl'=4,'x'=4] {'y','x'}, dimensions={0} | all-to-all | bytes 524288 | tf_op jit(solution)/shard_map/all_to_all | solution.py:223
  98.9 0.8 convert_multiply_fusion
  (16 shorter events, 0.1 us)
Async XLA Ops:
  2.2 16.3 %copy-start.1 = (bf16[512,256]{1,0:T(8,128)(2,1)S(1)}, bf16[512,256]{1,0:T(8,128)(2,1)}, u32[]{:S(2)}) copy-start(bf16[512,256]{1,0:T(8,128)(2,1)} %weight.3) | copy-start | bytes 786436
  2.2 12.6 %collective-permute-start = (bf16[128,384]{1,0:T(8,128)(2,1)S(1)}, bf16[128,384]{1,0:T(8,128)(2,1)S(1)}, u32[]{:S(2)}, u32[]{:S(2)}) collective-permute-start(bf16[128,384]{1,0:T(8,128)(2,1)S(1)} %get-tuple-element.29), channel_id=1, source_target_pairs={{0,32},{4,36},{8,40},{12,44},{32,0},{36,4},{40,8},{44,12},{1,33},{... | collective-permute-start | bytes 294920 | tf_op jit(solution)/shard_map/ppermute | solution.py:200
  10.0 5.7 %collective-permute-start.3 = (bf16[128,640]{1,0:T(8,128)(2,1)S(1)}, bf16[128,640]{1,0:T(8,128)(2,1)S(1)}, u32[]{:S(2)}, u32[]{:S(2)}) collective-permute-start(bf16[128,640]{1,0:T(8,128)(2,1)S(1)} %get-tuple-element.30.refs_0_), channel_id=1, source_target_pairs={{0,64},{1,65},{2,66},{3,67},{4,68},{5,69},{6,70},{7,71},{8,72},{9,... | collective-permute-start | bytes 491528 | tf_op jit(solution)/shard_map/ppermute | solution.py:215
  11.2 7.2 %collective-permute-start.2 = (bf16[128,640]{1,0:T(8,128)(2,1)S(1)}, bf16[128,640]{1,0:T(8,128)(2,1)S(1)}, u32[]{:S(2)}, u32[]{:S(2)}) collective-permute-start(bf16[128,640]{1,0:T(8,128)(2,1)S(1)} %get-tuple-element.30.refs_0_), channel_id=1, source_target_pairs={{0,128},{1,129},{2,130},{3,131},{4,132},{5,133},{6,134},{7,135},{8... | collective-permute-start | bytes 491528 | tf_op jit(solution)/shard_map/ppermute | solution.py:215
  13.7 4.8 %collective-permute-start.1 = (bf16[128,640]{1,0:T(8,128)(2,1)S(1)}, bf16[128,640]{1,0:T(8,128)(2,1)S(1)}, u32[]{:S(2)}, u32[]{:S(2)}) collective-permute-start(bf16[128,640]{1,0:T(8,128)(2,1)S(1)} %get-tuple-element.30.refs_0_), channel_id=1, source_target_pairs={{0,192},{1,193},{2,194},{3,195},{4,196},{5,197},{6,198},{7,199},{8... | collective-permute-start | bytes 491528 | tf_op jit(solution)/shard_map/ppermute | solution.py:215
  14.9 14.1 %copy-start = (bf16[2,128,128]{2,1,0:T(8,128)(2,1)S(1)}, bf16[2,128,128]{2,1,0:T(8,128)(2,1)}, u32[]{:S(2)}) copy-start(bf16[2,128,128]{2,1,0:T(8,128)(2,1)} %constant.4.clone.table) | copy-start | bytes 196612
  18.7 6.9 %collective-permute-start.10 = (bf16[256,384]{1,0:T(8,128)(2,1)S(1)}, bf16[256,384]{1,0:T(8,128)(2,1)S(1)}, u32[]{:S(2)}, u32[]{:S(2)}) collective-permute-start(bf16[256,384]{1,0:T(8,128)(2,1)S(1)} %pad_maximum_fusion.refs_0_), channel_id=1, source_target_pairs={{0,16},{16,0},{1,17},{17,1},{2,18},{18,2},{3,19},{19,3},{4,20},{20... | collective-permute-start | bytes 589832 | tf_op jit(solution)/shard_map/ppermute | solution.py:200
  21.2 7.8 %collective-permute-start.6 = (bf16[256,384]{1,0:T(8,128)(2,1)S(1)}, bf16[256,384]{1,0:T(8,128)(2,1)S(1)}, u32[]{:S(2)}, u32[]{:S(2)}) collective-permute-start(bf16[256,384]{1,0:T(8,128)(2,1)S(1)} %pad_maximum_fusion.refs_0_), channel_id=1, source_target_pairs={{0,8},{1,9},{2,10},{3,11},{4,12},{5,13},{6,14},{7,15},{8,32},{9,33... | collective-permute-start | bytes 589832 | tf_op jit(solution)/shard_map/ppermute | solution.py:215
  21.2 13.8 %collective-permute-start.9 = (bf16[640,256]{1,0:T(8,128)(2,1)S(1)}, bf16[640,256]{1,0:T(8,128)(2,1)S(1)}, u32[]{:S(2)}, u32[]{:S(2)}) collective-permute-start(bf16[640,256]{1,0:T(8,128)(2,1)S(1)} %get-tuple-element.32.rows_ref), channel_id=1, source_target_pairs={{0,1},{1,2},{2,3},{3,0},{4,5},{5,6},{6,7},{7,4},{8,9},{9,10},{10,1... | collective-permute-start | bytes 983048 | tf_op jit(solution)/shard_map/ppermute | solution.py:215
  22.3 12.8 %collective-permute-start.8 = (bf16[640,256]{1,0:T(8,128)(2,1)S(1)}, bf16[640,256]{1,0:T(8,128)(2,1)S(1)}, u32[]{:S(2)}, u32[]{:S(2)}) collective-permute-start(bf16[640,256]{1,0:T(8,128)(2,1)S(1)} %get-tuple-element.32.rows_ref), channel_id=1, source_target_pairs={{0,2},{1,3},{2,0},{3,1},{4,6},{5,7},{6,4},{7,5},{8,10},{9,11},{10,... | collective-permute-start | bytes 983048 | tf_op jit(solution)/shard_map/ppermute | solution.py:215
  24.6 10.4 %collective-permute-start.7 = (bf16[640,256]{1,0:T(8,128)(2,1)S(1)}, bf16[640,256]{1,0:T(8,128)(2,1)S(1)}, u32[]{:S(2)}, u32[]{:S(2)}) collective-permute-start(bf16[640,256]{1,0:T(8,128)(2,1)S(1)} %get-tuple-element.32.rows_ref), channel_id=1, source_target_pairs={{0,3},{1,0},{2,1},{3,2},{4,7},{5,4},{6,5},{7,6},{8,11},{9,8},{10,9... | collective-permute-start | bytes 983048 | tf_op jit(solution)/shard_map/ppermute | solution.py:215
  25.7 5.1 %collective-permute-start.5 = (bf16[256,384]{1,0:T(8,128)(2,1)S(1)}, bf16[256,384]{1,0:T(8,128)(2,1)S(1)}, u32[]{:S(2)}, u32[]{:S(2)}) collective-permute-start(bf16[256,384]{1,0:T(8,128)(2,1)S(1)} %pad_maximum_fusion.refs_0_), channel_id=1, source_target_pairs={{0,44},{4,0},{8,4},{12,8},{32,12},{36,32},{40,36},{44,40},{1,45},{... | collective-permute-start | bytes 589832 | tf_op jit(solution)/shard_map/ppermute | solution.py:200
  29.0 6.0 %collective-permute-start.4 = (bf16[256,384]{1,0:T(8,128)(2,1)S(1)}, bf16[256,384]{1,0:T(8,128)(2,1)S(1)}, u32[]{:S(2)}, u32[]{:S(2)}) collective-permute-start(bf16[256,384]{1,0:T(8,128)(2,1)S(1)} %pad_maximum_fusion.refs_0_), channel_id=1, source_target_pairs={{0,4},{4,8},{8,12},{12,32},{32,36},{36,40},{40,44},{44,0},{1,5},{5... | collective-permute-start | bytes 589832 | tf_op jit(solution)/shard_map/ppermute | solution.py:200
  35.0 5.3 %collective-permute-start.11 = (bf16[256,384]{1,0:T(8,128)(2,1)S(1)}, bf16[256,384]{1,0:T(8,128)(2,1)S(1)}, u32[]{:S(2)}, u32[]{:S(2)}) collective-permute-start(bf16[256,384]{1,0:T(8,128)(2,1)S(1)} %collective-permute-done.4.refs_1_.refs_2_), channel_id=1, source_target_pairs={{0,16},{16,0},{1,17},{17,1},{2,18},{18,2},{3,19},{19,3},{4,20},{20... | collective-permute-start | bytes 589832 | tf_op jit(solution)/shard_map/ppermute | solution.py:200
  38.0 2.3 %collective-permute-start.12 = (bf16[256,384]{1,0:T(8,128)(2,1)S(1)}, bf16[256,384]{1,0:T(8,128)(2,1)S(1)}, u32[]{:S(2)}, u32[]{:S(2)}) collective-permute-start(bf16[256,384]{1,0:T(8,128)(2,1)S(1)} %collective-permute-done.5.refs_2_.refs_3_), channel_id=1, source_target_pairs={{0,16},{16,0},{1,17},{17,1},{2,18},{18,2},{3,19},{19,3},{4,20},{20... | collective-permute-start | bytes 589832 | tf_op jit(solution)/shard_map/ppermute | solution.py:200
  38.1 2.3 %collective-permute-start.13 = (bf16[256,384]{1,0:T(8,128)(2,1)S(1)}, bf16[256,384]{1,0:T(8,128)(2,1)S(1)}, u32[]{:S(2)}, u32[]{:S(2)}) collective-permute-start(bf16[256,384]{1,0:T(8,128)(2,1)S(1)} %collective-permute-done.6.refs_3_.refs_4_), channel_id=1, source_target_pairs={{0,16},{16,0},{1,17},{17,1},{2,18},{18,2},{3,19},{19,3},{4,20},{20... | collective-permute-start | bytes 589832 | tf_op jit(solution)/shard_map/ppermute | solution.py:200
  41.6 12.6 %collective-permute-start.15 = (bf16[512,256]{1,0:T(8,128)(2,1)S(1)}, bf16[512,256]{1,0:T(8,128)(2,1)S(1)}, u32[]{:S(2)}, u32[]{:S(2)}) collective-permute-start(bf16[512,256]{1,0:T(8,128)(2,1)S(1)} %tile.10), channel_id=1, source_target_pairs={{0,2},{1,3},{2,0},{3,1},{4,6},{5,7},{6,4},{7,5},{8,10},{9,11},{10,... | collective-permute-start | bytes 786440 | tf_op jit(solution)/shard_map/ppermute | solution.py:215
  46.4 7.8 %collective-permute-start.14 = (bf16[512,256]{1,0:T(8,128)(2,1)S(1)}, bf16[512,256]{1,0:T(8,128)(2,1)S(1)}, u32[]{:S(2)}, u32[]{:S(2)}) collective-permute-start(bf16[512,256]{1,0:T(8,128)(2,1)S(1)} %tile.8), channel_id=1, source_target_pairs={{0,1},{1,2},{2,3},{3,0},{4,5},{5,6},{6,7},{7,4},{8,9},{9,10},{10,1... | collective-permute-start | bytes 786440 | tf_op jit(solution)/shard_map/ppermute | solution.py:215
  49.9 5.8 %collective-permute-start.16 = (bf16[512,256]{1,0:T(8,128)(2,1)S(1)}, bf16[512,256]{1,0:T(8,128)(2,1)S(1)}, u32[]{:S(2)}, u32[]{:S(2)}) collective-permute-start(bf16[512,256]{1,0:T(8,128)(2,1)S(1)} %tile.11), channel_id=1, source_target_pairs={{0,3},{1,0},{2,1},{3,2},{4,7},{5,4},{6,5},{7,6},{8,11},{9,8},{10,9... | collective-permute-start | bytes 786440 | tf_op jit(solution)/shard_map/ppermute | solution.py:215
  56.8 14.3 %all-to-all-start = ((bf16[16,32,256]{2,1,0:T(8,128)(2,1)}), bf16[16,32,256]{2,1,0:T(8,128)(2,1)S(1)}, u32[]{:S(2)}, u32[]{:S(2)}) async-start(bf16[16,32,256]{2,1,0:T(8,128)(2,1)} %bitcast.3), calls=%async_computation | async-start | bytes 524288 | tf_op jit(solution)/shard_map/all_to_all | solution.py:223
  63.5 5.8 %collective-permute-start.17 = (bf16[128,256]{1,0:T(8,128)(2,1)S(1)}, bf16[128,256]{1,0:T(8,128)(2,1)S(1)}, u32[]{:S(2)}, u32[]{:S(2)}) collective-permute-start(bf16[128,256]{1,0:T(8,128)(2,1)S(1)} %get-tuple-element.45), channel_id=1, source_target_pairs={{0,64},{1,65},{2,66},{3,67},{4,68},{5,69},{6,70},{7,71},{8,72},{9,... | collective-permute-start | bytes 196616 | tf_op jit(solution)/shard_map/ppermute | solution.py:215
  71.8 16.3 %all-to-all-start.1 = ((bf16[16,32,256]{2,1,0:T(8,128)(2,1)}), bf16[16,32,256]{2,1,0:T(8,128)(2,1)S(1)}, u32[]{:S(2)}, u32[]{:S(2)}) async-start(bf16[16,32,256]{2,1,0:T(8,128)(2,1)} %sum_spread.2), calls=%async_computation.1 | async-start | bytes 524288 | tf_op jit(solution)/shard_map/all_to_all | solution.py:223
  78.5 4.6 %collective-permute-start.18 = (bf16[128,256]{1,0:T(8,128)(2,1)S(1)}, bf16[128,256]{1,0:T(8,128)(2,1)S(1)}, u32[]{:S(2)}, u32[]{:S(2)}) collective-permute-start(bf16[128,256]{1,0:T(8,128)(2,1)S(1)} %get-tuple-element.52), channel_id=1, source_target_pairs={{0,128},{1,129},{2,130},{3,131},{4,132},{5,133},{6,134},{7,135},{8... | collective-permute-start | bytes 196616 | tf_op jit(solution)/shard_map/ppermute | solution.py:215
  79.5 3.6 %collective-permute-start.19 = (bf16[128,256]{1,0:T(8,128)(2,1)S(1)}, bf16[128,256]{1,0:T(8,128)(2,1)S(1)}, u32[]{:S(2)}, u32[]{:S(2)}) collective-permute-start(bf16[128,256]{1,0:T(8,128)(2,1)S(1)} %get-tuple-element.53), channel_id=1, source_target_pairs={{0,192},{1,193},{2,194},{3,195},{4,196},{5,197},{6,198},{7,199},{8... | collective-permute-start | bytes 196616 | tf_op jit(solution)/shard_map/ppermute | solution.py:215

commit v12 on v11

--- a/solution.py
+++ b/solution.py
@@ -257,12 +257,13 @@
         compiler_params=params(8),
         name="split",
     )(weight, *blocks)
-    pair = jnp.concatenate([pack, ring(pack, DEPTH, n_z, n_z // 2)], axis=0)
-    pair, line = lax.optimization_barrier((pair, line))
-    near = [ring(pair, DEPTH, n_z, d) for d in (1, -1)]
-    near.append(move(pair, sizes, lambda core: {"z": 2 - 4 * core}))
-    four = [pair, ring(pair, "core", 2, 1)]
+    pair = [pack, ring(pack, DEPTH, n_z, n_z // 2)]
+    four = jnp.concatenate(pair + [ring(part, "core", 2, 1) for part in pair], axis=0)
+    pair = jnp.concatenate(pair, axis=0)
+    pair, four, line = lax.optimization_barrier((pair, four, line))
+    far = move(pair, sizes, lambda core: {"z": 2 - 4 * core})
     lines = [line] + [turn(line, sizes, 1, -d) for d in range(1, n_side)]
+    near = move(four, sizes, lambda core: {"z": 1 - 2 * core})
     table = left_map(probes.shape[1])
 
     def tile(rows_in, columns, dtype, start=None):
@@ -275,18 +276,16 @@
             name="tile",
         )(table, rows_in, *([] if start is None else [start]), *columns)
 
-    begin = tile(line, four, F32)
-    near, lines, begin = lax.optimization_barrier((near, lines, begin))
-    columns = four + near
-    count = len(columns)
-    columns += [ring(part, "core", 2, 1) for part in near]
+    begin = tile(line, [four], F32)
+    near, far, lines, begin = lax.optimization_barrier((near, far, lines, begin))
+    columns = [four, near, far, ring(near, "core", 2, 1), ring(far, "core", 2, 1)]
 
     back = {}
     for d in (0, 3, 1, 2):
         if d == 2:
-            part = tile(lines[d], columns[count:], BF16, tile(lines[d], columns[:count], F32))
+            part = tile(lines[d], columns[3:], BF16, tile(lines[d], columns[:3], F32))
         elif d == 0:
-            part = tile(line, columns[len(four) :], F32, begin)
+            part = tile(line, columns[1:], F32, begin)
         else:
             part = tile(lines[d], columns, BF16)
         back[d] = part if d == 0 else turn(part, sizes, 1, d)

time: 101 us -> 98.5 us (0.975)
  waiting for transfers between devices: 24.5 us -> 19.3 us
  starting transfers between devices: 46.6 us -> 49.1 us
    ppermute x7 -> x5, waiting for transfers between devices: 5.11 us -> 0.01 us  [ring(): lax.ppermute(array, axis, [(i, (i + shift) % size) for i in range(size)])]
    ppermute x13 -> x14, starting transfers between devices: 18.5 us -> 22.7 us  [move(): return lax.ppermute(array, ALL, perm)]
    all_to_all x2, starting transfers between devices: 13.4 us -> 11.1 us  [exchange(): return lax.all_to_all(array, axes, split_axis=0, concat_axis=0, tiled=True)]
    ppermute x7 -> x5, starting transfers between devices: 14.7 us -> 15.4 us  [ring(): lax.ppermute(array, axis, [(i, (i + shift) % size) for i in range(size)])]
    ppermute x13 -> x14, waiting for transfers between devices: 13.3 us -> 13.3 us  [move(): return lax.ppermute(array, ALL, perm)]
  transfers between devices with their start and end apart: 22 -> 21, of which waited for: 10 -> 7; matrix products, arithmetic and copies ran while one was open for 0% -> 0% of each run, Pallas kernels for 11% -> 12%
where the time goes in v12:
time: 98.5 us; the launch traced here: 97.1 us
  starting transfers between devices  49.1 us (50%)
  waiting for transfers between devices  19.3 us (20%)
  Pallas kernels  16.3 us (17%)
  blocking collectives  10.7 us (11%)
    ppermute x14, starting transfers between devices, move(): return lax.ppermute(array, ALL, perm)  22.7 us
    ppermute x5, starting transfers between devices, ring(): lax.ppermute(array, axis, [(i, (i + shift) % size) for i in range(size)])  15.4 us
    ppermute x14, waiting for transfers between devices, move(): return lax.ppermute(array, ALL, perm)  13.3 us
    pallas_call x6, Pallas kernels, tile(): pl.pallas_call(functools.partial(tile_kernel, 256, 256, start is not None...  11.4 us
    all_to_all x2, starting transfers between devices, exchange(): return lax.all_to_all(array, axes, split_axis=0, concat_axis=0, tiled=True)  11.1 us
    all_to_all x1, blocking collectives, exchange(): return lax.all_to_all(array, axes, split_axis=0, concat_axis=0, tiled=True)  10.7 us
    all_to_all x2, waiting for transfers between devices, exchange(): return lax.all_to_all(array, axes, split_axis=0, concat_axis=0, tiled=True)  6.03 us
  transfers between devices with their start and end apart: 21, of which 7 were waited for; matrix products, arithmetic and copies ran while one was open for 0% of the time, Pallas kernels for 12%

profile of v12, /device:TPU:1, one launch (start us, length us, event | category | flops | bytes accessed | tf_op | source)
XLA Modules:
  0.0 97.1 jit_solution(15111193291272325766)
XLA Ops:
  0.6 1.5 %pack.1 = (bf16[128,384]{1,0:T(8,128)(2,1)S(1)}, bf16[128,640]{1,0:T(8,128)(2,1)S(1)}) custom-call(bf16[128,512]{1,0:T(8,128)(2,1)} %embeds.1, bf16[512,256]{1,0:T(8,128)(2,1)} %weight.3, f32[1,128]{1,0:T(1,128)} %bitcast.8, f32[15,128]{1,0:T(8,128)} %bitcast.6, f32[15,128]{1,0:T(8,128)} %bitcast.7), custom_call_target="tpu_custom_call" | custom-call | tf_op jit(solution)/shard_map/pack/pallas_call | solution.py:229
  2.2 0.0 copy-start.1
  2.2 7.8 %collective-permute-start = (bf16[128,384]{1,0:T(8,128)(2,1)S(1)}, bf16[128,384]{1,0:T(8,128)(2,1)S(1)}, u32[]{:S(2)}, u32[]{:S(2)}) collective-permute-start(bf16[128,384]{1,0:T(8,128)(2,1)S(1)} %get-tuple-element.29), channel_id=1, source_target_pairs={{0,32},{4,36},{8,40},{12,44},{32,0},{36,4},{40,8},{44,12},{1,33},{... | collective-permute-start | bytes 294920 | tf_op jit(solution)/shard_map/ppermute | solution.py:200
  10.0 1.2 %collective-permute-start.5 = (bf16[128,640]{1,0:T(8,128)(2,1)S(1)}, bf16[128,640]{1,0:T(8,128)(2,1)S(1)}, u32[]{:S(2)}, u32[]{:S(2)}) collective-permute-start(bf16[128,640]{1,0:T(8,128)(2,1)S(1)} %get-tuple-element.30.refs_0_), channel_id=1, source_target_pairs={{0,64},{1,65},{2,66},{3,67},{4,68},{5,69},{6,70},{7,71},{8,72},{9,... | collective-permute-start | bytes 491528 | tf_op jit(solution)/shard_map/ppermute | solution.py:215
  11.2 2.5 %collective-permute-start.4 = (bf16[128,640]{1,0:T(8,128)(2,1)S(1)}, bf16[128,640]{1,0:T(8,128)(2,1)S(1)}, u32[]{:S(2)}, u32[]{:S(2)}) collective-permute-start(bf16[128,640]{1,0:T(8,128)(2,1)S(1)} %get-tuple-element.30.refs_0_), channel_id=1, source_target_pairs={{0,128},{1,129},{2,130},{3,131},{4,132},{5,133},{6,134},{7,135},{8... | collective-permute-start | bytes 491528 | tf_op jit(solution)/shard_map/ppermute | solution.py:215
  13.7 1.2 %collective-permute-start.3 = (bf16[128,640]{1,0:T(8,128)(2,1)S(1)}, bf16[128,640]{1,0:T(8,128)(2,1)S(1)}, u32[]{:S(2)}, u32[]{:S(2)}) collective-permute-start(bf16[128,640]{1,0:T(8,128)(2,1)S(1)} %get-tuple-element.30.refs_0_), channel_id=1, source_target_pairs={{0,192},{1,193},{2,194},{3,195},{4,196},{5,197},{6,198},{7,199},{8... | collective-permute-start | bytes 491528 | tf_op jit(solution)/shard_map/ppermute | solution.py:215
  14.8 2.0 %collective-permute-start.1 = (bf16[128,384]{1,0:T(8,128)(2,1)S(1)}, bf16[128,384]{1,0:T(8,128)(2,1)S(1)}, u32[]{:S(2)}, u32[]{:S(2)}) collective-permute-start(bf16[128,384]{1,0:T(8,128)(2,1)S(1)} %get-tuple-element.29), channel_id=1, source_target_pairs={{0,16},{16,0},{1,17},{17,1},{2,18},{18,2},{3,19},{19,3},{4,20},{20... | collective-permute-start | bytes 294920 | tf_op jit(solution)/shard_map/ppermute | solution.py:200
  16.8 0.0 collective-permute-done
  16.8 0.0 collective-permute-start.2
  16.8 0.0 collective-permute-done.5.refs_3_
  16.8 1.6 %collective-permute-done.4.refs_2_ = bf16[128,640]{1,0:T(8,128)(2,1)S(1)} collective-permute-done((bf16[128,640]{1,0:T(8,128)(2,1)S(1)}, bf16[128,640]{1,0:T(8,128)(2,1)S(1)}, u32[]{:S(2)}, u32[]{:S(2)}) %collective-permute-start.4) | collective-permute-done | bytes 163872 | tf_op jit(solution)/shard_map/ppermute | solution.py:215
  18.4 0.0 collective-permute-done.3.refs_1_
  18.4 0.3 split.1
  18.7 0.0 copy-start
  18.8 0.0 collective-permute-done.2
  18.8 1.0 %collective-permute-start.6 = (bf16[512,384]{1,0:T(8,128)(2,1)S(1)}, bf16[512,384]{1,0:T(8,128)(2,1)S(1)}, u32[]{:S(2)}, u32[]{:S(2)}) collective-permute-start(bf16[512,384]{1,0:T(8,128)(2,1)S(1)} %pad_maximum_fusion.refs_0_), channel_id=1, source_target_pairs={{0,4},{1,5},{2,6},{3,7},{4,8},{5,9},{6,10},{7,11},{8,12},{9,13},{1... | collective-permute-start | bytes 1179656 | tf_op jit(solution)/shard_map/ppermute | solution.py:215
  19.9 1.3 %collective-permute-start.10 = (bf16[640,256]{1,0:T(8,128)(2,1)S(1)}, bf16[640,256]{1,0:T(8,128)(2,1)S(1)}, u32[]{:S(2)}, u32[]{:S(2)}) collective-permute-start(bf16[640,256]{1,0:T(8,128)(2,1)S(1)} %get-tuple-element.32.rows_ref), channel_id=1, source_target_pairs={{0,1},{1,2},{2,3},{3,0},{4,5},{5,6},{6,7},{7,4},{8,9},{9,10},{10,1... | collective-permute-start | bytes 983048 | tf_op jit(solution)/shard_map/ppermute | solution.py:215
  21.2 2.6 %collective-permute-start.9 = (bf16[640,256]{1,0:T(8,128)(2,1)S(1)}, bf16[640,256]{1,0:T(8,128)(2,1)S(1)}, u32[]{:S(2)}, u32[]{:S(2)}) collective-permute-start(bf16[640,256]{1,0:T(8,128)(2,1)S(1)} %get-tuple-element.32.rows_ref), channel_id=1, source_target_pairs={{0,2},{1,3},{2,0},{3,1},{4,6},{5,7},{6,4},{7,5},{8,10},{9,11},{10,... | collective-permute-start | bytes 983048 | tf_op jit(solution)/shard_map/ppermute | solution.py:215
  23.8 1.1 %collective-permute-start.8 = (bf16[640,256]{1,0:T(8,128)(2,1)S(1)}, bf16[640,256]{1,0:T(8,128)(2,1)S(1)}, u32[]{:S(2)}, u32[]{:S(2)}) collective-permute-start(bf16[640,256]{1,0:T(8,128)(2,1)S(1)} %get-tuple-element.32.rows_ref), channel_id=1, source_target_pairs={{0,3},{1,0},{2,1},{3,2},{4,7},{5,4},{6,5},{7,6},{8,11},{9,8},{10,9... | collective-permute-start | bytes 983048 | tf_op jit(solution)/shard_map/ppermute | solution.py:215
  24.9 2.3 %collective-permute-start.7 = (bf16[256,384]{1,0:T(8,128)(2,1)S(1)}, bf16[256,384]{1,0:T(8,128)(2,1)S(1)}, u32[]{:S(2)}, u32[]{:S(2)}) collective-permute-start(bf16[256,384]{1,0:T(8,128)(2,1)S(1)} %pad_maximum_fusion.1), channel_id=1, source_target_pairs={{0,8},{1,9},{2,10},{3,11},{4,12},{5,13},{6,14},{7,15},{8,32},{9,33... | collective-permute-start | bytes 589832 | tf_op jit(solution)/shard_map/ppermute | solution.py:215
  27.2 0.9 tile.6.refs_0_
  28.1 4.5 %collective-permute-done.7.refs_2_ = bf16[256,384]{1,0:T(8,128)(2,1)S(1)} collective-permute-done((bf16[256,384]{1,0:T(8,128)(2,1)S(1)}, bf16[256,384]{1,0:T(8,128)(2,1)S(1)}, u32[]{:S(2)}, u32[]{:S(2)}) %collective-permute-start.7) | collective-permute-done | bytes 196640 | tf_op jit(solution)/shard_map/ppermute | solution.py:215
  32.6 5.3 %collective-permute-start.11 = (bf16[512,384]{1,0:T(8,128)(2,1)S(1)}, bf16[512,384]{1,0:T(8,128)(2,1)S(1)}, u32[]{:S(2)}, u32[]{:S(2)}) collective-permute-start(bf16[512,384]{1,0:T(8,128)(2,1)S(1)} %collective-permute-done.6.refs_1_), channel_id=1, source_target_pairs={{0,16},{16,0},{1,17},{17,1},{2,18},{18,2},{3,19},{19,3},{4,20},{20... | collective-permute-start | bytes 1179656 | tf_op jit(solution)/shard_map/ppermute | solution.py:200
  37.9 0.3 collective-permute-start.12
  38.2 1.8 %tile.9.refs_0_ = f32[512,256]{1,0:T(8,128)S(1)} custom-call(bf16[2,128,128]{2,1,0:T(8,128)(2,1)S(1)} %copy-done, bf16[640,256]{1,0:T(8,128)(2,1)S(1)} %collective-permute-done.9.rows_ref, bf16[512,384]{1,0:T(8,128)(2,1)S(1)} %pad_maximum_fusion.refs_0_, bf16[512,384]{1,0:T(8,128)(2,1)S(1)} %collective-permute-done.6.refs_1_, ...), custom_call_target="tpu_custom_call" | custom-call | tf_op jit(solution)/shard_map/tile/pallas_call | solution.py:270
  40.0 1.2 %tile.10 = bf16[512,256]{1,0:T(8,128)(2,1)S(1)} custom-call(bf16[2,128,128]{2,1,0:T(8,128)(2,1)S(1)} %copy-done, bf16[640,256]{1,0:T(8,128)(2,1)S(1)} %collective-permute-done.9.rows_ref, f32[512,256]{1,0:T(8,128)S(1)} %tile.9.refs_0_, bf16[512,384]{1,0:T(8,128)(2,1)S(1)} %collective-permute-done.11.refs_3_.refs_1_, ...), custom_call_target="tpu_custom_call" | custom-call | tf_op jit(solution)/shard_map/tile/pallas_call | solution.py:270
  41.3 2.4 %collective-permute-start.14 = (bf16[512,256]{1,0:T(8,128)(2,1)S(1)}, bf16[512,256]{1,0:T(8,128)(2,1)S(1)}, u32[]{:S(2)}, u32[]{:S(2)}) collective-permute-start(bf16[512,256]{1,0:T(8,128)(2,1)S(1)} %tile.10), channel_id=1, source_target_pairs={{0,2},{1,3},{2,0},{3,1},{4,6},{5,7},{6,4},{7,5},{8,10},{9,11},{10,... | collective-permute-start | bytes 786440 | tf_op jit(solution)/shard_map/ppermute | solution.py:215
  43.7 2.7 %tile.8 = bf16[512,256]{1,0:T(8,128)(2,1)S(1)} custom-call(bf16[2,128,128]{2,1,0:T(8,128)(2,1)S(1)} %copy-done, bf16[640,256]{1,0:T(8,128)(2,1)S(1)} %collective-permute-done.8.rows_ref, bf16[512,384]{1,0:T(8,128)(2,1)S(1)} %pad_maximum_fusion.refs_0_, bf16[512,384]{1,0:T(8,128)(2,1)S(1)} %collective-permute-done.6.refs_1_, ...), custom_call_target="tpu_custom_call" | custom-call | tf_op jit(solution)/shard_map/tile/pallas_call | solution.py:270
  46.4 0.6 collective-permute-start.13
  47.0 2.7 %tile.11 = bf16[512,256]{1,0:T(8,128)(2,1)S(1)} custom-call(bf16[2,128,128]{2,1,0:T(8,128)(2,1)S(1)} %copy-done, bf16[640,256]{1,0:T(8,128)(2,1)S(1)} %collective-permute-done.10.rows_ref, bf16[512,384]{1,0:T(8,128)(2,1)S(1)} %pad_maximum_fusion.refs_0_, bf16[512,384]{1,0:T(8,128)(2,1)S(1)} %collective-permute-done.6.refs_1_, ...), custom_call_target="tpu_custom_call" | custom-call | tf_op jit(solution)/shard_map/tile/pallas_call | solution.py:270
  49.7 2.4 %collective-permute-start.15 = (bf16[512,256]{1,0:T(8,128)(2,1)S(1)}, bf16[512,256]{1,0:T(8,128)(2,1)S(1)}, u32[]{:S(2)}, u32[]{:S(2)}) collective-permute-start(bf16[512,256]{1,0:T(8,128)(2,1)S(1)} %tile.11), channel_id=1, source_target_pairs={{0,3},{1,0},{2,1},{3,2},{4,7},{5,4},{6,5},{7,6},{8,11},{9,8},{10,9... | collective-permute-start | bytes 786440 | tf_op jit(solution)/shard_map/ppermute | solution.py:215
  52.1 2.1 %tile.7.a = f32[512,256]{1,0:T(8,128)S(1)} custom-call(bf16[2,128,128]{2,1,0:T(8,128)(2,1)S(1)} %copy-done, bf16[640,256]{1,0:T(8,128)(2,1)S(1)} %get-tuple-element.32.rows_ref, f32[512,256]{1,0:T(8,128)S(1)} %tile.6.refs_0_, bf16[512,384]{1,0:T(8,128)(2,1)S(1)} %collective-permute-done.6.refs_1_, bf16[256,384]{1,0:T(8,128)(2,1)S(1)} %collective-permute-done.7.refs_2_, ...), custom_call_target="tpu_custom_call" | custom-call | tf_op jit(solution)/shard_map/tile/pallas_call | solution.py:270
  54.2 0.5 sum_rows.1
  54.7 0.7 collective-permute-done.15.last
  55.4 1.1 %last_rows.1 = (bf16[512,256]{1,0:T(8,128)(2,1)}, f32[128,256]{1,0:T(8,128)S(1)}, bf16[128,256]{1,0:T(8,128)(2,1)S(1)}, bf16[128,256]{1,0:T(8,128)(2,1)S(1)}, bf16[128,256]{1,0:T(8,128)(2,1)S(1)}) custom-call(f32[512,256]{1,0:T(8,128)S(1)} %get-tuple-element.41.total, f32[512,256]{1,0:T(8,128)S(1)} %get-tuple-element.42.weight, ...), custom_call_target="tpu_custom_call" | custom-call | tf_op jit(solution)/shard_map/last_rows/pallas_call | solution.py:304
  56.5 4.5 %all-to-all-start = ((bf16[16,32,256]{2,1,0:T(8,128)(2,1)}), bf16[16,32,256]{2,1,0:T(8,128)(2,1)S(1)}, u32[]{:S(2)}, u32[]{:S(2)}) async-start(bf16[16,32,256]{2,1,0:T(8,128)(2,1)} %bitcast.3), calls=%async_computation | async-start | bytes 524288 | tf_op jit(solution)/shard_map/all_to_all | solution.py:223
  61.0 1.4 %collective-permute-start.16 = (bf16[128,256]{1,0:T(8,128)(2,1)S(1)}, bf16[128,256]{1,0:T(8,128)(2,1)S(1)}, u32[]{:S(2)}, u32[]{:S(2)}) collective-permute-start(bf16[128,256]{1,0:T(8,128)(2,1)S(1)} %get-tuple-element.45), channel_id=1, source_target_pairs={{0,64},{1,65},{2,66},{3,67},{4,68},{5,69},{6,70},{7,71},{8,72},{9,... | collective-permute-start | bytes 196616 | tf_op jit(solution)/shard_map/ppermute | solution.py:215
  62.4 4.5 %collective-permute-done.16.b = bf16[128,256]{1,0:T(8,128)(2,1)S(1)} collective-permute-done((bf16[128,256]{1,0:T(8,128)(2,1)S(1)}, bf16[128,256]{1,0:T(8,128)(2,1)S(1)}, u32[]{:S(2)}, u32[]{:S(2)}) %collective-permute-start.16) | collective-permute-done | bytes 65568 | tf_op jit(solution)/shard_map/ppermute | solution.py:215
  66.8 1.7 %all-to-all-done.refs_0_ = bf16[16,32,256]{2,1,0:T(8,128)(2,1)S(1)} async-done(((bf16[16,32,256]{2,1,0:T(8,128)(2,1)}), bf16[16,32,256]{2,1,0:T(8,128)(2,1)S(1)}, u32[]{:S(2)}, u32[]{:S(2)}) %all-to-all-start) | async-done | bytes 262176 | tf_op jit(solution)/shard_map/all_to_all | solution.py:223
  68.6 0.8 sum_spread.2
  69.3 6.6 %all-to-all-start.1 = ((bf16[16,32,256]{2,1,0:T(8,128)(2,1)}), bf16[16,32,256]{2,1,0:T(8,128)(2,1)S(1)}, u32[]{:S(2)}, u32[]{:S(2)}) async-start(bf16[16,32,256]{2,1,0:T(8,128)(2,1)} %sum_spread.2), calls=%async_computation.1 | async-start | bytes 524288 | tf_op jit(solution)/shard_map/all_to_all | solution.py:223
  75.9 1.0 %collective-permute-start.17 = (bf16[128,256]{1,0:T(8,128)(2,1)S(1)}, bf16[128,256]{1,0:T(8,128)(2,1)S(1)}, u32[]{:S(2)}, u32[]{:S(2)}) collective-permute-start(bf16[128,256]{1,0:T(8,128)(2,1)S(1)} %get-tuple-element.52), channel_id=1, source_target_pairs={{0,128},{1,129},{2,130},{3,131},{4,132},{5,133},{6,134},{7,135},{8... | collective-permute-start | bytes 196616 | tf_op jit(solution)/shard_map/ppermute | solution.py:215
  76.9 1.7 %collective-permute-start.18 = (bf16[128,256]{1,0:T(8,128)(2,1)S(1)}, bf16[128,256]{1,0:T(8,128)(2,1)S(1)}, u32[]{:S(2)}, u32[]{:S(2)}) collective-permute-start(bf16[128,256]{1,0:T(8,128)(2,1)S(1)} %get-tuple-element.53), channel_id=1, source_target_pairs={{0,192},{1,193},{2,194},{3,195},{4,196},{5,197},{6,198},{7,199},{8... | collective-permute-start | bytes 196616 | tf_op jit(solution)/shard_map/ppermute | solution.py:215
  78.6 1.9 %collective-permute-done.17.c = bf16[128,256]{1,0:T(8,128)(2,1)S(1)} collective-permute-done((bf16[128,256]{1,0:T(8,128)(2,1)S(1)}, bf16[128,256]{1,0:T(8,128)(2,1)S(1)}, u32[]{:S(2)}, u32[]{:S(2)}) %collective-permute-start.17) | collective-permute-done | bytes 65568 | tf_op jit(solution)/shard_map/ppermute | solution.py:215
  80.5 0.7 finish_rows.1
  81.2 4.3 %all-to-all-done.1.refs_0_ = bf16[16,32,256]{2,1,0:T(8,128)(2,1)S(1)} async-done(((bf16[16,32,256]{2,1,0:T(8,128)(2,1)}), bf16[16,32,256]{2,1,0:T(8,128)(2,1)S(1)}, u32[]{:S(2)}, u32[]{:S(2)}) %all-to-all-start.1) | async-done | bytes 262176 | tf_op jit(solution)/shard_map/all_to_all | solution.py:223
  85.6 10.7 %all_to_all.15 = bf16[16,32,256]{2,1,0:T(8,128)(2,1)S(1)} all-to-all(bf16[16,32,256]{2,1,0:T(8,128)(2,1)S(1)} %sum_spread.3), channel_id=1, replica_groups=mesh['y'=4,'zh'=2,'core'=2,'zl'=4,'x'=4] {'y','x'}, dimensions={0} | all-to-all | bytes 524288 | tf_op jit(solution)/shard_map/all_to_all | solution.py:223
  96.3 0.8 convert_multiply_fusion
  (15 shorter events, 0.1 us)
Async XLA Ops:
  2.2 16.3 %copy-start.1 = (bf16[512,256]{1,0:T(8,128)(2,1)S(1)}, bf16[512,256]{1,0:T(8,128)(2,1)}, u32[]{:S(2)}) copy-start(bf16[512,256]{1,0:T(8,128)(2,1)} %weight.3) | copy-start | bytes 786436
  2.2 14.6 %collective-permute-start = (bf16[128,384]{1,0:T(8,128)(2,1)S(1)}, bf16[128,384]{1,0:T(8,128)(2,1)S(1)}, u32[]{:S(2)}, u32[]{:S(2)}) collective-permute-start(bf16[128,384]{1,0:T(8,128)(2,1)S(1)} %get-tuple-element.29), channel_id=1, source_target_pairs={{0,32},{4,36},{8,40},{12,44},{32,0},{36,4},{40,8},{44,12},{1,33},{... | collective-permute-start | bytes 294920 | tf_op jit(solution)/shard_map/ppermute | solution.py:200
  10.0 6.8 %collective-permute-start.5 = (bf16[128,640]{1,0:T(8,128)(2,1)S(1)}, bf16[128,640]{1,0:T(8,128)(2,1)S(1)}, u32[]{:S(2)}, u32[]{:S(2)}) collective-permute-start(bf16[128,640]{1,0:T(8,128)(2,1)S(1)} %get-tuple-element.30.refs_0_), channel_id=1, source_target_pairs={{0,64},{1,65},{2,66},{3,67},{4,68},{5,69},{6,70},{7,71},{8,72},{9,... | collective-permute-start | bytes 491528 | tf_op jit(solution)/shard_map/ppermute | solution.py:215
  11.2 7.2 %collective-permute-start.4 = (bf16[128,640]{1,0:T(8,128)(2,1)S(1)}, bf16[128,640]{1,0:T(8,128)(2,1)S(1)}, u32[]{:S(2)}, u32[]{:S(2)}) collective-permute-start(bf16[128,640]{1,0:T(8,128)(2,1)S(1)} %get-tuple-element.30.refs_0_), channel_id=1, source_target_pairs={{0,128},{1,129},{2,130},{3,131},{4,132},{5,133},{6,134},{7,135},{8... | collective-permute-start | bytes 491528 | tf_op jit(solution)/shard_map/ppermute | solution.py:215
  13.7 4.8 %collective-permute-start.3 = (bf16[128,640]{1,0:T(8,128)(2,1)S(1)}, bf16[128,640]{1,0:T(8,128)(2,1)S(1)}, u32[]{:S(2)}, u32[]{:S(2)}) collective-permute-start(bf16[128,640]{1,0:T(8,128)(2,1)S(1)} %get-tuple-element.30.refs_0_), channel_id=1, source_target_pairs={{0,192},{1,193},{2,194},{3,195},{4,196},{5,197},{6,198},{7,199},{8... | collective-permute-start | bytes 491528 | tf_op jit(solution)/shard_map/ppermute | solution.py:215
  14.8 3.9 %collective-permute-start.1 = (bf16[128,384]{1,0:T(8,128)(2,1)S(1)}, bf16[128,384]{1,0:T(8,128)(2,1)S(1)}, u32[]{:S(2)}, u32[]{:S(2)}) collective-permute-start(bf16[128,384]{1,0:T(8,128)(2,1)S(1)} %get-tuple-element.29), channel_id=1, source_target_pairs={{0,16},{16,0},{1,17},{17,1},{2,18},{18,2},{3,19},{19,3},{4,20},{20... | collective-permute-start | bytes 294920 | tf_op jit(solution)/shard_map/ppermute | solution.py:200
  16.8 2.0 %collective-permute-start.2 = (bf16[128,384]{1,0:T(8,128)(2,1)S(1)}, bf16[128,384]{1,0:T(8,128)(2,1)S(1)}, u32[]{:S(2)}, u32[]{:S(2)}) collective-permute-start(bf16[128,384]{1,0:T(8,128)(2,1)S(1)} %collective-permute-done), channel_id=1, source_target_pairs={{0,16},{16,0},{1,17},{17,1},{2,18},{18,2},{3,19},{19,3},{4,20},{20... | collective-permute-start | bytes 294920 | tf_op jit(solution)/shard_map/ppermute | solution.py:200
  18.7 8.4 %copy-start = (bf16[2,128,128]{2,1,0:T(8,128)(2,1)S(1)}, bf16[2,128,128]{2,1,0:T(8,128)(2,1)}, u32[]{:S(2)}) copy-start(bf16[2,128,128]{2,1,0:T(8,128)(2,1)} %constant.4.clone.table) | copy-start | bytes 196612
  18.8 13.8 %collective-permute-start.6 = (bf16[512,384]{1,0:T(8,128)(2,1)S(1)}, bf16[512,384]{1,0:T(8,128)(2,1)S(1)}, u32[]{:S(2)}, u32[]{:S(2)}) collective-permute-start(bf16[512,384]{1,0:T(8,128)(2,1)S(1)} %pad_maximum_fusion.refs_0_), channel_id=1, source_target_pairs={{0,4},{1,5},{2,6},{3,7},{4,8},{5,9},{6,10},{7,11},{8,12},{9,13},{1... | collective-permute-start | bytes 1179656 | tf_op jit(solution)/shard_map/ppermute | solution.py:215
  19.9 12.7 %collective-permute-start.10 = (bf16[640,256]{1,0:T(8,128)(2,1)S(1)}, bf16[640,256]{1,0:T(8,128)(2,1)S(1)}, u32[]{:S(2)}, u32[]{:S(2)}) collective-permute-start(bf16[640,256]{1,0:T(8,128)(2,1)S(1)} %get-tuple-element.32.rows_ref), channel_id=1, source_target_pairs={{0,1},{1,2},{2,3},{3,0},{4,5},{5,6},{6,7},{7,4},{8,9},{9,10},{10,1... | collective-permute-start | bytes 983048 | tf_op jit(solution)/shard_map/ppermute | solution.py:215
  21.2 11.4 %collective-permute-start.9 = (bf16[640,256]{1,0:T(8,128)(2,1)S(1)}, bf16[640,256]{1,0:T(8,128)(2,1)S(1)}, u32[]{:S(2)}, u32[]{:S(2)}) collective-permute-start(bf16[640,256]{1,0:T(8,128)(2,1)S(1)} %get-tuple-element.32.rows_ref), channel_id=1, source_target_pairs={{0,2},{1,3},{2,0},{3,1},{4,6},{5,7},{6,4},{7,5},{8,10},{9,11},{10,... | collective-permute-start | bytes 983048 | tf_op jit(solution)/shard_map/ppermute | solution.py:215
  23.8 8.8 %collective-permute-start.8 = (bf16[640,256]{1,0:T(8,128)(2,1)S(1)}, bf16[640,256]{1,0:T(8,128)(2,1)S(1)}, u32[]{:S(2)}, u32[]{:S(2)}) collective-permute-start(bf16[640,256]{1,0:T(8,128)(2,1)S(1)} %get-tuple-element.32.rows_ref), channel_id=1, source_target_pairs={{0,3},{1,0},{2,1},{3,2},{4,7},{5,4},{6,5},{7,6},{8,11},{9,8},{10,9... | collective-permute-start | bytes 983048 | tf_op jit(solution)/shard_map/ppermute | solution.py:215
  24.9 7.7 %collective-permute-start.7 = (bf16[256,384]{1,0:T(8,128)(2,1)S(1)}, bf16[256,384]{1,0:T(8,128)(2,1)S(1)}, u32[]{:S(2)}, u32[]{:S(2)}) collective-permute-start(bf16[256,384]{1,0:T(8,128)(2,1)S(1)} %pad_maximum_fusion.1), channel_id=1, source_target_pairs={{0,8},{1,9},{2,10},{3,11},{4,12},{5,13},{6,14},{7,15},{8,32},{9,33... | collective-permute-start | bytes 589832 | tf_op jit(solution)/shard_map/ppermute | solution.py:215
  32.6 7.4 %collective-permute-start.11 = (bf16[512,384]{1,0:T(8,128)(2,1)S(1)}, bf16[512,384]{1,0:T(8,128)(2,1)S(1)}, u32[]{:S(2)}, u32[]{:S(2)}) collective-permute-start(bf16[512,384]{1,0:T(8,128)(2,1)S(1)} %collective-permute-done.6.refs_1_), channel_id=1, source_target_pairs={{0,16},{16,0},{1,17},{17,1},{2,18},{18,2},{3,19},{19,3},{4,20},{20... | collective-permute-start | bytes 1179656 | tf_op jit(solution)/shard_map/ppermute | solution.py:200
  37.9 2.1 %collective-permute-start.12 = (bf16[256,384]{1,0:T(8,128)(2,1)S(1)}, bf16[256,384]{1,0:T(8,128)(2,1)S(1)}, u32[]{:S(2)}, u32[]{:S(2)}) collective-permute-start(bf16[256,384]{1,0:T(8,128)(2,1)S(1)} %collective-permute-done.7.refs_2_), channel_id=1, source_target_pairs={{0,16},{16,0},{1,17},{17,1},{2,18},{18,2},{3,19},{19,3},{4,20},{20... | collective-permute-start | bytes 589832 | tf_op jit(solution)/shard_map/ppermute | solution.py:200
  41.3 12.9 %collective-permute-start.14 = (bf16[512,256]{1,0:T(8,128)(2,1)S(1)}, bf16[512,256]{1,0:T(8,128)(2,1)S(1)}, u32[]{:S(2)}, u32[]{:S(2)}) collective-permute-start(bf16[512,256]{1,0:T(8,128)(2,1)S(1)} %tile.10), channel_id=1, source_target_pairs={{0,2},{1,3},{2,0},{3,1},{4,6},{5,7},{6,4},{7,5},{8,10},{9,11},{10,... | collective-permute-start | bytes 786440 | tf_op jit(solution)/shard_map/ppermute | solution.py:215
  46.4 7.8 %collective-permute-start.13 = (bf16[512,256]{1,0:T(8,128)(2,1)S(1)}, bf16[512,256]{1,0:T(8,128)(2,1)S(1)}, u32[]{:S(2)}, u32[]{:S(2)}) collective-permute-start(bf16[512,256]{1,0:T(8,128)(2,1)S(1)} %tile.8), channel_id=1, source_target_pairs={{0,1},{1,2},{2,3},{3,0},{4,5},{5,6},{6,7},{7,4},{8,9},{9,10},{10,1... | collective-permute-start | bytes 786440 | tf_op jit(solution)/shard_map/ppermute | solution.py:215
  49.7 5.7 %collective-permute-start.15 = (bf16[512,256]{1,0:T(8,128)(2,1)S(1)}, bf16[512,256]{1,0:T(8,128)(2,1)S(1)}, u32[]{:S(2)}, u32[]{:S(2)}) collective-permute-start(bf16[512,256]{1,0:T(8,128)(2,1)S(1)} %tile.11), channel_id=1, source_target_pairs={{0,3},{1,0},{2,1},{3,2},{4,7},{5,4},{6,5},{7,6},{8,11},{9,8},{10,9... | collective-permute-start | bytes 786440 | tf_op jit(solution)/shard_map/ppermute | solution.py:215
  56.5 12.1 %all-to-all-start = ((bf16[16,32,256]{2,1,0:T(8,128)(2,1)}), bf16[16,32,256]{2,1,0:T(8,128)(2,1)S(1)}, u32[]{:S(2)}, u32[]{:S(2)}) async-start(bf16[16,32,256]{2,1,0:T(8,128)(2,1)} %bitcast.3), calls=%async_computation | async-start | bytes 524288 | tf_op jit(solution)/shard_map/all_to_all | solution.py:223
  61.0 5.8 %collective-permute-start.16 = (bf16[128,256]{1,0:T(8,128)(2,1)S(1)}, bf16[128,256]{1,0:T(8,128)(2,1)S(1)}, u32[]{:S(2)}, u32[]{:S(2)}) collective-permute-start(bf16[128,256]{1,0:T(8,128)(2,1)S(1)} %get-tuple-element.45), channel_id=1, source_target_pairs={{0,64},{1,65},{2,66},{3,67},{4,68},{5,69},{6,70},{7,71},{8,72},{9,... | collective-permute-start | bytes 196616 | tf_op jit(solution)/shard_map/ppermute | solution.py:215
  69.3 16.2 %all-to-all-start.1 = ((bf16[16,32,256]{2,1,0:T(8,128)(2,1)}), bf16[16,32,256]{2,1,0:T(8,128)(2,1)S(1)}, u32[]{:S(2)}, u32[]{:S(2)}) async-start(bf16[16,32,256]{2,1,0:T(8,128)(2,1)} %sum_spread.2), calls=%async_computation.1 | async-start | bytes 524288 | tf_op jit(solution)/shard_map/all_to_all | solution.py:223
  75.9 4.6 %collective-permute-start.17 = (bf16[128,256]{1,0:T(8,128)(2,1)S(1)}, bf16[128,256]{1,0:T(8,128)(2,1)S(1)}, u32[]{:S(2)}, u32[]{:S(2)}) collective-permute-start(bf16[128,256]{1,0:T(8,128)(2,1)S(1)} %get-tuple-element.52), channel_id=1, source_target_pairs={{0,128},{1,129},{2,130},{3,131},{4,132},{5,133},{6,134},{7,135},{8... | collective-permute-start | bytes 196616 | tf_op jit(solution)/shard_map/ppermute | solution.py:215
  76.9 3.6 %collective-permute-start.18 = (bf16[128,256]{1,0:T(8,128)(2,1)S(1)}, bf16[128,256]{1,0:T(8,128)(2,1)S(1)}, u32[]{:S(2)}, u32[]{:S(2)}) collective-permute-start(bf16[128,256]{1,0:T(8,128)(2,1)S(1)} %get-tuple-element.53), channel_id=1, source_target_pairs={{0,192},{1,193},{2,194},{3,195},{4,196},{5,197},{6,198},{7,199},{8... | collective-permute-start | bytes 196616 | tf_op jit(solution)/shard_map/ppermute | solution.py:215

commit v13 on v12

--- a/solution.py
+++ b/solution.py
@@ -277,13 +277,16 @@
         )(table, rows_in, *([] if start is None else [start]), *columns)
 
     begin = tile(line, [four], F32)
-    near, far, lines, begin = lax.optimization_barrier((near, far, lines, begin))
-    columns = [four, near, far, ring(near, "core", 2, 1), ring(far, "core", 2, 1)]
+    halves = [near[: 2 * rows], near[2 * rows :]]
+    columns = [four, near, ring(halves[0], "core", 2, 1), far]
+    columns, lines, begin, halves = lax.optimization_barrier((columns, lines, begin, halves))
+    early = len(columns)
+    columns += [ring(part, "core", 2, 1) for part in (halves[1], far)]
 
     back = {}
     for d in (0, 3, 1, 2):
         if d == 2:
-            part = tile(lines[d], columns[3:], BF16, tile(lines[d], columns[:3], F32))
+            part = tile(lines[d], columns[early:], BF16, tile(lines[d], columns[:early], F32))
         elif d == 0:
             part = tile(line, columns[1:], F32, begin)
         else:
@@ -313,15 +316,12 @@
         compiler_params=params(16),
         name="last_rows",
     )(total, weight_sum, back[3], embeds_line)
-    arrived = [turn(other_rows[0], sizes, 0, 1)]
-
     n_plane = n_side * n_side
     pieces = exchange(partial.reshape(n_plane, -1, width), PLANE)
-    pieces, arrived[0] = lax.optimization_barrier((pieces, arrived[0]))
     spread = sum_spread([pieces], n_z * 2, BF16)
-    spread, other_rows[1], other_rows[2] = lax.optimization_barrier((spread, other_rows[1], other_rows[2]))
+    spread, other_rows = lax.optimization_barrier((spread, other_rows))
     pieces = exchange(spread, STACK)
-    arrived += [turn(other_rows[d], sizes, 0, d + 1) for d in (1, 2)]
+    arrived = [turn(block, sizes, 0, d + 1) for d, block in enumerate(other_rows)]
     grad_rows = pl.pallas_call(
         finish_rows_kernel,
         out_shape=jax.ShapeDtypeStruct((rows, width), F32),

time: 98.5 us -> 97.6 us (level)
  blocking collectives: 10.7 us -> 22.6 us
  waiting for transfers between devices: 19.3 us -> 9.83 us
  starting transfers between devices: 49.1 us -> 46.7 us
    all_to_all x1 -> x2, blocking collectives: 10.7 us -> 22.6 us  [exchange(): return lax.all_to_all(array, axes, split_axis=0, concat_axis=0, tiled=True)]
    ppermute x14, waiting for transfers between devices: 13.3 us -> 6.78 us  [move(): return lax.ppermute(array, ALL, perm)]
    all_to_all x2 -> x1, starting transfers between devices: 11.1 us -> 6.91 us  [exchange(): return lax.all_to_all(array, axes, split_axis=0, concat_axis=0, tiled=True)]
    ppermute x5 -> x6, starting transfers between devices: 15.4 us -> 18.4 us  [ring(): lax.ppermute(array, axis, [(i, (i + shift) % size) for i in range(size)])]
    all_to_all x2 -> x1, waiting for transfers between devices: 6.03 us -> 3.03 us  [exchange(): return lax.all_to_all(array, axes, split_axis=0, concat_axis=0, tiled=True)]
    ppermute x14, starting transfers between devices: 22.7 us -> 21.4 us  [move(): return lax.ppermute(array, ALL, perm)]
  transfers between devices with their start and end apart: 21 -> 21, of which waited for: 7 -> 6; matrix products, arithmetic and copies ran while one was open for 0% -> 0% of each run, Pallas kernels for 12% -> 12%
where the time goes in v13:
time: 97.6 us; the launch traced here: 96.3 us
  starting transfers between devices  46.7 us (48%)
  blocking collectives  22.6 us (23%)
  Pallas kernels  15.4 us (16%)
  waiting for transfers between devices  9.83 us (10%)
    all_to_all x2, blocking collectives, exchange(): return lax.all_to_all(array, axes, split_axis=0, concat_axis=0, tiled=True)  22.6 us
    ppermute x14, starting transfers between devices, move(): return lax.ppermute(array, ALL, perm)  21.4 us
    ppermute x6, starting transfers between devices, ring(): lax.ppermute(array, axis, [(i, (i + shift) % size) for i in range(size)])  18.4 us
    pallas_call x6, Pallas kernels, tile(): pl.pallas_call(functools.partial(tile_kernel, 256, 256, start is not None...  11.3 us
    all_to_all x1, starting transfers between devices, exchange(): return lax.all_to_all(array, axes, split_axis=0, concat_axis=0, tiled=True)  6.91 us
    ppermute x14, waiting for transfers between devices, move(): return lax.ppermute(array, ALL, perm)  6.78 us
    all_to_all x1, waiting for transfers between devices, exchange(): return lax.all_to_all(array, axes, split_axis=0, concat_axis=0, tiled=True)  3.03 us
  transfers between devices with their start and end apart: 21, of which 6 were waited for; matrix products, arithmetic and copies ran while one was open for 0% of the time, Pallas kernels for 12%

profile of v13, /device:TPU:1, one launch (start us, length us, event | category | flops | bytes accessed | tf_op | source)
XLA Modules:
  0.0 96.3 jit_solution(6486777385679055832)
XLA Ops:
  0.6 1.5 %pack.1 = (bf16[128,384]{1,0:T(8,128)(2,1)S(1)}, bf16[128,640]{1,0:T(8,128)(2,1)S(1)}) custom-call(bf16[128,512]{1,0:T(8,128)(2,1)} %embeds.1, bf16[512,256]{1,0:T(8,128)(2,1)} %weight.3, f32[1,128]{1,0:T(1,128)} %bitcast.9, f32[15,128]{1,0:T(8,128)} %bitcast.7, f32[15,128]{1,0:T(8,128)} %bitcast.8), custom_call_target="tpu_custom_call" | custom-call | tf_op jit(solution)/shard_map/pack/pallas_call | solution.py:229
  2.2 0.0 copy-start.1
  2.2 7.8 %collective-permute-start = (bf16[128,384]{1,0:T(8,128)(2,1)S(1)}, bf16[128,384]{1,0:T(8,128)(2,1)S(1)}, u32[]{:S(2)}, u32[]{:S(2)}) collective-permute-start(bf16[128,384]{1,0:T(8,128)(2,1)S(1)} %get-tuple-element.31), channel_id=1, source_target_pairs={{0,32},{4,36},{8,40},{12,44},{32,0},{36,4},{40,8},{44,12},{1,33},{... | collective-permute-start | bytes 294920 | tf_op jit(solution)/shard_map/ppermute | solution.py:200
  10.0 1.2 %collective-permute-start.5 = (bf16[128,640]{1,0:T(8,128)(2,1)S(1)}, bf16[128,640]{1,0:T(8,128)(2,1)S(1)}, u32[]{:S(2)}, u32[]{:S(2)}) collective-permute-start(bf16[128,640]{1,0:T(8,128)(2,1)S(1)} %get-tuple-element.32.refs_0_), channel_id=1, source_target_pairs={{0,64},{1,65},{2,66},{3,67},{4,68},{5,69},{6,70},{7,71},{8,72},{9,... | collective-permute-start | bytes 491528 | tf_op jit(solution)/shard_map/ppermute | solution.py:215
  11.2 2.5 %collective-permute-start.4 = (bf16[128,640]{1,0:T(8,128)(2,1)S(1)}, bf16[128,640]{1,0:T(8,128)(2,1)S(1)}, u32[]{:S(2)}, u32[]{:S(2)}) collective-permute-start(bf16[128,640]{1,0:T(8,128)(2,1)S(1)} %get-tuple-element.32.refs_0_), channel_id=1, source_target_pairs={{0,128},{1,129},{2,130},{3,131},{4,132},{5,133},{6,134},{7,135},{8... | collective-permute-start | bytes 491528 | tf_op jit(solution)/shard_map/ppermute | solution.py:215
  13.7 1.2 %collective-permute-start.3 = (bf16[128,640]{1,0:T(8,128)(2,1)S(1)}, bf16[128,640]{1,0:T(8,128)(2,1)S(1)}, u32[]{:S(2)}, u32[]{:S(2)}) collective-permute-start(bf16[128,640]{1,0:T(8,128)(2,1)S(1)} %get-tuple-element.32.refs_0_), channel_id=1, source_target_pairs={{0,192},{1,193},{2,194},{3,195},{4,196},{5,197},{6,198},{7,199},{8... | collective-permute-start | bytes 491528 | tf_op jit(solution)/shard_map/ppermute | solution.py:215
  14.8 2.0 %collective-permute-start.1 = (bf16[128,384]{1,0:T(8,128)(2,1)S(1)}, bf16[128,384]{1,0:T(8,128)(2,1)S(1)}, u32[]{:S(2)}, u32[]{:S(2)}) collective-permute-start(bf16[128,384]{1,0:T(8,128)(2,1)S(1)} %get-tuple-element.31), channel_id=1, source_target_pairs={{0,16},{16,0},{1,17},{17,1},{2,18},{18,2},{3,19},{19,3},{4,20},{20... | collective-permute-start | bytes 294920 | tf_op jit(solution)/shard_map/ppermute | solution.py:200
  16.8 0.0 collective-permute-done
  16.8 0.0 collective-permute-start.2
  16.8 0.0 collective-permute-done.5.refs_3_
  16.8 1.6 %collective-permute-done.4.refs_2_ = bf16[128,640]{1,0:T(8,128)(2,1)S(1)} collective-permute-done((bf16[128,640]{1,0:T(8,128)(2,1)S(1)}, bf16[128,640]{1,0:T(8,128)(2,1)S(1)}, u32[]{:S(2)}, u32[]{:S(2)}) %collective-permute-start.4) | collective-permute-done | bytes 163872 | tf_op jit(solution)/shard_map/ppermute | solution.py:215
  18.4 0.0 collective-permute-done.3.refs_1_
  18.4 0.3 split.1
  18.7 0.0 collective-permute-done.1
  18.8 0.0 copy-start
  18.8 1.1 %collective-permute-start.6 = (bf16[512,384]{1,0:T(8,128)(2,1)S(1)}, bf16[512,384]{1,0:T(8,128)(2,1)S(1)}, u32[]{:S(2)}, u32[]{:S(2)}) collective-permute-start(bf16[512,384]{1,0:T(8,128)(2,1)S(1)} %pad_maximum_fusion.refs_0_), channel_id=1, source_target_pairs={{0,4},{1,5},{2,6},{3,7},{4,8},{5,9},{6,10},{7,11},{8,12},{9,13},{1... | collective-permute-start | bytes 1179656 | tf_op jit(solution)/shard_map/ppermute | solution.py:215
  19.9 1.3 %collective-permute-start.11 = (bf16[640,256]{1,0:T(8,128)(2,1)S(1)}, bf16[640,256]{1,0:T(8,128)(2,1)S(1)}, u32[]{:S(2)}, u32[]{:S(2)}) collective-permute-start(bf16[640,256]{1,0:T(8,128)(2,1)S(1)} %get-tuple-element.34.rows_ref), channel_id=1, source_target_pairs={{0,1},{1,2},{2,3},{3,0},{4,5},{5,6},{6,7},{7,4},{8,9},{9,10},{10,1... | collective-permute-start | bytes 983048 | tf_op jit(solution)/shard_map/ppermute | solution.py:215
  21.2 2.6 %collective-permute-start.10 = (bf16[640,256]{1,0:T(8,128)(2,1)S(1)}, bf16[640,256]{1,0:T(8,128)(2,1)S(1)}, u32[]{:S(2)}, u32[]{:S(2)}) collective-permute-start(bf16[640,256]{1,0:T(8,128)(2,1)S(1)} %get-tuple-element.34.rows_ref), channel_id=1, source_target_pairs={{0,2},{1,3},{2,0},{3,1},{4,6},{5,7},{6,4},{7,5},{8,10},{9,11},{10,... | collective-permute-start | bytes 983048 | tf_op jit(solution)/shard_map/ppermute | solution.py:215
  23.8 1.1 %collective-permute-start.9 = (bf16[640,256]{1,0:T(8,128)(2,1)S(1)}, bf16[640,256]{1,0:T(8,128)(2,1)S(1)}, u32[]{:S(2)}, u32[]{:S(2)}) collective-permute-start(bf16[640,256]{1,0:T(8,128)(2,1)S(1)} %get-tuple-element.34.rows_ref), channel_id=1, source_target_pairs={{0,3},{1,0},{2,1},{3,2},{4,7},{5,4},{6,5},{7,6},{8,11},{9,8},{10,9... | collective-permute-start | bytes 983048 | tf_op jit(solution)/shard_map/ppermute | solution.py:215
  24.9 2.3 %collective-permute-start.8 = (bf16[256,384]{1,0:T(8,128)(2,1)S(1)}, bf16[256,384]{1,0:T(8,128)(2,1)S(1)}, u32[]{:S(2)}, u32[]{:S(2)}) collective-permute-start(bf16[256,384]{1,0:T(8,128)(2,1)S(1)} %pad_maximum_fusion.1), channel_id=1, source_target_pairs={{0,8},{1,9},{2,10},{3,11},{4,12},{5,13},{6,14},{7,15},{8,32},{9,33... | collective-permute-start | bytes 589832 | tf_op jit(solution)/shard_map/ppermute | solution.py:215
  27.2 3.1 %collective-permute-start.7 = (bf16[256,384]{1,0:T(8,128)(2,1)S(1)}, bf16[256,384]{1,0:T(8,128)(2,1)S(1)}, u32[]{:S(2)}, u32[]{:S(2)}) collective-permute-start(bf16[256,384]{1,0:T(8,128)(2,1)S(1)} %get-tuple-element.61), channel_id=1, source_target_pairs={{0,16},{16,0},{1,17},{17,1},{2,18},{18,2},{3,19},{19,3},{4,20},{20... | collective-permute-start | bytes 589832 | tf_op jit(solution)/shard_map/ppermute | solution.py:200
  30.4 0.9 tile.6.refs_0_
  31.3 1.3 %collective-permute-done.8.refs_3_ = bf16[256,384]{1,0:T(8,128)(2,1)S(1)} collective-permute-done((bf16[256,384]{1,0:T(8,128)(2,1)S(1)}, bf16[256,384]{1,0:T(8,128)(2,1)S(1)}, u32[]{:S(2)}, u32[]{:S(2)}) %collective-permute-start.8) | collective-permute-done | bytes 196640 | tf_op jit(solution)/shard_map/ppermute | solution.py:215
  32.6 5.2 %collective-permute-start.13 = (bf16[256,384]{1,0:T(8,128)(2,1)S(1)}, bf16[256,384]{1,0:T(8,128)(2,1)S(1)}, u32[]{:S(2)}, u32[]{:S(2)}) collective-permute-start(bf16[256,384]{1,0:T(8,128)(2,1)S(1)} %collective-permute-done.8.refs_3_), channel_id=1, source_target_pairs={{0,16},{16,0},{1,17},{17,1},{2,18},{18,2},{3,19},{19,3},{4,20},{20... | collective-permute-start | bytes 589832 | tf_op jit(solution)/shard_map/ppermute | solution.py:200
  37.8 0.3 collective-permute-start.12
  38.1 2.1 %tile.9.refs_0_ = f32[512,256]{1,0:T(8,128)S(1)} custom-call(bf16[2,128,128]{2,1,0:T(8,128)(2,1)S(1)} %copy-done, bf16[640,256]{1,0:T(8,128)(2,1)S(1)} %collective-permute-done.10.rows_ref, bf16[512,384]{1,0:T(8,128)(2,1)S(1)} %pad_maximum_fusion.refs_0_, bf16[512,384]{1,0:T(8,128)(2,1)S(1)} %collective-permute-done.6.refs_1_, ...), custom_call_target="tpu_custom_call" | custom-call | tf_op jit(solution)/shard_map/tile/pallas_call | solution.py:270
  40.2 0.9 tile.10
  41.1 2.4 %collective-permute-start.15 = (bf16[512,256]{1,0:T(8,128)(2,1)S(1)}, bf16[512,256]{1,0:T(8,128)(2,1)S(1)}, u32[]{:S(2)}, u32[]{:S(2)}) collective-permute-start(bf16[512,256]{1,0:T(8,128)(2,1)S(1)} %tile.10), channel_id=1, source_target_pairs={{0,2},{1,3},{2,0},{3,1},{4,6},{5,7},{6,4},{7,5},{8,10},{9,11},{10,... | collective-permute-start | bytes 786440 | tf_op jit(solution)/shard_map/ppermute | solution.py:215
  43.5 2.7 %tile.8 = bf16[512,256]{1,0:T(8,128)(2,1)S(1)} custom-call(bf16[2,128,128]{2,1,0:T(8,128)(2,1)S(1)} %copy-done, bf16[640,256]{1,0:T(8,128)(2,1)S(1)} %collective-permute-done.9.rows_ref, bf16[512,384]{1,0:T(8,128)(2,1)S(1)} %pad_maximum_fusion.refs_0_, bf16[512,384]{1,0:T(8,128)(2,1)S(1)} %collective-permute-done.6.refs_1_, ...), custom_call_target="tpu_custom_call" | custom-call | tf_op jit(solution)/shard_map/tile/pallas_call | solution.py:270
  46.2 0.6 collective-permute-start.14
  46.8 2.7 %tile.11 = bf16[512,256]{1,0:T(8,128)(2,1)S(1)} custom-call(bf16[2,128,128]{2,1,0:T(8,128)(2,1)S(1)} %copy-done, bf16[640,256]{1,0:T(8,128)(2,1)S(1)} %collective-permute-done.11.rows_ref, bf16[512,384]{1,0:T(8,128)(2,1)S(1)} %pad_maximum_fusion.refs_0_, bf16[512,384]{1,0:T(8,128)(2,1)S(1)} %collective-permute-done.6.refs_1_, ...), custom_call_target="tpu_custom_call" | custom-call | tf_op jit(solution)/shard_map/tile/pallas_call | solution.py:270
  49.4 2.4 %collective-permute-start.16 = (bf16[512,256]{1,0:T(8,128)(2,1)S(1)}, bf16[512,256]{1,0:T(8,128)(2,1)S(1)}, u32[]{:S(2)}, u32[]{:S(2)}) collective-permute-start(bf16[512,256]{1,0:T(8,128)(2,1)S(1)} %tile.11), channel_id=1, source_target_pairs={{0,3},{1,0},{2,1},{3,2},{4,7},{5,4},{6,5},{7,6},{8,11},{9,8},{10,9... | collective-permute-start | bytes 786440 | tf_op jit(solution)/shard_map/ppermute | solution.py:215
  51.9 2.1 %tile.7.a = f32[512,256]{1,0:T(8,128)S(1)} custom-call(bf16[2,128,128]{2,1,0:T(8,128)(2,1)S(1)} %copy-done, bf16[640,256]{1,0:T(8,128)(2,1)S(1)} %get-tuple-element.34.rows_ref, f32[512,256]{1,0:T(8,128)S(1)} %tile.6.refs_0_, bf16[512,384]{1,0:T(8,128)(2,1)S(1)} %collective-permute-done.6.refs_1_, bf16[256,384]{1,0:T(8,128)(2,1)S(1)} %collective-permute-done.7.refs_2_, ...), custom_call_target="tpu_custom_call" | custom-call | tf_op jit(solution)/shard_map/tile/pallas_call | solution.py:270
  54.0 0.5 sum_rows.1
  54.5 0.7 collective-permute-done.16.last
  55.2 0.3 last_rows.1
  55.6 11.8 %all_to_all.15.refs_0_ = bf16[16,32,256]{2,1,0:T(8,128)(2,1)S(1)} all-to-all(bf16[16,32,256]{2,1,0:T(8,128)(2,1)S(1)} %bitcast.5), channel_id=1, replica_groups=mesh['y'=4,'zh'=2,'core'=2,'zl'=4,'x'=4] {'y','x'}, dimensions={0} | all-to-all | bytes 524288 | tf_op jit(solution)/shard_map/all_to_all | solution.py:223
  67.4 0.8 sum_spread.2
  68.2 6.9 %all-to-all-start.1 = ((bf16[16,32,256]{2,1,0:T(8,128)(2,1)}), bf16[16,32,256]{2,1,0:T(8,128)(2,1)S(1)}, u32[]{:S(2)}, u32[]{:S(2)}) async-start(bf16[16,32,256]{2,1,0:T(8,128)(2,1)} %sum_spread.2), calls=%async_computation.1 | async-start | bytes 524288 | tf_op jit(solution)/shard_map/all_to_all | solution.py:223
  75.1 0.3 collective-permute-start.17
  75.4 1.4 %collective-permute-start.18 = (bf16[128,256]{1,0:T(8,128)(2,1)S(1)}, bf16[128,256]{1,0:T(8,128)(2,1)S(1)}, u32[]{:S(2)}, u32[]{:S(2)}) collective-permute-start(bf16[128,256]{1,0:T(8,128)(2,1)S(1)} %get-tuple-element.56), channel_id=1, source_target_pairs={{0,128},{1,129},{2,130},{3,131},{4,132},{5,133},{6,134},{7,135},{8... | collective-permute-start | bytes 196616 | tf_op jit(solution)/shard_map/ppermute | solution.py:215
  76.7 1.1 %collective-permute-start.19 = (bf16[128,256]{1,0:T(8,128)(2,1)S(1)}, bf16[128,256]{1,0:T(8,128)(2,1)S(1)}, u32[]{:S(2)}, u32[]{:S(2)}) collective-permute-start(bf16[128,256]{1,0:T(8,128)(2,1)S(1)} %get-tuple-element.57), channel_id=1, source_target_pairs={{0,192},{1,193},{2,194},{3,195},{4,196},{5,197},{6,198},{7,199},{8... | collective-permute-start | bytes 196616 | tf_op jit(solution)/shard_map/ppermute | solution.py:215
  77.9 2.5 %collective-permute-done.17.b = bf16[128,256]{1,0:T(8,128)(2,1)S(1)} collective-permute-done((bf16[128,256]{1,0:T(8,128)(2,1)S(1)}, bf16[128,256]{1,0:T(8,128)(2,1)S(1)}, u32[]{:S(2)}, u32[]{:S(2)}) %collective-permute-start.17) | collective-permute-done | bytes 65568 | tf_op jit(solution)/shard_map/ppermute | solution.py:215
  80.4 0.6 collective-permute-done.19.d
  81.0 0.7 finish_rows.1
  81.7 3.0 %all-to-all-done.1.refs_0_ = bf16[16,32,256]{2,1,0:T(8,128)(2,1)S(1)} async-done(((bf16[16,32,256]{2,1,0:T(8,128)(2,1)}), bf16[16,32,256]{2,1,0:T(8,128)(2,1)S(1)}, u32[]{:S(2)}, u32[]{:S(2)}) %all-to-all-start.1) | async-done | bytes 262176 | tf_op jit(solution)/shard_map/all_to_all | solution.py:223
  84.8 10.7 %all_to_all.16 = bf16[16,32,256]{2,1,0:T(8,128)(2,1)S(1)} all-to-all(bf16[16,32,256]{2,1,0:T(8,128)(2,1)S(1)} %sum_spread.3), channel_id=1, replica_groups=mesh['y'=4,'zh'=2,'core'=2,'zl'=4,'x'=4] {'y','x'}, dimensions={0} | all-to-all | bytes 524288 | tf_op jit(solution)/shard_map/all_to_all | solution.py:223
  95.5 0.8 convert_multiply_fusion
  (17 shorter events, 0.2 us)
Async XLA Ops:
  2.2 16.3 %copy-start.1 = (bf16[512,256]{1,0:T(8,128)(2,1)S(1)}, bf16[512,256]{1,0:T(8,128)(2,1)}, u32[]{:S(2)}) copy-start(bf16[512,256]{1,0:T(8,128)(2,1)} %weight.3) | copy-start | bytes 786436
  2.2 14.6 %collective-permute-start = (bf16[128,384]{1,0:T(8,128)(2,1)S(1)}, bf16[128,384]{1,0:T(8,128)(2,1)S(1)}, u32[]{:S(2)}, u32[]{:S(2)}) collective-permute-start(bf16[128,384]{1,0:T(8,128)(2,1)S(1)} %get-tuple-element.31), channel_id=1, source_target_pairs={{0,32},{4,36},{8,40},{12,44},{32,0},{36,4},{40,8},{44,12},{1,33},{... | collective-permute-start | bytes 294920 | tf_op jit(solution)/shard_map/ppermute | solution.py:200
  10.0 6.8 %collective-permute-start.5 = (bf16[128,640]{1,0:T(8,128)(2,1)S(1)}, bf16[128,640]{1,0:T(8,128)(2,1)S(1)}, u32[]{:S(2)}, u32[]{:S(2)}) collective-permute-start(bf16[128,640]{1,0:T(8,128)(2,1)S(1)} %get-tuple-element.32.refs_0_), channel_id=1, source_target_pairs={{0,64},{1,65},{2,66},{3,67},{4,68},{5,69},{6,70},{7,71},{8,72},{9,... | collective-permute-start | bytes 491528 | tf_op jit(solution)/shard_map/ppermute | solution.py:215
  11.2 7.2 %collective-permute-start.4 = (bf16[128,640]{1,0:T(8,128)(2,1)S(1)}, bf16[128,640]{1,0:T(8,128)(2,1)S(1)}, u32[]{:S(2)}, u32[]{:S(2)}) collective-permute-start(bf16[128,640]{1,0:T(8,128)(2,1)S(1)} %get-tuple-element.32.refs_0_), channel_id=1, source_target_pairs={{0,128},{1,129},{2,130},{3,131},{4,132},{5,133},{6,134},{7,135},{8... | collective-permute-start | bytes 491528 | tf_op jit(solution)/shard_map/ppermute | solution.py:215
  13.7 4.8 %collective-permute-start.3 = (bf16[128,640]{1,0:T(8,128)(2,1)S(1)}, bf16[128,640]{1,0:T(8,128)(2,1)S(1)}, u32[]{:S(2)}, u32[]{:S(2)}) collective-permute-start(bf16[128,640]{1,0:T(8,128)(2,1)S(1)} %get-tuple-element.32.refs_0_), channel_id=1, source_target_pairs={{0,192},{1,193},{2,194},{3,195},{4,196},{5,197},{6,198},{7,199},{8... | collective-permute-start | bytes 491528 | tf_op jit(solution)/shard_map/ppermute | solution.py:215
  14.8 3.9 %collective-permute-start.1 = (bf16[128,384]{1,0:T(8,128)(2,1)S(1)}, bf16[128,384]{1,0:T(8,128)(2,1)S(1)}, u32[]{:S(2)}, u32[]{:S(2)}) collective-permute-start(bf16[128,384]{1,0:T(8,128)(2,1)S(1)} %get-tuple-element.31), channel_id=1, source_target_pairs={{0,16},{16,0},{1,17},{17,1},{2,18},{18,2},{3,19},{19,3},{4,20},{20... | collective-permute-start | bytes 294920 | tf_op jit(solution)/shard_map/ppermute | solution.py:200
  16.8 2.0 %collective-permute-start.2 = (bf16[128,384]{1,0:T(8,128)(2,1)S(1)}, bf16[128,384]{1,0:T(8,128)(2,1)S(1)}, u32[]{:S(2)}, u32[]{:S(2)}) collective-permute-start(bf16[128,384]{1,0:T(8,128)(2,1)S(1)} %collective-permute-done), channel_id=1, source_target_pairs={{0,16},{16,0},{1,17},{17,1},{2,18},{18,2},{3,19},{19,3},{4,20},{20... | collective-permute-start | bytes 294920 | tf_op jit(solution)/shard_map/ppermute | solution.py:200
  18.8 11.5 %copy-start = (bf16[2,128,128]{2,1,0:T(8,128)(2,1)S(1)}, bf16[2,128,128]{2,1,0:T(8,128)(2,1)}, u32[]{:S(2)}) copy-start(bf16[2,128,128]{2,1,0:T(8,128)(2,1)} %constant.4.clone.table) | copy-start | bytes 196612
  18.8 8.4 %collective-permute-start.6 = (bf16[512,384]{1,0:T(8,128)(2,1)S(1)}, bf16[512,384]{1,0:T(8,128)(2,1)S(1)}, u32[]{:S(2)}, u32[]{:S(2)}) collective-permute-start(bf16[512,384]{1,0:T(8,128)(2,1)S(1)} %pad_maximum_fusion.refs_0_), channel_id=1, source_target_pairs={{0,4},{1,5},{2,6},{3,7},{4,8},{5,9},{6,10},{7,11},{8,12},{9,13},{1... | collective-permute-start | bytes 1179656 | tf_op jit(solution)/shard_map/ppermute | solution.py:215
  19.9 17.9 %collective-permute-start.11 = (bf16[640,256]{1,0:T(8,128)(2,1)S(1)}, bf16[640,256]{1,0:T(8,128)(2,1)S(1)}, u32[]{:S(2)}, u32[]{:S(2)}) collective-permute-start(bf16[640,256]{1,0:T(8,128)(2,1)S(1)} %get-tuple-element.34.rows_ref), channel_id=1, source_target_pairs={{0,1},{1,2},{2,3},{3,0},{4,5},{5,6},{6,7},{7,4},{8,9},{9,10},{10,1... | collective-permute-start | bytes 983048 | tf_op jit(solution)/shard_map/ppermute | solution.py:215
  21.2 16.6 %collective-permute-start.10 = (bf16[640,256]{1,0:T(8,128)(2,1)S(1)}, bf16[640,256]{1,0:T(8,128)(2,1)S(1)}, u32[]{:S(2)}, u32[]{:S(2)}) collective-permute-start(bf16[640,256]{1,0:T(8,128)(2,1)S(1)} %get-tuple-element.34.rows_ref), channel_id=1, source_target_pairs={{0,2},{1,3},{2,0},{3,1},{4,6},{5,7},{6,4},{7,5},{8,10},{9,11},{10,... | collective-permute-start | bytes 983048 | tf_op jit(solution)/shard_map/ppermute | solution.py:215
  23.8 14.0 %collective-permute-start.9 = (bf16[640,256]{1,0:T(8,128)(2,1)S(1)}, bf16[640,256]{1,0:T(8,128)(2,1)S(1)}, u32[]{:S(2)}, u32[]{:S(2)}) collective-permute-start(bf16[640,256]{1,0:T(8,128)(2,1)S(1)} %get-tuple-element.34.rows_ref), channel_id=1, source_target_pairs={{0,3},{1,0},{2,1},{3,2},{4,7},{5,4},{6,5},{7,6},{8,11},{9,8},{10,9... | collective-permute-start | bytes 983048 | tf_op jit(solution)/shard_map/ppermute | solution.py:215
  24.9 7.7 %collective-permute-start.8 = (bf16[256,384]{1,0:T(8,128)(2,1)S(1)}, bf16[256,384]{1,0:T(8,128)(2,1)S(1)}, u32[]{:S(2)}, u32[]{:S(2)}) collective-permute-start(bf16[256,384]{1,0:T(8,128)(2,1)S(1)} %pad_maximum_fusion.1), channel_id=1, source_target_pairs={{0,8},{1,9},{2,10},{3,11},{4,12},{5,13},{6,14},{7,15},{8,32},{9,33... | collective-permute-start | bytes 589832 | tf_op jit(solution)/shard_map/ppermute | solution.py:215
  27.2 10.6 %collective-permute-start.7 = (bf16[256,384]{1,0:T(8,128)(2,1)S(1)}, bf16[256,384]{1,0:T(8,128)(2,1)S(1)}, u32[]{:S(2)}, u32[]{:S(2)}) collective-permute-start(bf16[256,384]{1,0:T(8,128)(2,1)S(1)} %get-tuple-element.61), channel_id=1, source_target_pairs={{0,16},{16,0},{1,17},{17,1},{2,18},{18,2},{3,19},{19,3},{4,20},{20... | collective-permute-start | bytes 589832 | tf_op jit(solution)/shard_map/ppermute | solution.py:200
  32.6 7.6 %collective-permute-start.13 = (bf16[256,384]{1,0:T(8,128)(2,1)S(1)}, bf16[256,384]{1,0:T(8,128)(2,1)S(1)}, u32[]{:S(2)}, u32[]{:S(2)}) collective-permute-start(bf16[256,384]{1,0:T(8,128)(2,1)S(1)} %collective-permute-done.8.refs_3_), channel_id=1, source_target_pairs={{0,16},{16,0},{1,17},{17,1},{2,18},{18,2},{3,19},{19,3},{4,20},{20... | collective-permute-start | bytes 589832 | tf_op jit(solution)/shard_map/ppermute | solution.py:200
  37.8 2.4 %collective-permute-start.12 = (bf16[256,384]{1,0:T(8,128)(2,1)S(1)}, bf16[256,384]{1,0:T(8,128)(2,1)S(1)}, u32[]{:S(2)}, u32[]{:S(2)}) collective-permute-start(bf16[256,384]{1,0:T(8,128)(2,1)S(1)} %get-tuple-element.41), channel_id=1, source_target_pairs={{0,16},{16,0},{1,17},{17,1},{2,18},{18,2},{3,19},{19,3},{4,20},{20... | collective-permute-start | bytes 589832 | tf_op jit(solution)/shard_map/ppermute | solution.py:200
  41.1 12.9 %collective-permute-start.15 = (bf16[512,256]{1,0:T(8,128)(2,1)S(1)}, bf16[512,256]{1,0:T(8,128)(2,1)S(1)}, u32[]{:S(2)}, u32[]{:S(2)}) collective-permute-start(bf16[512,256]{1,0:T(8,128)(2,1)S(1)} %tile.10), channel_id=1, source_target_pairs={{0,2},{1,3},{2,0},{3,1},{4,6},{5,7},{6,4},{7,5},{8,10},{9,11},{10,... | collective-permute-start | bytes 786440 | tf_op jit(solution)/shard_map/ppermute | solution.py:215
  46.2 7.8 %collective-permute-start.14 = (bf16[512,256]{1,0:T(8,128)(2,1)S(1)}, bf16[512,256]{1,0:T(8,128)(2,1)S(1)}, u32[]{:S(2)}, u32[]{:S(2)}) collective-permute-start(bf16[512,256]{1,0:T(8,128)(2,1)S(1)} %tile.8), channel_id=1, source_target_pairs={{0,1},{1,2},{2,3},{3,0},{4,5},{5,6},{6,7},{7,4},{8,9},{9,10},{10,1... | collective-permute-start | bytes 786440 | tf_op jit(solution)/shard_map/ppermute | solution.py:215
  49.4 5.8 %collective-permute-start.16 = (bf16[512,256]{1,0:T(8,128)(2,1)S(1)}, bf16[512,256]{1,0:T(8,128)(2,1)S(1)}, u32[]{:S(2)}, u32[]{:S(2)}) collective-permute-start(bf16[512,256]{1,0:T(8,128)(2,1)S(1)} %tile.11), channel_id=1, source_target_pairs={{0,3},{1,0},{2,1},{3,2},{4,7},{5,4},{6,5},{7,6},{8,11},{9,8},{10,9... | collective-permute-start | bytes 786440 | tf_op jit(solution)/shard_map/ppermute | solution.py:215
  68.2 16.5 %all-to-all-start.1 = ((bf16[16,32,256]{2,1,0:T(8,128)(2,1)}), bf16[16,32,256]{2,1,0:T(8,128)(2,1)S(1)}, u32[]{:S(2)}, u32[]{:S(2)}) async-start(bf16[16,32,256]{2,1,0:T(8,128)(2,1)} %sum_spread.2), calls=%async_computation.1 | async-start | bytes 524288 | tf_op jit(solution)/shard_map/all_to_all | solution.py:223
  75.1 5.3 %collective-permute-start.17 = (bf16[128,256]{1,0:T(8,128)(2,1)S(1)}, bf16[128,256]{1,0:T(8,128)(2,1)S(1)}, u32[]{:S(2)}, u32[]{:S(2)}) collective-permute-start(bf16[128,256]{1,0:T(8,128)(2,1)S(1)} %get-tuple-element.55), channel_id=1, source_target_pairs={{0,64},{1,65},{2,66},{3,67},{4,68},{5,69},{6,70},{7,71},{8,72},{9,... | collective-permute-start | bytes 196616 | tf_op jit(solution)/shard_map/ppermute | solution.py:215
  75.4 5.0 %collective-permute-start.18 = (bf16[128,256]{1,0:T(8,128)(2,1)S(1)}, bf16[128,256]{1,0:T(8,128)(2,1)S(1)}, u32[]{:S(2)}, u32[]{:S(2)}) collective-permute-start(bf16[128,256]{1,0:T(8,128)(2,1)S(1)} %get-tuple-element.56), channel_id=1, source_target_pairs={{0,128},{1,129},{2,130},{3,131},{4,132},{5,133},{6,134},{7,135},{8... | collective-permute-start | bytes 196616 | tf_op jit(solution)/shard_map/ppermute | solution.py:215
  76.7 4.2 %collective-permute-start.19 = (bf16[128,256]{1,0:T(8,128)(2,1)S(1)}, bf16[128,256]{1,0:T(8,128)(2,1)S(1)}, u32[]{:S(2)}, u32[]{:S(2)}) collective-permute-start(bf16[128,256]{1,0:T(8,128)(2,1)S(1)} %get-tuple-element.57), channel_id=1, source_target_pairs={{0,192},{1,193},{2,194},{3,195},{4,196},{5,197},{6,198},{7,199},{8... | collective-permute-start | bytes 196616 | tf_op jit(solution)/shard_map/ppermute | solution.py:215

commit v14 on v13

--- a/solution.py
+++ b/solution.py
@@ -276,22 +276,21 @@
             name="tile",
         )(table, rows_in, *([] if start is None else [start]), *columns)
 
-    begin = tile(line, [four], F32)
+    first = n_side - 1
+    begin = tile(lines[first], [four, near], F32)
     halves = [near[: 2 * rows], near[2 * rows :]]
     columns = [four, near, ring(halves[0], "core", 2, 1), far]
     columns, lines, begin, halves = lax.optimization_barrier((columns, lines, begin, halves))
     early = len(columns)
-    columns += [ring(part, "core", 2, 1) for part in (halves[1], far)]
+    columns += [ring(part, "core", 2, 1) for part in (halves[1], columns[-1])]
 
     back = {}
-    for d in (0, 3, 1, 2):
-        if d == 2:
-            part = tile(lines[d], columns[early:], BF16, tile(lines[d], columns[:early], F32))
-        elif d == 0:
-            part = tile(line, columns[1:], F32, begin)
+    for d in range(n_side):
+        if d == first:
+            part = tile(lines[d], columns[early:], BF16, tile(lines[d], columns[2:early], F32, begin))
         else:
-            part = tile(lines[d], columns, BF16)
-        back[d] = part if d == 0 else turn(part, sizes, 1, d)
+            part = tile(lines[d], columns, BF16 if d else F32)
+        back[d] = turn(part, sizes, 1, d) if d else part
 
     total, weight_sum = pl.pallas_call(
         sum_rows_kernel,
@@ -303,7 +302,7 @@
         out_specs=[VMEM] * 2,
         compiler_params=params(16),
         name="sum_rows",
-    )(back[0], back[1], back[2], embeds_line)
+    )(back[0], back[2], back[3], embeds_line)
     partial, own_rows, *other_rows = pl.pallas_call(
         last_rows_kernel,
         out_shape=[
@@ -315,7 +314,7 @@
         out_specs=[VMEM] * (n_side + 1),
         compiler_params=params(16),
         name="last_rows",
-    )(total, weight_sum, back[3], embeds_line)
+    )(total, weight_sum, back[1], embeds_line)
     n_plane = n_side * n_side
     pieces = exchange(partial.reshape(n_plane, -1, width), PLANE)
     spread = sum_spread([pieces], n_z * 2, BF16)

time: 97.6 us -> 96.3 us (0.987)
  waiting for transfers between devices: 9.83 us -> 12 us
  blocking collectives: 22.6 us -> 20.8 us
  starting transfers between devices: 46.7 us -> 45 us
    ppermute x14, waiting for transfers between devices: 6.78 us -> 8.73 us  [move(): return lax.ppermute(array, ALL, perm)]
    ppermute x14, starting transfers between devices: 21.4 us -> 19.6 us  [move(): return lax.ppermute(array, ALL, perm)]
    all_to_all x2, blocking collectives: 22.6 us -> 20.8 us  [exchange(): return lax.all_to_all(array, axes, split_axis=0, concat_axis=0, tiled=True)]
  transfers between devices with their start and end apart: 21 -> 21, of which waited for: 6 -> 8; matrix products, arithmetic and copies ran while one was open for 0% -> 0% of each run, Pallas kernels for 12% -> 12%
where the time goes in v14:
time: 96.3 us; the launch traced here: 95 us
  starting transfers between devices  45 us (47%)
  blocking collectives  20.8 us (22%)
  Pallas kernels  15.4 us (16%)
  waiting for transfers between devices  12 us (12%)
    all_to_all x2, blocking collectives, exchange(): return lax.all_to_all(array, axes, split_axis=0, concat_axis=0, tiled=True)  20.8 us
    ppermute x14, starting transfers between devices, move(): return lax.ppermute(array, ALL, perm)  19.6 us
    ppermute x6, starting transfers between devices, ring(): lax.ppermute(array, axis, [(i, (i + shift) % size) for i in range(size)])  18.5 us
    pallas_call x6, Pallas kernels, tile(): pl.pallas_call(functools.partial(tile_kernel, 256, 256, start is not None...  11.2 us
    ppermute x14, waiting for transfers between devices, move(): return lax.ppermute(array, ALL, perm)  8.73 us
    all_to_all x1, starting transfers between devices, exchange(): return lax.all_to_all(array, axes, split_axis=0, concat_axis=0, tiled=True)  6.93 us
    all_to_all x1, waiting for transfers between devices, exchange(): return lax.all_to_all(array, axes, split_axis=0, concat_axis=0, tiled=True)  2.99 us
  transfers between devices with their start and end apart: 21, of which 8 were waited for; matrix products, arithmetic and copies ran while one was open for 0% of the time, Pallas kernels for 12%

profile of v14, /device:TPU:1, one launch (start us, length us, event | category | flops | bytes accessed | tf_op | source)
XLA Modules:
  0.0 95.0 jit_solution(12579686487354437365)
XLA Ops:
  0.6 1.5 %pack.1 = (bf16[128,384]{1,0:T(8,128)(2,1)S(1)}, bf16[128,640]{1,0:T(8,128)(2,1)S(1)}) custom-call(bf16[128,512]{1,0:T(8,128)(2,1)} %embeds.1, bf16[512,256]{1,0:T(8,128)(2,1)} %weight.3, f32[1,128]{1,0:T(1,128)} %bitcast.9, f32[15,128]{1,0:T(8,128)} %bitcast.7, f32[15,128]{1,0:T(8,128)} %bitcast.8), custom_call_target="tpu_custom_call" | custom-call | tf_op jit(solution)/shard_map/pack/pallas_call | solution.py:229
  2.2 0.0 copy-start.1
  2.2 7.8 %collective-permute-start = (bf16[128,384]{1,0:T(8,128)(2,1)S(1)}, bf16[128,384]{1,0:T(8,128)(2,1)S(1)}, u32[]{:S(2)}, u32[]{:S(2)}) collective-permute-start(bf16[128,384]{1,0:T(8,128)(2,1)S(1)} %get-tuple-element.32), channel_id=1, source_target_pairs={{0,32},{4,36},{8,40},{12,44},{32,0},{36,4},{40,8},{44,12},{1,33},{... | collective-permute-start | bytes 294920 | tf_op jit(solution)/shard_map/ppermute | solution.py:200
  10.0 1.2 %collective-permute-start.5 = (bf16[128,640]{1,0:T(8,128)(2,1)S(1)}, bf16[128,640]{1,0:T(8,128)(2,1)S(1)}, u32[]{:S(2)}, u32[]{:S(2)}) collective-permute-start(bf16[128,640]{1,0:T(8,128)(2,1)S(1)} %get-tuple-element.33.refs_0_), channel_id=1, source_target_pairs={{0,64},{1,65},{2,66},{3,67},{4,68},{5,69},{6,70},{7,71},{8,72},{9,... | collective-permute-start | bytes 491528 | tf_op jit(solution)/shard_map/ppermute | solution.py:215
  11.2 2.5 %collective-permute-start.4 = (bf16[128,640]{1,0:T(8,128)(2,1)S(1)}, bf16[128,640]{1,0:T(8,128)(2,1)S(1)}, u32[]{:S(2)}, u32[]{:S(2)}) collective-permute-start(bf16[128,640]{1,0:T(8,128)(2,1)S(1)} %get-tuple-element.33.refs_0_), channel_id=1, source_target_pairs={{0,128},{1,129},{2,130},{3,131},{4,132},{5,133},{6,134},{7,135},{8... | collective-permute-start | bytes 491528 | tf_op jit(solution)/shard_map/ppermute | solution.py:215
  13.7 1.2 %collective-permute-start.3 = (bf16[128,640]{1,0:T(8,128)(2,1)S(1)}, bf16[128,640]{1,0:T(8,128)(2,1)S(1)}, u32[]{:S(2)}, u32[]{:S(2)}) collective-permute-start(bf16[128,640]{1,0:T(8,128)(2,1)S(1)} %get-tuple-element.33.refs_0_), channel_id=1, source_target_pairs={{0,192},{1,193},{2,194},{3,195},{4,196},{5,197},{6,198},{7,199},{8... | collective-permute-start | bytes 491528 | tf_op jit(solution)/shard_map/ppermute | solution.py:215
  14.8 2.0 %collective-permute-start.1 = (bf16[128,384]{1,0:T(8,128)(2,1)S(1)}, bf16[128,384]{1,0:T(8,128)(2,1)S(1)}, u32[]{:S(2)}, u32[]{:S(2)}) collective-permute-start(bf16[128,384]{1,0:T(8,128)(2,1)S(1)} %get-tuple-element.32), channel_id=1, source_target_pairs={{0,16},{16,0},{1,17},{17,1},{2,18},{18,2},{3,19},{19,3},{4,20},{20... | collective-permute-start | bytes 294920 | tf_op jit(solution)/shard_map/ppermute | solution.py:200
  16.8 0.0 collective-permute-start.2
  16.8 1.6 %collective-permute-done.4.refs_2_ = bf16[128,640]{1,0:T(8,128)(2,1)S(1)} collective-permute-done((bf16[128,640]{1,0:T(8,128)(2,1)S(1)}, bf16[128,640]{1,0:T(8,128)(2,1)S(1)}, u32[]{:S(2)}, u32[]{:S(2)}) %collective-permute-start.4) | collective-permute-done | bytes 163872 | tf_op jit(solution)/shard_map/ppermute | solution.py:215
  18.4 0.3 split.1
  18.8 0.0 collective-permute-done.1
  18.8 0.0 copy-start
  18.8 1.0 %collective-permute-start.6 = (bf16[512,384]{1,0:T(8,128)(2,1)S(1)}, bf16[512,384]{1,0:T(8,128)(2,1)S(1)}, u32[]{:S(2)}, u32[]{:S(2)}) collective-permute-start(bf16[512,384]{1,0:T(8,128)(2,1)S(1)} %pad_maximum_fusion.refs_0_), channel_id=1, source_target_pairs={{0,4},{1,5},{2,6},{3,7},{4,8},{5,9},{6,10},{7,11},{8,12},{9,13},{1... | collective-permute-start | bytes 1179656 | tf_op jit(solution)/shard_map/ppermute | solution.py:215
  19.9 1.3 %collective-permute-start.11 = (bf16[640,256]{1,0:T(8,128)(2,1)S(1)}, bf16[640,256]{1,0:T(8,128)(2,1)S(1)}, u32[]{:S(2)}, u32[]{:S(2)}) collective-permute-start(bf16[640,256]{1,0:T(8,128)(2,1)S(1)} %get-tuple-element.38.rows_ref), channel_id=1, source_target_pairs={{0,1},{1,2},{2,3},{3,0},{4,5},{5,6},{6,7},{7,4},{8,9},{9,10},{10,1... | collective-permute-start | bytes 983048 | tf_op jit(solution)/shard_map/ppermute | solution.py:215
  21.2 2.6 %collective-permute-start.10 = (bf16[640,256]{1,0:T(8,128)(2,1)S(1)}, bf16[640,256]{1,0:T(8,128)(2,1)S(1)}, u32[]{:S(2)}, u32[]{:S(2)}) collective-permute-start(bf16[640,256]{1,0:T(8,128)(2,1)S(1)} %get-tuple-element.38.rows_ref), channel_id=1, source_target_pairs={{0,2},{1,3},{2,0},{3,1},{4,6},{5,7},{6,4},{7,5},{8,10},{9,11},{10,... | collective-permute-start | bytes 983048 | tf_op jit(solution)/shard_map/ppermute | solution.py:215
  23.8 1.1 %collective-permute-start.9 = (bf16[640,256]{1,0:T(8,128)(2,1)S(1)}, bf16[640,256]{1,0:T(8,128)(2,1)S(1)}, u32[]{:S(2)}, u32[]{:S(2)}) collective-permute-start(bf16[640,256]{1,0:T(8,128)(2,1)S(1)} %get-tuple-element.38.rows_ref), channel_id=1, source_target_pairs={{0,3},{1,0},{2,1},{3,2},{4,7},{5,4},{6,5},{7,6},{8,11},{9,8},{10,9... | collective-permute-start | bytes 983048 | tf_op jit(solution)/shard_map/ppermute | solution.py:215
  24.9 2.3 %collective-permute-start.8 = (bf16[256,384]{1,0:T(8,128)(2,1)S(1)}, bf16[256,384]{1,0:T(8,128)(2,1)S(1)}, u32[]{:S(2)}, u32[]{:S(2)}) collective-permute-start(bf16[256,384]{1,0:T(8,128)(2,1)S(1)} %pad_maximum_fusion.1), channel_id=1, source_target_pairs={{0,8},{1,9},{2,10},{3,11},{4,12},{5,13},{6,14},{7,15},{8,32},{9,33... | collective-permute-start | bytes 589832 | tf_op jit(solution)/shard_map/ppermute | solution.py:215
  27.2 3.1 %collective-permute-start.7 = (bf16[256,384]{1,0:T(8,128)(2,1)S(1)}, bf16[256,384]{1,0:T(8,128)(2,1)S(1)}, u32[]{:S(2)}, u32[]{:S(2)}) collective-permute-start(bf16[256,384]{1,0:T(8,128)(2,1)S(1)} %get-tuple-element.63), channel_id=1, source_target_pairs={{0,16},{16,0},{1,17},{17,1},{2,18},{18,2},{3,19},{19,3},{4,20},{20... | collective-permute-start | bytes 589832 | tf_op jit(solution)/shard_map/ppermute | solution.py:200
  30.4 0.0 collective-permute-done.11.rows_ref
  30.4 1.5 %tile.6.refs_0_ = f32[512,256]{1,0:T(8,128)S(1)} custom-call(bf16[2,128,128]{2,1,0:T(8,128)(2,1)S(1)} %copy-done, bf16[640,256]{1,0:T(8,128)(2,1)S(1)} %collective-permute-done.11.rows_ref, bf16[512,384]{1,0:T(8,128)(2,1)S(1)} %pad_maximum_fusion.refs_0_, bf16[512,384]{1,0:T(8,128)(2,1)S(1)} %collective-permute-done.6.refs_1_), custom_call_target="tpu_custom_call" | custom-call | tf_op jit(solution)/shard_map/tile/pallas_call | solution.py:270
  31.9 0.7 collective-permute-done.8.refs_3_.refs_2_
  32.6 5.3 %collective-permute-start.12 = (bf16[256,384]{1,0:T(8,128)(2,1)S(1)}, bf16[256,384]{1,0:T(8,128)(2,1)S(1)}, u32[]{:S(2)}, u32[]{:S(2)}) collective-permute-start(bf16[256,384]{1,0:T(8,128)(2,1)S(1)} %get-tuple-element.43), channel_id=1, source_target_pairs={{0,16},{16,0},{1,17},{17,1},{2,18},{18,2},{3,19},{19,3},{4,20},{20... | collective-permute-start | bytes 589832 | tf_op jit(solution)/shard_map/ppermute | solution.py:200
  37.9 0.3 collective-permute-start.13
  38.2 0.9 tile.9.refs_0_
  39.1 0.3 collective-permute-done.13.refs_5_.refs_2_
  39.4 0.9 tile.10
  40.2 2.4 %collective-permute-start.15 = (bf16[512,256]{1,0:T(8,128)(2,1)S(1)}, bf16[512,256]{1,0:T(8,128)(2,1)S(1)}, u32[]{:S(2)}, u32[]{:S(2)}) collective-permute-start(bf16[512,256]{1,0:T(8,128)(2,1)S(1)} %tile.10), channel_id=1, source_target_pairs={{0,3},{1,0},{2,1},{3,2},{4,7},{5,4},{6,5},{7,6},{8,11},{9,8},{10,9... | collective-permute-start | bytes 786440 | tf_op jit(solution)/shard_map/ppermute | solution.py:215
  42.6 2.7 %tile.8 = bf16[512,256]{1,0:T(8,128)(2,1)S(1)} custom-call(bf16[2,128,128]{2,1,0:T(8,128)(2,1)S(1)} %copy-done, bf16[640,256]{1,0:T(8,128)(2,1)S(1)} %collective-permute-done.10.rows_ref, bf16[512,384]{1,0:T(8,128)(2,1)S(1)} %pad_maximum_fusion.refs_0_, bf16[512,384]{1,0:T(8,128)(2,1)S(1)} %collective-permute-done.6.refs_1_, ...), custom_call_target="tpu_custom_call" | custom-call | tf_op jit(solution)/shard_map/tile/pallas_call | solution.py:270
  45.3 0.7 collective-permute-start.14
  45.9 2.7 %tile.11 = bf16[512,256]{1,0:T(8,128)(2,1)S(1)} custom-call(bf16[2,128,128]{2,1,0:T(8,128)(2,1)S(1)} %copy-done, bf16[640,256]{1,0:T(8,128)(2,1)S(1)} %collective-permute-done.9.rows_ref, bf16[512,384]{1,0:T(8,128)(2,1)S(1)} %pad_maximum_fusion.refs_0_, bf16[512,384]{1,0:T(8,128)(2,1)S(1)} %collective-permute-done.6.refs_1_, ...), custom_call_target="tpu_custom_call" | custom-call | tf_op jit(solution)/shard_map/tile/pallas_call | solution.py:270
  48.6 0.6 collective-permute-start.16
  49.2 2.7 %tile.7.a = f32[512,256]{1,0:T(8,128)S(1)} custom-call(bf16[2,128,128]{2,1,0:T(8,128)(2,1)S(1)} %copy-done, bf16[640,256]{1,0:T(8,128)(2,1)S(1)} %get-tuple-element.38.rows_ref, bf16[512,384]{1,0:T(8,128)(2,1)S(1)} %pad_maximum_fusion.refs_0_, bf16[512,384]{1,0:T(8,128)(2,1)S(1)} %collective-permute-done.6.refs_1_, ...), custom_call_target="tpu_custom_call" | custom-call | tf_op jit(solution)/shard_map/tile/pallas_call | solution.py:270
  51.9 0.2 collective-permute-done.14.b
  52.1 0.5 sum_rows.1
  52.6 3.1 %collective-permute-done.16.last = bf16[512,256]{1,0:T(8,128)(2,1)S(1)} collective-permute-done((bf16[512,256]{1,0:T(8,128)(2,1)S(1)}, bf16[512,256]{1,0:T(8,128)(2,1)S(1)}, u32[]{:S(2)}, u32[]{:S(2)}) %collective-permute-start.16) | collective-permute-done | bytes 262176 | tf_op jit(solution)/shard_map/ppermute | solution.py:215
  55.7 0.3 last_rows.1
  56.0 10.1 %all_to_all.15.refs_0_ = bf16[16,32,256]{2,1,0:T(8,128)(2,1)S(1)} all-to-all(bf16[16,32,256]{2,1,0:T(8,128)(2,1)S(1)} %bitcast.5), channel_id=1, replica_groups=mesh['y'=4,'zh'=2,'core'=2,'zl'=4,'x'=4] {'y','x'}, dimensions={0} | all-to-all | bytes 524288 | tf_op jit(solution)/shard_map/all_to_all | solution.py:223
  66.1 0.8 sum_spread.2
  66.9 6.9 %all-to-all-start.1 = ((bf16[16,32,256]{2,1,0:T(8,128)(2,1)}), bf16[16,32,256]{2,1,0:T(8,128)(2,1)S(1)}, u32[]{:S(2)}, u32[]{:S(2)}) async-start(bf16[16,32,256]{2,1,0:T(8,128)(2,1)} %sum_spread.2), calls=%async_computation.1 | async-start | bytes 524288 | tf_op jit(solution)/shard_map/all_to_all | solution.py:223
  73.8 0.3 collective-permute-start.17
  74.1 1.4 %collective-permute-start.18 = (bf16[128,256]{1,0:T(8,128)(2,1)S(1)}, bf16[128,256]{1,0:T(8,128)(2,1)S(1)}, u32[]{:S(2)}, u32[]{:S(2)}) collective-permute-start(bf16[128,256]{1,0:T(8,128)(2,1)S(1)} %get-tuple-element.58), channel_id=1, source_target_pairs={{0,128},{1,129},{2,130},{3,131},{4,132},{5,133},{6,134},{7,135},{8... | collective-permute-start | bytes 196616 | tf_op jit(solution)/shard_map/ppermute | solution.py:215
  75.5 1.1 %collective-permute-start.19 = (bf16[128,256]{1,0:T(8,128)(2,1)S(1)}, bf16[128,256]{1,0:T(8,128)(2,1)S(1)}, u32[]{:S(2)}, u32[]{:S(2)}) collective-permute-start(bf16[128,256]{1,0:T(8,128)(2,1)S(1)} %get-tuple-element.59), channel_id=1, source_target_pairs={{0,192},{1,193},{2,194},{3,195},{4,196},{5,197},{6,198},{7,199},{8... | collective-permute-start | bytes 196616 | tf_op jit(solution)/shard_map/ppermute | solution.py:215
  76.6 2.5 %collective-permute-done.17.b = bf16[128,256]{1,0:T(8,128)(2,1)S(1)} collective-permute-done((bf16[128,256]{1,0:T(8,128)(2,1)S(1)}, bf16[128,256]{1,0:T(8,128)(2,1)S(1)}, u32[]{:S(2)}, u32[]{:S(2)}) %collective-permute-start.17) | collective-permute-done | bytes 65568 | tf_op jit(solution)/shard_map/ppermute | solution.py:215
  79.2 0.6 collective-permute-done.19.d
  79.7 0.7 finish_rows.1
  80.4 3.0 %all-to-all-done.1.refs_0_ = bf16[16,32,256]{2,1,0:T(8,128)(2,1)S(1)} async-done(((bf16[16,32,256]{2,1,0:T(8,128)(2,1)}), bf16[16,32,256]{2,1,0:T(8,128)(2,1)S(1)}, u32[]{:S(2)}, u32[]{:S(2)}) %all-to-all-start.1) | async-done | bytes 262176 | tf_op jit(solution)/shard_map/all_to_all | solution.py:223
  83.5 10.7 %all_to_all.16 = bf16[16,32,256]{2,1,0:T(8,128)(2,1)S(1)} all-to-all(bf16[16,32,256]{2,1,0:T(8,128)(2,1)S(1)} %sum_spread.3), channel_id=1, replica_groups=mesh['y'=4,'zh'=2,'core'=2,'zl'=4,'x'=4] {'y','x'}, dimensions={0} | all-to-all | bytes 524288 | tf_op jit(solution)/shard_map/all_to_all | solution.py:223
  94.2 0.8 convert_multiply_fusion
  (17 shorter events, 0.2 us)
Async XLA Ops:
  2.2 16.3 %copy-start.1 = (bf16[512,256]{1,0:T(8,128)(2,1)S(1)}, bf16[512,256]{1,0:T(8,128)(2,1)}, u32[]{:S(2)}) copy-start(bf16[512,256]{1,0:T(8,128)(2,1)} %weight.3) | copy-start | bytes 786436
  2.2 14.6 %collective-permute-start = (bf16[128,384]{1,0:T(8,128)(2,1)S(1)}, bf16[128,384]{1,0:T(8,128)(2,1)S(1)}, u32[]{:S(2)}, u32[]{:S(2)}) collective-permute-start(bf16[128,384]{1,0:T(8,128)(2,1)S(1)} %get-tuple-element.32), channel_id=1, source_target_pairs={{0,32},{4,36},{8,40},{12,44},{32,0},{36,4},{40,8},{44,12},{1,33},{... | collective-permute-start | bytes 294920 | tf_op jit(solution)/shard_map/ppermute | solution.py:200
  10.0 6.8 %collective-permute-start.5 = (bf16[128,640]{1,0:T(8,128)(2,1)S(1)}, bf16[128,640]{1,0:T(8,128)(2,1)S(1)}, u32[]{:S(2)}, u32[]{:S(2)}) collective-permute-start(bf16[128,640]{1,0:T(8,128)(2,1)S(1)} %get-tuple-element.33.refs_0_), channel_id=1, source_target_pairs={{0,64},{1,65},{2,66},{3,67},{4,68},{5,69},{6,70},{7,71},{8,72},{9,... | collective-permute-start | bytes 491528 | tf_op jit(solution)/shard_map/ppermute | solution.py:215
  11.2 7.2 %collective-permute-start.4 = (bf16[128,640]{1,0:T(8,128)(2,1)S(1)}, bf16[128,640]{1,0:T(8,128)(2,1)S(1)}, u32[]{:S(2)}, u32[]{:S(2)}) collective-permute-start(bf16[128,640]{1,0:T(8,128)(2,1)S(1)} %get-tuple-element.33.refs_0_), channel_id=1, source_target_pairs={{0,128},{1,129},{2,130},{3,131},{4,132},{5,133},{6,134},{7,135},{8... | collective-permute-start | bytes 491528 | tf_op jit(solution)/shard_map/ppermute | solution.py:215
  13.7 4.8 %collective-permute-start.3 = (bf16[128,640]{1,0:T(8,128)(2,1)S(1)}, bf16[128,640]{1,0:T(8,128)(2,1)S(1)}, u32[]{:S(2)}, u32[]{:S(2)}) collective-permute-start(bf16[128,640]{1,0:T(8,128)(2,1)S(1)} %get-tuple-element.33.refs_0_), channel_id=1, source_target_pairs={{0,192},{1,193},{2,194},{3,195},{4,196},{5,197},{6,198},{7,199},{8... | collective-permute-start | bytes 491528 | tf_op jit(solution)/shard_map/ppermute | solution.py:215
  14.8 3.9 %collective-permute-start.1 = (bf16[128,384]{1,0:T(8,128)(2,1)S(1)}, bf16[128,384]{1,0:T(8,128)(2,1)S(1)}, u32[]{:S(2)}, u32[]{:S(2)}) collective-permute-start(bf16[128,384]{1,0:T(8,128)(2,1)S(1)} %get-tuple-element.32), channel_id=1, source_target_pairs={{0,16},{16,0},{1,17},{17,1},{2,18},{18,2},{3,19},{19,3},{4,20},{20... | collective-permute-start | bytes 294920 | tf_op jit(solution)/shard_map/ppermute | solution.py:200
  16.8 2.0 %collective-permute-start.2 = (bf16[128,384]{1,0:T(8,128)(2,1)S(1)}, bf16[128,384]{1,0:T(8,128)(2,1)S(1)}, u32[]{:S(2)}, u32[]{:S(2)}) collective-permute-start(bf16[128,384]{1,0:T(8,128)(2,1)S(1)} %collective-permute-done), channel_id=1, source_target_pairs={{0,16},{16,0},{1,17},{17,1},{2,18},{18,2},{3,19},{19,3},{4,20},{20... | collective-permute-start | bytes 294920 | tf_op jit(solution)/shard_map/ppermute | solution.py:200
  18.8 11.5 %copy-start = (bf16[2,128,128]{2,1,0:T(8,128)(2,1)S(1)}, bf16[2,128,128]{2,1,0:T(8,128)(2,1)}, u32[]{:S(2)}) copy-start(bf16[2,128,128]{2,1,0:T(8,128)(2,1)} %constant.4.clone.table) | copy-start | bytes 196612
  18.8 8.4 %collective-permute-start.6 = (bf16[512,384]{1,0:T(8,128)(2,1)S(1)}, bf16[512,384]{1,0:T(8,128)(2,1)S(1)}, u32[]{:S(2)}, u32[]{:S(2)}) collective-permute-start(bf16[512,384]{1,0:T(8,128)(2,1)S(1)} %pad_maximum_fusion.refs_0_), channel_id=1, source_target_pairs={{0,4},{1,5},{2,6},{3,7},{4,8},{5,9},{6,10},{7,11},{8,12},{9,13},{1... | collective-permute-start | bytes 1179656 | tf_op jit(solution)/shard_map/ppermute | solution.py:215
  19.9 10.5 %collective-permute-start.11 = (bf16[640,256]{1,0:T(8,128)(2,1)S(1)}, bf16[640,256]{1,0:T(8,128)(2,1)S(1)}, u32[]{:S(2)}, u32[]{:S(2)}) collective-permute-start(bf16[640,256]{1,0:T(8,128)(2,1)S(1)} %get-tuple-element.38.rows_ref), channel_id=1, source_target_pairs={{0,1},{1,2},{2,3},{3,0},{4,5},{5,6},{6,7},{7,4},{8,9},{9,10},{10,1... | collective-permute-start | bytes 983048 | tf_op jit(solution)/shard_map/ppermute | solution.py:215
  21.2 11.4 %collective-permute-start.10 = (bf16[640,256]{1,0:T(8,128)(2,1)S(1)}, bf16[640,256]{1,0:T(8,128)(2,1)S(1)}, u32[]{:S(2)}, u32[]{:S(2)}) collective-permute-start(bf16[640,256]{1,0:T(8,128)(2,1)S(1)} %get-tuple-element.38.rows_ref), channel_id=1, source_target_pairs={{0,2},{1,3},{2,0},{3,1},{4,6},{5,7},{6,4},{7,5},{8,10},{9,11},{10,... | collective-permute-start | bytes 983048 | tf_op jit(solution)/shard_map/ppermute | solution.py:215
  23.8 8.8 %collective-permute-start.9 = (bf16[640,256]{1,0:T(8,128)(2,1)S(1)}, bf16[640,256]{1,0:T(8,128)(2,1)S(1)}, u32[]{:S(2)}, u32[]{:S(2)}) collective-permute-start(bf16[640,256]{1,0:T(8,128)(2,1)S(1)} %get-tuple-element.38.rows_ref), channel_id=1, source_target_pairs={{0,3},{1,0},{2,1},{3,2},{4,7},{5,4},{6,5},{7,6},{8,11},{9,8},{10,9... | collective-permute-start | bytes 983048 | tf_op jit(solution)/shard_map/ppermute | solution.py:215
  24.9 7.7 %collective-permute-start.8 = (bf16[256,384]{1,0:T(8,128)(2,1)S(1)}, bf16[256,384]{1,0:T(8,128)(2,1)S(1)}, u32[]{:S(2)}, u32[]{:S(2)}) collective-permute-start(bf16[256,384]{1,0:T(8,128)(2,1)S(1)} %pad_maximum_fusion.1), channel_id=1, source_target_pairs={{0,8},{1,9},{2,10},{3,11},{4,12},{5,13},{6,14},{7,15},{8,32},{9,33... | collective-permute-start | bytes 589832 | tf_op jit(solution)/shard_map/ppermute | solution.py:215
  27.2 5.4 %collective-permute-start.7 = (bf16[256,384]{1,0:T(8,128)(2,1)S(1)}, bf16[256,384]{1,0:T(8,128)(2,1)S(1)}, u32[]{:S(2)}, u32[]{:S(2)}) collective-permute-start(bf16[256,384]{1,0:T(8,128)(2,1)S(1)} %get-tuple-element.63), channel_id=1, source_target_pairs={{0,16},{16,0},{1,17},{17,1},{2,18},{18,2},{3,19},{19,3},{4,20},{20... | collective-permute-start | bytes 589832 | tf_op jit(solution)/shard_map/ppermute | solution.py:200
  32.6 6.4 %collective-permute-start.12 = (bf16[256,384]{1,0:T(8,128)(2,1)S(1)}, bf16[256,384]{1,0:T(8,128)(2,1)S(1)}, u32[]{:S(2)}, u32[]{:S(2)}) collective-permute-start(bf16[256,384]{1,0:T(8,128)(2,1)S(1)} %get-tuple-element.43), channel_id=1, source_target_pairs={{0,16},{16,0},{1,17},{17,1},{2,18},{18,2},{3,19},{19,3},{4,20},{20... | collective-permute-start | bytes 589832 | tf_op jit(solution)/shard_map/ppermute | solution.py:200
  37.9 1.4 %collective-permute-start.13 = (bf16[256,384]{1,0:T(8,128)(2,1)S(1)}, bf16[256,384]{1,0:T(8,128)(2,1)S(1)}, u32[]{:S(2)}, u32[]{:S(2)}) collective-permute-start(bf16[256,384]{1,0:T(8,128)(2,1)S(1)} %collective-permute-done.8.refs_3_.refs_2_), channel_id=1, source_target_pairs={{0,16},{16,0},{1,17},{17,1},{2,18},{18,2},{3,19},{19,3},{4,20},{20... | collective-permute-start | bytes 589832 | tf_op jit(solution)/shard_map/ppermute | solution.py:200
  40.2 11.7 %collective-permute-start.15 = (bf16[512,256]{1,0:T(8,128)(2,1)S(1)}, bf16[512,256]{1,0:T(8,128)(2,1)S(1)}, u32[]{:S(2)}, u32[]{:S(2)}) collective-permute-start(bf16[512,256]{1,0:T(8,128)(2,1)S(1)} %tile.10), channel_id=1, source_target_pairs={{0,3},{1,0},{2,1},{3,2},{4,7},{5,4},{6,5},{7,6},{8,11},{9,8},{10,9... | collective-permute-start | bytes 786440 | tf_op jit(solution)/shard_map/ppermute | solution.py:215
  45.3 6.8 %collective-permute-start.14 = (bf16[512,256]{1,0:T(8,128)(2,1)S(1)}, bf16[512,256]{1,0:T(8,128)(2,1)S(1)}, u32[]{:S(2)}, u32[]{:S(2)}) collective-permute-start(bf16[512,256]{1,0:T(8,128)(2,1)S(1)} %tile.8), channel_id=1, source_target_pairs={{0,2},{1,3},{2,0},{3,1},{4,6},{5,7},{6,4},{7,5},{8,10},{9,11},{10,... | collective-permute-start | bytes 786440 | tf_op jit(solution)/shard_map/ppermute | solution.py:215
  48.6 7.0 %collective-permute-start.16 = (bf16[512,256]{1,0:T(8,128)(2,1)S(1)}, bf16[512,256]{1,0:T(8,128)(2,1)S(1)}, u32[]{:S(2)}, u32[]{:S(2)}) collective-permute-start(bf16[512,256]{1,0:T(8,128)(2,1)S(1)} %tile.11), channel_id=1, source_target_pairs={{0,1},{1,2},{2,3},{3,0},{4,5},{5,6},{6,7},{7,4},{8,9},{9,10},{10,1... | collective-permute-start | bytes 786440 | tf_op jit(solution)/shard_map/ppermute | solution.py:215
  66.9 16.5 %all-to-all-start.1 = ((bf16[16,32,256]{2,1,0:T(8,128)(2,1)}), bf16[16,32,256]{2,1,0:T(8,128)(2,1)S(1)}, u32[]{:S(2)}, u32[]{:S(2)}) async-start(bf16[16,32,256]{2,1,0:T(8,128)(2,1)} %sum_spread.2), calls=%async_computation.1 | async-start | bytes 524288 | tf_op jit(solution)/shard_map/all_to_all | solution.py:223
  73.8 5.3 %collective-permute-start.17 = (bf16[128,256]{1,0:T(8,128)(2,1)S(1)}, bf16[128,256]{1,0:T(8,128)(2,1)S(1)}, u32[]{:S(2)}, u32[]{:S(2)}) collective-permute-start(bf16[128,256]{1,0:T(8,128)(2,1)S(1)} %get-tuple-element.57), channel_id=1, source_target_pairs={{0,64},{1,65},{2,66},{3,67},{4,68},{5,69},{6,70},{7,71},{8,72},{9,... | collective-permute-start | bytes 196616 | tf_op jit(solution)/shard_map/ppermute | solution.py:215
  74.1 5.0 %collective-permute-start.18 = (bf16[128,256]{1,0:T(8,128)(2,1)S(1)}, bf16[128,256]{1,0:T(8,128)(2,1)S(1)}, u32[]{:S(2)}, u32[]{:S(2)}) collective-permute-start(bf16[128,256]{1,0:T(8,128)(2,1)S(1)} %get-tuple-element.58), channel_id=1, source_target_pairs={{0,128},{1,129},{2,130},{3,131},{4,132},{5,133},{6,134},{7,135},{8... | collective-permute-start | bytes 196616 | tf_op jit(solution)/shard_map/ppermute | solution.py:215
  75.5 4.2 %collective-permute-start.19 = (bf16[128,256]{1,0:T(8,128)(2,1)S(1)}, bf16[128,256]{1,0:T(8,128)(2,1)S(1)}, u32[]{:S(2)}, u32[]{:S(2)}) collective-permute-start(bf16[128,256]{1,0:T(8,128)(2,1)S(1)} %get-tuple-element.59), channel_id=1, source_target_pairs={{0,192},{1,193},{2,194},{3,195},{4,196},{5,197},{6,198},{7,199},{8... | collective-permute-start | bytes 196616 | tf_op jit(solution)/shard_map/ppermute | solution.py:215

commit v15 on v14

--- a/solution.py
+++ b/solution.py
@@ -277,7 +277,7 @@
         )(table, rows_in, *([] if start is None else [start]), *columns)
 
     first = n_side - 1
-    begin = tile(lines[first], [four, near], F32)
+    begin = {d: tile(lines[d], [four, near], F32) for d in (first, first - 1)}
     halves = [near[: 2 * rows], near[2 * rows :]]
     columns = [four, near, ring(halves[0], "core", 2, 1), far]
     columns, lines, begin, halves = lax.optimization_barrier((columns, lines, begin, halves))
@@ -287,7 +287,9 @@
     back = {}
     for d in range(n_side):
         if d == first:
-            part = tile(lines[d], columns[early:], BF16, tile(lines[d], columns[2:early], F32, begin))
+            part = tile(lines[d], columns[early:], BF16, tile(lines[d], columns[2:early], F32, begin[d]))
+        elif d in begin:
+            part = tile(lines[d], columns[2:], BF16, begin[d])
         else:
             part = tile(lines[d], columns, BF16 if d else F32)
         back[d] = turn(part, sizes, 1, d) if d else part

time: 96.3 us -> 94.8 us (0.984)
  starting transfers between devices: 45 us -> 43.7 us
    ppermute x6, starting transfers between devices: 18.5 us -> 17.4 us  [ring(): lax.ppermute(array, axis, [(i, (i + shift) % size) for i in range(size)])]
    pallas_call x6 -> x7, Pallas kernels: 11.2 us -> 11.5 us  [tile(): pl.pallas_call(functools.partial(tile_kernel, 256, 256, start is not None...]
  transfers between devices with their start and end apart: 21 -> 21, of which waited for: 8 -> 8; matrix products, arithmetic and copies ran while one was open for 0% -> 0% of each run, Pallas kernels for 12% -> 13%
where the time goes in v15:
time: 94.8 us; the launch traced here: 93.5 us
  starting transfers between devices  43.7 us (46%)
  blocking collectives  20.8 us (22%)
  Pallas kernels  15.7 us (17%)
  waiting for transfers between devices  11.5 us (12%)
    all_to_all x2, blocking collectives, exchange(): return lax.all_to_all(array, axes, split_axis=0, concat_axis=0, tiled=True)  20.8 us
    ppermute x14, starting transfers between devices, move(): return lax.ppermute(array, ALL, perm)  19.4 us
    ppermute x6, starting transfers between devices, ring(): lax.ppermute(array, axis, [(i, (i + shift) % size) for i in range(size)])  17.4 us
    pallas_call x7, Pallas kernels, tile(): pl.pallas_call(functools.partial(tile_kernel, 256, 256, start is not None...  11.5 us
    ppermute x14, waiting for transfers between devices, move(): return lax.ppermute(array, ALL, perm)  8.18 us
    all_to_all x1, starting transfers between devices, exchange(): return lax.all_to_all(array, axes, split_axis=0, concat_axis=0, tiled=True)  6.93 us
    all_to_all x1, waiting for transfers between devices, exchange(): return lax.all_to_all(array, axes, split_axis=0, concat_axis=0, tiled=True)  2.99 us
  transfers between devices with their start and end apart: 21, of which 8 were waited for; matrix products, arithmetic and copies ran while one was open for 0% of the time, Pallas kernels for 13%

profile of v15, /device:TPU:1, one launch (start us, length us, event | category | flops | bytes accessed | tf_op | source)
XLA Modules:
  0.0 93.5 jit_solution(16473598705826628835)
XLA Ops:
  0.6 1.5 %pack.1 = (bf16[128,384]{1,0:T(8,128)(2,1)S(1)}, bf16[128,640]{1,0:T(8,128)(2,1)S(1)}) custom-call(bf16[128,512]{1,0:T(8,128)(2,1)} %embeds.1, bf16[512,256]{1,0:T(8,128)(2,1)} %weight.3, f32[1,128]{1,0:T(1,128)} %bitcast.9, f32[15,128]{1,0:T(8,128)} %bitcast.7, f32[15,128]{1,0:T(8,128)} %bitcast.8), custom_call_target="tpu_custom_call" | custom-call | tf_op jit(solution)/shard_map/pack/pallas_call | solution.py:229
  2.2 0.0 copy-start.1
  2.2 7.8 %collective-permute-start = (bf16[128,384]{1,0:T(8,128)(2,1)S(1)}, bf16[128,384]{1,0:T(8,128)(2,1)S(1)}, u32[]{:S(2)}, u32[]{:S(2)}) collective-permute-start(bf16[128,384]{1,0:T(8,128)(2,1)S(1)} %get-tuple-element.33), channel_id=1, source_target_pairs={{0,32},{4,36},{8,40},{12,44},{32,0},{36,4},{40,8},{44,12},{1,33},{... | collective-permute-start | bytes 294920 | tf_op jit(solution)/shard_map/ppermute | solution.py:200
  10.0 1.2 %collective-permute-start.5 = (bf16[128,640]{1,0:T(8,128)(2,1)S(1)}, bf16[128,640]{1,0:T(8,128)(2,1)S(1)}, u32[]{:S(2)}, u32[]{:S(2)}) collective-permute-start(bf16[128,640]{1,0:T(8,128)(2,1)S(1)} %get-tuple-element.34.refs_0_), channel_id=1, source_target_pairs={{0,64},{1,65},{2,66},{3,67},{4,68},{5,69},{6,70},{7,71},{8,72},{9,... | collective-permute-start | bytes 491528 | tf_op jit(solution)/shard_map/ppermute | solution.py:215
  11.2 2.5 %collective-permute-start.4 = (bf16[128,640]{1,0:T(8,128)(2,1)S(1)}, bf16[128,640]{1,0:T(8,128)(2,1)S(1)}, u32[]{:S(2)}, u32[]{:S(2)}) collective-permute-start(bf16[128,640]{1,0:T(8,128)(2,1)S(1)} %get-tuple-element.34.refs_0_), channel_id=1, source_target_pairs={{0,128},{1,129},{2,130},{3,131},{4,132},{5,133},{6,134},{7,135},{8... | collective-permute-start | bytes 491528 | tf_op jit(solution)/shard_map/ppermute | solution.py:215
  13.7 1.2 %collective-permute-start.3 = (bf16[128,640]{1,0:T(8,128)(2,1)S(1)}, bf16[128,640]{1,0:T(8,128)(2,1)S(1)}, u32[]{:S(2)}, u32[]{:S(2)}) collective-permute-start(bf16[128,640]{1,0:T(8,128)(2,1)S(1)} %get-tuple-element.34.refs_0_), channel_id=1, source_target_pairs={{0,192},{1,193},{2,194},{3,195},{4,196},{5,197},{6,198},{7,199},{8... | collective-permute-start | bytes 491528 | tf_op jit(solution)/shard_map/ppermute | solution.py:215
  14.8 2.0 %collective-permute-start.1 = (bf16[128,384]{1,0:T(8,128)(2,1)S(1)}, bf16[128,384]{1,0:T(8,128)(2,1)S(1)}, u32[]{:S(2)}, u32[]{:S(2)}) collective-permute-start(bf16[128,384]{1,0:T(8,128)(2,1)S(1)} %get-tuple-element.33), channel_id=1, source_target_pairs={{0,16},{16,0},{1,17},{17,1},{2,18},{18,2},{3,19},{19,3},{4,20},{20... | collective-permute-start | bytes 294920 | tf_op jit(solution)/shard_map/ppermute | solution.py:200
  16.8 0.0 collective-permute-start.2
  16.8 1.6 %collective-permute-done.4.refs_2_ = bf16[128,640]{1,0:T(8,128)(2,1)S(1)} collective-permute-done((bf16[128,640]{1,0:T(8,128)(2,1)S(1)}, bf16[128,640]{1,0:T(8,128)(2,1)S(1)}, u32[]{:S(2)}, u32[]{:S(2)}) %collective-permute-start.4) | collective-permute-done | bytes 163872 | tf_op jit(solution)/shard_map/ppermute | solution.py:215
  18.4 0.3 split.1
  18.8 0.0 collective-permute-done.1
  18.8 0.0 copy-start
  18.8 1.0 %collective-permute-start.6 = (bf16[512,384]{1,0:T(8,128)(2,1)S(1)}, bf16[512,384]{1,0:T(8,128)(2,1)S(1)}, u32[]{:S(2)}, u32[]{:S(2)}) collective-permute-start(bf16[512,384]{1,0:T(8,128)(2,1)S(1)} %pad_maximum_fusion.refs_0_), channel_id=1, source_target_pairs={{0,4},{1,5},{2,6},{3,7},{4,8},{5,9},{6,10},{7,11},{8,12},{9,13},{1... | collective-permute-start | bytes 1179656 | tf_op jit(solution)/shard_map/ppermute | solution.py:215
  19.9 1.3 %collective-permute-start.11 = (bf16[640,256]{1,0:T(8,128)(2,1)S(1)}, bf16[640,256]{1,0:T(8,128)(2,1)S(1)}, u32[]{:S(2)}, u32[]{:S(2)}) collective-permute-start(bf16[640,256]{1,0:T(8,128)(2,1)S(1)} %get-tuple-element.39.rows_ref), channel_id=1, source_target_pairs={{0,1},{1,2},{2,3},{3,0},{4,5},{5,6},{6,7},{7,4},{8,9},{9,10},{10,1... | collective-permute-start | bytes 983048 | tf_op jit(solution)/shard_map/ppermute | solution.py:215
  21.2 2.6 %collective-permute-start.10 = (bf16[640,256]{1,0:T(8,128)(2,1)S(1)}, bf16[640,256]{1,0:T(8,128)(2,1)S(1)}, u32[]{:S(2)}, u32[]{:S(2)}) collective-permute-start(bf16[640,256]{1,0:T(8,128)(2,1)S(1)} %get-tuple-element.39.rows_ref), channel_id=1, source_target_pairs={{0,2},{1,3},{2,0},{3,1},{4,6},{5,7},{6,4},{7,5},{8,10},{9,11},{10,... | collective-permute-start | bytes 983048 | tf_op jit(solution)/shard_map/ppermute | solution.py:215
  23.8 1.1 %collective-permute-start.9 = (bf16[640,256]{1,0:T(8,128)(2,1)S(1)}, bf16[640,256]{1,0:T(8,128)(2,1)S(1)}, u32[]{:S(2)}, u32[]{:S(2)}) collective-permute-start(bf16[640,256]{1,0:T(8,128)(2,1)S(1)} %get-tuple-element.39.rows_ref), channel_id=1, source_target_pairs={{0,3},{1,0},{2,1},{3,2},{4,7},{5,4},{6,5},{7,6},{8,11},{9,8},{10,9... | collective-permute-start | bytes 983048 | tf_op jit(solution)/shard_map/ppermute | solution.py:215
  24.9 2.3 %collective-permute-start.8 = (bf16[256,384]{1,0:T(8,128)(2,1)S(1)}, bf16[256,384]{1,0:T(8,128)(2,1)S(1)}, u32[]{:S(2)}, u32[]{:S(2)}) collective-permute-start(bf16[256,384]{1,0:T(8,128)(2,1)S(1)} %pad_maximum_fusion.1), channel_id=1, source_target_pairs={{0,8},{1,9},{2,10},{3,11},{4,12},{5,13},{6,14},{7,15},{8,32},{9,33... | collective-permute-start | bytes 589832 | tf_op jit(solution)/shard_map/ppermute | solution.py:215
  27.2 3.1 %collective-permute-start.7 = (bf16[256,384]{1,0:T(8,128)(2,1)S(1)}, bf16[256,384]{1,0:T(8,128)(2,1)S(1)}, u32[]{:S(2)}, u32[]{:S(2)}) collective-permute-start(bf16[256,384]{1,0:T(8,128)(2,1)S(1)} %get-tuple-element.65), channel_id=1, source_target_pairs={{0,16},{16,0},{1,17},{17,1},{2,18},{18,2},{3,19},{19,3},{4,20},{20... | collective-permute-start | bytes 589832 | tf_op jit(solution)/shard_map/ppermute | solution.py:200
  30.4 1.5 %tile.8.refs_0_ = f32[512,256]{1,0:T(8,128)S(1)} custom-call(bf16[2,128,128]{2,1,0:T(8,128)(2,1)S(1)} %copy-done, bf16[640,256]{1,0:T(8,128)(2,1)S(1)} %collective-permute-done.11.rows_ref, bf16[512,384]{1,0:T(8,128)(2,1)S(1)} %pad_maximum_fusion.refs_0_, bf16[512,384]{1,0:T(8,128)(2,1)S(1)} %collective-permute-done.6.refs_1_), custom_call_target="tpu_custom_call" | custom-call | tf_op jit(solution)/shard_map/tile/pallas_call | solution.py:270
  31.9 0.2 collective-permute-done.10.rows_ref
  32.1 1.5 %tile.7.refs_0_ = f32[512,256]{1,0:T(8,128)S(1)} custom-call(bf16[2,128,128]{2,1,0:T(8,128)(2,1)S(1)} %copy-done, bf16[640,256]{1,0:T(8,128)(2,1)S(1)} %collective-permute-done.10.rows_ref, bf16[512,384]{1,0:T(8,128)(2,1)S(1)} %pad_maximum_fusion.refs_0_, bf16[512,384]{1,0:T(8,128)(2,1)S(1)} %collective-permute-done.6.refs_1_), custom_call_target="tpu_custom_call" | custom-call | tf_op jit(solution)/shard_map/tile/pallas_call | solution.py:270
  33.6 4.2 %collective-permute-start.12 = (bf16[256,384]{1,0:T(8,128)(2,1)S(1)}, bf16[256,384]{1,0:T(8,128)(2,1)S(1)}, u32[]{:S(2)}, u32[]{:S(2)}) collective-permute-start(bf16[256,384]{1,0:T(8,128)(2,1)S(1)} %get-tuple-element.44), channel_id=1, source_target_pairs={{0,16},{16,0},{1,17},{17,1},{2,18},{18,2},{3,19},{19,3},{4,20},{20... | collective-permute-start | bytes 589832 | tf_op jit(solution)/shard_map/ppermute | solution.py:200
  37.8 0.3 collective-permute-start.13
  38.1 0.9 tile.11.refs_0_
  39.0 0.3 collective-permute-done.13.refs_5_.refs_4_.refs_2_
  39.3 0.9 tile.12
  40.1 2.4 %collective-permute-start.15 = (bf16[512,256]{1,0:T(8,128)(2,1)S(1)}, bf16[512,256]{1,0:T(8,128)(2,1)S(1)}, u32[]{:S(2)}, u32[]{:S(2)}) collective-permute-start(bf16[512,256]{1,0:T(8,128)(2,1)S(1)} %tile.12), channel_id=1, source_target_pairs={{0,3},{1,0},{2,1},{3,2},{4,7},{5,4},{6,5},{7,6},{8,11},{9,8},{10,9... | collective-permute-start | bytes 786440 | tf_op jit(solution)/shard_map/ppermute | solution.py:215
  42.5 1.4 %tile.10 = bf16[512,256]{1,0:T(8,128)(2,1)S(1)} custom-call(bf16[2,128,128]{2,1,0:T(8,128)(2,1)S(1)} %copy-done, bf16[640,256]{1,0:T(8,128)(2,1)S(1)} %collective-permute-done.10.rows_ref, f32[512,256]{1,0:T(8,128)S(1)} %tile.7.refs_0_, bf16[256,384]{1,0:T(8,128)(2,1)S(1)} %collective-permute-done.7.refs_2_.refs_1_, ...), custom_call_target="tpu_custom_call" | custom-call | tf_op jit(solution)/shard_map/tile/pallas_call | solution.py:270
  43.9 0.7 collective-permute-start.14
  44.6 2.7 %tile.13 = bf16[512,256]{1,0:T(8,128)(2,1)S(1)} custom-call(bf16[2,128,128]{2,1,0:T(8,128)(2,1)S(1)} %copy-done, bf16[640,256]{1,0:T(8,128)(2,1)S(1)} %collective-permute-done.9.rows_ref, bf16[512,384]{1,0:T(8,128)(2,1)S(1)} %pad_maximum_fusion.refs_0_, bf16[512,384]{1,0:T(8,128)(2,1)S(1)} %collective-permute-done.6.refs_1_, ...), custom_call_target="tpu_custom_call" | custom-call | tf_op jit(solution)/shard_map/tile/pallas_call | solution.py:270
  47.3 0.4 collective-permute-start.16
  47.7 2.7 %tile.9.a = f32[512,256]{1,0:T(8,128)S(1)} custom-call(bf16[2,128,128]{2,1,0:T(8,128)(2,1)S(1)} %copy-done, bf16[640,256]{1,0:T(8,128)(2,1)S(1)} %get-tuple-element.39.rows_ref, bf16[512,384]{1,0:T(8,128)(2,1)S(1)} %pad_maximum_fusion.refs_0_, bf16[512,384]{1,0:T(8,128)(2,1)S(1)} %collective-permute-done.6.refs_1_, ...), custom_call_target="tpu_custom_call" | custom-call | tf_op jit(solution)/shard_map/tile/pallas_call | solution.py:270
  50.4 0.4 collective-permute-done.14.b
  50.8 0.5 sum_rows.1
  51.2 2.9 %collective-permute-done.16.last = bf16[512,256]{1,0:T(8,128)(2,1)S(1)} collective-permute-done((bf16[512,256]{1,0:T(8,128)(2,1)S(1)}, bf16[512,256]{1,0:T(8,128)(2,1)S(1)}, u32[]{:S(2)}, u32[]{:S(2)}) %collective-permute-start.16) | collective-permute-done | bytes 262176 | tf_op jit(solution)/shard_map/ppermute | solution.py:215
  54.1 0.3 last_rows.1
  54.5 10.1 %all_to_all.15.refs_0_ = bf16[16,32,256]{2,1,0:T(8,128)(2,1)S(1)} all-to-all(bf16[16,32,256]{2,1,0:T(8,128)(2,1)S(1)} %bitcast.5), channel_id=1, replica_groups=mesh['y'=4,'zh'=2,'core'=2,'zl'=4,'x'=4] {'y','x'}, dimensions={0} | all-to-all | bytes 524288 | tf_op jit(solution)/shard_map/all_to_all | solution.py:223
  64.6 0.8 sum_spread.2
  65.4 6.9 %all-to-all-start.1 = ((bf16[16,32,256]{2,1,0:T(8,128)(2,1)}), bf16[16,32,256]{2,1,0:T(8,128)(2,1)S(1)}, u32[]{:S(2)}, u32[]{:S(2)}) async-start(bf16[16,32,256]{2,1,0:T(8,128)(2,1)} %sum_spread.2), calls=%async_computation.1 | async-start | bytes 524288 | tf_op jit(solution)/shard_map/all_to_all | solution.py:223
  72.3 0.3 collective-permute-start.17
  72.6 1.4 %collective-permute-start.18 = (bf16[128,256]{1,0:T(8,128)(2,1)S(1)}, bf16[128,256]{1,0:T(8,128)(2,1)S(1)}, u32[]{:S(2)}, u32[]{:S(2)}) collective-permute-start(bf16[128,256]{1,0:T(8,128)(2,1)S(1)} %get-tuple-element.60), channel_id=1, source_target_pairs={{0,128},{1,129},{2,130},{3,131},{4,132},{5,133},{6,134},{7,135},{8... | collective-permute-start | bytes 196616 | tf_op jit(solution)/shard_map/ppermute | solution.py:215
  74.0 1.1 %collective-permute-start.19 = (bf16[128,256]{1,0:T(8,128)(2,1)S(1)}, bf16[128,256]{1,0:T(8,128)(2,1)S(1)}, u32[]{:S(2)}, u32[]{:S(2)}) collective-permute-start(bf16[128,256]{1,0:T(8,128)(2,1)S(1)} %get-tuple-element.61), channel_id=1, source_target_pairs={{0,192},{1,193},{2,194},{3,195},{4,196},{5,197},{6,198},{7,199},{8... | collective-permute-start | bytes 196616 | tf_op jit(solution)/shard_map/ppermute | solution.py:215
  75.1 2.5 %collective-permute-done.17.b = bf16[128,256]{1,0:T(8,128)(2,1)S(1)} collective-permute-done((bf16[128,256]{1,0:T(8,128)(2,1)S(1)}, bf16[128,256]{1,0:T(8,128)(2,1)S(1)}, u32[]{:S(2)}, u32[]{:S(2)}) %collective-permute-start.17) | collective-permute-done | bytes 65568 | tf_op jit(solution)/shard_map/ppermute | solution.py:215
  77.6 0.6 collective-permute-done.19.d
  78.2 0.7 finish_rows.1
  78.9 3.0 %all-to-all-done.1.refs_0_ = bf16[16,32,256]{2,1,0:T(8,128)(2,1)S(1)} async-done(((bf16[16,32,256]{2,1,0:T(8,128)(2,1)}), bf16[16,32,256]{2,1,0:T(8,128)(2,1)S(1)}, u32[]{:S(2)}, u32[]{:S(2)}) %all-to-all-start.1) | async-done | bytes 262176 | tf_op jit(solution)/shard_map/all_to_all | solution.py:223
  81.9 10.7 %all_to_all.16 = bf16[16,32,256]{2,1,0:T(8,128)(2,1)S(1)} all-to-all(bf16[16,32,256]{2,1,0:T(8,128)(2,1)S(1)} %sum_spread.3), channel_id=1, replica_groups=mesh['y'=4,'zh'=2,'core'=2,'zl'=4,'x'=4] {'y','x'}, dimensions={0} | all-to-all | bytes 524288 | tf_op jit(solution)/shard_map/all_to_all | solution.py:223
  92.6 0.8 convert_multiply_fusion
  (18 shorter events, 0.2 us)
Async XLA Ops:
  2.2 16.3 %copy-start.1 = (bf16[512,256]{1,0:T(8,128)(2,1)S(1)}, bf16[512,256]{1,0:T(8,128)(2,1)}, u32[]{:S(2)}) copy-start(bf16[512,256]{1,0:T(8,128)(2,1)} %weight.3) | copy-start | bytes 786436
  2.2 14.6 %collective-permute-start = (bf16[128,384]{1,0:T(8,128)(2,1)S(1)}, bf16[128,384]{1,0:T(8,128)(2,1)S(1)}, u32[]{:S(2)}, u32[]{:S(2)}) collective-permute-start(bf16[128,384]{1,0:T(8,128)(2,1)S(1)} %get-tuple-element.33), channel_id=1, source_target_pairs={{0,32},{4,36},{8,40},{12,44},{32,0},{36,4},{40,8},{44,12},{1,33},{... | collective-permute-start | bytes 294920 | tf_op jit(solution)/shard_map/ppermute | solution.py:200
  10.0 6.8 %collective-permute-start.5 = (bf16[128,640]{1,0:T(8,128)(2,1)S(1)}, bf16[128,640]{1,0:T(8,128)(2,1)S(1)}, u32[]{:S(2)}, u32[]{:S(2)}) collective-permute-start(bf16[128,640]{1,0:T(8,128)(2,1)S(1)} %get-tuple-element.34.refs_0_), channel_id=1, source_target_pairs={{0,64},{1,65},{2,66},{3,67},{4,68},{5,69},{6,70},{7,71},{8,72},{9,... | collective-permute-start | bytes 491528 | tf_op jit(solution)/shard_map/ppermute | solution.py:215
  11.2 7.2 %collective-permute-start.4 = (bf16[128,640]{1,0:T(8,128)(2,1)S(1)}, bf16[128,640]{1,0:T(8,128)(2,1)S(1)}, u32[]{:S(2)}, u32[]{:S(2)}) collective-permute-start(bf16[128,640]{1,0:T(8,128)(2,1)S(1)} %get-tuple-element.34.refs_0_), channel_id=1, source_target_pairs={{0,128},{1,129},{2,130},{3,131},{4,132},{5,133},{6,134},{7,135},{8... | collective-permute-start | bytes 491528 | tf_op jit(solution)/shard_map/ppermute | solution.py:215
  13.7 4.8 %collective-permute-start.3 = (bf16[128,640]{1,0:T(8,128)(2,1)S(1)}, bf16[128,640]{1,0:T(8,128)(2,1)S(1)}, u32[]{:S(2)}, u32[]{:S(2)}) collective-permute-start(bf16[128,640]{1,0:T(8,128)(2,1)S(1)} %get-tuple-element.34.refs_0_), channel_id=1, source_target_pairs={{0,192},{1,193},{2,194},{3,195},{4,196},{5,197},{6,198},{7,199},{8... | collective-permute-start | bytes 491528 | tf_op jit(solution)/shard_map/ppermute | solution.py:215
  14.8 3.9 %collective-permute-start.1 = (bf16[128,384]{1,0:T(8,128)(2,1)S(1)}, bf16[128,384]{1,0:T(8,128)(2,1)S(1)}, u32[]{:S(2)}, u32[]{:S(2)}) collective-permute-start(bf16[128,384]{1,0:T(8,128)(2,1)S(1)} %get-tuple-element.33), channel_id=1, source_target_pairs={{0,16},{16,0},{1,17},{17,1},{2,18},{18,2},{3,19},{19,3},{4,20},{20... | collective-permute-start | bytes 294920 | tf_op jit(solution)/shard_map/ppermute | solution.py:200
  16.8 2.0 %collective-permute-start.2 = (bf16[128,384]{1,0:T(8,128)(2,1)S(1)}, bf16[128,384]{1,0:T(8,128)(2,1)S(1)}, u32[]{:S(2)}, u32[]{:S(2)}) collective-permute-start(bf16[128,384]{1,0:T(8,128)(2,1)S(1)} %collective-permute-done), channel_id=1, source_target_pairs={{0,16},{16,0},{1,17},{17,1},{2,18},{18,2},{3,19},{19,3},{4,20},{20... | collective-permute-start | bytes 294920 | tf_op jit(solution)/shard_map/ppermute | solution.py:200
  18.8 11.5 %copy-start = (bf16[2,128,128]{2,1,0:T(8,128)(2,1)S(1)}, bf16[2,128,128]{2,1,0:T(8,128)(2,1)}, u32[]{:S(2)}) copy-start(bf16[2,128,128]{2,1,0:T(8,128)(2,1)} %constant.4.clone.table) | copy-start | bytes 196612
  18.8 8.4 %collective-permute-start.6 = (bf16[512,384]{1,0:T(8,128)(2,1)S(1)}, bf16[512,384]{1,0:T(8,128)(2,1)S(1)}, u32[]{:S(2)}, u32[]{:S(2)}) collective-permute-start(bf16[512,384]{1,0:T(8,128)(2,1)S(1)} %pad_maximum_fusion.refs_0_), channel_id=1, source_target_pairs={{0,4},{1,5},{2,6},{3,7},{4,8},{5,9},{6,10},{7,11},{8,12},{9,13},{1... | collective-permute-start | bytes 1179656 | tf_op jit(solution)/shard_map/ppermute | solution.py:215
  19.9 10.5 %collective-permute-start.11 = (bf16[640,256]{1,0:T(8,128)(2,1)S(1)}, bf16[640,256]{1,0:T(8,128)(2,1)S(1)}, u32[]{:S(2)}, u32[]{:S(2)}) collective-permute-start(bf16[640,256]{1,0:T(8,128)(2,1)S(1)} %get-tuple-element.39.rows_ref), channel_id=1, source_target_pairs={{0,1},{1,2},{2,3},{3,0},{4,5},{5,6},{6,7},{7,4},{8,9},{9,10},{10,1... | collective-permute-start | bytes 983048 | tf_op jit(solution)/shard_map/ppermute | solution.py:215
  21.2 10.9 %collective-permute-start.10 = (bf16[640,256]{1,0:T(8,128)(2,1)S(1)}, bf16[640,256]{1,0:T(8,128)(2,1)S(1)}, u32[]{:S(2)}, u32[]{:S(2)}) collective-permute-start(bf16[640,256]{1,0:T(8,128)(2,1)S(1)} %get-tuple-element.39.rows_ref), channel_id=1, source_target_pairs={{0,2},{1,3},{2,0},{3,1},{4,6},{5,7},{6,4},{7,5},{8,10},{9,11},{10,... | collective-permute-start | bytes 983048 | tf_op jit(solution)/shard_map/ppermute | solution.py:215
  23.8 9.8 %collective-permute-start.9 = (bf16[640,256]{1,0:T(8,128)(2,1)S(1)}, bf16[640,256]{1,0:T(8,128)(2,1)S(1)}, u32[]{:S(2)}, u32[]{:S(2)}) collective-permute-start(bf16[640,256]{1,0:T(8,128)(2,1)S(1)} %get-tuple-element.39.rows_ref), channel_id=1, source_target_pairs={{0,3},{1,0},{2,1},{3,2},{4,7},{5,4},{6,5},{7,6},{8,11},{9,8},{10,9... | collective-permute-start | bytes 983048 | tf_op jit(solution)/shard_map/ppermute | solution.py:215
  24.9 8.7 %collective-permute-start.8 = (bf16[256,384]{1,0:T(8,128)(2,1)S(1)}, bf16[256,384]{1,0:T(8,128)(2,1)S(1)}, u32[]{:S(2)}, u32[]{:S(2)}) collective-permute-start(bf16[256,384]{1,0:T(8,128)(2,1)S(1)} %pad_maximum_fusion.1), channel_id=1, source_target_pairs={{0,8},{1,9},{2,10},{3,11},{4,12},{5,13},{6,14},{7,15},{8,32},{9,33... | collective-permute-start | bytes 589832 | tf_op jit(solution)/shard_map/ppermute | solution.py:215
  27.2 6.4 %collective-permute-start.7 = (bf16[256,384]{1,0:T(8,128)(2,1)S(1)}, bf16[256,384]{1,0:T(8,128)(2,1)S(1)}, u32[]{:S(2)}, u32[]{:S(2)}) collective-permute-start(bf16[256,384]{1,0:T(8,128)(2,1)S(1)} %get-tuple-element.65), channel_id=1, source_target_pairs={{0,16},{16,0},{1,17},{17,1},{2,18},{18,2},{3,19},{19,3},{4,20},{20... | collective-permute-start | bytes 589832 | tf_op jit(solution)/shard_map/ppermute | solution.py:200
  33.6 5.3 %collective-permute-start.12 = (bf16[256,384]{1,0:T(8,128)(2,1)S(1)}, bf16[256,384]{1,0:T(8,128)(2,1)S(1)}, u32[]{:S(2)}, u32[]{:S(2)}) collective-permute-start(bf16[256,384]{1,0:T(8,128)(2,1)S(1)} %get-tuple-element.44), channel_id=1, source_target_pairs={{0,16},{16,0},{1,17},{17,1},{2,18},{18,2},{3,19},{19,3},{4,20},{20... | collective-permute-start | bytes 589832 | tf_op jit(solution)/shard_map/ppermute | solution.py:200
  37.8 1.4 %collective-permute-start.13 = (bf16[256,384]{1,0:T(8,128)(2,1)S(1)}, bf16[256,384]{1,0:T(8,128)(2,1)S(1)}, u32[]{:S(2)}, u32[]{:S(2)}) collective-permute-start(bf16[256,384]{1,0:T(8,128)(2,1)S(1)} %collective-permute-done.8.refs_3_.refs_2_), channel_id=1, source_target_pairs={{0,16},{16,0},{1,17},{17,1},{2,18},{18,2},{3,19},{19,3},{4,20},{20... | collective-permute-start | bytes 589832 | tf_op jit(solution)/shard_map/ppermute | solution.py:200
  40.1 10.2 %collective-permute-start.15 = (bf16[512,256]{1,0:T(8,128)(2,1)S(1)}, bf16[512,256]{1,0:T(8,128)(2,1)S(1)}, u32[]{:S(2)}, u32[]{:S(2)}) collective-permute-start(bf16[512,256]{1,0:T(8,128)(2,1)S(1)} %tile.12), channel_id=1, source_target_pairs={{0,3},{1,0},{2,1},{3,2},{4,7},{5,4},{6,5},{7,6},{8,11},{9,8},{10,9... | collective-permute-start | bytes 786440 | tf_op jit(solution)/shard_map/ppermute | solution.py:215
  43.9 6.8 %collective-permute-start.14 = (bf16[512,256]{1,0:T(8,128)(2,1)S(1)}, bf16[512,256]{1,0:T(8,128)(2,1)S(1)}, u32[]{:S(2)}, u32[]{:S(2)}) collective-permute-start(bf16[512,256]{1,0:T(8,128)(2,1)S(1)} %tile.10), channel_id=1, source_target_pairs={{0,2},{1,3},{2,0},{3,1},{4,6},{5,7},{6,4},{7,5},{8,10},{9,11},{10,... | collective-permute-start | bytes 786440 | tf_op jit(solution)/shard_map/ppermute | solution.py:215
  47.3 6.8 %collective-permute-start.16 = (bf16[512,256]{1,0:T(8,128)(2,1)S(1)}, bf16[512,256]{1,0:T(8,128)(2,1)S(1)}, u32[]{:S(2)}, u32[]{:S(2)}) collective-permute-start(bf16[512,256]{1,0:T(8,128)(2,1)S(1)} %tile.13), channel_id=1, source_target_pairs={{0,1},{1,2},{2,3},{3,0},{4,5},{5,6},{6,7},{7,4},{8,9},{9,10},{10,1... | collective-permute-start | bytes 786440 | tf_op jit(solution)/shard_map/ppermute | solution.py:215
  65.4 16.5 %all-to-all-start.1 = ((bf16[16,32,256]{2,1,0:T(8,128)(2,1)}), bf16[16,32,256]{2,1,0:T(8,128)(2,1)S(1)}, u32[]{:S(2)}, u32[]{:S(2)}) async-start(bf16[16,32,256]{2,1,0:T(8,128)(2,1)} %sum_spread.2), calls=%async_computation.1 | async-start | bytes 524288 | tf_op jit(solution)/shard_map/all_to_all | solution.py:223
  72.3 5.3 %collective-permute-start.17 = (bf16[128,256]{1,0:T(8,128)(2,1)S(1)}, bf16[128,256]{1,0:T(8,128)(2,1)S(1)}, u32[]{:S(2)}, u32[]{:S(2)}) collective-permute-start(bf16[128,256]{1,0:T(8,128)(2,1)S(1)} %get-tuple-element.59), channel_id=1, source_target_pairs={{0,64},{1,65},{2,66},{3,67},{4,68},{5,69},{6,70},{7,71},{8,72},{9,... | collective-permute-start | bytes 196616 | tf_op jit(solution)/shard_map/ppermute | solution.py:215
  72.6 5.0 %collective-permute-start.18 = (bf16[128,256]{1,0:T(8,128)(2,1)S(1)}, bf16[128,256]{1,0:T(8,128)(2,1)S(1)}, u32[]{:S(2)}, u32[]{:S(2)}) collective-permute-start(bf16[128,256]{1,0:T(8,128)(2,1)S(1)} %get-tuple-element.60), channel_id=1, source_target_pairs={{0,128},{1,129},{2,130},{3,131},{4,132},{5,133},{6,134},{7,135},{8... | collective-permute-start | bytes 196616 | tf_op jit(solution)/shard_map/ppermute | solution.py:215
  74.0 4.2 %collective-permute-start.19 = (bf16[128,256]{1,0:T(8,128)(2,1)S(1)}, bf16[128,256]{1,0:T(8,128)(2,1)S(1)}, u32[]{:S(2)}, u32[]{:S(2)}) collective-permute-start(bf16[128,256]{1,0:T(8,128)(2,1)S(1)} %get-tuple-element.61), channel_id=1, source_target_pairs={{0,192},{1,193},{2,194},{3,195},{4,196},{5,197},{6,198},{7,199},{8... | collective-permute-start | bytes 196616 | tf_op jit(solution)/shard_map/ppermute | solution.py:215

commit v16 on v15

--- a/solution.py
+++ b/solution.py
@@ -279,10 +279,10 @@
     first = n_side - 1
     begin = {d: tile(lines[d], [four, near], F32) for d in (first, first - 1)}
     halves = [near[: 2 * rows], near[2 * rows :]]
-    columns = [four, near, ring(halves[0], "core", 2, 1), far]
-    columns, lines, begin, halves = lax.optimization_barrier((columns, lines, begin, halves))
+    columns = [four, near] + [ring(part, "core", 2, 1) for part in halves] + [far]
+    columns, lines, begin = lax.optimization_barrier((columns, lines, begin))
     early = len(columns)
-    columns += [ring(part, "core", 2, 1) for part in (halves[1], columns[-1])]
+    columns.append(ring(columns[-1], "core", 2, 1))
 
     back = {}
     for d in range(n_side):

time: 94.8 us -> 94.5 us (level)
  transfers between devices with their start and end apart: 21 -> 21, of which waited for: 8 -> 6; matrix products, arithmetic and copies ran while one was open for 0% -> 0% of each run, Pallas kernels for 13% -> 13%
where the time goes in v16:
time: 94.5 us; the launch traced here: 93.2 us
  starting transfers between devices  43.8 us (46%)
  blocking collectives  20.8 us (22%)
  Pallas kernels  15.8 us (17%)
  waiting for transfers between devices  11 us (12%)
    all_to_all x2, blocking collectives, exchange(): return lax.all_to_all(array, axes, split_axis=0, concat_axis=0, tiled=True)  20.8 us
    ppermute x14, starting transfers between devices, move(): return lax.ppermute(array, ALL, perm)  19.4 us
    ppermute x6, starting transfers between devices, ring(): lax.ppermute(array, axis, [(i, (i + shift) % size) for i in range(size)])  17.6 us
    pallas_call x7, Pallas kernels, tile(): pl.pallas_call(functools.partial(tile_kernel, 256, 256, start is not None...  11.6 us
    ppermute x14, waiting for transfers between devices, move(): return lax.ppermute(array, ALL, perm)  8 us
    all_to_all x1, starting transfers between devices, exchange(): return lax.all_to_all(array, axes, split_axis=0, concat_axis=0, tiled=True)  6.86 us
    all_to_all x1, waiting for transfers between devices, exchange(): return lax.all_to_all(array, axes, split_axis=0, concat_axis=0, tiled=True)  2.99 us
  transfers between devices with their start and end apart: 21, of which 6 were waited for; matrix products, arithmetic and copies ran while one was open for 0% of the time, Pallas kernels for 13%

profile of v16, /device:TPU:1, one launch (start us, length us, event | category | flops | bytes accessed | tf_op | source)
XLA Modules:
  0.0 93.2 jit_solution(12901249356520583361)
XLA Ops:
  0.6 1.5 %pack.1 = (bf16[128,384]{1,0:T(8,128)(2,1)S(1)}, bf16[128,640]{1,0:T(8,128)(2,1)S(1)}) custom-call(bf16[128,512]{1,0:T(8,128)(2,1)} %embeds.1, bf16[512,256]{1,0:T(8,128)(2,1)} %weight.3, f32[1,128]{1,0:T(1,128)} %bitcast.9, f32[15,128]{1,0:T(8,128)} %bitcast.7, f32[15,128]{1,0:T(8,128)} %bitcast.8), custom_call_target="tpu_custom_call" | custom-call | tf_op jit(solution)/shard_map/pack/pallas_call | solution.py:229
  2.2 0.0 copy-start.1
  2.2 7.8 %collective-permute-start = (bf16[128,384]{1,0:T(8,128)(2,1)S(1)}, bf16[128,384]{1,0:T(8,128)(2,1)S(1)}, u32[]{:S(2)}, u32[]{:S(2)}) collective-permute-start(bf16[128,384]{1,0:T(8,128)(2,1)S(1)} %get-tuple-element.33), channel_id=1, source_target_pairs={{0,32},{4,36},{8,40},{12,44},{32,0},{36,4},{40,8},{44,12},{1,33},{... | collective-permute-start | bytes 294920 | tf_op jit(solution)/shard_map/ppermute | solution.py:200
  10.0 1.2 %collective-permute-start.5 = (bf16[128,640]{1,0:T(8,128)(2,1)S(1)}, bf16[128,640]{1,0:T(8,128)(2,1)S(1)}, u32[]{:S(2)}, u32[]{:S(2)}) collective-permute-start(bf16[128,640]{1,0:T(8,128)(2,1)S(1)} %get-tuple-element.34.refs_0_), channel_id=1, source_target_pairs={{0,64},{1,65},{2,66},{3,67},{4,68},{5,69},{6,70},{7,71},{8,72},{9,... | collective-permute-start | bytes 491528 | tf_op jit(solution)/shard_map/ppermute | solution.py:215
  11.2 2.5 %collective-permute-start.4 = (bf16[128,640]{1,0:T(8,128)(2,1)S(1)}, bf16[128,640]{1,0:T(8,128)(2,1)S(1)}, u32[]{:S(2)}, u32[]{:S(2)}) collective-permute-start(bf16[128,640]{1,0:T(8,128)(2,1)S(1)} %get-tuple-element.34.refs_0_), channel_id=1, source_target_pairs={{0,128},{1,129},{2,130},{3,131},{4,132},{5,133},{6,134},{7,135},{8... | collective-permute-start | bytes 491528 | tf_op jit(solution)/shard_map/ppermute | solution.py:215
  13.7 1.2 %collective-permute-start.3 = (bf16[128,640]{1,0:T(8,128)(2,1)S(1)}, bf16[128,640]{1,0:T(8,128)(2,1)S(1)}, u32[]{:S(2)}, u32[]{:S(2)}) collective-permute-start(bf16[128,640]{1,0:T(8,128)(2,1)S(1)} %get-tuple-element.34.refs_0_), channel_id=1, source_target_pairs={{0,192},{1,193},{2,194},{3,195},{4,196},{5,197},{6,198},{7,199},{8... | collective-permute-start | bytes 491528 | tf_op jit(solution)/shard_map/ppermute | solution.py:215
  14.8 2.0 %collective-permute-start.1 = (bf16[128,384]{1,0:T(8,128)(2,1)S(1)}, bf16[128,384]{1,0:T(8,128)(2,1)S(1)}, u32[]{:S(2)}, u32[]{:S(2)}) collective-permute-start(bf16[128,384]{1,0:T(8,128)(2,1)S(1)} %get-tuple-element.33), channel_id=1, source_target_pairs={{0,16},{16,0},{1,17},{17,1},{2,18},{18,2},{3,19},{19,3},{4,20},{20... | collective-permute-start | bytes 294920 | tf_op jit(solution)/shard_map/ppermute | solution.py:200
  16.8 0.0 collective-permute-start.2
  16.8 1.6 %collective-permute-done.4.refs_2_ = bf16[128,640]{1,0:T(8,128)(2,1)S(1)} collective-permute-done((bf16[128,640]{1,0:T(8,128)(2,1)S(1)}, bf16[128,640]{1,0:T(8,128)(2,1)S(1)}, u32[]{:S(2)}, u32[]{:S(2)}) %collective-permute-start.4) | collective-permute-done | bytes 163872 | tf_op jit(solution)/shard_map/ppermute | solution.py:215
  18.4 0.3 split.1
  18.8 0.0 collective-permute-done.1
  18.8 0.0 copy-start
  18.8 1.0 %collective-permute-start.6 = (bf16[512,384]{1,0:T(8,128)(2,1)S(1)}, bf16[512,384]{1,0:T(8,128)(2,1)S(1)}, u32[]{:S(2)}, u32[]{:S(2)}) collective-permute-start(bf16[512,384]{1,0:T(8,128)(2,1)S(1)} %pad_maximum_fusion.refs_0_), channel_id=1, source_target_pairs={{0,4},{1,5},{2,6},{3,7},{4,8},{5,9},{6,10},{7,11},{8,12},{9,13},{1... | collective-permute-start | bytes 1179656 | tf_op jit(solution)/shard_map/ppermute | solution.py:215
  19.9 1.3 %collective-permute-start.12 = (bf16[640,256]{1,0:T(8,128)(2,1)S(1)}, bf16[640,256]{1,0:T(8,128)(2,1)S(1)}, u32[]{:S(2)}, u32[]{:S(2)}) collective-permute-start(bf16[640,256]{1,0:T(8,128)(2,1)S(1)} %get-tuple-element.39.rows_ref), channel_id=1, source_target_pairs={{0,1},{1,2},{2,3},{3,0},{4,5},{5,6},{6,7},{7,4},{8,9},{9,10},{10,1... | collective-permute-start | bytes 983048 | tf_op jit(solution)/shard_map/ppermute | solution.py:215
  21.2 2.6 %collective-permute-start.11 = (bf16[640,256]{1,0:T(8,128)(2,1)S(1)}, bf16[640,256]{1,0:T(8,128)(2,1)S(1)}, u32[]{:S(2)}, u32[]{:S(2)}) collective-permute-start(bf16[640,256]{1,0:T(8,128)(2,1)S(1)} %get-tuple-element.39.rows_ref), channel_id=1, source_target_pairs={{0,2},{1,3},{2,0},{3,1},{4,6},{5,7},{6,4},{7,5},{8,10},{9,11},{10,... | collective-permute-start | bytes 983048 | tf_op jit(solution)/shard_map/ppermute | solution.py:215
  23.8 1.1 %collective-permute-start.10 = (bf16[640,256]{1,0:T(8,128)(2,1)S(1)}, bf16[640,256]{1,0:T(8,128)(2,1)S(1)}, u32[]{:S(2)}, u32[]{:S(2)}) collective-permute-start(bf16[640,256]{1,0:T(8,128)(2,1)S(1)} %get-tuple-element.39.rows_ref), channel_id=1, source_target_pairs={{0,3},{1,0},{2,1},{3,2},{4,7},{5,4},{6,5},{7,6},{8,11},{9,8},{10,9... | collective-permute-start | bytes 983048 | tf_op jit(solution)/shard_map/ppermute | solution.py:215
  24.9 2.3 %collective-permute-start.9 = (bf16[256,384]{1,0:T(8,128)(2,1)S(1)}, bf16[256,384]{1,0:T(8,128)(2,1)S(1)}, u32[]{:S(2)}, u32[]{:S(2)}) collective-permute-start(bf16[256,384]{1,0:T(8,128)(2,1)S(1)} %pad_maximum_fusion.1), channel_id=1, source_target_pairs={{0,8},{1,9},{2,10},{3,11},{4,12},{5,13},{6,14},{7,15},{8,32},{9,33... | collective-permute-start | bytes 589832 | tf_op jit(solution)/shard_map/ppermute | solution.py:215
  27.2 3.1 %collective-permute-start.8 = (bf16[256,384]{1,0:T(8,128)(2,1)S(1)}, bf16[256,384]{1,0:T(8,128)(2,1)S(1)}, u32[]{:S(2)}, u32[]{:S(2)}) collective-permute-start(bf16[256,384]{1,0:T(8,128)(2,1)S(1)} %get-tuple-element.64), channel_id=1, source_target_pairs={{0,16},{16,0},{1,17},{17,1},{2,18},{18,2},{3,19},{19,3},{4,20},{20... | collective-permute-start | bytes 589832 | tf_op jit(solution)/shard_map/ppermute | solution.py:200
  30.4 0.0 collective-permute-done.12.rows_ref
  30.4 0.2 collective-permute-start.7
  30.6 1.5 %tile.8.refs_0_ = f32[512,256]{1,0:T(8,128)S(1)} custom-call(bf16[2,128,128]{2,1,0:T(8,128)(2,1)S(1)} %copy-done, bf16[640,256]{1,0:T(8,128)(2,1)S(1)} %collective-permute-done.12.rows_ref, bf16[512,384]{1,0:T(8,128)(2,1)S(1)} %pad_maximum_fusion.refs_0_, bf16[512,384]{1,0:T(8,128)(2,1)S(1)} %collective-permute-done.6.refs_1_), custom_call_target="tpu_custom_call" | custom-call | tf_op jit(solution)/shard_map/tile/pallas_call | solution.py:270
  32.1 0.0 collective-permute-done.11.rows_ref
  32.1 1.5 %tile.7.refs_0_ = f32[512,256]{1,0:T(8,128)S(1)} custom-call(bf16[2,128,128]{2,1,0:T(8,128)(2,1)S(1)} %copy-done, bf16[640,256]{1,0:T(8,128)(2,1)S(1)} %collective-permute-done.11.rows_ref, bf16[512,384]{1,0:T(8,128)(2,1)S(1)} %pad_maximum_fusion.refs_0_, bf16[512,384]{1,0:T(8,128)(2,1)S(1)} %collective-permute-done.6.refs_1_), custom_call_target="tpu_custom_call" | custom-call | tf_op jit(solution)/shard_map/tile/pallas_call | solution.py:270
  33.6 4.5 %collective-permute-start.13 = (bf16[256,384]{1,0:T(8,128)(2,1)S(1)}, bf16[256,384]{1,0:T(8,128)(2,1)S(1)}, u32[]{:S(2)}, u32[]{:S(2)}) collective-permute-start(bf16[256,384]{1,0:T(8,128)(2,1)S(1)} %collective-permute-done.9.refs_4_.refs_3_), channel_id=1, source_target_pairs={{0,16},{16,0},{1,17},{17,1},{2,18},{18,2},{3,19},{19,3},{4,20},{20... | collective-permute-start | bytes 589832 | tf_op jit(solution)/shard_map/ppermute | solution.py:200
  38.1 1.2 %tile.11.refs_0_ = f32[512,256]{1,0:T(8,128)S(1)} custom-call(bf16[2,128,128]{2,1,0:T(8,128)(2,1)S(1)} %copy-done, bf16[640,256]{1,0:T(8,128)(2,1)S(1)} %collective-permute-done.12.rows_ref, f32[512,256]{1,0:T(8,128)S(1)} %tile.8.refs_0_, bf16[256,384]{1,0:T(8,128)(2,1)S(1)} %collective-permute-done.7.refs_2_.refs_1_, ...), custom_call_target="tpu_custom_call" | custom-call | tf_op jit(solution)/shard_map/tile/pallas_call | solution.py:270
  39.3 0.6 tile.12
  39.9 2.4 %collective-permute-start.15 = (bf16[512,256]{1,0:T(8,128)(2,1)S(1)}, bf16[512,256]{1,0:T(8,128)(2,1)S(1)}, u32[]{:S(2)}, u32[]{:S(2)}) collective-permute-start(bf16[512,256]{1,0:T(8,128)(2,1)S(1)} %tile.12), channel_id=1, source_target_pairs={{0,3},{1,0},{2,1},{3,2},{4,7},{5,4},{6,5},{7,6},{8,11},{9,8},{10,9... | collective-permute-start | bytes 786440 | tf_op jit(solution)/shard_map/ppermute | solution.py:215
  42.3 1.4 %tile.10 = bf16[512,256]{1,0:T(8,128)(2,1)S(1)} custom-call(bf16[2,128,128]{2,1,0:T(8,128)(2,1)S(1)} %copy-done, bf16[640,256]{1,0:T(8,128)(2,1)S(1)} %collective-permute-done.11.rows_ref, f32[512,256]{1,0:T(8,128)S(1)} %tile.7.refs_0_, bf16[256,384]{1,0:T(8,128)(2,1)S(1)} %collective-permute-done.7.refs_2_.refs_1_, ...), custom_call_target="tpu_custom_call" | custom-call | tf_op jit(solution)/shard_map/tile/pallas_call | solution.py:270
  43.7 0.7 collective-permute-start.14
  44.4 2.7 %tile.13 = bf16[512,256]{1,0:T(8,128)(2,1)S(1)} custom-call(bf16[2,128,128]{2,1,0:T(8,128)(2,1)S(1)} %copy-done, bf16[640,256]{1,0:T(8,128)(2,1)S(1)} %collective-permute-done.10.rows_ref, bf16[512,384]{1,0:T(8,128)(2,1)S(1)} %pad_maximum_fusion.refs_0_, bf16[512,384]{1,0:T(8,128)(2,1)S(1)} %collective-permute-done.6.refs_1_, ...), custom_call_target="tpu_custom_call" | custom-call | tf_op jit(solution)/shard_map/tile/pallas_call | solution.py:270
  47.1 0.4 collective-permute-start.16
  47.5 2.7 %tile.9.a = f32[512,256]{1,0:T(8,128)S(1)} custom-call(bf16[2,128,128]{2,1,0:T(8,128)(2,1)S(1)} %copy-done, bf16[640,256]{1,0:T(8,128)(2,1)S(1)} %get-tuple-element.39.rows_ref, bf16[512,384]{1,0:T(8,128)(2,1)S(1)} %pad_maximum_fusion.refs_0_, bf16[512,384]{1,0:T(8,128)(2,1)S(1)} %collective-permute-done.6.refs_1_, ...), custom_call_target="tpu_custom_call" | custom-call | tf_op jit(solution)/shard_map/tile/pallas_call | solution.py:270
  50.2 0.4 collective-permute-done.14.b
  50.6 0.5 sum_rows.1
  51.0 2.9 %collective-permute-done.16.last = bf16[512,256]{1,0:T(8,128)(2,1)S(1)} collective-permute-done((bf16[512,256]{1,0:T(8,128)(2,1)S(1)}, bf16[512,256]{1,0:T(8,128)(2,1)S(1)}, u32[]{:S(2)}, u32[]{:S(2)}) %collective-permute-start.16) | collective-permute-done | bytes 262176 | tf_op jit(solution)/shard_map/ppermute | solution.py:215
  53.9 0.3 last_rows.1
  54.3 10.1 %all_to_all.15.refs_0_ = bf16[16,32,256]{2,1,0:T(8,128)(2,1)S(1)} all-to-all(bf16[16,32,256]{2,1,0:T(8,128)(2,1)S(1)} %bitcast.5), channel_id=1, replica_groups=mesh['y'=4,'zh'=2,'core'=2,'zl'=4,'x'=4] {'y','x'}, dimensions={0} | all-to-all | bytes 524288 | tf_op jit(solution)/shard_map/all_to_all | solution.py:223
  64.4 0.8 sum_spread.2
  65.2 6.9 %all-to-all-start.1 = ((bf16[16,32,256]{2,1,0:T(8,128)(2,1)}), bf16[16,32,256]{2,1,0:T(8,128)(2,1)S(1)}, u32[]{:S(2)}, u32[]{:S(2)}) async-start(bf16[16,32,256]{2,1,0:T(8,128)(2,1)} %sum_spread.2), calls=%async_computation.1 | async-start | bytes 524288 | tf_op jit(solution)/shard_map/all_to_all | solution.py:223
  72.0 0.3 collective-permute-start.17
  72.3 1.4 %collective-permute-start.18 = (bf16[128,256]{1,0:T(8,128)(2,1)S(1)}, bf16[128,256]{1,0:T(8,128)(2,1)S(1)}, u32[]{:S(2)}, u32[]{:S(2)}) collective-permute-start(bf16[128,256]{1,0:T(8,128)(2,1)S(1)} %get-tuple-element.60), channel_id=1, source_target_pairs={{0,128},{1,129},{2,130},{3,131},{4,132},{5,133},{6,134},{7,135},{8... | collective-permute-start | bytes 196616 | tf_op jit(solution)/shard_map/ppermute | solution.py:215
  73.7 1.1 %collective-permute-start.19 = (bf16[128,256]{1,0:T(8,128)(2,1)S(1)}, bf16[128,256]{1,0:T(8,128)(2,1)S(1)}, u32[]{:S(2)}, u32[]{:S(2)}) collective-permute-start(bf16[128,256]{1,0:T(8,128)(2,1)S(1)} %get-tuple-element.61), channel_id=1, source_target_pairs={{0,192},{1,193},{2,194},{3,195},{4,196},{5,197},{6,198},{7,199},{8... | collective-permute-start | bytes 196616 | tf_op jit(solution)/shard_map/ppermute | solution.py:215
  74.8 2.5 %collective-permute-done.17.b = bf16[128,256]{1,0:T(8,128)(2,1)S(1)} collective-permute-done((bf16[128,256]{1,0:T(8,128)(2,1)S(1)}, bf16[128,256]{1,0:T(8,128)(2,1)S(1)}, u32[]{:S(2)}, u32[]{:S(2)}) %collective-permute-start.17) | collective-permute-done | bytes 65568 | tf_op jit(solution)/shard_map/ppermute | solution.py:215
  77.3 0.6 collective-permute-done.19.d
  77.9 0.7 finish_rows.1
  78.6 3.0 %all-to-all-done.1.refs_0_ = bf16[16,32,256]{2,1,0:T(8,128)(2,1)S(1)} async-done(((bf16[16,32,256]{2,1,0:T(8,128)(2,1)}), bf16[16,32,256]{2,1,0:T(8,128)(2,1)S(1)}, u32[]{:S(2)}, u32[]{:S(2)}) %all-to-all-start.1) | async-done | bytes 262176 | tf_op jit(solution)/shard_map/all_to_all | solution.py:223
  81.6 10.7 %all_to_all.16 = bf16[16,32,256]{2,1,0:T(8,128)(2,1)S(1)} all-to-all(bf16[16,32,256]{2,1,0:T(8,128)(2,1)S(1)} %sum_spread.3), channel_id=1, replica_groups=mesh['y'=4,'zh'=2,'core'=2,'zl'=4,'x'=4] {'y','x'}, dimensions={0} | all-to-all | bytes 524288 | tf_op jit(solution)/shard_map/all_to_all | solution.py:223
  92.3 0.8 convert_multiply_fusion
  (18 shorter events, 0.2 us)
Async XLA Ops:
  2.2 16.3 %copy-start.1 = (bf16[512,256]{1,0:T(8,128)(2,1)S(1)}, bf16[512,256]{1,0:T(8,128)(2,1)}, u32[]{:S(2)}) copy-start(bf16[512,256]{1,0:T(8,128)(2,1)} %weight.3) | copy-start | bytes 786436
  2.2 14.6 %collective-permute-start = (bf16[128,384]{1,0:T(8,128)(2,1)S(1)}, bf16[128,384]{1,0:T(8,128)(2,1)S(1)}, u32[]{:S(2)}, u32[]{:S(2)}) collective-permute-start(bf16[128,384]{1,0:T(8,128)(2,1)S(1)} %get-tuple-element.33), channel_id=1, source_target_pairs={{0,32},{4,36},{8,40},{12,44},{32,0},{36,4},{40,8},{44,12},{1,33},{... | collective-permute-start | bytes 294920 | tf_op jit(solution)/shard_map/ppermute | solution.py:200
  10.0 6.8 %collective-permute-start.5 = (bf16[128,640]{1,0:T(8,128)(2,1)S(1)}, bf16[128,640]{1,0:T(8,128)(2,1)S(1)}, u32[]{:S(2)}, u32[]{:S(2)}) collective-permute-start(bf16[128,640]{1,0:T(8,128)(2,1)S(1)} %get-tuple-element.34.refs_0_), channel_id=1, source_target_pairs={{0,64},{1,65},{2,66},{3,67},{4,68},{5,69},{6,70},{7,71},{8,72},{9,... | collective-permute-start | bytes 491528 | tf_op jit(solution)/shard_map/ppermute | solution.py:215
  11.2 7.2 %collective-permute-start.4 = (bf16[128,640]{1,0:T(8,128)(2,1)S(1)}, bf16[128,640]{1,0:T(8,128)(2,1)S(1)}, u32[]{:S(2)}, u32[]{:S(2)}) collective-permute-start(bf16[128,640]{1,0:T(8,128)(2,1)S(1)} %get-tuple-element.34.refs_0_), channel_id=1, source_target_pairs={{0,128},{1,129},{2,130},{3,131},{4,132},{5,133},{6,134},{7,135},{8... | collective-permute-start | bytes 491528 | tf_op jit(solution)/shard_map/ppermute | solution.py:215
  13.7 4.8 %collective-permute-start.3 = (bf16[128,640]{1,0:T(8,128)(2,1)S(1)}, bf16[128,640]{1,0:T(8,128)(2,1)S(1)}, u32[]{:S(2)}, u32[]{:S(2)}) collective-permute-start(bf16[128,640]{1,0:T(8,128)(2,1)S(1)} %get-tuple-element.34.refs_0_), channel_id=1, source_target_pairs={{0,192},{1,193},{2,194},{3,195},{4,196},{5,197},{6,198},{7,199},{8... | collective-permute-start | bytes 491528 | tf_op jit(solution)/shard_map/ppermute | solution.py:215
  14.8 3.9 %collective-permute-start.1 = (bf16[128,384]{1,0:T(8,128)(2,1)S(1)}, bf16[128,384]{1,0:T(8,128)(2,1)S(1)}, u32[]{:S(2)}, u32[]{:S(2)}) collective-permute-start(bf16[128,384]{1,0:T(8,128)(2,1)S(1)} %get-tuple-element.33), channel_id=1, source_target_pairs={{0,16},{16,0},{1,17},{17,1},{2,18},{18,2},{3,19},{19,3},{4,20},{20... | collective-permute-start | bytes 294920 | tf_op jit(solution)/shard_map/ppermute | solution.py:200
  16.8 2.0 %collective-permute-start.2 = (bf16[128,384]{1,0:T(8,128)(2,1)S(1)}, bf16[128,384]{1,0:T(8,128)(2,1)S(1)}, u32[]{:S(2)}, u32[]{:S(2)}) collective-permute-start(bf16[128,384]{1,0:T(8,128)(2,1)S(1)} %collective-permute-done), channel_id=1, source_target_pairs={{0,16},{16,0},{1,17},{17,1},{2,18},{18,2},{3,19},{19,3},{4,20},{20... | collective-permute-start | bytes 294920 | tf_op jit(solution)/shard_map/ppermute | solution.py:200
  18.8 11.7 %copy-start = (bf16[2,128,128]{2,1,0:T(8,128)(2,1)S(1)}, bf16[2,128,128]{2,1,0:T(8,128)(2,1)}, u32[]{:S(2)}) copy-start(bf16[2,128,128]{2,1,0:T(8,128)(2,1)} %constant.4.clone.table) | copy-start | bytes 196612
  18.8 8.4 %collective-permute-start.6 = (bf16[512,384]{1,0:T(8,128)(2,1)S(1)}, bf16[512,384]{1,0:T(8,128)(2,1)S(1)}, u32[]{:S(2)}, u32[]{:S(2)}) collective-permute-start(bf16[512,384]{1,0:T(8,128)(2,1)S(1)} %pad_maximum_fusion.refs_0_), channel_id=1, source_target_pairs={{0,4},{1,5},{2,6},{3,7},{4,8},{5,9},{6,10},{7,11},{8,12},{9,13},{1... | collective-permute-start | bytes 1179656 | tf_op jit(solution)/shard_map/ppermute | solution.py:215
  19.9 10.5 %collective-permute-start.12 = (bf16[640,256]{1,0:T(8,128)(2,1)S(1)}, bf16[640,256]{1,0:T(8,128)(2,1)S(1)}, u32[]{:S(2)}, u32[]{:S(2)}) collective-permute-start(bf16[640,256]{1,0:T(8,128)(2,1)S(1)} %get-tuple-element.39.rows_ref), channel_id=1, source_target_pairs={{0,1},{1,2},{2,3},{3,0},{4,5},{5,6},{6,7},{7,4},{8,9},{9,10},{10,1... | collective-permute-start | bytes 983048 | tf_op jit(solution)/shard_map/ppermute | solution.py:215
  21.2 10.9 %collective-permute-start.11 = (bf16[640,256]{1,0:T(8,128)(2,1)S(1)}, bf16[640,256]{1,0:T(8,128)(2,1)S(1)}, u32[]{:S(2)}, u32[]{:S(2)}) collective-permute-start(bf16[640,256]{1,0:T(8,128)(2,1)S(1)} %get-tuple-element.39.rows_ref), channel_id=1, source_target_pairs={{0,2},{1,3},{2,0},{3,1},{4,6},{5,7},{6,4},{7,5},{8,10},{9,11},{10,... | collective-permute-start | bytes 983048 | tf_op jit(solution)/shard_map/ppermute | solution.py:215
  23.8 9.8 %collective-permute-start.10 = (bf16[640,256]{1,0:T(8,128)(2,1)S(1)}, bf16[640,256]{1,0:T(8,128)(2,1)S(1)}, u32[]{:S(2)}, u32[]{:S(2)}) collective-permute-start(bf16[640,256]{1,0:T(8,128)(2,1)S(1)} %get-tuple-element.39.rows_ref), channel_id=1, source_target_pairs={{0,3},{1,0},{2,1},{3,2},{4,7},{5,4},{6,5},{7,6},{8,11},{9,8},{10,9... | collective-permute-start | bytes 983048 | tf_op jit(solution)/shard_map/ppermute | solution.py:215
  24.9 8.7 %collective-permute-start.9 = (bf16[256,384]{1,0:T(8,128)(2,1)S(1)}, bf16[256,384]{1,0:T(8,128)(2,1)S(1)}, u32[]{:S(2)}, u32[]{:S(2)}) collective-permute-start(bf16[256,384]{1,0:T(8,128)(2,1)S(1)} %pad_maximum_fusion.1), channel_id=1, source_target_pairs={{0,8},{1,9},{2,10},{3,11},{4,12},{5,13},{6,14},{7,15},{8,32},{9,33... | collective-permute-start | bytes 589832 | tf_op jit(solution)/shard_map/ppermute | solution.py:215
  27.2 6.4 %collective-permute-start.8 = (bf16[256,384]{1,0:T(8,128)(2,1)S(1)}, bf16[256,384]{1,0:T(8,128)(2,1)S(1)}, u32[]{:S(2)}, u32[]{:S(2)}) collective-permute-start(bf16[256,384]{1,0:T(8,128)(2,1)S(1)} %get-tuple-element.64), channel_id=1, source_target_pairs={{0,16},{16,0},{1,17},{17,1},{2,18},{18,2},{3,19},{19,3},{4,20},{20... | collective-permute-start | bytes 589832 | tf_op jit(solution)/shard_map/ppermute | solution.py:200
  30.4 3.3 %collective-permute-start.7 = (bf16[256,384]{1,0:T(8,128)(2,1)S(1)}, bf16[256,384]{1,0:T(8,128)(2,1)S(1)}, u32[]{:S(2)}, u32[]{:S(2)}) collective-permute-start(bf16[256,384]{1,0:T(8,128)(2,1)S(1)} %get-tuple-element.65), channel_id=1, source_target_pairs={{0,16},{16,0},{1,17},{17,1},{2,18},{18,2},{3,19},{19,3},{4,20},{20... | collective-permute-start | bytes 589832 | tf_op jit(solution)/shard_map/ppermute | solution.py:200
  33.6 5.7 %collective-permute-start.13 = (bf16[256,384]{1,0:T(8,128)(2,1)S(1)}, bf16[256,384]{1,0:T(8,128)(2,1)S(1)}, u32[]{:S(2)}, u32[]{:S(2)}) collective-permute-start(bf16[256,384]{1,0:T(8,128)(2,1)S(1)} %collective-permute-done.9.refs_4_.refs_3_), channel_id=1, source_target_pairs={{0,16},{16,0},{1,17},{17,1},{2,18},{18,2},{3,19},{19,3},{4,20},{20... | collective-permute-start | bytes 589832 | tf_op jit(solution)/shard_map/ppermute | solution.py:200
  39.9 10.2 %collective-permute-start.15 = (bf16[512,256]{1,0:T(8,128)(2,1)S(1)}, bf16[512,256]{1,0:T(8,128)(2,1)S(1)}, u32[]{:S(2)}, u32[]{:S(2)}) collective-permute-start(bf16[512,256]{1,0:T(8,128)(2,1)S(1)} %tile.12), channel_id=1, source_target_pairs={{0,3},{1,0},{2,1},{3,2},{4,7},{5,4},{6,5},{7,6},{8,11},{9,8},{10,9... | collective-permute-start | bytes 786440 | tf_op jit(solution)/shard_map/ppermute | solution.py:215
  43.7 6.8 %collective-permute-start.14 = (bf16[512,256]{1,0:T(8,128)(2,1)S(1)}, bf16[512,256]{1,0:T(8,128)(2,1)S(1)}, u32[]{:S(2)}, u32[]{:S(2)}) collective-permute-start(bf16[512,256]{1,0:T(8,128)(2,1)S(1)} %tile.10), channel_id=1, source_target_pairs={{0,2},{1,3},{2,0},{3,1},{4,6},{5,7},{6,4},{7,5},{8,10},{9,11},{10,... | collective-permute-start | bytes 786440 | tf_op jit(solution)/shard_map/ppermute | solution.py:215
  47.1 6.8 %collective-permute-start.16 = (bf16[512,256]{1,0:T(8,128)(2,1)S(1)}, bf16[512,256]{1,0:T(8,128)(2,1)S(1)}, u32[]{:S(2)}, u32[]{:S(2)}) collective-permute-start(bf16[512,256]{1,0:T(8,128)(2,1)S(1)} %tile.13), channel_id=1, source_target_pairs={{0,1},{1,2},{2,3},{3,0},{4,5},{5,6},{6,7},{7,4},{8,9},{9,10},{10,1... | collective-permute-start | bytes 786440 | tf_op jit(solution)/shard_map/ppermute | solution.py:215
  65.2 16.4 %all-to-all-start.1 = ((bf16[16,32,256]{2,1,0:T(8,128)(2,1)}), bf16[16,32,256]{2,1,0:T(8,128)(2,1)S(1)}, u32[]{:S(2)}, u32[]{:S(2)}) async-start(bf16[16,32,256]{2,1,0:T(8,128)(2,1)} %sum_spread.2), calls=%async_computation.1 | async-start | bytes 524288 | tf_op jit(solution)/shard_map/all_to_all | solution.py:223
  72.0 5.3 %collective-permute-start.17 = (bf16[128,256]{1,0:T(8,128)(2,1)S(1)}, bf16[128,256]{1,0:T(8,128)(2,1)S(1)}, u32[]{:S(2)}, u32[]{:S(2)}) collective-permute-start(bf16[128,256]{1,0:T(8,128)(2,1)S(1)} %get-tuple-element.59), channel_id=1, source_target_pairs={{0,64},{1,65},{2,66},{3,67},{4,68},{5,69},{6,70},{7,71},{8,72},{9,... | collective-permute-start | bytes 196616 | tf_op jit(solution)/shard_map/ppermute | solution.py:215
  72.3 5.0 %collective-permute-start.18 = (bf16[128,256]{1,0:T(8,128)(2,1)S(1)}, bf16[128,256]{1,0:T(8,128)(2,1)S(1)}, u32[]{:S(2)}, u32[]{:S(2)}) collective-permute-start(bf16[128,256]{1,0:T(8,128)(2,1)S(1)} %get-tuple-element.60), channel_id=1, source_target_pairs={{0,128},{1,129},{2,130},{3,131},{4,132},{5,133},{6,134},{7,135},{8... | collective-permute-start | bytes 196616 | tf_op jit(solution)/shard_map/ppermute | solution.py:215
  73.7 4.2 %collective-permute-start.19 = (bf16[128,256]{1,0:T(8,128)(2,1)S(1)}, bf16[128,256]{1,0:T(8,128)(2,1)S(1)}, u32[]{:S(2)}, u32[]{:S(2)}) collective-permute-start(bf16[128,256]{1,0:T(8,128)(2,1)S(1)} %get-tuple-element.61), channel_id=1, source_target_pairs={{0,192},{1,193},{2,194},{3,195},{4,196},{5,197},{6,198},{7,199},{8... | collective-permute-start | bytes 196616 | tf_op jit(solution)/shard_map/ppermute | solution.py:215

commit v17 on v16

--- a/solution.py
+++ b/solution.py
@@ -34,7 +34,7 @@
 
 def pack_kernel(embeds, weight, solve, probes, probe_solves, packed, extended, weight_in, solve_in, probes_in, probe_solves_in, sems):
     rows, width = embeds.shape[0], weight.shape[1]
-    embeds_in = extended.at[:, 128:]
+    embeds_in = extended.at[:rows, :]
     loads = [
         pltpu.make_async_copy(source, target, sems.at[k])
         for k, (source, target) in enumerate(
@@ -49,14 +49,8 @@
     ]
     for load in loads:
         load.start()
-    for load in loads:
+    for load in loads[2:]:
         load.wait()
-    feats = jnp.dot(embeds_in[...], weight_in[...], preferred_element_type=F32).astype(BF16)
-    wide = feats.astype(F32)
-    sq = jnp.sum(wide * wide, axis=1, keepdims=True)
-    sq_hi = sq.astype(BF16).astype(F32)
-    sq_mid = (sq - sq_hi).astype(BF16).astype(F32)
-    sq_lo = sq - sq_hi - sq_mid
     fold = math.sqrt(5.0 / 3.0 * ROOT5)
     scale = (2.0 * probes.shape[0]) ** (-0.5) * fold
     both = jnp.concatenate(
@@ -65,24 +59,38 @@
     ).T
     hi = both.astype(BF16).astype(F32)
     lo = both - hi
+    pair = jnp.concatenate([hi, lo], axis=1)
+    part = rows // 8
+    extended[rows:, :] = jnp.concatenate(
+        [pair[k * part : (k + 1) * part] for k in range(8)], axis=1
+    ).astype(BF16)
+    for load in loads[:2]:
+        load.wait()
+    feats = jnp.dot(embeds_in[...], weight_in[...], preferred_element_type=F32).astype(BF16)
+    wide = feats.astype(F32)
+    sq = jnp.sum(wide * wide, axis=1, keepdims=True)
+    sq_hi = sq.astype(BF16).astype(F32)
+    sq_mid = (sq - sq_hi).astype(BF16).astype(F32)
+    sq_lo = sq - sq_hi - sq_mid
     lane = lax.broadcasted_iota(jnp.int32, (rows, 32), 1)
     tail = jnp.where(lane == 0, sq_hi, jnp.where(lane == 1, sq_mid, jnp.where(lane == 2, sq_lo, 0.0)))
-    tail = jnp.concatenate([hi, lo, hi, tail], axis=1).astype(BF16)
-    extended[:, :128] = tail
     packed[:, :width] = feats
-    packed[:, width:] = tail
+    packed[:, width:] = jnp.concatenate([pair, hi, tail], axis=1).astype(BF16)
 
 
 def split_kernel(count, weight, *refs):
     line, embeds = refs[count:]
-    rows, width = refs[0].shape[0], weight.shape[1]
+    rows = embeds.shape[0] // count
     for k, ref in enumerate(refs[:count]):
         block = slice(k * rows, (k + 1) * rows)
-        own = ref[:, 128:]
+        own = ref[:rows, :]
         line[block, :] = jnp.dot(own, weight[...], preferred_element_type=F32).astype(BF16)
         embeds[block, :] = own
     for k in range(0, count, 2):
-        both = [ref[:, :64].astype(F32) for ref in refs[k : k + 2]]
+        both = []
+        for ref in refs[k : k + 2]:
+            folded = ref[rows:, :].astype(F32)
+            both.append(jnp.concatenate([folded[:, 64 * p : 64 * p + 64] for p in range(8)], axis=0))
         line[count * rows :, k * 64 : k * 64 + 128] = jnp.concatenate(both, axis=1).astype(BF16)
 
 
@@ -230,7 +238,7 @@
         pack_kernel,
         out_shape=[
             jax.ShapeDtypeStruct((rows, width + 128), BF16),
-            jax.ShapeDtypeStruct((rows, 128 + embeds.shape[1]), BF16),
+            jax.ShapeDtypeStruct((rows + rows // 8, embeds.shape[1]), BF16),
         ],
         in_specs=[pl.BlockSpec(memory_space=pltpu.HBM)] * 5,
         out_specs=[VMEM] * 2,

time: 94.5 us -> 94.5 us (level)
  transfers between devices with their start and end apart: 21 -> 21, of which waited for: 6 -> 7; matrix products, arithmetic and copies ran while one was open for 0% -> 0% of each run, Pallas kernels for 13% -> 13%
where the time goes in v17:
time: 94.5 us; the launch traced here: 93.2 us
  starting transfers between devices  44.2 us (47%)
  blocking collectives  20.8 us (22%)
  Pallas kernels  15.7 us (17%)
  waiting for transfers between devices  10.5 us (11%)
    all_to_all x2, blocking collectives, exchange(): return lax.all_to_all(array, axes, split_axis=0, concat_axis=0, tiled=True)  20.8 us
    ppermute x14, starting transfers between devices, move(): return lax.ppermute(array, ALL, perm)  19.8 us
    ppermute x6, starting transfers between devices, ring(): lax.ppermute(array, axis, [(i, (i + shift) % size) for i in range(size)])  17.2 us
    pallas_call x7, Pallas kernels, tile(): pl.pallas_call(functools.partial(tile_kernel, 256, 256, start is not None...  11.6 us
    ppermute x14, waiting for transfers between devices, move(): return lax.ppermute(array, ALL, perm)  7.54 us
    all_to_all x1, starting transfers between devices, exchange(): return lax.all_to_all(array, axes, split_axis=0, concat_axis=0, tiled=True)  7.2 us
    all_to_all x1, waiting for transfers between devices, exchange(): return lax.all_to_all(array, axes, split_axis=0, concat_axis=0, tiled=True)  2.99 us
  transfers between devices with their start and end apart: 21, of which 7 were waited for; matrix products, arithmetic and copies ran while one was open for 0% of the time, Pallas kernels for 13%

profile of v17, /device:TPU:1, one launch (start us, length us, event | category | flops | bytes accessed | tf_op | source)
XLA Modules:
  0.0 93.2 jit_solution(7643045621530305464)
XLA Ops:
  0.6 1.5 %pack.1 = (bf16[128,384]{1,0:T(8,128)(2,1)S(1)}, bf16[144,512]{1,0:T(8,128)(2,1)S(1)}) custom-call(bf16[128,512]{1,0:T(8,128)(2,1)} %embeds.1, bf16[512,256]{1,0:T(8,128)(2,1)} %weight.3, f32[1,128]{1,0:T(1,128)} %bitcast.9, f32[15,128]{1,0:T(8,128)} %bitcast.7, f32[15,128]{1,0:T(8,128)} %bitcast.8), custom_call_target="tpu_custom_call" | custom-call | tf_op jit(solution)/shard_map/pack/pallas_call | solution.py:237
  2.1 0.0 copy-start.1
  2.2 7.8 %collective-permute-start = (bf16[128,384]{1,0:T(8,128)(2,1)S(1)}, bf16[128,384]{1,0:T(8,128)(2,1)S(1)}, u32[]{:S(2)}, u32[]{:S(2)}) collective-permute-start(bf16[128,384]{1,0:T(8,128)(2,1)S(1)} %get-tuple-element.33), channel_id=1, source_target_pairs={{0,32},{4,36},{8,40},{12,44},{32,0},{36,4},{40,8},{44,12},{1,33},{... | collective-permute-start | bytes 294920 | tf_op jit(solution)/shard_map/ppermute | solution.py:208
  10.0 1.2 %collective-permute-start.5 = (bf16[144,512]{1,0:T(8,128)(2,1)S(1)}, bf16[144,512]{1,0:T(8,128)(2,1)S(1)}, u32[]{:S(2)}, u32[]{:S(2)}) collective-permute-start(bf16[144,512]{1,0:T(8,128)(2,1)S(1)} %get-tuple-element.34.refs_0_), channel_id=1, source_target_pairs={{0,64},{1,65},{2,66},{3,67},{4,68},{5,69},{6,70},{7,71},{8,72},{9,... | collective-permute-start | bytes 442376 | tf_op jit(solution)/shard_map/ppermute | solution.py:223
  11.2 2.4 %collective-permute-start.4 = (bf16[144,512]{1,0:T(8,128)(2,1)S(1)}, bf16[144,512]{1,0:T(8,128)(2,1)S(1)}, u32[]{:S(2)}, u32[]{:S(2)}) collective-permute-start(bf16[144,512]{1,0:T(8,128)(2,1)S(1)} %get-tuple-element.34.refs_0_), channel_id=1, source_target_pairs={{0,128},{1,129},{2,130},{3,131},{4,132},{5,133},{6,134},{7,135},{8... | collective-permute-start | bytes 442376 | tf_op jit(solution)/shard_map/ppermute | solution.py:223
  13.6 1.2 %collective-permute-start.3 = (bf16[144,512]{1,0:T(8,128)(2,1)S(1)}, bf16[144,512]{1,0:T(8,128)(2,1)S(1)}, u32[]{:S(2)}, u32[]{:S(2)}) collective-permute-start(bf16[144,512]{1,0:T(8,128)(2,1)S(1)} %get-tuple-element.34.refs_0_), channel_id=1, source_target_pairs={{0,192},{1,193},{2,194},{3,195},{4,196},{5,197},{6,198},{7,199},{8... | collective-permute-start | bytes 442376 | tf_op jit(solution)/shard_map/ppermute | solution.py:223
  14.8 2.0 %collective-permute-start.1 = (bf16[128,384]{1,0:T(8,128)(2,1)S(1)}, bf16[128,384]{1,0:T(8,128)(2,1)S(1)}, u32[]{:S(2)}, u32[]{:S(2)}) collective-permute-start(bf16[128,384]{1,0:T(8,128)(2,1)S(1)} %get-tuple-element.33), channel_id=1, source_target_pairs={{0,16},{16,0},{1,17},{17,1},{2,18},{18,2},{3,19},{19,3},{4,20},{20... | collective-permute-start | bytes 294920 | tf_op jit(solution)/shard_map/ppermute | solution.py:208
  16.8 0.0 collective-permute-start.2
  16.8 0.9 %collective-permute-done.4.refs_2_ = bf16[144,512]{1,0:T(8,128)(2,1)S(1)} collective-permute-done((bf16[144,512]{1,0:T(8,128)(2,1)S(1)}, bf16[144,512]{1,0:T(8,128)(2,1)S(1)}, u32[]{:S(2)}, u32[]{:S(2)}) %collective-permute-start.4) | collective-permute-done | bytes 147488 | tf_op jit(solution)/shard_map/ppermute | solution.py:223
  17.7 0.0 collective-permute-done.3.refs_1_
  17.7 0.3 split.1
  18.1 0.0 collective-permute-done.2
  18.1 0.0 copy-start
  18.2 1.7 %collective-permute-start.6 = (bf16[512,384]{1,0:T(8,128)(2,1)S(1)}, bf16[512,384]{1,0:T(8,128)(2,1)S(1)}, u32[]{:S(2)}, u32[]{:S(2)}) collective-permute-start(bf16[512,384]{1,0:T(8,128)(2,1)S(1)} %pad_maximum_fusion.refs_0_), channel_id=1, source_target_pairs={{0,4},{1,5},{2,6},{3,7},{4,8},{5,9},{6,10},{7,11},{8,12},{9,13},{1... | collective-permute-start | bytes 1179656 | tf_op jit(solution)/shard_map/ppermute | solution.py:223
  19.9 1.3 %collective-permute-start.12 = (bf16[640,256]{1,0:T(8,128)(2,1)S(1)}, bf16[640,256]{1,0:T(8,128)(2,1)S(1)}, u32[]{:S(2)}, u32[]{:S(2)}) collective-permute-start(bf16[640,256]{1,0:T(8,128)(2,1)S(1)} %get-tuple-element.39.rows_ref), channel_id=1, source_target_pairs={{0,1},{1,2},{2,3},{3,0},{4,5},{5,6},{6,7},{7,4},{8,9},{9,10},{10,1... | collective-permute-start | bytes 983048 | tf_op jit(solution)/shard_map/ppermute | solution.py:223
  21.2 2.6 %collective-permute-start.11 = (bf16[640,256]{1,0:T(8,128)(2,1)S(1)}, bf16[640,256]{1,0:T(8,128)(2,1)S(1)}, u32[]{:S(2)}, u32[]{:S(2)}) collective-permute-start(bf16[640,256]{1,0:T(8,128)(2,1)S(1)} %get-tuple-element.39.rows_ref), channel_id=1, source_target_pairs={{0,2},{1,3},{2,0},{3,1},{4,6},{5,7},{6,4},{7,5},{8,10},{9,11},{10,... | collective-permute-start | bytes 983048 | tf_op jit(solution)/shard_map/ppermute | solution.py:223
  23.8 1.1 %collective-permute-start.10 = (bf16[640,256]{1,0:T(8,128)(2,1)S(1)}, bf16[640,256]{1,0:T(8,128)(2,1)S(1)}, u32[]{:S(2)}, u32[]{:S(2)}) collective-permute-start(bf16[640,256]{1,0:T(8,128)(2,1)S(1)} %get-tuple-element.39.rows_ref), channel_id=1, source_target_pairs={{0,3},{1,0},{2,1},{3,2},{4,7},{5,4},{6,5},{7,6},{8,11},{9,8},{10,9... | collective-permute-start | bytes 983048 | tf_op jit(solution)/shard_map/ppermute | solution.py:223
  24.8 2.3 %collective-permute-start.9 = (bf16[256,384]{1,0:T(8,128)(2,1)S(1)}, bf16[256,384]{1,0:T(8,128)(2,1)S(1)}, u32[]{:S(2)}, u32[]{:S(2)}) collective-permute-start(bf16[256,384]{1,0:T(8,128)(2,1)S(1)} %pad_maximum_fusion.1), channel_id=1, source_target_pairs={{0,8},{1,9},{2,10},{3,11},{4,12},{5,13},{6,14},{7,15},{8,32},{9,33... | collective-permute-start | bytes 589832 | tf_op jit(solution)/shard_map/ppermute | solution.py:223
  27.2 2.9 %collective-permute-start.8 = (bf16[256,384]{1,0:T(8,128)(2,1)S(1)}, bf16[256,384]{1,0:T(8,128)(2,1)S(1)}, u32[]{:S(2)}, u32[]{:S(2)}) collective-permute-start(bf16[256,384]{1,0:T(8,128)(2,1)S(1)} %get-tuple-element.64), channel_id=1, source_target_pairs={{0,16},{16,0},{1,17},{17,1},{2,18},{18,2},{3,19},{19,3},{4,20},{20... | collective-permute-start | bytes 589832 | tf_op jit(solution)/shard_map/ppermute | solution.py:208
  30.2 0.2 collective-permute-start.7
  30.3 1.5 %tile.8.refs_0_ = f32[512,256]{1,0:T(8,128)S(1)} custom-call(bf16[2,128,128]{2,1,0:T(8,128)(2,1)S(1)} %copy-done, bf16[640,256]{1,0:T(8,128)(2,1)S(1)} %collective-permute-done.12.rows_ref, bf16[512,384]{1,0:T(8,128)(2,1)S(1)} %pad_maximum_fusion.refs_0_, bf16[512,384]{1,0:T(8,128)(2,1)S(1)} %collective-permute-done.6.refs_1_), custom_call_target="tpu_custom_call" | custom-call | tf_op jit(solution)/shard_map/tile/pallas_call | solution.py:278
  31.9 0.2 collective-permute-done.11.rows_ref
  32.0 1.5 %tile.7.refs_0_ = f32[512,256]{1,0:T(8,128)S(1)} custom-call(bf16[2,128,128]{2,1,0:T(8,128)(2,1)S(1)} %copy-done, bf16[640,256]{1,0:T(8,128)(2,1)S(1)} %collective-permute-done.11.rows_ref, bf16[512,384]{1,0:T(8,128)(2,1)S(1)} %pad_maximum_fusion.refs_0_, bf16[512,384]{1,0:T(8,128)(2,1)S(1)} %collective-permute-done.6.refs_1_), custom_call_target="tpu_custom_call" | custom-call | tf_op jit(solution)/shard_map/tile/pallas_call | solution.py:278
  33.6 4.3 %collective-permute-start.13 = (bf16[256,384]{1,0:T(8,128)(2,1)S(1)}, bf16[256,384]{1,0:T(8,128)(2,1)S(1)}, u32[]{:S(2)}, u32[]{:S(2)}) collective-permute-start(bf16[256,384]{1,0:T(8,128)(2,1)S(1)} %collective-permute-done.9.refs_4_.refs_3_), channel_id=1, source_target_pairs={{0,16},{16,0},{1,17},{17,1},{2,18},{18,2},{3,19},{19,3},{4,20},{20... | collective-permute-start | bytes 589832 | tf_op jit(solution)/shard_map/ppermute | solution.py:208
  37.9 1.2 %tile.11.refs_0_ = f32[512,256]{1,0:T(8,128)S(1)} custom-call(bf16[2,128,128]{2,1,0:T(8,128)(2,1)S(1)} %copy-done, bf16[640,256]{1,0:T(8,128)(2,1)S(1)} %collective-permute-done.12.rows_ref, f32[512,256]{1,0:T(8,128)S(1)} %tile.8.refs_0_, bf16[256,384]{1,0:T(8,128)(2,1)S(1)} %collective-permute-done.7.refs_2_.refs_1_, ...), custom_call_target="tpu_custom_call" | custom-call | tf_op jit(solution)/shard_map/tile/pallas_call | solution.py:278
  39.1 0.6 tile.12
  39.7 2.4 %collective-permute-start.15 = (bf16[512,256]{1,0:T(8,128)(2,1)S(1)}, bf16[512,256]{1,0:T(8,128)(2,1)S(1)}, u32[]{:S(2)}, u32[]{:S(2)}) collective-permute-start(bf16[512,256]{1,0:T(8,128)(2,1)S(1)} %tile.12), channel_id=1, source_target_pairs={{0,3},{1,0},{2,1},{3,2},{4,7},{5,4},{6,5},{7,6},{8,11},{9,8},{10,9... | collective-permute-start | bytes 786440 | tf_op jit(solution)/shard_map/ppermute | solution.py:223
  42.1 1.4 %tile.10 = bf16[512,256]{1,0:T(8,128)(2,1)S(1)} custom-call(bf16[2,128,128]{2,1,0:T(8,128)(2,1)S(1)} %copy-done, bf16[640,256]{1,0:T(8,128)(2,1)S(1)} %collective-permute-done.11.rows_ref, f32[512,256]{1,0:T(8,128)S(1)} %tile.7.refs_0_, bf16[256,384]{1,0:T(8,128)(2,1)S(1)} %collective-permute-done.7.refs_2_.refs_1_, ...), custom_call_target="tpu_custom_call" | custom-call | tf_op jit(solution)/shard_map/tile/pallas_call | solution.py:278
  43.5 0.5 collective-permute-start.14
  44.0 2.7 %tile.13 = bf16[512,256]{1,0:T(8,128)(2,1)S(1)} custom-call(bf16[2,128,128]{2,1,0:T(8,128)(2,1)S(1)} %copy-done, bf16[640,256]{1,0:T(8,128)(2,1)S(1)} %collective-permute-done.10.rows_ref, bf16[512,384]{1,0:T(8,128)(2,1)S(1)} %pad_maximum_fusion.refs_0_, bf16[512,384]{1,0:T(8,128)(2,1)S(1)} %collective-permute-done.6.refs_1_, ...), custom_call_target="tpu_custom_call" | custom-call | tf_op jit(solution)/shard_map/tile/pallas_call | solution.py:278
  46.7 0.4 collective-permute-start.16
  47.1 2.7 %tile.9.a = f32[512,256]{1,0:T(8,128)S(1)} custom-call(bf16[2,128,128]{2,1,0:T(8,128)(2,1)S(1)} %copy-done, bf16[640,256]{1,0:T(8,128)(2,1)S(1)} %get-tuple-element.39.rows_ref, bf16[512,384]{1,0:T(8,128)(2,1)S(1)} %pad_maximum_fusion.refs_0_, bf16[512,384]{1,0:T(8,128)(2,1)S(1)} %collective-permute-done.6.refs_1_, ...), custom_call_target="tpu_custom_call" | custom-call | tf_op jit(solution)/shard_map/tile/pallas_call | solution.py:278
  49.8 0.6 collective-permute-done.14.b
  50.3 0.5 sum_rows.1
  50.8 2.7 %collective-permute-done.16.last = bf16[512,256]{1,0:T(8,128)(2,1)S(1)} collective-permute-done((bf16[512,256]{1,0:T(8,128)(2,1)S(1)}, bf16[512,256]{1,0:T(8,128)(2,1)S(1)}, u32[]{:S(2)}, u32[]{:S(2)}) %collective-permute-start.16) | collective-permute-done | bytes 262176 | tf_op jit(solution)/shard_map/ppermute | solution.py:223
  53.5 0.3 last_rows.1
  53.9 10.1 %all_to_all.15.refs_0_ = bf16[16,32,256]{2,1,0:T(8,128)(2,1)S(1)} all-to-all(bf16[16,32,256]{2,1,0:T(8,128)(2,1)S(1)} %bitcast.5), channel_id=1, replica_groups=mesh['y'=4,'zh'=2,'core'=2,'zl'=4,'x'=4] {'y','x'}, dimensions={0} | all-to-all | bytes 524288 | tf_op jit(solution)/shard_map/all_to_all | solution.py:231
  64.0 0.8 sum_spread.2
  64.8 7.2 %all-to-all-start.1 = ((bf16[16,32,256]{2,1,0:T(8,128)(2,1)}), bf16[16,32,256]{2,1,0:T(8,128)(2,1)S(1)}, u32[]{:S(2)}, u32[]{:S(2)}) async-start(bf16[16,32,256]{2,1,0:T(8,128)(2,1)} %sum_spread.2), calls=%async_computation.1 | async-start | bytes 524288 | tf_op jit(solution)/shard_map/all_to_all | solution.py:231
  72.0 0.3 collective-permute-start.17
  72.3 1.4 %collective-permute-start.18 = (bf16[128,256]{1,0:T(8,128)(2,1)S(1)}, bf16[128,256]{1,0:T(8,128)(2,1)S(1)}, u32[]{:S(2)}, u32[]{:S(2)}) collective-permute-start(bf16[128,256]{1,0:T(8,128)(2,1)S(1)} %get-tuple-element.60), channel_id=1, source_target_pairs={{0,128},{1,129},{2,130},{3,131},{4,132},{5,133},{6,134},{7,135},{8... | collective-permute-start | bytes 196616 | tf_op jit(solution)/shard_map/ppermute | solution.py:223
  73.6 1.1 %collective-permute-start.19 = (bf16[128,256]{1,0:T(8,128)(2,1)S(1)}, bf16[128,256]{1,0:T(8,128)(2,1)S(1)}, u32[]{:S(2)}, u32[]{:S(2)}) collective-permute-start(bf16[128,256]{1,0:T(8,128)(2,1)S(1)} %get-tuple-element.61), channel_id=1, source_target_pairs={{0,192},{1,193},{2,194},{3,195},{4,196},{5,197},{6,198},{7,199},{8... | collective-permute-start | bytes 196616 | tf_op jit(solution)/shard_map/ppermute | solution.py:223
  74.8 2.5 %collective-permute-done.17.b = bf16[128,256]{1,0:T(8,128)(2,1)S(1)} collective-permute-done((bf16[128,256]{1,0:T(8,128)(2,1)S(1)}, bf16[128,256]{1,0:T(8,128)(2,1)S(1)}, u32[]{:S(2)}, u32[]{:S(2)}) %collective-permute-start.17) | collective-permute-done | bytes 65568 | tf_op jit(solution)/shard_map/ppermute | solution.py:223
  77.3 0.6 collective-permute-done.19.d
  77.9 0.7 finish_rows.1
  78.6 3.0 %all-to-all-done.1.refs_0_ = bf16[16,32,256]{2,1,0:T(8,128)(2,1)S(1)} async-done(((bf16[16,32,256]{2,1,0:T(8,128)(2,1)}), bf16[16,32,256]{2,1,0:T(8,128)(2,1)S(1)}, u32[]{:S(2)}, u32[]{:S(2)}) %all-to-all-start.1) | async-done | bytes 262176 | tf_op jit(solution)/shard_map/all_to_all | solution.py:231
  81.6 10.7 %all_to_all.16 = bf16[16,32,256]{2,1,0:T(8,128)(2,1)S(1)} all-to-all(bf16[16,32,256]{2,1,0:T(8,128)(2,1)S(1)} %sum_spread.3), channel_id=1, replica_groups=mesh['y'=4,'zh'=2,'core'=2,'zl'=4,'x'=4] {'y','x'}, dimensions={0} | all-to-all | bytes 524288 | tf_op jit(solution)/shard_map/all_to_all | solution.py:231
  92.3 0.8 convert_multiply_fusion
  (18 shorter events, 0.2 us)
Async XLA Ops:
  2.1 15.6 %copy-start.1 = (bf16[512,256]{1,0:T(8,128)(2,1)S(1)}, bf16[512,256]{1,0:T(8,128)(2,1)}, u32[]{:S(2)}) copy-start(bf16[512,256]{1,0:T(8,128)(2,1)} %weight.3) | copy-start | bytes 786436
  2.2 14.6 %collective-permute-start = (bf16[128,384]{1,0:T(8,128)(2,1)S(1)}, bf16[128,384]{1,0:T(8,128)(2,1)S(1)}, u32[]{:S(2)}, u32[]{:S(2)}) collective-permute-start(bf16[128,384]{1,0:T(8,128)(2,1)S(1)} %get-tuple-element.33), channel_id=1, source_target_pairs={{0,32},{4,36},{8,40},{12,44},{32,0},{36,4},{40,8},{44,12},{1,33},{... | collective-permute-start | bytes 294920 | tf_op jit(solution)/shard_map/ppermute | solution.py:208
  10.0 6.8 %collective-permute-start.5 = (bf16[144,512]{1,0:T(8,128)(2,1)S(1)}, bf16[144,512]{1,0:T(8,128)(2,1)S(1)}, u32[]{:S(2)}, u32[]{:S(2)}) collective-permute-start(bf16[144,512]{1,0:T(8,128)(2,1)S(1)} %get-tuple-element.34.refs_0_), channel_id=1, source_target_pairs={{0,64},{1,65},{2,66},{3,67},{4,68},{5,69},{6,70},{7,71},{8,72},{9,... | collective-permute-start | bytes 442376 | tf_op jit(solution)/shard_map/ppermute | solution.py:223
  11.2 6.6 %collective-permute-start.4 = (bf16[144,512]{1,0:T(8,128)(2,1)S(1)}, bf16[144,512]{1,0:T(8,128)(2,1)S(1)}, u32[]{:S(2)}, u32[]{:S(2)}) collective-permute-start(bf16[144,512]{1,0:T(8,128)(2,1)S(1)} %get-tuple-element.34.refs_0_), channel_id=1, source_target_pairs={{0,128},{1,129},{2,130},{3,131},{4,132},{5,133},{6,134},{7,135},{8... | collective-permute-start | bytes 442376 | tf_op jit(solution)/shard_map/ppermute | solution.py:223
  13.6 4.1 %collective-permute-start.3 = (bf16[144,512]{1,0:T(8,128)(2,1)S(1)}, bf16[144,512]{1,0:T(8,128)(2,1)S(1)}, u32[]{:S(2)}, u32[]{:S(2)}) collective-permute-start(bf16[144,512]{1,0:T(8,128)(2,1)S(1)} %get-tuple-element.34.refs_0_), channel_id=1, source_target_pairs={{0,192},{1,193},{2,194},{3,195},{4,196},{5,197},{6,198},{7,199},{8... | collective-permute-start | bytes 442376 | tf_op jit(solution)/shard_map/ppermute | solution.py:223
  14.8 3.3 %collective-permute-start.1 = (bf16[128,384]{1,0:T(8,128)(2,1)S(1)}, bf16[128,384]{1,0:T(8,128)(2,1)S(1)}, u32[]{:S(2)}, u32[]{:S(2)}) collective-permute-start(bf16[128,384]{1,0:T(8,128)(2,1)S(1)} %get-tuple-element.33), channel_id=1, source_target_pairs={{0,16},{16,0},{1,17},{17,1},{2,18},{18,2},{3,19},{19,3},{4,20},{20... | collective-permute-start | bytes 294920 | tf_op jit(solution)/shard_map/ppermute | solution.py:208
  16.8 1.3 %collective-permute-start.2 = (bf16[128,384]{1,0:T(8,128)(2,1)S(1)}, bf16[128,384]{1,0:T(8,128)(2,1)S(1)}, u32[]{:S(2)}, u32[]{:S(2)}) collective-permute-start(bf16[128,384]{1,0:T(8,128)(2,1)S(1)} %collective-permute-done), channel_id=1, source_target_pairs={{0,16},{16,0},{1,17},{17,1},{2,18},{18,2},{3,19},{19,3},{4,20},{20... | collective-permute-start | bytes 294920 | tf_op jit(solution)/shard_map/ppermute | solution.py:208
  18.1 12.2 %copy-start = (bf16[2,128,128]{2,1,0:T(8,128)(2,1)S(1)}, bf16[2,128,128]{2,1,0:T(8,128)(2,1)}, u32[]{:S(2)}) copy-start(bf16[2,128,128]{2,1,0:T(8,128)(2,1)} %constant.4.clone.table) | copy-start | bytes 196612
  18.2 9.0 %collective-permute-start.6 = (bf16[512,384]{1,0:T(8,128)(2,1)S(1)}, bf16[512,384]{1,0:T(8,128)(2,1)S(1)}, u32[]{:S(2)}, u32[]{:S(2)}) collective-permute-start(bf16[512,384]{1,0:T(8,128)(2,1)S(1)} %pad_maximum_fusion.refs_0_), channel_id=1, source_target_pairs={{0,4},{1,5},{2,6},{3,7},{4,8},{5,9},{6,10},{7,11},{8,12},{9,13},{1... | collective-permute-start | bytes 1179656 | tf_op jit(solution)/shard_map/ppermute | solution.py:223
  19.9 10.3 %collective-permute-start.12 = (bf16[640,256]{1,0:T(8,128)(2,1)S(1)}, bf16[640,256]{1,0:T(8,128)(2,1)S(1)}, u32[]{:S(2)}, u32[]{:S(2)}) collective-permute-start(bf16[640,256]{1,0:T(8,128)(2,1)S(1)} %get-tuple-element.39.rows_ref), channel_id=1, source_target_pairs={{0,1},{1,2},{2,3},{3,0},{4,5},{5,6},{6,7},{7,4},{8,9},{9,10},{10,1... | collective-permute-start | bytes 983048 | tf_op jit(solution)/shard_map/ppermute | solution.py:223
  21.2 10.9 %collective-permute-start.11 = (bf16[640,256]{1,0:T(8,128)(2,1)S(1)}, bf16[640,256]{1,0:T(8,128)(2,1)S(1)}, u32[]{:S(2)}, u32[]{:S(2)}) collective-permute-start(bf16[640,256]{1,0:T(8,128)(2,1)S(1)} %get-tuple-element.39.rows_ref), channel_id=1, source_target_pairs={{0,2},{1,3},{2,0},{3,1},{4,6},{5,7},{6,4},{7,5},{8,10},{9,11},{10,... | collective-permute-start | bytes 983048 | tf_op jit(solution)/shard_map/ppermute | solution.py:223
  23.8 9.8 %collective-permute-start.10 = (bf16[640,256]{1,0:T(8,128)(2,1)S(1)}, bf16[640,256]{1,0:T(8,128)(2,1)S(1)}, u32[]{:S(2)}, u32[]{:S(2)}) collective-permute-start(bf16[640,256]{1,0:T(8,128)(2,1)S(1)} %get-tuple-element.39.rows_ref), channel_id=1, source_target_pairs={{0,3},{1,0},{2,1},{3,2},{4,7},{5,4},{6,5},{7,6},{8,11},{9,8},{10,9... | collective-permute-start | bytes 983048 | tf_op jit(solution)/shard_map/ppermute | solution.py:223
  24.8 8.7 %collective-permute-start.9 = (bf16[256,384]{1,0:T(8,128)(2,1)S(1)}, bf16[256,384]{1,0:T(8,128)(2,1)S(1)}, u32[]{:S(2)}, u32[]{:S(2)}) collective-permute-start(bf16[256,384]{1,0:T(8,128)(2,1)S(1)} %pad_maximum_fusion.1), channel_id=1, source_target_pairs={{0,8},{1,9},{2,10},{3,11},{4,12},{5,13},{6,14},{7,15},{8,32},{9,33... | collective-permute-start | bytes 589832 | tf_op jit(solution)/shard_map/ppermute | solution.py:223
  27.2 6.4 %collective-permute-start.8 = (bf16[256,384]{1,0:T(8,128)(2,1)S(1)}, bf16[256,384]{1,0:T(8,128)(2,1)S(1)}, u32[]{:S(2)}, u32[]{:S(2)}) collective-permute-start(bf16[256,384]{1,0:T(8,128)(2,1)S(1)} %get-tuple-element.64), channel_id=1, source_target_pairs={{0,16},{16,0},{1,17},{17,1},{2,18},{18,2},{3,19},{19,3},{4,20},{20... | collective-permute-start | bytes 589832 | tf_op jit(solution)/shard_map/ppermute | solution.py:208
  30.2 3.4 %collective-permute-start.7 = (bf16[256,384]{1,0:T(8,128)(2,1)S(1)}, bf16[256,384]{1,0:T(8,128)(2,1)S(1)}, u32[]{:S(2)}, u32[]{:S(2)}) collective-permute-start(bf16[256,384]{1,0:T(8,128)(2,1)S(1)} %get-tuple-element.65), channel_id=1, source_target_pairs={{0,16},{16,0},{1,17},{17,1},{2,18},{18,2},{3,19},{19,3},{4,20},{20... | collective-permute-start | bytes 589832 | tf_op jit(solution)/shard_map/ppermute | solution.py:208
  33.6 5.5 %collective-permute-start.13 = (bf16[256,384]{1,0:T(8,128)(2,1)S(1)}, bf16[256,384]{1,0:T(8,128)(2,1)S(1)}, u32[]{:S(2)}, u32[]{:S(2)}) collective-permute-start(bf16[256,384]{1,0:T(8,128)(2,1)S(1)} %collective-permute-done.9.refs_4_.refs_3_), channel_id=1, source_target_pairs={{0,16},{16,0},{1,17},{17,1},{2,18},{18,2},{3,19},{19,3},{4,20},{20... | collective-permute-start | bytes 589832 | tf_op jit(solution)/shard_map/ppermute | solution.py:208
  39.7 10.0 %collective-permute-start.15 = (bf16[512,256]{1,0:T(8,128)(2,1)S(1)}, bf16[512,256]{1,0:T(8,128)(2,1)S(1)}, u32[]{:S(2)}, u32[]{:S(2)}) collective-permute-start(bf16[512,256]{1,0:T(8,128)(2,1)S(1)} %tile.12), channel_id=1, source_target_pairs={{0,3},{1,0},{2,1},{3,2},{4,7},{5,4},{6,5},{7,6},{8,11},{9,8},{10,9... | collective-permute-start | bytes 786440 | tf_op jit(solution)/shard_map/ppermute | solution.py:223
  43.5 6.8 %collective-permute-start.14 = (bf16[512,256]{1,0:T(8,128)(2,1)S(1)}, bf16[512,256]{1,0:T(8,128)(2,1)S(1)}, u32[]{:S(2)}, u32[]{:S(2)}) collective-permute-start(bf16[512,256]{1,0:T(8,128)(2,1)S(1)} %tile.10), channel_id=1, source_target_pairs={{0,2},{1,3},{2,0},{3,1},{4,6},{5,7},{6,4},{7,5},{8,10},{9,11},{10,... | collective-permute-start | bytes 786440 | tf_op jit(solution)/shard_map/ppermute | solution.py:223
  46.7 6.8 %collective-permute-start.16 = (bf16[512,256]{1,0:T(8,128)(2,1)S(1)}, bf16[512,256]{1,0:T(8,128)(2,1)S(1)}, u32[]{:S(2)}, u32[]{:S(2)}) collective-permute-start(bf16[512,256]{1,0:T(8,128)(2,1)S(1)} %tile.13), channel_id=1, source_target_pairs={{0,1},{1,2},{2,3},{3,0},{4,5},{5,6},{6,7},{7,4},{8,9},{9,10},{10,1... | collective-permute-start | bytes 786440 | tf_op jit(solution)/shard_map/ppermute | solution.py:223
  64.8 16.8 %all-to-all-start.1 = ((bf16[16,32,256]{2,1,0:T(8,128)(2,1)}), bf16[16,32,256]{2,1,0:T(8,128)(2,1)S(1)}, u32[]{:S(2)}, u32[]{:S(2)}) async-start(bf16[16,32,256]{2,1,0:T(8,128)(2,1)} %sum_spread.2), calls=%async_computation.1 | async-start | bytes 524288 | tf_op jit(solution)/shard_map/all_to_all | solution.py:231
  72.0 5.3 %collective-permute-start.17 = (bf16[128,256]{1,0:T(8,128)(2,1)S(1)}, bf16[128,256]{1,0:T(8,128)(2,1)S(1)}, u32[]{:S(2)}, u32[]{:S(2)}) collective-permute-start(bf16[128,256]{1,0:T(8,128)(2,1)S(1)} %get-tuple-element.59), channel_id=1, source_target_pairs={{0,64},{1,65},{2,66},{3,67},{4,68},{5,69},{6,70},{7,71},{8,72},{9,... | collective-permute-start | bytes 196616 | tf_op jit(solution)/shard_map/ppermute | solution.py:223
  72.3 5.0 %collective-permute-start.18 = (bf16[128,256]{1,0:T(8,128)(2,1)S(1)}, bf16[128,256]{1,0:T(8,128)(2,1)S(1)}, u32[]{:S(2)}, u32[]{:S(2)}) collective-permute-start(bf16[128,256]{1,0:T(8,128)(2,1)S(1)} %get-tuple-element.60), channel_id=1, source_target_pairs={{0,128},{1,129},{2,130},{3,131},{4,132},{5,133},{6,134},{7,135},{8... | collective-permute-start | bytes 196616 | tf_op jit(solution)/shard_map/ppermute | solution.py:223
  73.6 4.2 %collective-permute-start.19 = (bf16[128,256]{1,0:T(8,128)(2,1)S(1)}, bf16[128,256]{1,0:T(8,128)(2,1)S(1)}, u32[]{:S(2)}, u32[]{:S(2)}) collective-permute-start(bf16[128,256]{1,0:T(8,128)(2,1)S(1)} %get-tuple-element.61), channel_id=1, source_target_pairs={{0,192},{1,193},{2,194},{3,195},{4,196},{5,197},{6,198},{7,199},{8... | collective-permute-start | bytes 196616 | tf_op jit(solution)/shard_map/ppermute | solution.py:223
